TPU v7x, 32 devices: a whole 2x2x4 slice. The times are simulated.
32 devices in a mesh: beam: 8 (over z, y), slab: 4 (over x, core).
Axes of the slice: x: 2, y: 2, z: 4, core: 2. Of those that a mesh axis runs over, the one named last changes fastest.
Arguments:
- pot_first: bfloat16 [4096, 4096], P('beam'), may hold values from -3.140625 to 3.140625
- pot_second: bfloat16 [4096, 4096], P('beam'), may hold values from -3.140625 to 3.140625
- beam_index: int32 [4, 2], replicated, may hold values from -3 to 3
- aberration: float32 [4], replicated, may hold values from -3.140625 to 3.140625
- tile_table: int32 [32, 4], replicated, may hold values from 0 to 4095, as said below
- tile_count: int32 [32], replicated, may hold values from 1 to 4, as said below
Outputs:
- detector_sums: float32 [32, 4, 3, 16], P(('beam', 'slab'))
Inputs may be any that keep to these rules, and one draw needn't show every extreme that they name: `tile_table`: group the blocks by the beam index of their device, block // 4; among the 16 slots of one group, active or not, exactly 2 name a tile of row band b, for every band b = ty // 8. The first tile_count[block] slots of a block are active; some block has all 4 active.
All inputs are finite; a program needn't handle non-finite values.
Results may differ from a plain program's by a relative error of at most 0.012.
The roundings to bfloat16 on the way count: a program that leaves them out, or rounds other values in their place, can miss the bound.
Values may be sent and summed in bfloat16 or wider, within the bound.
No kernel may reach another device: no remote copies, remote signals or barrier semaphores. Data moves between devices by JAX's collectives and lax.ppermute only.
A program may use at most 192 MiB of HBM per device.

v0:
```python
import math

import jax
import jax.numpy as jnp
from jax import lax
from jax.sharding import PartitionSpec as P

A = 64
N = 4096
F = 64
G = 3
NDET = 16


def rounded(values):
    return lax.optimization_barrier(values.astype(jnp.bfloat16)).astype(jnp.float32)


def radix_tables(factor):
    digits = jnp.arange(A, dtype=jnp.int32)
    product = digits[:, None] * digits[None, :] % A
    angles = 2.0 * math.pi / A * product.astype(jnp.float32)
    return (rounded(jnp.cos(angles)) * factor, rounded(jnp.sin(angles)) * factor)


def radix_block(orient, factor):
    cosine, sine_tab = radix_tables(factor)
    upper_half = jnp.concatenate([cosine, -orient * sine_tab], axis=1)
    lower_half = jnp.concatenate([orient * sine_tab, cosine], axis=1)
    return jnp.concatenate([upper_half, lower_half], axis=0).astype(jnp.bfloat16)


def paired_block():
    cosine, sine_tab = radix_tables(1.0 / A)
    blocks = jnp.stack(
        [jnp.stack([cosine, -sine_tab], axis=-1), jnp.stack([sine_tab, cosine], axis=-1)], axis=1
    )
    return blocks.reshape(2 * A, 2 * A).astype(jnp.bfloat16)


def twist_table(orient):
    digits = jnp.arange(A, dtype=jnp.int32)
    product = digits[:, None] * digits[None, :] % N
    angles = 2.0 * math.pi / N * product.astype(jnp.float32)
    return (jnp.cos(angles), orient * jnp.sin(angles))


def apply_twist(values, cosine, turned, part_axis):
    real_part = jnp.take(values, 0, axis=part_axis)
    imag_part = jnp.take(values, 1, axis=part_axis)
    stacked = jnp.stack(
        [real_part * cosine + imag_part * turned, imag_part * cosine - real_part * turned],
        axis=part_axis,
    )
    return stacked.astype(jnp.bfloat16)


def radix_section(values, table):
    flat = values.reshape(-1, table.shape[0])
    return jnp.dot(flat, table, preferred_element_type=jnp.float32).reshape(values.shape)


def coefficients(tile_ids, beam_rows, shifts):
    across = N // A
    offsets = jnp.arange(G, dtype=jnp.int32)
    spot_y = (tile_ids // across)[:, None] * A + A // 2 + offsets[None, :]
    spot_x = (tile_ids % across)[:, None] * A + A // 2 + 2 * offsets[None, :]
    wave_y = jnp.remainder(F * beam_rows[:, 0], N)[:, None, None]
    wave_x = jnp.remainder(F * beam_rows[:, 1], N)[:, None, None]
    windings = (wave_y * spot_y[None] % N + wave_x * spot_x[None] % N) % N
    phases = shifts[:, None, None] + 2.0 * math.pi / N * windings.astype(jnp.float32)
    return (jnp.cos(phases), -jnp.sin(phases))


def detector_weights(beam_total):
    digits = jnp.arange(A, dtype=jnp.int32)
    signed = jnp.where(digits < A // 2, digits, digits - A)
    radius = (signed[:, None] ** 2 + signed[None, :] ** 2).reshape(A * A)
    step_width = A // (2 * NDET)
    bin_index = jnp.arange(NDET, dtype=jnp.int32)
    member = (radius[:, None] >= (step_width * bin_index[None, :]) ** 2) & (
        radius[:, None] < (step_width * (bin_index[None, :] + 1)) ** 2
    )
    counts = jnp.sum(member.astype(jnp.float32), axis=0)
    return jnp.where(member, A * A / (beam_total * counts), 0.0)


def phase_pair(values):
    angles = -math.pi / N * (values % (2 * N)).astype(jnp.float32)
    return (jnp.cos(angles), jnp.sin(angles))


def shards(pot_first, pot_second, beam_index, aberration, tile_table, tile_count):
    field_count = lax.axis_size("beam")
    hold_count = lax.axis_size("slab")
    field_pos = lax.axis_index("beam")
    hold_pos = lax.axis_index("slab")
    band_rows = pot_first.shape[0]
    band_tiles = band_rows // A
    width_k = A // field_count
    across = N // A
    beam_total = beam_index.shape[0]
    local_count = beam_total // hold_count
    forward_tab = radix_block(1.0, 1.0 / A)
    inverse_tab = radix_block(-1.0, 1.0)
    fwd_cos, fwd_turn = twist_table(1.0)
    inv_cos, inv_turn = twist_table(-1.0)
    digits = jnp.arange(A, dtype=jnp.int32)
    row_ids = field_pos * band_rows + jnp.arange(band_rows, dtype=jnp.int32)
    columns = A * digits[None, :] + digits[:, None]
    first_pot = pot_first.astype(jnp.float32).reshape(band_rows, A, A).transpose(0, 2, 1)
    second_pot = pot_second.astype(jnp.float32).reshape(band_rows, A, A)
    freq_y = digits[:, None] + A * digits[None, :]
    freq_x = (
        field_pos * width_k + jnp.arange(width_k, dtype=jnp.int32)[:, None] + A * digits[None, :]
    )
    square_y = jnp.where(freq_y < N // 2, freq_y, freq_y - N) ** 2
    square_x = jnp.where(freq_x < N // 2, freq_x, freq_x - N) ** 2
    cos_y, sin_y = phase_pair(square_y)
    cos_x, sin_x = phase_pair(square_x)
    beam_row = lax.dynamic_index_in_dim(beam_index, hold_pos * local_count + 0, 0, keepdims=False)
    wave_y = jnp.remainder(F * beam_row[0], N)
    wave_x = jnp.remainder(F * beam_row[1], N)
    row_angles = 2.0 * math.pi / N * (wave_y * row_ids % N).astype(jnp.float32)
    col_angles = 2.0 * math.pi / N * (wave_x * columns % N).astype(jnp.float32)
    row_cos = jnp.cos(row_angles)[:, None, None]
    row_sin = jnp.sin(row_angles)[:, None, None]
    col_cos = jnp.cos(col_angles)[None]
    col_sin = jnp.sin(col_angles)[None]
    plane_cos = row_cos * col_cos - row_sin * col_sin
    plane_sin = row_sin * col_cos + row_cos * col_sin
    first_cos = jnp.cos(first_pot)
    first_sin = jnp.sin(first_pot)
    incident = jnp.stack(
        [
            plane_cos * first_cos - plane_sin * first_sin,
            plane_cos * first_sin + plane_sin * first_cos,
        ],
        axis=2,
    ).astype(jnp.bfloat16)
    sectioned = radix_section(incident.reshape(band_rows, A, 2 * A), forward_tab).reshape(
        band_rows, A, 2, A
    )
    sectioned = apply_twist(sectioned, fwd_cos, fwd_turn, 2)
    sectioned = sectioned.transpose(0, 3, 2, 1).reshape(band_rows, A, 2 * A)
    spectrum = radix_section(sectioned, forward_tab).astype(jnp.bfloat16)
    columns_all = lax.all_to_all(spectrum, "beam", split_axis=1, concat_axis=0, tiled=True)
    sectioned = (
        columns_all.reshape(A, A, width_k, 2, A)
        .transpose(1, 2, 4, 3, 0)
        .reshape(A, width_k, A, 2 * A)
    )
    sectioned = radix_section(sectioned, forward_tab).reshape(A, width_k, A, 2, A)
    sectioned = apply_twist(sectioned, fwd_cos[:, None, None, :], fwd_turn[:, None, None, :], 3)
    sectioned = sectioned.transpose(4, 1, 2, 3, 0).reshape(A, width_k, A, 2 * A)
    spectrum = radix_section(sectioned, forward_tab).reshape(A, width_k, A, 2, A)
    spec_real = spectrum[:, :, :, 0, :]
    spec_imag = spectrum[:, :, :, 1, :]
    inside = square_x[None, :, :, None] + square_y[:, None, None, :] <= (N // 3) ** 2
    prop_cos = jnp.where(
        inside,
        cos_x[None, :, :, None] * cos_y[:, None, None, :]
        - sin_x[None, :, :, None] * sin_y[:, None, None, :],
        0.0,
    )
    prop_sin = jnp.where(
        inside,
        sin_x[None, :, :, None] * cos_y[:, None, None, :]
        + cos_x[None, :, :, None] * sin_y[:, None, None, :],
        0.0,
    )
    shifted = jnp.stack(
        [spec_real * prop_cos - spec_imag * prop_sin, spec_real * prop_sin + spec_imag * prop_cos],
        axis=3,
    ).astype(jnp.bfloat16)
    sectioned = radix_section(shifted.reshape(A, width_k, A, 2 * A), inverse_tab).reshape(
        A, width_k, A, 2, A
    )
    sectioned = apply_twist(sectioned, inv_cos[:, None, None, :], inv_turn[:, None, None, :], 3)
    sectioned = sectioned.transpose(4, 1, 2, 3, 0).reshape(A, width_k, A, 2 * A)
    sectioned = (
        radix_section(sectioned, inverse_tab).reshape(A, width_k, A, 2, A).astype(jnp.bfloat16)
    )
    sectioned = sectioned.transpose(4, 0, 1, 3, 2).reshape(N, width_k, 2 * A)
    rows_back = lax.all_to_all(sectioned, "beam", split_axis=0, concat_axis=1, tiled=True)
    sectioned = radix_section(rows_back, inverse_tab).reshape(band_rows, A, 2, A)
    sectioned = apply_twist(sectioned, inv_cos, inv_turn, 2)
    sectioned = sectioned.transpose(0, 3, 2, 1).reshape(band_rows, A, 2 * A)
    field_wave = (
        radix_section(sectioned, inverse_tab).reshape(band_rows, A, 2, A).transpose(0, 3, 1, 2)
    )
    second_cos = jnp.cos(second_pot)
    second_sin = jnp.sin(second_pot)
    exit_real = field_wave[..., 0] * second_cos - field_wave[..., 1] * second_sin
    exit_imag = field_wave[..., 0] * second_sin + field_wave[..., 1] * second_cos
    exit_list = [jnp.stack([exit_real, exit_imag], axis=-1).reshape(band_tiles, A, A, 2 * A)]
    exit_all = jnp.stack(exit_list, axis=0)
    blocks_dev = tile_table.shape[0] // (field_count * hold_count)
    slot_count = tile_table.shape[1]
    share_slots = blocks_dev * slot_count
    length = hold_count * share_slots
    capacity = length // field_count
    owner_lists = tile_table.reshape(field_count, length)
    owner_band = owner_lists // across // band_tiles
    matched = (owner_band == field_pos).astype(jnp.int32)
    rank_all = jnp.cumsum(matched, axis=1) - 1
    picked = (matched[:, None, :] == 1) & (
        rank_all[:, None, :] == jnp.arange(capacity, dtype=jnp.int32)[None, :, None]
    )
    chosen = jnp.sum(jnp.where(picked, owner_lists[:, None, :], 0), axis=2)
    outgoing = exit_all[:, chosen // across - field_pos * band_tiles, :, chosen % across, :]
    received = lax.all_to_all(
        outgoing.astype(jnp.bfloat16), "beam", split_axis=0, concat_axis=0, tiled=True
    ).astype(outgoing.dtype)
    own_list = lax.dynamic_index_in_dim(owner_lists, field_pos, 0, keepdims=False)
    own_band = own_list // across // band_tiles
    band_ids = jnp.arange(field_count, dtype=jnp.int32)
    member = own_band[None, :] == band_ids[:, None]
    own_rank = jnp.sum(
        jnp.where(member, jnp.cumsum(member.astype(jnp.int32), axis=1) - 1, 0), axis=0
    )
    tiles_own = received.reshape(field_count * capacity, local_count, A, 2 * A)[
        own_band * capacity + own_rank
    ]
    highest = lax.Precision.HIGHEST
    local_rows = lax.dynamic_slice_in_dim(beam_index, hold_pos * local_count, local_count, 0)
    local_shift = lax.dynamic_slice_in_dim(aberration, hold_pos * local_count, local_count, 0)
    coef_cos, coef_sin = coefficients(own_list, local_rows, local_shift)
    tile_parts = tiles_own.reshape(length, local_count, A, A, 2)
    tile_real = tile_parts[..., 0]
    tile_imag = tile_parts[..., 1]
    pattern = "blg,lbyx->lgyx"
    partial_real = jnp.einsum(pattern, coef_cos, tile_real, precision=highest) - jnp.einsum(
        pattern, coef_sin, tile_imag, precision=highest
    )
    partial_imag = jnp.einsum(pattern, coef_cos, tile_imag, precision=highest) + jnp.einsum(
        pattern, coef_sin, tile_real, precision=highest
    )
    partial_value = jnp.stack([partial_real, partial_imag], axis=-1).reshape(length, G, A, 2 * A)
    probes = lax.psum_scatter(
        partial_value.astype(jnp.bfloat16), "slab", scatter_dimension=0, tiled=True
    )
    paired = paired_block()
    spectrum = radix_section(probes, paired).astype(jnp.bfloat16)
    spectrum = (
        spectrum.reshape(share_slots, G, A, A, 2)
        .transpose(0, 1, 3, 2, 4)
        .reshape(share_slots, G, A, 2 * A)
    )
    spectrum = radix_section(spectrum, paired).reshape(share_slots * G, A * A, 2)
    intensity = spectrum[..., 0] ** 2 + spectrum[..., 1] ** 2
    weights = detector_weights(beam_total)
    binned = jnp.dot(intensity, weights, precision=highest).reshape(blocks_dev, slot_count, G, NDET)
    first_block = (field_pos * hold_count + hold_pos) * blocks_dev
    counts = lax.dynamic_slice_in_dim(tile_count, first_block, blocks_dev, 0)
    active = jnp.arange(slot_count, dtype=jnp.int32)[None, :] < counts[:, None]
    return jnp.where(active[:, :, None, None], binned, 0.0)


def solution(mesh):
    return jax.shard_map(
        shards,
        mesh=mesh,
        in_specs=(P("beam", None), P("beam", None), P(), P(), P(), P()),
        out_specs=P(("beam", "slab"), None, None, None),
        check_vma=False,
    )
```

profile of v0, /device:TPU:0, one launch (start us, length us, event | category | flops | bytes accessed | tf_op | source)
XLA Modules:
  0.0 1107.7 jit_solution(18040382489499413891)
XLA Ops:
  6.5 0.7 copy-done
  10.0 6.5 copy.116
  16.5 31.7 %convert_sine_fusion.1 = (f32[512,4096]{0,1:T(8,128)}, f32[512,4096]{0,1:T(8,128)}) fusion(bf16[512,4096]{0,1:T(8,128)(2,1)} %copy.116), kind=kLoop, calls=%fused_computation.26 | loop fusion | flops 2097152 | bytes 20971520 | tf_op jit(solution)/shard_map/sin | solution.py:133
  48.6 10.1 fusion.20
  58.6 6.2 pad_maximum_fusion.4
  64.8 9.7 fusion.9
  74.6 4.0 fusion.16
  78.6 6.2 pad_maximum_fusion.5
  84.8 16.2 %fusion.13 = bf16[512,64,128]{2,0,1:T(8,128)(2,1)} fusion(bf16[512,64,128]{0,1,2:T(8,128)(2,1)} %bitcast.314, bf16[64,64]{1,0:T(8,128)(2,1)S(1)} %get-tuple-element.96, bf16[64,64]{1,0:T(8,128)(2,1)S(1)} %get-tuple-element.84, bf16[64,64]{1,0:T(8,128)(2,1)S(1)} %get-tuple-element.83), kind=kOutput, calls=%fused_computation.57 | convolution fusion | flops 1078067200 | bytes 16801792 | tf_op jit(solution)/shard_map/dot_general | solution.py:60
  100.9 7.6 all-to-all-start
  109.1 182.5 %all-to-all-done = bf16[512,64,128]{2,0,1:T(8,128)(2,1)} async-done(((bf16[512,64,128]{2,0,1:T(8,128)(2,1)}), bf16[512,64,128]{2,0,1:T(8,128)(2,1)}, u32[]{:S(2)}, u32[]{:S(2)}) %all-to-all-start) | async-done | bytes 8388640 | tf_op jit(solution)/shard_map/all_to_all | solution.py:147
  291.6 12.8 %copy.124 = bf16[512,8,8,128]{0,1,3,2:T(8,128)(2,1)} copy(bf16[512,8,8,128]{3,0,2,1:T(8,128)(2,1)} %bitcast.29) | data formatting | bytes 16777216 | tf_op jit(solution)/shard_map/all_to_all | solution.py:147
  304.3 21.2 %reshape.1092 = bf16[64,64,8,2,64]{1,0,4,3,2:T(8,128)(2,1)} reshape(bf16[8,512,8,128]{1,0,3,2:T(8,128)(2,1)} %bitcast.313) | data formatting | bytes 16777216 | tf_op jit(solution)/shard_map/reshape | solution.py:149
  325.6 43.0 %copy.125 = bf16[64,8,64,2,64]{4,3,2,1,0:T(2,128)(2,1)} copy(bf16[64,8,64,2,64]{0,4,2,3,1:T(8,128)(2,1)} %bitcast.305) | data formatting | bytes 16777216 | tf_op jit(solution)/shard_map/transpose | solution.py:150
  368.6 26.9 %reshape.1260 = bf16[64,8,64,128,1]{3,2,1,0,4:T(8,128)(2,1)} reshape(bf16[64,8,64,2,64]{4,3,2,1,0:T(2,128)(2,1)} %copy.125) | data formatting | bytes 16777216 | tf_op jit(solution)/shard_map/dot_general | solution.py:60
  395.5 19.0 %fusion.7 = f32[64,8,64,2,64]{4,2,3,1,0:T(8,128)} fusion(bf16[2,64,128,1,1]{2,1,0,4,3:T(8,128)(2,1)S(1)} %bitcast.326, bf16[64,8,64,128,1]{3,2,1,0,4:T(8,128)(2,1)} %reshape.1260), kind=kOutput, calls=%fused_computation.41 | convolution fusion | flops 1073741824 | bytes 25198592 | tf_op jit(solution)/shard_map/dot_general | solution.py:60
  414.5 12.3 %fusion.2 = (bf16[64,8,64,1,64]{4,2,1,0,3:T(8,128)(2,1)S(1)}, bf16[64,8,64,1,64]{4,2,1,0,3:T(8,128)(2,1)S(1)}) fusion(f32[64,8,64,2,64]{4,2,3,1,0:T(8,128)} %fusion.7, f32[64,64]{1,0:T(8,128)S(1)} %get-tuple-element.99, f32[64,64]{1,0:T(8,128)S(1)} %get-tuple-element.100), kind=kLoop, calls=%fused_computation.29 | loop fusion | flops 16777216 | bytes 25198592 | tf_op jit(solution)/shard_map/stack | solution.py:51
  426.8 7.9 pad_maximum_fusion
  434.7 28.1 %copy.159 = bf16[64,8,64,128,1]{3,2,4,1,0:T(8,128)(2,1)} copy(bf16[64,8,64,128,1]{0,2,1,3,4:T(8,128)(2,1)} %bitcast.303) | data formatting | bytes 16777216 | tf_op jit(solution)/shard_map/dot_general | solution.py:60
  462.8 19.0 %fusion.107 = f32[64,8,64,2,64]{4,2,3,1,0:T(8,128)} fusion(bf16[64,8,64,128,1]{3,2,4,1,0:T(8,128)(2,1)} %copy.159, bf16[2,64,128,1,1]{2,1,0,4,3:T(8,128)(2,1)S(1)} %bitcast.327), kind=kOutput, calls=%fused_computation.263 | convolution fusion | flops 1073741824 | bytes 25198592 | tf_op jit(solution)/shard_map/dot_general | solution.py:60
  481.8 17.8 %subtract_convert_fusion.1 = (bf16[64,8,64,1,64]{4,2,3,1,0:T(8,128)(2,1)S(1)}, bf16[64,8,64,1,64]{4,2,3,1,0:T(8,128)(2,1)}) fusion(f32[64,8,64,2,64]{4,2,3,1,0:T(8,128)} %fusion.107, f32[64,64]{1,0:T(8,128)S(1)} %get-tuple-element.93, f32[8,64]{1,0:T(8,128)S(1)} %get-tuple-element.89, f32[64,64]{1,0:T(8,128)S(1)} %get-tuple-element.92, ...), kind=kLoop, calls=%fused_computation.18 | loop fusion | flops 37748736 | bytes 25221120 | tf_op jit(solution)/shard_map/convert.26
  499.6 7.2 pad_maximum_fusion.1
  506.9 14.7 %copy.128 = bf16[64,8,64,2,64]{4,3,2,1,0:T(2,128)(2,1)} copy(bf16[64,8,64,2,64]{4,2,3,1,0:T(8,128)(2,1)S(1)} %pad_maximum_fusion.1) | data formatting | bytes 16777216 | tf_op jit(solution)/shard_map/stack | solution.py:172
  521.6 27.1 %reshape.1263 = bf16[64,8,64,128,1]{3,2,1,0,4:T(8,128)(2,1)} reshape(bf16[64,8,64,2,64]{4,3,2,1,0:T(2,128)(2,1)} %copy.128) | data formatting | bytes 16777216 | tf_op jit(solution)/shard_map/convert_element_type | solution.py:175
  548.7 19.0 %fusion.108 = f32[64,8,64,2,64]{4,2,1,0,3:T(8,128)} fusion(bf16[64,8,64,128,1]{3,2,1,0,4:T(8,128)(2,1)} %reshape.1263, bf16[2,64,128,1,1]{2,1,4,3,0:T(8,128)(2,1)S(1)} %bitcast.321), kind=kOutput, calls=%fused_computation.264 | convolution fusion | flops 1073741824 | bytes 25198592 | tf_op jit(solution)/shard_map/dot_general | solution.py:60
  567.7 12.2 %fusion.4 = (bf16[64,8,64,1,64]{4,2,1,0,3:T(8,128)(2,1)S(1)}, bf16[64,8,64,1,64]{4,2,1,0,3:T(8,128)(2,1)S(1)}) fusion(f32[64,8,64,2,64]{4,2,1,0,3:T(8,128)} %fusion.108, f32[64,64]{1,0:T(8,128)S(1)} %broadcast_multiply_fusion, f32[64,64]{1,0:T(8,128)S(1)} %get-tuple-element.100), kind=kLoop, calls=%fused_computation.31 | loop fusion | flops 16777216 | bytes 25198592 | tf_op jit(solution)/shard_map/stack | solution.py:51
  579.9 7.9 pad_maximum_fusion.2
  587.8 27.7 %copy.162 = bf16[64,8,64,128,1]{3,2,4,1,0:T(8,128)(2,1)} copy(bf16[64,8,64,128,1]{0,2,1,3,4:T(8,128)(2,1)} %bitcast.304) | data formatting | bytes 16777216 | tf_op jit(solution)/shard_map/dot_general | solution.py:60
  615.6 13.7 %convert_bitcast_fusion = bf16[64,64,8,2,64]{0,4,3,2,1:T(8,128)(2,1)} fusion(bf16[64,8,64,128,1]{3,2,4,1,0:T(8,128)(2,1)} %copy.162, bf16[2,64,128,1,1]{2,1,0,4,3:T(8,128)(2,1)S(1)} %bitcast.322), kind=kOutput, calls=%fused_computation.14 | convolution fusion | flops 1077936128 | bytes 16809984 | tf_op jit(solution)/shard_map/dot_general | solution.py:60
  629.2 43.0 %copy.177 = bf16[64,64,8,2,64]{4,3,2,1,0:T(2,128)(2,1)} copy(bf16[64,64,8,2,64]{0,4,3,2,1:T(8,128)(2,1)} %convert_bitcast_fusion) | data formatting | bytes 16777216 | tf_op jit(solution)/shard_map/reshape | solution.py:184
  672.2 27.3 %reshape.1273 = bf16[4096,8,128]{2,1,0:T(8,128)(2,1)} reshape(bf16[64,64,8,2,64]{4,3,2,1,0:T(2,128)(2,1)} %copy.177) | data formatting | bytes 16777216 | tf_op jit(solution)/shard_map/reshape | solution.py:184
  699.5 5.0 all-to-all-start.1
  704.5 6.5 copy.139
  712.0 31.8 %convert_cosine_fusion = (f32[512,4096]{0,1:T(8,128)}, f32[512,4096]{0,1:T(8,128)}) fusion(bf16[512,4096]{0,1:T(8,128)(2,1)} %copy.139), kind=kLoop, calls=%fused_computation.25 | loop fusion | flops 2097152 | bytes 20971520 | tf_op jit(solution)/shard_map/cos | solution.py:192
  743.8 142.9 %all-to-all-done.1 = bf16[4096,8,128]{2,1,0:T(8,128)(2,1)} async-done(((bf16[4096,8,128]{2,1,0:T(8,128)(2,1)}), bf16[4096,8,128]{2,1,0:T(8,128)(2,1)}, u32[]{:S(2)}, u32[]{:S(2)}) %all-to-all-start.1) | async-done | bytes 8388640 | tf_op jit(solution)/shard_map/all_to_all | solution.py:185
  886.7 8.9 copy.135
  895.6 5.7 fusion.109
  901.3 4.7 fusion.18
  906.0 7.6 pad_maximum_fusion.6
  913.7 15.6 %convolution_bitcast_fusion = f32[512,64,64,2]{0,1,3,2:T(8,128)} fusion(bf16[2,64,128,1]{2,1,0,3:T(8,128)(2,1)S(1)} %bitcast.324, bf16[512,64,128,1]{0,1,2,3:T(8,128)(2,1)} %bitcast.306), kind=kOutput, calls=%fused_computation.28 | convolution fusion | flops 1073741824 | bytes 25198592 | tf_op jit(solution)/shard_map/dot_general | solution.py:60
  929.3 21.0 %multiply_subtract_fusion = (bf16[512,64,64,1]{0,1,3,2:T(8,128)(2,1)}, bf16[512,64,64,1]{0,1,3,2:T(8,128)(2,1)}) fusion(f32[512,64,64,2]{0,1,3,2:T(8,128)} %convolution_bitcast_fusion, f32[512,64,64,1]{0,2,1,3:T(8,128)} %bitcast.312, f32[512,64,64,1]{0,2,1,3:T(8,128)S(1)} %bitcast.311), kind=kLoop, calls=%fused_computation.48 | loop fusion | flops 16777216 | bytes 41943040 | tf_op jit(solution)/shard_map/sub | solution.py:194
  950.3 7.5 pad_maximum_fusion.3
  957.8 21.2 %reshape.1225 = bf16[8,64,64,128]{1,0,2,3:T(8,128)(2,1)} reshape(bf16[512,64,64,2]{0,1,3,2:T(8,128)(2,1)} %pad_maximum_fusion.3) | data formatting | bytes 16777216 | tf_op jit(solution)/shard_map/stack;reshape | solution.py:197
  979.0 21.2 %copy.145 = bf16[8,64,64,128]{3,1,2,0:T(8,128)(2,1)} copy(bf16[8,64,64,128]{1,0,2,3:T(8,128)(2,1)} %reshape.1225) | data formatting | bytes 16777216 | tf_op jit(solution)/shard_map/stack;reshape | solution.py:197
  1000.2 4.7 gather_fusion
  1004.9 3.6 all-to-all-start.2
  1008.6 0.6 dynamic_slice.16
  1009.2 0.8 fusion.84
  1010.0 7.6 all-to-all-done.2
  1017.5 0.6 gather_fusion.1
  1020.1 1.6 copy.150
  1021.7 1.8 copy.151
  1023.7 1.1 copy.152
  1024.8 3.2 reshape.1269
  1028.1 3.2 convert_element_type.256
  1031.5 0.6 dynamic_slice.15
  1032.1 0.6 iota_compare_fusion.2
  1033.0 13.1 %reduce-scatter.2.cloned.1.call-done = bf16[4,3,64,128]{3,2,1,0:T(8,128)(2,1)} async-done(((bf16[16,3,64,128]{3,2,1,0:T(8,128)(2,1)}), bf16[4,3,64,128]{3,2,1,0:T(8,128)(2,1)}) %reduce-scatter.2.cloned.1.call-update) | async-done | bytes 196624 | tf_op jit(solution)/shard_map/reduce_scatter | solution.py:240
  1046.1 1.1 convolution_convert_fusion
  1047.4 0.7 copy.154
  1048.7 26.5 %reshape_reshape.5 = f32[12,4096,2]{2,1,0:T(8,128)} reshape(f32[768,128]{1,0:T(8,128)S(1)} %fusion.110) | data formatting | bytes 786432 | tf_op jit(solution)/shard_map/reshape;reshape | solution.py:250
  1075.2 23.7 %fusion.1 = f32[12,4096]{1,0:T(8,128)S(1)} fusion(f32[12,4096,2]{2,1,0:T(8,128)} %reshape_reshape.5), kind=kLoop, calls=%fused_computation.4 | loop fusion | flops 147456 | bytes 589824 | tf_op jit(solution)/shard_map/add | solution.py:251
  1099.1 0.9 fusion.22
  1100.0 0.6 copy.155
  (82 shorter events, 6.6 us)
Async XLA Ops:
  6.5 0.7 copy-start
  9.3 99.2 %copy-start.4 = (bf16[64,64]{1,0:T(8,128)(2,1)}, bf16[64,64]{1,0:T(8,128)(2,1)S(1)}, u32[]{:S(2)}) copy-start(bf16[64,64]{1,0:T(8,128)(2,1)S(1)} %cosine_convert_fusion) | copy-start | bytes 24580
  9.4 99.1 %copy-start.2 = (bf16[64,64]{1,0:T(8,128)(2,1)}, bf16[64,64]{1,0:T(8,128)(2,1)S(1)}, u32[]{:S(2)}) copy-start(bf16[64,64]{1,0:T(8,128)(2,1)S(1)} %sine_convert_fusion) | copy-start | bytes 24580
  100.9 190.6 %all-to-all-start = ((bf16[512,64,128]{2,0,1:T(8,128)(2,1)}), bf16[512,64,128]{2,0,1:T(8,128)(2,1)}, u32[]{:S(2)}, u32[]{:S(2)}) async-start(bf16[512,64,128]{2,0,1:T(8,128)(2,1)} %fusion.13), calls=%async_computation | async-start | bytes 16777216 | tf_op jit(solution)/shard_map/all_to_all | solution.py:147
  699.5 187.1 %all-to-all-start.1 = ((bf16[4096,8,128]{2,1,0:T(8,128)(2,1)}), bf16[4096,8,128]{2,1,0:T(8,128)(2,1)}, u32[]{:S(2)}, u32[]{:S(2)}) async-start(bf16[4096,8,128]{2,1,0:T(8,128)(2,1)} %reshape.1273), calls=%async_computation.1 | async-start | bytes 16777216 | tf_op jit(solution)/shard_map/all_to_all | solution.py:185
  704.5 6.5 copy-start.6
  906.0 23.2 %slice-start = ((s8[8388608]{0:T(1024)(128)(4,1)}), s8[4194304]{0:T(1024)(128)(4,1)S(1)}, s32[]{:S(2)}) async-start(s8[8388608]{0:T(1024)(128)(4,1)} %bitcast.309), calls=%async_computation.5 | async-start | bytes 8388608
  913.6 15.6 %slice-start.1 = ((s8[8388608]{0:T(1024)(128)(4,1)}), s8[4194304]{0:T(1024)(128)(4,1)S(1)}, s32[]{:S(2)}) async-start(s8[8388608]{0:T(1024)(128)(4,1)} %bitcast.309), calls=%async_computation.6 | async-start | bytes 8388608
  979.0 29.6 %copy-start.7 = (f32[4]{0:T(128)S(1)}, f32[4]{0:T(128)}, u32[]{:S(2)}) copy-start(f32[4]{0:T(128)} %param.17) | copy-start | bytes 52
  1004.9 12.7 %all-to-all-start.2 = ((bf16[8,2,1,64,128]{4,3,1,2,0:T(8,128)(2,1)}), bf16[8,2,1,64,128]{4,3,1,2,0:T(8,128)(2,1)S(1)}, u32[]{:S(2)}, u32[]{:S(2)}) async-start(bf16[8,2,1,64,128]{4,3,1,2,0:T(8,128)(2,1)} %bitcast.74), calls=%async_computation.2 | async-start | bytes 524288 | tf_op jit(solution)/shard_map/all_to_all | solution.py:212
  1008.5 37.6 %reduce-scatter.2.cloned.1.call-start = ((), (), s32[]{:S(2)}) async-start(), calls=%async_computation.4 | async-start | bytes 983040 | tf_op jit(solution)/shard_map/reduce_scatter | solution.py:240
  1018.2 5.5 copy-start.5
  1018.2 5.5 copy-start.3
  1019.8 11.7 %copy-start.8 = (s32[32]{0:T(128)S(1)}, s32[32]{0:T(128)}, u32[]{:S(2)}) copy-start(s32[32]{0:T(128)} %param.19) | copy-start | bytes 388
  1075.2 25.4 %copy-start.1 = (s32[4,2]{0,1:T(2,128)S(1)}, s32[4,2]{0,1:T(2,128)}, u32[]{:S(2)}) copy-start(s32[4,2]{0,1:T(2,128)} %param.16) | copy-start | bytes 100
Sparse Core Ops, SparseCore 0:
  1023.7 22.2 reduce-scatter.1
where the time goes:
time: 1120 us; the launch traced here: 1110 us
  local copies, waits for them, and re-layouts  385 us (34%)
  waiting for transfers between devices  346 us (31%)
  other arithmetic  225 us (20%)
  matrix products  120 us (11%)
  starting transfers between devices  16.2 us (1%)
  between operations  15.5 us (1%)
    all_to_all x1, waiting for transfers between devices, shards(): lax.all_to_all(spectrum, 'beam', split_axis=1, concat_axis=0, tiled=True)  182 us
    all_to_all x1, waiting for transfers between devices, shards(): lax.all_to_all(sectioned, 'beam', split_axis=0, concat_axis=1, tiled=True)  143 us
    dot_general x10, matrix products, radix_section(): jnp.dot(flat, table, preferred_element_type=jnp.float32)  119 us
    dot_general x5, local copies, waits for them, and re-layouts, radix_section(): jnp.dot(flat, table, preferred_element_type=jnp.float32)  83 us
    reshape x2, local copies, waits for them, and re-layouts, shards(): sectioned = sectioned.transpose(4, 0, 1, 3, 2).reshape(N, width_k, 2 * A)  70.3 us
    another operation x8, other arithmetic, apply_twist(): jnp.stack([real_part * cosine + imag_part * turned, imag_part * cosine -...  62.9 us
    transpose x1, local copies, waits for them, and re-layouts, shards(): sectioned = columns_all.reshape(A, A, width_k, 2, A).transpose(1, 2, 4, 3...  43 us
    another operation x2, local copies, waits for them, and re-layouts, shards(): exit_all = jnp.stack(exit_list, axis=0)  42.4 us
  transfers between devices with their start and end apart: 4, of which 4 were waited for; matrix products, arithmetic and copies ran while one was open for 5% of the time, Pallas kernels for 0%

commit v1 on v0

v1 whole, which is shorter than its diff:
```python
import functools
import math

import jax
import jax.numpy as jnp
import ml_dtypes
import numpy as np
from jax import lax
from jax.experimental import pallas as pl
from jax.experimental.pallas import tpu as pltpu
from jax.sharding import PartitionSpec as P

A = 64
N = 4096
F = 64
G = 3
NDET = 16
QMAX = 3
LIMIT = N // 3
K2_LOW = -(LIMIT // A + 1 + QMAX)
K2_COUNT = 2 * (LIMIT // A + 1 + QMAX)
PART = 104
ROWS = 2 * PART
LANES = 128
SUB = 16
HIGH = A // SUB
HALF = A // 2
PAIRS = A // 2
PARTS = 2
VMEM = 60 * 1024 * 1024
PITCH = A + 1
BF = jnp.bfloat16
F32 = jnp.float32


def low(values):
    return np.asarray(values, dtype=np.float32).astype(ml_dtypes.bfloat16)


def turn(numerator, period):
    return np.exp(2j * np.pi * (numerator % period) / period)


def digits_k2():
    return K2_LOW + np.arange(K2_COUNT)


def spread(table):
    both = np.stack([table.real, table.imag])
    eye = np.eye(SUB)
    out = both[:, :, None, :, None] * eye[None, None, :, None, :]
    return low(out.reshape(2 * table.shape[0] * SUB, table.shape[1] * SUB))


def real_rows(table):
    return np.block([[table.real, -table.imag], [table.imag, table.real]])


def section_forward(k1):
    n1 = np.arange(A)
    return spread(np.conj(turn(k1[:, None] * n1[None, :], A)) / A)


def last_forward_x(k1_pair):
    n2 = np.arange(A)
    out = np.zeros((2, PART, 2, 2, A))
    for ks, k1 in enumerate(k1_pair):
        freq = k1 + A * digits_k2()
        table = np.conj(turn(freq[:, None] * n2[None, :], N)) / A
        block = real_rows(table).reshape(2, K2_COUNT, 2, A)
        out[:, ks * K2_COUNT : (ks + 1) * K2_COUNT, ks] = block
    return low(out.reshape(ROWS, 4 * A))


def last_forward_y(k1_pair):
    n2 = np.arange(A)
    out = np.zeros((ROWS, 2, 2 * A))
    for e, k1 in enumerate(k1_pair):
        freq = k1 + A * digits_k2()
        table = np.conj(turn(freq[:, None] * n2[None, :], N)) / A
        out[e * 2 * K2_COUNT : (e + 1) * 2 * K2_COUNT, e] = real_rows(table)
    return low(out.reshape(ROWS, 4 * A))


def first_inverse(k1):
    n2 = np.arange(A)
    freq = k1 + A * digits_k2()
    return turn(n2[:, None] * freq[None, :], N) * np.conj(turn(freq * freq, 2 * N))[None, :]


def first_inverse_y(k1_pair):
    out = np.zeros((2, 2 * A, ROWS))
    for e, k1 in enumerate(k1_pair):
        out[e, :, e * 2 * K2_COUNT : (e + 1) * 2 * K2_COUNT] = real_rows(first_inverse(k1))
    return low(out.reshape(4 * A, ROWS))


def first_inverse_x(k1_pair):
    out = np.zeros((LANES, 2, 2, A))
    for ks, k1 in enumerate(k1_pair):
        table = first_inverse(k1).T
        out[ks * K2_COUNT : (ks + 1) * K2_COUNT, 0, ks] = table.real
        out[ks * K2_COUNT : (ks + 1) * K2_COUNT, 1, ks] = table.imag
    return low(out.reshape(LANES, 4 * A))


def sine_cosine(x):
    u = x * x
    s = F32(SIN_FIT[-1])
    for c in SIN_FIT[-2::-1]:
        s = s * u + F32(c)
    q = F32(COS_FIT[-1])
    for c in COS_FIT[-2::-1]:
        q = q * u + F32(c)
    return s * x, q


def fit(function, degree):
    top = 3.1421**2
    nodes = 0.5 * top * (1 - np.cos(np.pi * (np.arange(64) + 0.5) / 64))
    cheb = np.polynomial.chebyshev.Chebyshev.fit(
        nodes, function(np.sqrt(nodes)), degree, domain=[0, top]
    )
    return [float(c) for c in cheb.convert(kind=np.polynomial.Polynomial).coef]


SIN_FIT = fit(lambda x: np.sinc(x / np.pi), 5)
COS_FIT = fit(np.cos, 5)


def dot(a, b):
    return jnp.dot(a, b, preferred_element_type=F32)


def cost(micros):
    return pl.CostEstimate(flops=int(micros * 1.1e9), bytes_accessed=0, transcendentals=0)


def forward_x_kernel(sel, pot, section, last, *rest):
    *outs, cos_ref, sin_ref, twisted = rest
    fields = len(outs)
    lanes = cos_ref.shape[2]
    half = section.shape[1] // 2

    def chunk(t, carry):
        block = pot[:, 0, :, pl.ds(pl.multiple_of(t * LANES, LANES), LANES)]
        values = block.reshape(lanes, LANES).astype(F32).T
        sine, cosine = sine_cosine(values)
        cos_ref[pl.ds(2 * t, 2)] = cosine.astype(BF).reshape(2, A, lanes)
        sin_ref[pl.ds(2 * t, 2)] = sine.astype(BF).reshape(2, A, lanes)
        return carry

    lax.fori_loop(0, N // LANES, chunk, 0, unroll=4)
    table = section[0]
    for m in range(HIGH):
        span = slice(m * SUB, (m + 1) * SUB)
        part_cos = cos_ref[:, span, :].reshape(A * SUB, lanes)
        part_sin = sin_ref[:, span, :].reshape(A * SUB, lanes)
        if lanes % LANES == 0:
            both = dot(table, jnp.concatenate([part_cos, part_sin], axis=1))
            of_cos, of_sin = both[:, :lanes], both[:, lanes:]
        else:
            of_cos, of_sin = dot(table, part_cos), dot(table, part_sin)
        real = of_cos[:half] - of_sin[half:]
        imag = of_cos[half:] + of_sin[:half]
        twisted[:, m * SUB : (m + 1) * SUB, :] = real.astype(BF).reshape(2 * fields, SUB, lanes)
        twisted[:, A + m * SUB : A + (m + 1) * SUB, :] = imag.astype(BF).reshape(
            2 * fields, SUB, lanes
        )
    for o in range(fields):
        d = sel[1] ^ o
        lines = twisted[pl.ds(2 * d, 2)].reshape(4 * A, lanes)
        outs[o][0] = dot(last[0, d], lines).astype(BF)


def forward_x(sel, pot, section, last, fields, part):
    groups = pot.shape[0] // A
    lanes = groups * SUB
    steps = HIGH // PARTS
    return pl.pallas_call(
        forward_x_kernel,
        grid_spec=pltpu.PrefetchScalarGridSpec(
            num_scalar_prefetch=1,
            grid=(steps,),
            in_specs=[
                pl.BlockSpec((groups, 1, SUB, N), lambda i, s: (0, part * steps + i, 0, 0)),
                pl.BlockSpec((1,) + section.shape[1:], lambda i, s: (s[0], 0, 0)),
                pl.BlockSpec((1,) + last.shape[1:], lambda i, s: (s[0], 0, 0, 0)),
            ],
            out_specs=[pl.BlockSpec((1, ROWS, lanes), lambda i, s: (i, 0, 0))] * fields,
            scratch_shapes=[
                pltpu.VMEM((A, A, lanes), BF),
                pltpu.VMEM((A, A, lanes), BF),
                pltpu.VMEM((2 * fields, 2 * A, lanes), BF),
            ],
        ),
        out_shape=[jax.ShapeDtypeStruct((steps, ROWS, lanes), BF)] * fields,
        compiler_params=pltpu.CompilerParams(vmem_limit_bytes=VMEM),
        cost_estimate=cost(9),
        name="forward_x",
    )(sel, pot.reshape(groups, HIGH, SUB, N), section, last)


def section_step(sel, groups, section, gathered, twisted, start):
    chunk_rows = 16 * SUB
    for g, group in enumerate(groups):
        block = group[0].astype(F32)
        zeros = jnp.zeros((LANES - PART, LANES), F32)
        both = jnp.concatenate([block[:PART], zeros, block[PART:], zeros], axis=0)
        spot = pl.multiple_of(sel[g] * LANES, LANES)
        gathered[:, pl.ds(spot, LANES)] = both.astype(BF)
    values = gathered[...]
    for c in range(A // 16):
        rows = slice(c * chunk_rows, (c + 1) * chunk_rows)
        turned = slice(A * SUB + c * chunk_rows, A * SUB + (c + 1) * chunk_rows)
        dims = (((1,), (1,)), ((), ()))
        by_cos = lax.dot_general(section[rows, :], values, dims, preferred_element_type=F32)
        by_sin = lax.dot_general(section[turned, :], values, dims, preferred_element_type=F32)
        real = by_cos[:, :LANES] - by_sin[:, LANES:]
        imag = by_cos[:, LANES:] + by_sin[:, :LANES]
        spot = slice(c * 16, (c + 1) * 16)
        twisted[spot, 0, pl.ds(start, SUB), :] = real.astype(BF).reshape(16, SUB, LANES)
        twisted[spot, 1, pl.ds(start, SUB), :] = imag.astype(BF).reshape(16, SUB, LANES)


def forward_y_first_kernel(sel, *refs):
    *groups, section, twisted, gathered = refs
    start = pl.multiple_of(pl.program_id(0) * SUB, SUB)
    section_step(sel, groups, section, gathered, twisted, start)


def forward_y_first(sel, groups, section):
    steps = HIGH // PARTS
    return pl.pallas_call(
        forward_y_first_kernel,
        grid_spec=pltpu.PrefetchScalarGridSpec(
            num_scalar_prefetch=1,
            grid=(steps,),
            in_specs=[pl.BlockSpec((1, ROWS, LANES), lambda i, s: (i, 0, 0))] * len(groups)
            + [pl.BlockSpec(section.shape, lambda i, s: (0, 0))],
            out_specs=pl.BlockSpec((A, 2, A // PARTS, LANES), lambda i, s: (0, 0, 0, 0)),
            scratch_shapes=[pltpu.VMEM((2 * LANES, A * SUB), BF)],
        ),
        out_shape=jax.ShapeDtypeStruct((A, 2, A // PARTS, LANES), BF),
        compiler_params=pltpu.CompilerParams(vmem_limit_bytes=VMEM),
        cost_estimate=cost(4),
        name="forward_y_first",
    )(sel, *groups, section)


def forward_y_kernel(steps, sel, *refs):
    *groups, section, earlier, last, out, gathered, twisted = refs
    step = pl.program_id(0)
    first = HIGH // PARTS

    @pl.when(step < first)
    def _():
        start = pl.multiple_of(step * SUB, SUB)
        section_step(sel, groups, section, gathered, twisted, start)

    @pl.when(step >= first)
    def _():
        count = PAIRS // steps
        base = (step - first) * count
        for q in range(count):
            rows = []
            for e in range(2):
                for part in range(2):
                    rows.append(earlier[2 * (base + q) + e, part])
                    rows.append(twisted[2 * (base + q) + e, part])
            out[q] = dot(last[q], jnp.concatenate(rows, axis=0)).astype(BF)


def forward_y(sel, groups, section, earlier, last):
    steps = 2
    first = HIGH // PARTS
    count = PAIRS // steps

    def late(i, s):
        return (jnp.maximum(i - first, 0), 0, 0)

    return pl.pallas_call(
        functools.partial(forward_y_kernel, steps),
        grid_spec=pltpu.PrefetchScalarGridSpec(
            num_scalar_prefetch=1,
            grid=(first + steps,),
            in_specs=[
                pl.BlockSpec((1, ROWS, LANES), lambda i, s: (jnp.minimum(i, first - 1), 0, 0))
            ]
            * len(groups)
            + [
                pl.BlockSpec(section.shape, lambda i, s: (0, 0)),
                pl.BlockSpec(earlier.shape, lambda i, s: (0, 0, 0, 0)),
                pl.BlockSpec((count, ROWS, 4 * A), late),
            ],
            out_specs=pl.BlockSpec((count, ROWS, LANES), late),
            scratch_shapes=[
                pltpu.VMEM((2 * LANES, A * SUB), BF),
                pltpu.VMEM((A, 2, A // PARTS, LANES), BF),
            ],
        ),
        out_shape=jax.ShapeDtypeStruct((PAIRS, ROWS, LANES), BF),
        compiler_params=pltpu.CompilerParams(vmem_limit_bytes=VMEM),
        cost_estimate=cost(8),
        name="forward_y",
    )(sel, *groups, section, earlier, last)


def inverse_kernel(steps, sel, spec, freq_y, square_x, table_y, table_x, after, out, mid):
    step = pl.program_id(0)
    count = PAIRS // steps
    each = HALF // steps
    limit = F32(LIMIT * LIMIT)

    @pl.when(step < steps)
    def _():
        def pair(q, carry):
            pair_id = step * count + q
            offset = (2 * pair_id + sel[2]).astype(F32)
            row_freq = freq_y[...] + offset
            inside = row_freq * row_freq + square_x[...] <= limit
            values = jnp.where(inside, spec[q].astype(F32), 0.0).astype(BF)
            mixed = dot(table_y[q], values)
            for e in range(2):
                for part in range(2):
                    rows = slice((2 * e + part) * A, (2 * e + part + 1) * A)
                    spot = part * A * PITCH + 2 * pair_id + e
                    mid[pl.ds(spot, A, stride=PITCH), :] = mixed[rows]
            return carry

        lax.fori_loop(0, count, pair, 0, unroll=4)

    @pl.when(step >= steps)
    def _():
        def line(i, carry):
            by = (step - steps) * each + i
            rows = []
            for b in range(2):
                for part in range(2):
                    start = part * A * PITCH + (by + b * HALF) * PITCH
                    rows.append(mid[pl.ds(start, A), :].astype(BF))
            product = dot(jnp.concatenate(rows, axis=0), table_x[0, 0])
            for b in range(2):
                re = product[2 * b * A : (2 * b + 1) * A]
                im = product[(2 * b + 1) * A : (2 * b + 2) * A]
                span = slice(b * LANES, (b + 1) * LANES)
                out[i, :A, span] = (re[:, :LANES] - im[:, LANES:]).astype(BF)
                out[i, A:, span] = (re[:, LANES:] + im[:, :LANES]).astype(BF)
            return carry

        lax.fori_loop(0, each, line, 0, unroll=4)


def inverse(sel, spec, freq_y, square_x, table_y, table_x, after):
    steps = 2
    count = PAIRS // steps
    each = HALF // steps

    def early(i, s):
        return jnp.minimum(i, steps - 1)

    return pl.pallas_call(
        functools.partial(inverse_kernel, steps),
        grid_spec=pltpu.PrefetchScalarGridSpec(
            num_scalar_prefetch=1,
            grid=(2 * steps,),
            in_specs=[
                pl.BlockSpec((count, ROWS, LANES), lambda i, s: (early(i, s), 0, 0)),
                pl.BlockSpec((ROWS, LANES), lambda i, s: (0, 0)),
                pl.BlockSpec((1, LANES), lambda i, s: (0, 0)),
                pl.BlockSpec((count, 4 * A, ROWS), lambda i, s: (early(i, s), 0, 0)),
                pl.BlockSpec((1, 1) + table_x.shape[2:], lambda i, s: (s[0], s[1], 0, 0)),
                pl.BlockSpec(memory_space=pl.ANY),
            ],
            out_specs=pl.BlockSpec(
                (each, 2 * A, 2 * LANES), lambda i, s: (jnp.maximum(i - steps, 0), 0, 0)
            ),
            scratch_shapes=[pltpu.VMEM((2 * A * PITCH, LANES), F32)],
        ),
        out_shape=jax.ShapeDtypeStruct((HALF, 2 * A, 2 * LANES), BF),
        compiler_params=pltpu.CompilerParams(vmem_limit_bytes=VMEM),
        cost_estimate=cost(8.5),
        name="inverse",
    )(sel, spec, freq_y, square_x, table_y, table_x, after)


def collect_kernel(sheet_count, *refs):
    sheets, weights, outs = refs[:sheet_count], refs[sheet_count], refs[sheet_count + 1 :]
    tiles = weights.shape[0] // 4
    group = tiles // len(outs)
    lane = lax.broadcasted_iota(jnp.int32, (tiles, LANES), 1)
    lower = lane < A

    def line(i, carry):
        stacked = sheets[0][i]
        if len(sheets) > 1:
            stacked = jnp.concatenate([sheet[i] for sheet in sheets], axis=0)
        sums = dot(weights[...], stacked)
        for part in range(2):
            even = sums[2 * part * tiles : (2 * part + 1) * tiles]
            odd = sums[(2 * part + 1) * tiles : (2 * part + 2) * tiles]
            keep = jnp.where(lower, even[:, :LANES], odd[:, LANES:])
            move = jnp.where(lower, even[:, LANES:], odd[:, :LANES])
            total = (keep + pltpu.roll(move, A, 1)).astype(BF)
            for o, out in enumerate(outs):
                out[part, i] = total[o * group : (o + 1) * group]
        return carry

    lax.fori_loop(0, outs[0].shape[1], line, 0, unroll=2)


def collect(sheets, weights, fields, part):
    tiles = weights.shape[0] // 4
    group = tiles // fields
    lines = HALF // PARTS
    steps = 2
    each = lines // steps
    sheet_spec = pl.BlockSpec((each, 2 * A, 2 * LANES), lambda i: (part * steps + i, 0, 0))
    return pl.pallas_call(
        functools.partial(collect_kernel, len(sheets)),
        grid=(steps,),
        in_specs=[sheet_spec] * len(sheets) + [pl.BlockSpec(weights.shape, lambda i: (0, 0))],
        out_specs=[pl.BlockSpec((2, each, group, LANES), lambda i: (0, i, 0, 0))] * fields,
        out_shape=[jax.ShapeDtypeStruct((2, lines, group, LANES), BF)] * fields,
        compiler_params=pltpu.CompilerParams(vmem_limit_bytes=VMEM),
        cost_estimate=cost(6),
        name="collect",
    )(*sheets, weights)


def crop_kernel(rows, cols, odd, mine, pot, after, out, held, sems):
    slots = out.shape[0]

    def copy(i):
        return pltpu.make_async_copy(
            pot.at[
                pl.ds(pl.multiple_of(rows[i] * A, A), A),
                pl.ds(pl.multiple_of(cols[i] * LANES, LANES), LANES),
            ],
            held.at[i],
            sems.at[i],
        )

    def begin(i, carry):
        copy(i).start()
        return carry

    def finish(i, carry):
        copy(i).wait()
        block = held[i].astype(F32)
        block = jnp.where(odd[i] == 1, pltpu.roll(block, A, 1), block)
        lane = lax.broadcasted_iota(jnp.int32, (HALF, LANES), 1)
        packed = jnp.where(lane < A, block[:HALF], pltpu.roll(block[HALF:], A, 1))
        out[i] = jnp.where(mine[i] == 1, packed, 0.0).astype(BF)
        return carry

    lax.fori_loop(0, slots, begin, 0)
    lax.fori_loop(0, slots, finish, 0)


def crop(rows, cols, odd, mine, pot, after):
    slots = rows.shape[0]
    return pl.pallas_call(
        crop_kernel,
        in_specs=[pl.BlockSpec(memory_space=pltpu.SMEM)] * 4
        + [pl.BlockSpec(memory_space=pl.ANY)] * 2,
        out_specs=pl.BlockSpec(memory_space=pltpu.VMEM),
        out_shape=jax.ShapeDtypeStruct((slots, HALF, LANES), BF),
        scratch_shapes=[pltpu.VMEM((slots, A, LANES), BF), pltpu.SemaphoreType.DMA((slots,))],
        compiler_params=pltpu.CompilerParams(vmem_limit_bytes=VMEM),
        cost_estimate=cost(7),
        name="crop",
    )(rows, cols, odd, mine, pot, after)


def detect_kernel(alpha, counts, fields, pot, plane, across, down, bins, out, lines):
    beams, slots = fields.shape[0], fields.shape[1]
    for s in range(slots):
        waves = []
        for j in range(beams):
            re, im = fields[j, s, 0].astype(F32), fields[j, s, 1].astype(F32)
            cos, sin = plane[j, 0], plane[j, 1]
            waves.append((re * cos - im * sin, re * sin + im * cos))
        turned, level = sine_cosine(pot[s].astype(F32))
        for g in range(G):
            real = jnp.zeros((HALF, LANES), F32)
            imag = jnp.zeros((HALF, LANES), F32)
            for j in range(beams):
                cos, sin = alpha[0, j, s * G + g], alpha[1, j, s * G + g]
                re, im = waves[j]
                real = real + cos * re - sin * im
                imag = imag + cos * im + sin * re
            lines[2 * (s * G + g)] = (real * level - imag * turned).astype(BF)
            lines[2 * (s * G + g) + 1] = (real * turned + imag * level).astype(BF)
    total = slots * G
    first = dot(lines[...].reshape(2 * total * HALF, LANES), across[...])
    first = first.reshape(total, 2, HALF, 2 * LANES)
    real = (first[:, 0, :, :LANES] + first[:, 1, :, LANES:]).astype(BF)
    imag = (first[:, 1, :, :LANES] - first[:, 0, :, LANES:]).astype(BF)
    lane = lax.broadcasted_iota(jnp.int32, (A, LANES), 1)
    for i in range(total):
        both = jnp.concatenate([real[i], imag[i]], axis=1)
        mixed = dot(down[...], both)
        even, odd = mixed[: 2 * A], mixed[2 * A :]
        re_cos = even[:A, :LANES] + pltpu.roll(odd[:A, :LANES], A, 1)
        re_sin = even[A:, :LANES] + pltpu.roll(odd[A:, :LANES], A, 1)
        im_cos = even[:A, LANES:] + pltpu.roll(odd[:A, LANES:], A, 1)
        im_sin = even[A:, LANES:] + pltpu.roll(odd[A:, LANES:], A, 1)
        re = re_cos + im_sin
        im = im_cos - re_sin
        power = jnp.where(lane < A, re * re + im * im, 0.0)
        sums = jnp.sum(power[None] * bins[...], axis=1)
        block, slot = divmod(i // G, slots // counts.shape[0])
        active = slot < counts[block]
        out[i] = jnp.where(active, sums, 0.0)


def detect(alpha, counts, fields, pot, plane, across, down, bins):
    slots = fields.shape[1]
    smem = pl.BlockSpec(memory_space=pltpu.SMEM)
    vmem = pl.BlockSpec(memory_space=pltpu.VMEM)
    return pl.pallas_call(
        detect_kernel,
        in_specs=[smem, smem] + [vmem] * 6,
        out_specs=vmem,
        out_shape=jax.ShapeDtypeStruct((slots * G, NDET, LANES), F32),
        scratch_shapes=[pltpu.VMEM((2 * slots * G, HALF, LANES), BF)],
        compiler_params=pltpu.CompilerParams(vmem_limit_bytes=VMEM),
        name="detect",
    )(alpha, counts, fields, pot, plane, across, down, bins)


def detect_tables(beam_total):
    n = np.arange(A)
    table = turn(n[:, None] * n[None, :], A) / A
    cos, sin = table.real, table.imag
    zero = np.zeros((A, A))
    across = np.block([[cos, zero, sin, zero], [zero, cos, zero, sin]])
    rows = np.concatenate([cos, sin], axis=0)
    down = np.concatenate([rows[:, :HALF], rows[:, HALF:]], axis=0)
    signed = np.where(n < A // 2, n, n - A)
    radius = signed[:, None] ** 2 + signed[None, :] ** 2
    width = A // (2 * NDET)
    bins = np.zeros((NDET, A, LANES))
    for d in range(NDET):
        member = (radius >= (width * d) ** 2) & (radius < (width * (d + 1)) ** 2)
        bins[d, :, :A] = member * (A * A / (beam_total * member.sum()))
    return low(across), low(down), bins.astype(np.float32)


def coefficients(tile_ids, beam_rows, shifts):
    across = N // A
    offsets = jnp.arange(G, dtype=jnp.int32)
    spot_y = (tile_ids // across)[:, None] * A + A // 2 + offsets[None, :]
    spot_x = (tile_ids % across)[:, None] * A + A // 2 + 2 * offsets[None, :]
    wave_y = jnp.remainder(F * beam_rows[:, 0], N)[:, None, None]
    wave_x = jnp.remainder(F * beam_rows[:, 1], N)[:, None, None]
    windings = (wave_y * spot_y[None] % N + wave_x * spot_x[None] % N) % N
    phases = shifts[:, None, None] + 2.0 * math.pi / N * windings.astype(F32)
    return jnp.stack([jnp.cos(phases), -jnp.sin(phases)])


def tile_weights(tile_ids, beam_row, k1_pairs):
    across = N // A
    ty = tile_ids // across - beam_row[0]
    tx = tile_ids % across - beam_row[1]
    k1y = jnp.arange(A, dtype=jnp.int32)
    k1x = k1_pairs[:, None] + jnp.arange(2, dtype=jnp.int32)[None, :]
    winding = (
        k1y[None, None, None, :] * ty[None, :, None, None]
        + (k1x.T[:, None, :] * tx[None, :, None])[..., None]
    )
    angle = 2.0 * math.pi / A * (winding % A).astype(F32)
    cos, sin = jnp.cos(angle), jnp.sin(angle)
    upper = jnp.stack([cos, -sin], axis=3)
    under = jnp.stack([sin, cos], axis=3)
    both = jnp.stack([upper, under]).astype(BF)
    return both.reshape(4 * tile_ids.shape[0], k1_pairs.shape[0] * 2 * A)


def plane_waves(beam_index):
    by = jnp.arange(HALF, dtype=jnp.int32)[:, None] + HALF * (jnp.arange(LANES) // A)[None, :]
    bx = jnp.broadcast_to((jnp.arange(LANES, dtype=jnp.int32) % A)[None, :], by.shape)
    row_y = beam_index[:, 0][:, None, None]
    row_x = beam_index[:, 1][:, None, None]
    winding = (row_y * by[None] + row_x * bx[None] + HALF * (row_y + row_x)) % A
    angle = 2.0 * math.pi / A * winding.astype(F32)
    return jnp.stack([jnp.cos(angle), jnp.sin(angle)], axis=1)


def shards(pot_first, pot_second, beam_index, aberration, tile_table, tile_count):
    field_count = lax.axis_size("beam")
    hold_count = lax.axis_size("slab")
    field_pos = lax.axis_index("beam")
    hold_pos = lax.axis_index("slab")
    band_rows = pot_first.shape[0]
    band_tiles = band_rows // A
    width_k = A // field_count
    sheets = width_k // 2
    across = N // A
    beam_total = beam_index.shape[0]
    share = hold_pos % sheets

    section_x = np.stack(
        [
            section_forward(
                np.array(
                    [width_k * p + 2 * t + ks for p in range(field_count) for ks in range(2)]
                )
            )
            for t in range(sheets)
        ]
    )
    last_x = np.stack(
        [
            np.stack(
                [
                    last_forward_x([width_k * p + 2 * t, width_k * p + 2 * t + 1])
                    for p in range(field_count)
                ]
            )
            for t in range(sheets)
        ]
    )
    section_y = section_forward(np.arange(A))
    last_y = np.stack([last_forward_y([2 * q, 2 * q + 1]) for q in range(PAIRS)])
    inverse_y = np.stack([first_inverse_y([2 * q, 2 * q + 1]) for q in range(PAIRS)])
    inverse_x = np.stack(
        [
            np.stack(
                [
                    first_inverse_x([width_k * p + 2 * t, width_k * p + 2 * t + 1])
                    for t in range(sheets)
                ]
            )
            for p in range(field_count)
        ]
    )

    blocks_dev = tile_table.shape[0] // (field_count * hold_count)
    slot_count = tile_table.shape[1]
    own_slots = blocks_dev * slot_count
    table = tile_table.reshape(field_count, hold_count, own_slots)
    others = field_pos ^ jnp.arange(field_count, dtype=jnp.int32)
    mates = hold_pos ^ jnp.arange(hold_count, dtype=jnp.int32)

    def trade(arrays, axis, count):
        out = [arrays[0]]
        for o in range(1, count):
            out.append(lax.ppermute(arrays[o], axis, [(i, i ^ o) for i in range(count)]))
        return out

    sel = jnp.stack([share, field_pos]).astype(jnp.int32)
    received = []
    for part in range(PARTS):
        lines = forward_x(sel, pot_first, section_x, last_x, field_count, part)
        lines = trade(lines, "beam", field_count)
        if lines[0].shape[2] != LANES:
            ratio = LANES // lines[0].shape[2]
            stacked = jnp.stack(lines)[others]
            stacked = stacked.reshape((field_count // ratio, ratio) + lines[0].shape)
            stacked = stacked.transpose(0, 2, 3, 1, 4).reshape(
                field_count // ratio, lines[0].shape[0], ROWS, LANES
            )
            lines = [stacked[g] for g in range(stacked.shape[0])]
            places = jnp.arange(len(lines), dtype=jnp.int32)
        else:
            places = others
        received.append(lines)
    earlier = forward_y_first(places, received[0], section_y)
    spec = forward_y(places, received[1], section_y, earlier, last_y)
    specs = [spec]
    for x in range(1, sheets):
        top = 1 << (x.bit_length() - 1)
        bit, source = (top, 0) if x == top else (x ^ top, top)
        swap = [(i, i ^ bit) for i in range(hold_count)]
        specs.append(lax.ppermute(specs[source], "slab", swap))

    ids = lax.dynamic_index_in_dim(table, hold_pos, 1, keepdims=False)[others].reshape(-1)
    tile_y, tile_x = ids // across, ids % across
    mine = (tile_y // band_tiles == field_pos).astype(jnp.int32)
    rows = jnp.clip(tile_y - field_pos * band_tiles, 0, band_tiles - 1)
    crops = crop(rows, tile_x // 2, tile_x % 2, mine, pot_second, spec)
    crops = crops.reshape(field_count, own_slots, HALF, LANES)
    crops = trade([crops[o] for o in range(field_count)], "beam", field_count)
    crop_total = functools.reduce(jnp.add, [c.astype(F32) for c in crops]).astype(BF)

    beam_row = lax.dynamic_index_in_dim(beam_index, hold_pos, 0, keepdims=False)
    pair_ids = share ^ jnp.arange(sheets, dtype=jnp.int32)
    k1_pairs = field_pos * width_k + 2 * pair_ids
    ordered = table[others][:, mates].reshape(-1)
    weights = tile_weights(ordered, beam_row, k1_pairs)
    row = np.arange(ROWS)
    base = (row // (2 * K2_COUNT)) + A * (K2_LOW + row % K2_COUNT)
    base = np.where(row < 4 * K2_COUNT, base, 0)
    freq_y = np.broadcast_to(base[:, None], (ROWS, LANES)).astype(np.float32)
    lane = jnp.arange(LANES, dtype=jnp.int32)[None, None, :]
    freq_x = (
        k1_pairs[:, None, None]
        + lane // K2_COUNT
        + A * (K2_LOW + lane % K2_COUNT)
        + F * beam_row[1]
    )
    square_x = jnp.where(lane < 2 * K2_COUNT, freq_x * freq_x, N * N).astype(F32)
    waves = []
    for x in range(sheets):
        sel = jnp.stack([field_pos, pair_ids[x], F * beam_row[0]]).astype(jnp.int32)
        after = crops[0] if x >= 2 else spec
        waves.append(inverse(sel, specs[x], freq_y, square_x[x], inverse_y, inverse_x, after))
    halves = []
    for part in range(PARTS):
        partial = trade(collect(waves, weights, field_count, part), "beam", field_count)
        total = functools.reduce(jnp.add, [t.astype(F32) for t in partial])
        halves.append(total.astype(BF).transpose(2, 0, 1, 3))
    tiles = jnp.concatenate(halves, axis=2).reshape(hold_count, own_slots, 2, HALF, LANES)
    fields = jnp.stack(trade([tiles[x] for x in range(hold_count)], "slab", hold_count))

    own = lax.dynamic_index_in_dim(
        lax.dynamic_index_in_dim(table, field_pos, 0, keepdims=False), hold_pos, 0, keepdims=False
    )
    beams = beam_index[mates]
    alpha = coefficients(own, beams, aberration[mates]).reshape(2, beam_total, own_slots * G)
    first_block = (field_pos * hold_count + hold_pos) * blocks_dev
    counts = lax.dynamic_slice_in_dim(tile_count, first_block, blocks_dev, 0)
    bins = detect_tables(beam_total)
    sums = detect(alpha, counts, fields, crop_total, plane_waves(beams), *bins)
    return jnp.sum(sums, axis=2).reshape(blocks_dev, slot_count, G, NDET)


def solution(mesh):
    return jax.shard_map(
        shards,
        mesh=mesh,
        in_specs=(P("beam", None), P("beam", None), P(), P(), P(), P()),
        out_specs=P(("beam", "slab"), None, None, None),
        check_vma=False,
    )
```

time: 1120 us -> 239 us (0.21); the launches traced: 1110 us -> 238 us
  local copies, waits for them, and re-layouts: 385 us -> 21.3 us
  waiting for transfers between devices: 346 us -> 30.5 us
  other arithmetic: 225 us -> 15.1 us
  matrix products: 120 us -> 0 us
  Pallas kernels: 0 us -> 97.6 us
  starting transfers between devices: 16.2 us -> 71.4 us
  between operations: 15.5 us -> 1.99 us
    all_to_all x3 -> x0, waiting for transfers between devices: 333 us -> none  [the longest x1 182 us: shards(): lax.all_to_all(spectrum, 'beam', split_axis=1, concat_axis=0, tiled=True)]
    dot_general x11 -> x0, matrix products: 120 us -> none  [the longest x10 119 us: radix_section(): jnp.dot(flat, table, preferred_element_type=jnp.float32)]
    another operation x22 -> x9, other arithmetic: 113 us -> 7.6 us  [the longest x2 3.81 us: shards(): sel = jnp.stack([field_pos, pair_ids[x], F * beam_row[0]]).astype(jnp.int32)]
    pallas_call x0 -> x12, Pallas kernels: none -> 97.6 us  [the longest x4 33.7 us: inverse(): pl.pallas_call(functools.partial(inverse_kernel, steps), grid_spec=pltpu....]
    reshape x4 -> x6, local copies, waits for them, and re-layouts: 91.6 us -> 1.01 us  [the longest x2 0.61 us: shards(): return jnp.sum(sums, axis=2).reshape(blocks_dev, slot_count, G, NDET)]
    another operation x8 -> x0, local copies, waits for them, and re-layouts: 86.1 us -> none  [the longest x2 42.4 us: shards(): exit_all = jnp.stack(exit_list, axis=0)]
    dot_general x5 -> x0, local copies, waits for them, and re-layouts: 83 us -> none  [radix_section(): jnp.dot(flat, table, preferred_element_type=jnp.float32)]
    ppermute x0 -> x41, starting transfers between devices: none -> 71.4 us  [the longest x38 69.9 us: trade(): lax.ppermute(arrays[o], axis, [(i, i ^ o) for i in range(count)])]
  transfers between devices with their start and end apart: 4 -> 41, of which waited for: 4 -> 7; matrix products, arithmetic and copies ran while one was open for 5% -> 13% of each run, Pallas kernels for 0% -> 24%
where the time goes in v1:
time: 239 us; the launch traced here: 238 us
  Pallas kernels  97.6 us (41%)
  starting transfers between devices  71.4 us (30%)
  waiting for transfers between devices  30.5 us (13%)
  local copies, waits for them, and re-layouts  21.3 us (9%)
  other arithmetic  15.1 us (6%)
    ppermute x38, starting transfers between devices, trade(): lax.ppermute(arrays[o], axis, [(i, i ^ o) for i in range(count)])  69.9 us
    pallas_call x4, Pallas kernels, inverse(): pl.pallas_call(functools.partial(inverse_kernel, steps), grid_spec=pltpu....  33.7 us
    pallas_call x2, Pallas kernels, forward_x(): pl.pallas_call(forward_x_kernel, grid_spec=pltpu.PrefetchScalarGridSpec(n...  22 us
    ppermute x3, waiting for transfers between devices, shards(): specs.append(lax.ppermute(specs[source], 'slab', swap))  15.9 us
    ppermute x38, waiting for transfers between devices, trade(): lax.ppermute(arrays[o], axis, [(i, i ^ o) for i in range(count)])  14.5 us
    pallas_call x2, Pallas kernels, collect(): pl.pallas_call(functools.partial(collect_kernel, len(sheets)), grid=(step...  13.9 us
    pallas_call x1, Pallas kernels, forward_y(): pl.pallas_call(functools.partial(forward_y_kernel, steps), grid_spec=pltp...  9.97 us
    pallas_call x14, local copies, waits for them, and re-layouts, collect(): pl.pallas_call(functools.partial(collect_kernel, len(sheets)), grid=(step...  7.73 us
  transfers between devices with their start and end apart: 41, of which 7 were waited for; matrix products, arithmetic and copies ran while one was open for 13% of the time, Pallas kernels for 24%

profile of v1, /device:TPU:0, one launch (start us, length us, event | category | flops | bytes accessed | tf_op | source)
XLA Modules:
  0.0 237.9 jit_solution(593961439060782233)
XLA Ops:
  0.6 11.0 %forward_x.3 = (bf16[2,208,128]{2,1,0:T(8,128)(2,1)}, bf16[2,208,128]{2,1,0:T(8,128)(2,1)}, bf16[2,208,128]{2,1,0:T(8,128)(2,1)}, bf16[2,208,128]{2,1,0:T(8,128)...) custom-call(s32[2]{0:T(128)} %pad_add_fusion.sel, ...), custom_call_target="tpu_custom_call" | custom-call | flops 9900000256 | tf_op jit(solution)/shard_map/forward_x/pallas_call | solution.py:180
  11.6 4.1 %collective-permute-start.10 = (bf16[2,208,128]{2,1,0:T(8,128)(2,1)}, bf16[2,208,128]{2,1,0:T(8,128)(2,1)S(1)}, u32[]{:S(2)}, u32[]{:S(2)}) collective-permute-start(bf16[2,208,128]{2,1,0:T(8,128)(2,1)} %get-tuple-element.49), channel_id=1, source_target_pairs={{0,16},{4,20},{8,24},{12,28},{16,0},{20,4},{24,8},{28,12},{1,17},{... | collective-permute-start | bytes 319496 | tf_op jit(solution)/shard_map/ppermute | solution.py:650
  15.7 1.3 collective-permute-start.11
  17.0 3.6 %collective-permute-start.12 = (bf16[2,208,128]{2,1,0:T(8,128)(2,1)}, bf16[2,208,128]{2,1,0:T(8,128)(2,1)S(1)}, u32[]{:S(2)}, u32[]{:S(2)}) collective-permute-start(bf16[2,208,128]{2,1,0:T(8,128)(2,1)} %get-tuple-element.51), channel_id=1, source_target_pairs={{0,24},{4,28},{8,16},{12,20},{16,8},{20,12},{24,0},{28,4},{1,25},{... | collective-permute-start | bytes 319496 | tf_op jit(solution)/shard_map/ppermute | solution.py:650
  20.6 1.7 collective-permute-start.7
  22.3 11.0 %forward_x.2 = (bf16[2,208,128]{2,1,0:T(8,128)(2,1)}, bf16[2,208,128]{2,1,0:T(8,128)(2,1)}, bf16[2,208,128]{2,1,0:T(8,128)(2,1)}, bf16[2,208,128]{2,1,0:T(8,128)...) custom-call(s32[2]{0:T(128)} %pad_add_fusion.sel, ...), custom_call_target="tpu_custom_call" | custom-call | flops 9900000256 | tf_op jit(solution)/shard_map/forward_x/pallas_call | solution.py:180
  41.4 1.3 fusion.34
  42.9 1.1 negate_convert_fusion
  45.0 1.4 reshape.948.refs_4_
  48.6 1.9 add_add_fusion.2
  51.0 1.9 add_add_fusion
  53.0 1.8 collective-permute-start.9
  54.9 1.7 collective-permute-start
  57.3 1.8 collective-permute-start.2
  59.1 2.5 %collective-permute-start.3 = (bf16[2,208,128]{2,1,0:T(8,128)(2,1)S(1)}, bf16[2,208,128]{2,1,0:T(8,128)(2,1)S(1)}, u32[]{:S(2)}, u32[]{:S(2)}) collective-permute-start(bf16[2,208,128]{2,1,0:T(8,128)(2,1)S(1)} %copy-done.19), channel_id=1, source_target_pairs={{0,16},{4,20},{8,24},{12,28},{16,0},{20,4},{24,8},{28,12},{1,17},{... | collective-permute-start | bytes 319496 | tf_op jit(solution)/shard_map/ppermute | solution.py:650
  61.6 2.6 %collective-permute-start.4 = (bf16[2,208,128]{2,1,0:T(8,128)(2,1)S(1)}, bf16[2,208,128]{2,1,0:T(8,128)(2,1)S(1)}, u32[]{:S(2)}, u32[]{:S(2)}) collective-permute-start(bf16[2,208,128]{2,1,0:T(8,128)(2,1)S(1)} %copy-done.17), channel_id=1, source_target_pairs={{0,20},{4,16},{8,28},{12,24},{16,4},{20,0},{24,12},{28,8},{1,21},{... | collective-permute-start | bytes 319496 | tf_op jit(solution)/shard_map/ppermute | solution.py:650
  64.2 2.7 %collective-permute-start.5 = (bf16[2,208,128]{2,1,0:T(8,128)(2,1)S(1)}, bf16[2,208,128]{2,1,0:T(8,128)(2,1)S(1)}, u32[]{:S(2)}, u32[]{:S(2)}) collective-permute-start(bf16[2,208,128]{2,1,0:T(8,128)(2,1)S(1)} %copy-done.15), channel_id=1, source_target_pairs={{0,24},{4,28},{8,16},{12,20},{16,8},{20,12},{24,0},{28,4},{1,25},{... | collective-permute-start | bytes 319496 | tf_op jit(solution)/shard_map/ppermute | solution.py:650
  67.0 1.9 collective-permute-start.6
  68.9 7.0 %forward_y_first.1.refs_9_ = bf16[64,2,32,128]{3,2,1,0:T(8,128)(2,1)} custom-call(s32[8]{0:T(128)} %iota_xor_fusion.sel, bf16[2,208,128]{2,1,0:T(8,128)(2,1)} %get-tuple-element.45.refs_0_, bf16[2,208,128]{2,1,0:T(8,128)(2,1)} %copy-done.20, bf16[2,208,128]{2,1,0:T(8,128)(2,1)} %copy-done.28, bf16[2,208,128]{2,1,0:T(8,128)(2,1)} %copy-done.30, ...), custom_call_target="tpu_custom_call" | custom-call | flops 4400000000 | tf_op jit(solution)/shard_map/forward_y_first/pallas_call | solution.py:234
  76.0 1.9 collective-permute-done.4.refs_5_
  78.7 10.0 %forward_y.1.spec.after = bf16[32,208,128]{2,1,0:T(8,128)(2,1)} custom-call(s32[8]{0:T(128)} %iota_xor_fusion.sel, bf16[2,208,128]{2,1,0:T(8,128)(2,1)} %get-tuple-element.37.refs_0_, bf16[2,208,128]{2,1,0:T(8,128)(2,1)} %copy-done.26, bf16[2,208,128]{2,1,0:T(8,128)(2,1)} %copy-done.27, bf16[2,208,128]{2,1,0:T(8,128)(2,1)} %copy-done.29, ...), custom_call_target="tpu_custom_call" | custom-call | flops 8800000000 | tf_op jit(solution)/shard_map/forward_y/pallas_call | solution.py:282
  88.7 1.5 collective-permute-start.15
  90.1 7.1 %crop.1 = bf16[32,32,128]{2,1,0:T(8,128)(2,1)} custom-call(s32[32]{0:T(128)} %subtract_clamp_fusion.rows, s32[32]{0:T(128)} %and_select_fusion.6.cols, s32[32]{0:T(128)} %get-tuple-element.74.odd, s32[32]{0:T(128)} %get-tuple-element.71.mine, bf16[512,4096]{1,0:T(8,128)(2,1)} %pot.1, bf16[32,208,128]{2,1,0:T(8,128)(2,1)} %forward_y.1.spec.after), custom_call_target="tpu_custom_call" | custom-call | flops 7699999744 | tf_op jit(solution)/shard_map/crop/pallas_call | solution.py:463
  97.2 1.5 fusion.36
  98.7 8.4 %inverse.4.refs_0_ = bf16[32,128,256]{2,1,0:T(8,128)(2,1)} custom-call(s32[3]{0:T(128)} %get-tuple-element.118.sel, bf16[32,208,128]{2,1,0:T(8,128)(2,1)} %forward_y.1.spec.after, f32[208,128]{1,0:T(8,128)} %constant.279.clone.freq_y, f32[1,128]{1,0:T(1,128)} %get-tuple-element.100.square_x, bf16[32,256,208]{2,1,0:T(8,128)(2,1)} %constant.280.clone.table_y, ...), custom_call_target="tpu_custom_call" | custom-call | flops 9349999616 | tf_op jit(solution)/shard_map/inverse/pallas_call | solution.py:362
  107.2 15.9 %collective-permute-done.15.spec = bf16[32,208,128]{2,1,0:T(8,128)(2,1)S(1)} collective-permute-done((bf16[32,208,128]{2,1,0:T(8,128)(2,1)}, bf16[32,208,128]{2,1,0:T(8,128)(2,1)S(1)}, u32[]{:S(2)}, u32[]{:S(2)}) %collective-permute-start.15) | collective-permute-done | bytes 1703968 | tf_op jit(solution)/shard_map/ppermute | solution.py:677
  123.1 1.2 copy-done.11
  124.3 8.4 %inverse.6.refs_2_ = bf16[32,128,256]{2,1,0:T(8,128)(2,1)} custom-call(s32[3]{0:T(128)} %get-tuple-element.120.sel, bf16[32,208,128]{2,1,0:T(8,128)(2,1)} %copy-done.11, f32[208,128]{1,0:T(8,128)} %constant.279.clone.freq_y, f32[1,128]{1,0:T(1,128)} %get-tuple-element.98.square_x, bf16[32,256,208]{2,1,0:T(8,128)(2,1)} %constant.280.clone.table_y, ...), custom_call_target="tpu_custom_call" | custom-call | flops 9349999616 | tf_op jit(solution)/shard_map/inverse/pallas_call | solution.py:362
  132.7 8.4 %inverse.5.refs_1_ = bf16[32,128,256]{2,1,0:T(8,128)(2,1)} custom-call(s32[3]{0:T(128)} %get-tuple-element.119.sel, bf16[32,208,128]{2,1,0:T(8,128)(2,1)} %collective-permute-done.14.spec, f32[208,128]{1,0:T(8,128)} %constant.279.clone.freq_y, f32[1,128]{1,0:T(1,128)} %get-tuple-element.99.square_x, bf16[32,256,208]{2,1,0:T(8,128)(2,1)} %constant.280.clone.table_y, ...), custom_call_target="tpu_custom_call" | custom-call | flops 9349999616 | tf_op jit(solution)/shard_map/inverse/pallas_call | solution.py:362
  141.1 8.5 %inverse.7.refs_3_ = bf16[32,128,256]{2,1,0:T(8,128)(2,1)} custom-call(s32[3]{0:T(128)} %get-tuple-element.121.sel, bf16[32,208,128]{2,1,0:T(8,128)(2,1)} %collective-permute-done.16.spec, f32[208,128]{1,0:T(8,128)} %constant.279.clone.freq_y, f32[1,128]{1,0:T(1,128)} %get-tuple-element.97.square_x, bf16[32,256,208]{2,1,0:T(8,128)(2,1)} %constant.280.clone.table_y, ...), custom_call_target="tpu_custom_call" | custom-call | flops 9349999616 | tf_op jit(solution)/shard_map/inverse/pallas_call | solution.py:362
  149.6 7.0 %collect.3 = (bf16[2,16,16,128]{3,2,1,0:T(8,128)(2,1)}, bf16[2,16,16,128]{3,2,1,0:T(8,128)(2,1)}, bf16[2,16,16,128]{3,2,1,0:T(8,128)(2,1)}, bf16[2,16,16,128]{3,...) custom-call(bf16[32,128,256]{2,1,0:T(8,128)(2,1)} %inverse.4.refs_0_, ...), custom_call_target="tpu_custom_call" | custom-call | flops 6600000000 | tf_op jit(solution)/shard_map/collect/pallas_call | solution.py:419
  156.6 0.9 copy.78
  157.6 0.9 collective-permute-start.24
  158.5 0.9 copy.79
  159.5 6.6 %collective-permute-start.25 = (bf16[2,16,16,128]{3,1,0,2:T(8,128)(2,1)S(1)}, bf16[2,16,16,128]{3,1,0,2:T(8,128)(2,1)S(1)}, u32[]{:S(2)}, u32[]{:S(2)}) collective-permute-start(bf16[2,16,16,128]{3,1,0,2:T(8,128)(2,1)S(1)} %copy.79), channel_id=1, source_target_pairs={{0,8},{4,12},{8,0},{12,4},{16,24},{20,28},{24,16},{28,20},{1,9},{5... | collective-permute-start | bytes 393224 | tf_op jit(solution)/shard_map/ppermute | solution.py:650
  166.0 0.9 copy.80
  167.0 0.9 copy.81
  168.0 2.6 %collective-permute-start.27 = (bf16[2,16,16,128]{3,1,0,2:T(8,128)(2,1)S(1)}, bf16[2,16,16,128]{3,1,0,2:T(8,128)(2,1)S(1)}, u32[]{:S(2)}, u32[]{:S(2)}) collective-permute-start(bf16[2,16,16,128]{3,1,0,2:T(8,128)(2,1)S(1)} %copy.81), channel_id=1, source_target_pairs={{0,16},{4,20},{8,24},{12,28},{16,0},{20,4},{24,8},{28,12},{1,17},{... | collective-permute-start | bytes 393224 | tf_op jit(solution)/shard_map/ppermute | solution.py:650
  170.7 6.8 %collect.2 = (bf16[2,16,16,128]{3,2,1,0:T(8,128)(2,1)}, bf16[2,16,16,128]{3,2,1,0:T(8,128)(2,1)}, bf16[2,16,16,128]{3,2,1,0:T(8,128)(2,1)}, bf16[2,16,16,128]{3,...) custom-call(bf16[32,128,256]{2,1,0:T(8,128)(2,1)} %inverse.4.refs_0_, ...), custom_call_target="tpu_custom_call" | custom-call | flops 6600000000 | tf_op jit(solution)/shard_map/collect/pallas_call | solution.py:419
  177.6 1.3 collective-permute-start.28
  179.0 0.9 copy.69
  180.0 0.9 copy.70
  180.9 1.6 collective-permute-start.29
  182.5 2.3 collective-permute-start.30
  184.8 1.5 collective-permute-start.17
  188.4 0.9 copy.71
  189.3 0.9 copy.72
  190.4 2.1 collective-permute-done.28
  192.5 3.7 %collective-permute-start.20 = (bf16[2,16,16,128]{3,1,0,2:T(8,128)(2,1)S(1)}, bf16[2,16,16,128]{3,1,0,2:T(8,128)(2,1)S(1)}, u32[]{:S(2)}, u32[]{:S(2)}) collective-permute-start(bf16[2,16,16,128]{3,1,0,2:T(8,128)(2,1)S(1)} %copy.72), channel_id=1, source_target_pairs={{0,16},{4,20},{8,24},{12,28},{16,0},{20,4},{24,8},{28,12},{1,17},{... | collective-permute-start | bytes 393224 | tf_op jit(solution)/shard_map/ppermute | solution.py:650
  196.2 5.1 %collective-permute-start.21 = (bf16[2,16,16,128]{3,1,0,2:T(8,128)(2,1)S(1)}, bf16[2,16,16,128]{3,1,0,2:T(8,128)(2,1)S(1)}, u32[]{:S(2)}, u32[]{:S(2)}) collective-permute-start(bf16[2,16,16,128]{3,1,0,2:T(8,128)(2,1)S(1)} %copy.73), channel_id=1, source_target_pairs={{0,20},{4,16},{8,28},{12,24},{16,4},{20,0},{24,12},{28,8},{1,21},{... | collective-permute-start | bytes 393224 | tf_op jit(solution)/shard_map/ppermute | solution.py:650
  201.3 1.0 collective-permute-start.22
  202.3 2.8 %collective-permute-start.23 = (bf16[2,16,16,128]{3,1,0,2:T(8,128)(2,1)S(1)}, bf16[2,16,16,128]{3,1,0,2:T(8,128)(2,1)S(1)}, u32[]{:S(2)}, u32[]{:S(2)}) collective-permute-start(bf16[2,16,16,128]{3,1,0,2:T(8,128)(2,1)S(1)} %copy.75), channel_id=1, source_target_pairs={{0,28},{4,24},{8,20},{12,16},{16,12},{20,8},{24,4},{28,0},{1,29},{... | collective-permute-start | bytes 393224 | tf_op jit(solution)/shard_map/ppermute | solution.py:650
  205.2 1.6 collective-permute-start.34
  206.9 4.3 %collective-permute-done.20 = bf16[2,16,16,128]{3,1,0,2:T(8,128)(2,1)S(1)} collective-permute-done((bf16[2,16,16,128]{3,1,0,2:T(8,128)(2,1)S(1)}, bf16[2,16,16,128]{3,1,0,2:T(8,128)(2,1)S(1)}, u32[]{:S(2)}, u32[]{:S(2)}) %collective-permute-start.20) | collective-permute-done | bytes 131104 | tf_op jit(solution)/shard_map/ppermute | solution.py:650
  211.2 3.8 %collective-permute-done.21 = bf16[2,16,16,128]{3,1,0,2:T(8,128)(2,1)S(1)} collective-permute-done((bf16[2,16,16,128]{3,1,0,2:T(8,128)(2,1)S(1)}, bf16[2,16,16,128]{3,1,0,2:T(8,128)(2,1)S(1)}, u32[]{:S(2)}, u32[]{:S(2)}) %collective-permute-start.21) | collective-permute-done | bytes 131104 | tf_op jit(solution)/shard_map/ppermute | solution.py:650
  215.0 3.7 %collective-permute-start.37 = (bf16[4,32,128]{2,1,0:T(8,128)(2,1)S(1)}, bf16[4,32,128]{2,1,0:T(8,128)(2,1)S(1)}, u32[]{:S(2)}, u32[]{:S(2)}) collective-permute-start(bf16[4,32,128]{2,1,0:T(8,128)(2,1)S(1)} %get-tuple-element.80), channel_id=1, source_target_pairs={{0,16},{4,20},{8,24},{12,28},{16,0},{20,4},{24,8},{28,12},{1,17},{... | collective-permute-start | bytes 98312 | tf_op jit(solution)/shard_map/ppermute | solution.py:650
  218.7 3.1 %collective-permute-start.38 = (bf16[4,32,128]{2,1,0:T(8,128)(2,1)S(1)}, bf16[4,32,128]{2,1,0:T(8,128)(2,1)S(1)}, u32[]{:S(2)}, u32[]{:S(2)}) collective-permute-start(bf16[4,32,128]{2,1,0:T(8,128)(2,1)S(1)} %get-tuple-element.79), channel_id=1, source_target_pairs={{0,20},{4,16},{8,28},{12,24},{16,4},{20,0},{24,12},{28,8},{1,21},{... | collective-permute-start | bytes 98312 | tf_op jit(solution)/shard_map/ppermute | solution.py:650
  222.0 1.2 collective-permute-start.39
  223.1 2.7 %collective-permute-start.40 = (bf16[4,32,128]{2,1,0:T(8,128)(2,1)S(1)}, bf16[4,32,128]{2,1,0:T(8,128)(2,1)S(1)}, u32[]{:S(2)}, u32[]{:S(2)}) collective-permute-start(bf16[4,32,128]{2,1,0:T(8,128)(2,1)S(1)} %get-tuple-element.77), channel_id=1, source_target_pairs={{0,28},{4,24},{8,20},{12,16},{16,12},{20,8},{24,4},{28,0},{1,29},{... | collective-permute-start | bytes 98312 | tf_op jit(solution)/shard_map/ppermute | solution.py:650
  226.0 1.5 collective-permute-start.32
  227.8 1.9 collective-permute-done.40
  229.7 1.4 add_convert_fusion.2.pot
  232.3 4.0 %detect.1 = f32[12,16,128]{2,1,0:T(8,128)} custom-call(f32[2,4,12]{2,1,0:T(4,128)} %pad_maximum_fusion.4.alpha, s32[1]{0:T(128)} %dynamic_slice.18.counts, bf16[4,4,2,32,128]{4,3,2,1,0:T(8,128)(2,1)} %pad_maximum_fusion.1.fields, bf16[4,32,128]{2,1,0:T(8,128)(2,1)} %add_convert_fusion.2.pot, f32[4,2,32,128]{3,2,1,0:T(8,128)} %pad_maximum_fusion.2.plane, ...), custom_call_target="tpu_custom_call" | custom-call | tf_op jit(solution)/shard_map/detect/pallas_call | solution.py:522
  236.3 1.0 reduce_sum.9
  (190 shorter events, 17.6 us)
Async XLA Ops:
  0.0 47.9 %copy-start = (f32[4]{0:T(128)S(1)}, f32[4]{0:T(128)}, u32[]{:S(2)}) copy-start(f32[4]{0:T(128)} %param.19) | copy-start | bytes 52
  11.6 41.3 %collective-permute-start.10 = (bf16[2,208,128]{2,1,0:T(8,128)(2,1)}, bf16[2,208,128]{2,1,0:T(8,128)(2,1)S(1)}, u32[]{:S(2)}, u32[]{:S(2)}) collective-permute-start(bf16[2,208,128]{2,1,0:T(8,128)(2,1)} %get-tuple-element.49), channel_id=1, source_target_pairs={{0,16},{4,20},{8,24},{12,28},{16,0},{20,4},{24,8},{28,12},{1,17},{... | collective-permute-start | bytes 319496 | tf_op jit(solution)/shard_map/ppermute | solution.py:650
  15.7 37.3 %collective-permute-start.11 = (bf16[2,208,128]{2,1,0:T(8,128)(2,1)}, bf16[2,208,128]{2,1,0:T(8,128)(2,1)S(1)}, u32[]{:S(2)}, u32[]{:S(2)}) collective-permute-start(bf16[2,208,128]{2,1,0:T(8,128)(2,1)} %get-tuple-element.50), channel_id=1, source_target_pairs={{0,20},{4,16},{8,28},{12,24},{16,4},{20,0},{24,12},{28,8},{1,21},{... | collective-permute-start | bytes 319496 | tf_op jit(solution)/shard_map/ppermute | solution.py:650
  17.0 37.9 %collective-permute-start.12 = (bf16[2,208,128]{2,1,0:T(8,128)(2,1)}, bf16[2,208,128]{2,1,0:T(8,128)(2,1)S(1)}, u32[]{:S(2)}, u32[]{:S(2)}) collective-permute-start(bf16[2,208,128]{2,1,0:T(8,128)(2,1)} %get-tuple-element.51), channel_id=1, source_target_pairs={{0,24},{4,28},{8,16},{12,20},{16,8},{20,12},{24,0},{28,4},{1,25},{... | collective-permute-start | bytes 319496 | tf_op jit(solution)/shard_map/ppermute | solution.py:650
  20.6 36.0 %collective-permute-start.13 = (bf16[2,208,128]{2,1,0:T(8,128)(2,1)}, bf16[2,208,128]{2,1,0:T(8,128)(2,1)S(1)}, u32[]{:S(2)}, u32[]{:S(2)}) collective-permute-start(bf16[2,208,128]{2,1,0:T(8,128)(2,1)} %get-tuple-element.52), channel_id=1, source_target_pairs={{0,28},{4,24},{8,20},{12,16},{16,12},{20,8},{24,4},{28,0},{1,29},{... | collective-permute-start | bytes 319496 | tf_op jit(solution)/shard_map/ppermute | solution.py:650
  20.6 12.7 %copy-start.10 = (s32[32,4]{0,1:T(4,128)S(1)}, s32[32,4]{0,1:T(4,128)}, u32[]{:S(2)}) copy-start(s32[32,4]{0,1:T(4,128)} %param.20) | copy-start | bytes 1540
  20.6 13.0 %copy-start.9 = (s32[4,2]{0,1:T(2,128)S(1)}, s32[4,2]{0,1:T(2,128)}, u32[]{:S(2)}) copy-start(s32[4,2]{0,1:T(2,128)} %param.18) | copy-start | bytes 100
  20.6 36.7 %collective-permute-start.7 = (bf16[2,208,128]{2,1,0:T(8,128)(2,1)}, bf16[2,208,128]{2,1,0:T(8,128)(2,1)S(1)}, u32[]{:S(2)}, u32[]{:S(2)}) collective-permute-start(bf16[2,208,128]{2,1,0:T(8,128)(2,1)} %get-tuple-element.46), channel_id=1, source_target_pairs={{0,4},{4,0},{8,12},{12,8},{16,20},{20,16},{24,28},{28,24},{1,5},{5... | collective-permute-start | bytes 319496 | tf_op jit(solution)/shard_map/ppermute | solution.py:650
  44.1 12.5 %copy-start.24 = (bf16[2,208,128]{2,1,0:T(8,128)(2,1)S(1)}, bf16[2,208,128]{2,1,0:T(8,128)(2,1)}, u32[]{:S(2)}) copy-start(bf16[2,208,128]{2,1,0:T(8,128)(2,1)} %get-tuple-element.39) | copy-start | bytes 319492
  44.1 13.2 %copy-start.21 = (bf16[2,208,128]{2,1,0:T(8,128)(2,1)S(1)}, bf16[2,208,128]{2,1,0:T(8,128)(2,1)}, u32[]{:S(2)}) copy-start(bf16[2,208,128]{2,1,0:T(8,128)(2,1)} %get-tuple-element.40) | copy-start | bytes 319492
  44.1 15.0 %copy-start.19 = (bf16[2,208,128]{2,1,0:T(8,128)(2,1)S(1)}, bf16[2,208,128]{2,1,0:T(8,128)(2,1)}, u32[]{:S(2)}) copy-start(bf16[2,208,128]{2,1,0:T(8,128)(2,1)} %get-tuple-element.41) | copy-start | bytes 319492
  44.1 17.5 %copy-start.17 = (bf16[2,208,128]{2,1,0:T(8,128)(2,1)S(1)}, bf16[2,208,128]{2,1,0:T(8,128)(2,1)}, u32[]{:S(2)}) copy-start(bf16[2,208,128]{2,1,0:T(8,128)(2,1)} %get-tuple-element.42) | copy-start | bytes 319492
  44.1 20.1 %copy-start.15 = (bf16[2,208,128]{2,1,0:T(8,128)(2,1)S(1)}, bf16[2,208,128]{2,1,0:T(8,128)(2,1)}, u32[]{:S(2)}) copy-start(bf16[2,208,128]{2,1,0:T(8,128)(2,1)} %get-tuple-element.43) | copy-start | bytes 319492
  44.2 22.8 %copy-start.13 = (bf16[2,208,128]{2,1,0:T(8,128)(2,1)S(1)}, bf16[2,208,128]{2,1,0:T(8,128)(2,1)}, u32[]{:S(2)}) copy-start(bf16[2,208,128]{2,1,0:T(8,128)(2,1)} %get-tuple-element.44) | copy-start | bytes 319492
  52.9 16.0 %copy-start.12 = (bf16[2,208,128]{2,1,0:T(8,128)(2,1)}, bf16[2,208,128]{2,1,0:T(8,128)(2,1)S(1)}, u32[]{:S(2)}) copy-start(bf16[2,208,128]{2,1,0:T(8,128)(2,1)S(1)} %collective-permute-done.10.refs_4_) | copy-start | bytes 319492
  52.9 6.2 %collective-permute-start.8 = (bf16[2,208,128]{2,1,0:T(8,128)(2,1)S(1)}, bf16[2,208,128]{2,1,0:T(8,128)(2,1)S(1)}, u32[]{:S(2)}, u32[]{:S(2)}) collective-permute-start(bf16[2,208,128]{2,1,0:T(8,128)(2,1)S(1)} %copy-done.23), channel_id=1, source_target_pairs={{0,8},{4,12},{8,0},{12,4},{16,24},{20,28},{24,16},{28,20},{1,9},{5... | collective-permute-start | bytes 319496 | tf_op jit(solution)/shard_map/ppermute | solution.py:650
  53.0 15.9 %copy-start.14 = (bf16[2,208,128]{2,1,0:T(8,128)(2,1)}, bf16[2,208,128]{2,1,0:T(8,128)(2,1)S(1)}, u32[]{:S(2)}) copy-start(bf16[2,208,128]{2,1,0:T(8,128)(2,1)S(1)} %collective-permute-done.11.refs_5_) | copy-start | bytes 319492
  53.0 8.6 %collective-permute-start.9 = (bf16[2,208,128]{2,1,0:T(8,128)(2,1)S(1)}, bf16[2,208,128]{2,1,0:T(8,128)(2,1)S(1)}, u32[]{:S(2)}, u32[]{:S(2)}) collective-permute-start(bf16[2,208,128]{2,1,0:T(8,128)(2,1)S(1)} %copy-done.22), channel_id=1, source_target_pairs={{0,12},{4,8},{8,4},{12,0},{16,28},{20,24},{24,20},{28,16},{1,13},{... | collective-permute-start | bytes 319496 | tf_op jit(solution)/shard_map/ppermute | solution.py:650
  54.8 14.0 %copy-start.16 = (bf16[2,208,128]{2,1,0:T(8,128)(2,1)}, bf16[2,208,128]{2,1,0:T(8,128)(2,1)S(1)}, u32[]{:S(2)}) copy-start(bf16[2,208,128]{2,1,0:T(8,128)(2,1)S(1)} %collective-permute-done.12.refs_6_) | copy-start | bytes 319492
  54.9 9.4 %collective-permute-start = (bf16[2,208,128]{2,1,0:T(8,128)(2,1)S(1)}, bf16[2,208,128]{2,1,0:T(8,128)(2,1)S(1)}, u32[]{:S(2)}, u32[]{:S(2)}) collective-permute-start(bf16[2,208,128]{2,1,0:T(8,128)(2,1)S(1)} %copy-done.25), channel_id=1, source_target_pairs={{0,4},{4,0},{8,12},{12,8},{16,20},{20,16},{24,28},{28,24},{1,5},{5... | collective-permute-start | bytes 319496 | tf_op jit(solution)/shard_map/ppermute | solution.py:650
  56.6 12.3 %copy-start.18 = (bf16[2,208,128]{2,1,0:T(8,128)(2,1)}, bf16[2,208,128]{2,1,0:T(8,128)(2,1)S(1)}, u32[]{:S(2)}) copy-start(bf16[2,208,128]{2,1,0:T(8,128)(2,1)S(1)} %collective-permute-done.13.refs_7_) | copy-start | bytes 319492
  56.6 10.4 %collective-permute-start.1 = (bf16[2,208,128]{2,1,0:T(8,128)(2,1)S(1)}, bf16[2,208,128]{2,1,0:T(8,128)(2,1)S(1)}, u32[]{:S(2)}, u32[]{:S(2)}) collective-permute-start(bf16[2,208,128]{2,1,0:T(8,128)(2,1)S(1)} %copy-done.24), channel_id=1, source_target_pairs={{0,8},{4,12},{8,0},{12,4},{16,24},{20,28},{24,16},{28,20},{1,9},{5... | collective-permute-start | bytes 319496 | tf_op jit(solution)/shard_map/ppermute | solution.py:650
  57.3 11.6 %copy-start.20 = (bf16[2,208,128]{2,1,0:T(8,128)(2,1)}, bf16[2,208,128]{2,1,0:T(8,128)(2,1)S(1)}, u32[]{:S(2)}) copy-start(bf16[2,208,128]{2,1,0:T(8,128)(2,1)S(1)} %collective-permute-done.7.refs_1_) | copy-start | bytes 319492
  57.3 18.7 %collective-permute-start.2 = (bf16[2,208,128]{2,1,0:T(8,128)(2,1)S(1)}, bf16[2,208,128]{2,1,0:T(8,128)(2,1)S(1)}, u32[]{:S(2)}, u32[]{:S(2)}) collective-permute-start(bf16[2,208,128]{2,1,0:T(8,128)(2,1)S(1)} %copy-done.21), channel_id=1, source_target_pairs={{0,12},{4,8},{8,4},{12,0},{16,28},{20,24},{24,20},{28,16},{1,13},{... | collective-permute-start | bytes 319496 | tf_op jit(solution)/shard_map/ppermute | solution.py:650
  59.1 16.9 %collective-permute-start.3 = (bf16[2,208,128]{2,1,0:T(8,128)(2,1)S(1)}, bf16[2,208,128]{2,1,0:T(8,128)(2,1)S(1)}, u32[]{:S(2)}, u32[]{:S(2)}) collective-permute-start(bf16[2,208,128]{2,1,0:T(8,128)(2,1)S(1)} %copy-done.19), channel_id=1, source_target_pairs={{0,16},{4,20},{8,24},{12,28},{16,0},{20,4},{24,8},{28,12},{1,17},{... | collective-permute-start | bytes 319496 | tf_op jit(solution)/shard_map/ppermute | solution.py:650
  61.6 16.4 %collective-permute-start.4 = (bf16[2,208,128]{2,1,0:T(8,128)(2,1)S(1)}, bf16[2,208,128]{2,1,0:T(8,128)(2,1)S(1)}, u32[]{:S(2)}, u32[]{:S(2)}) collective-permute-start(bf16[2,208,128]{2,1,0:T(8,128)(2,1)S(1)} %copy-done.17), channel_id=1, source_target_pairs={{0,20},{4,16},{8,28},{12,24},{16,4},{20,0},{24,12},{28,8},{1,21},{... | collective-permute-start | bytes 319496 | tf_op jit(solution)/shard_map/ppermute | solution.py:650
  64.2 11.7 %copy-start.26 = (bf16[2,208,128]{2,1,0:T(8,128)(2,1)}, bf16[2,208,128]{2,1,0:T(8,128)(2,1)S(1)}, u32[]{:S(2)}) copy-start(bf16[2,208,128]{2,1,0:T(8,128)(2,1)S(1)} %collective-permute-done.refs_1_) | copy-start | bytes 319492
  64.2 13.7 %collective-permute-start.5 = (bf16[2,208,128]{2,1,0:T(8,128)(2,1)S(1)}, bf16[2,208,128]{2,1,0:T(8,128)(2,1)S(1)}, u32[]{:S(2)}, u32[]{:S(2)}) collective-permute-start(bf16[2,208,128]{2,1,0:T(8,128)(2,1)S(1)} %copy-done.15), channel_id=1, source_target_pairs={{0,24},{4,28},{8,16},{12,20},{16,8},{20,12},{24,0},{28,4},{1,25},{... | collective-permute-start | bytes 319496 | tf_op jit(solution)/shard_map/ppermute | solution.py:650
  67.0 11.0 %collective-permute-start.6 = (bf16[2,208,128]{2,1,0:T(8,128)(2,1)S(1)}, bf16[2,208,128]{2,1,0:T(8,128)(2,1)S(1)}, u32[]{:S(2)}, u32[]{:S(2)}) collective-permute-start(bf16[2,208,128]{2,1,0:T(8,128)(2,1)S(1)} %copy-done.13), channel_id=1, source_target_pairs={{0,28},{4,24},{8,20},{12,16},{16,12},{20,8},{24,4},{28,0},{1,29},{... | collective-permute-start | bytes 319496 | tf_op jit(solution)/shard_map/ppermute | solution.py:650
  88.7 34.4 %collective-permute-start.15 = (bf16[32,208,128]{2,1,0:T(8,128)(2,1)}, bf16[32,208,128]{2,1,0:T(8,128)(2,1)S(1)}, u32[]{:S(2)}, u32[]{:S(2)}) collective-permute-start(bf16[32,208,128]{2,1,0:T(8,128)(2,1)} %forward_y.1.spec.after), channel_id=1, source_target_pairs={{0,2},{1,3},{2,0},{3,1},{4,6},{5,7},{6,4},{7,5},{8,10},{9,11},{10,... | collective-permute-start | bytes 5111816 | tf_op jit(solution)/shard_map/ppermute | solution.py:677
  90.1 42.6 %collective-permute-start.14 = (bf16[32,208,128]{2,1,0:T(8,128)(2,1)}, bf16[32,208,128]{2,1,0:T(8,128)(2,1)}, u32[]{:S(2)}, u32[]{:S(2)}) collective-permute-start(bf16[32,208,128]{2,1,0:T(8,128)(2,1)} %forward_y.1.spec.after), channel_id=1, source_target_pairs={{0,1},{1,0},{2,3},{3,2},{4,5},{5,4},{6,7},{7,6},{8,9},{9,8},{10,11... | collective-permute-start | bytes 5111816 | tf_op jit(solution)/shard_map/ppermute | solution.py:677
  123.1 18.0 %collective-permute-start.16 = (bf16[32,208,128]{2,1,0:T(8,128)(2,1)S(1)}, bf16[32,208,128]{2,1,0:T(8,128)(2,1)}, u32[]{:S(2)}, u32[]{:S(2)}) collective-permute-start(bf16[32,208,128]{2,1,0:T(8,128)(2,1)S(1)} %collective-permute-done.15.spec), channel_id=1, source_target_pairs={{0,1},{1,0},{2,3},{3,2},{4,5},{5,4},{6,7},{7,6},{8,9},{9,8},{10,11... | collective-permute-start | bytes 5111816 | tf_op jit(solution)/shard_map/ppermute | solution.py:677
  157.6 23.3 %collective-permute-start.24 = (bf16[2,16,16,128]{3,1,0,2:T(8,128)(2,1)S(1)}, bf16[2,16,16,128]{3,1,0,2:T(8,128)(2,1)S(1)}, u32[]{:S(2)}, u32[]{:S(2)}) collective-permute-start(bf16[2,16,16,128]{3,1,0,2:T(8,128)(2,1)S(1)} %copy.78), channel_id=1, source_target_pairs={{0,4},{4,0},{8,12},{12,8},{16,20},{20,16},{24,28},{28,24},{1,5},{5... | collective-permute-start | bytes 393224 | tf_op jit(solution)/shard_map/ppermute | solution.py:650
  159.5 23.0 %collective-permute-start.25 = (bf16[2,16,16,128]{3,1,0,2:T(8,128)(2,1)S(1)}, bf16[2,16,16,128]{3,1,0,2:T(8,128)(2,1)S(1)}, u32[]{:S(2)}, u32[]{:S(2)}) collective-permute-start(bf16[2,16,16,128]{3,1,0,2:T(8,128)(2,1)S(1)} %copy.79), channel_id=1, source_target_pairs={{0,8},{4,12},{8,0},{12,4},{16,24},{20,28},{24,16},{28,20},{1,9},{5... | collective-permute-start | bytes 393224 | tf_op jit(solution)/shard_map/ppermute | solution.py:650
  167.0 17.9 %collective-permute-start.26 = (bf16[2,16,16,128]{3,1,0,2:T(8,128)(2,1)S(1)}, bf16[2,16,16,128]{3,1,0,2:T(8,128)(2,1)S(1)}, u32[]{:S(2)}, u32[]{:S(2)}) collective-permute-start(bf16[2,16,16,128]{3,1,0,2:T(8,128)(2,1)S(1)} %copy.80), channel_id=1, source_target_pairs={{0,12},{4,8},{8,4},{12,0},{16,28},{20,24},{24,20},{28,16},{1,13},{... | collective-permute-start | bytes 393224 | tf_op jit(solution)/shard_map/ppermute | solution.py:650
  168.0 10.9 %copy-start.7 = (bf16[2,16,16,128]{3,2,1,0:T(8,128)(2,1)S(1)}, bf16[2,16,16,128]{3,2,1,0:T(8,128)(2,1)}, u32[]{:S(2)}) copy-start(bf16[2,16,16,128]{3,2,1,0:T(8,128)(2,1)} %get-tuple-element.67) | copy-start | bytes 393220
  168.0 11.0 %copy-start.6 = (bf16[2,16,16,128]{3,2,1,0:T(8,128)(2,1)S(1)}, bf16[2,16,16,128]{3,2,1,0:T(8,128)(2,1)}, u32[]{:S(2)}) copy-start(bf16[2,16,16,128]{3,2,1,0:T(8,128)(2,1)} %get-tuple-element.68) | copy-start | bytes 393220
  168.0 19.1 %copy-start.35 = (s32[32]{0:T(128)S(1)}, s32[32]{0:T(128)}, u32[]{:S(2)}) copy-start(s32[32]{0:T(128)} %param.21) | copy-start | bytes 388
  168.0 18.3 %collective-permute-start.27 = (bf16[2,16,16,128]{3,1,0,2:T(8,128)(2,1)S(1)}, bf16[2,16,16,128]{3,1,0,2:T(8,128)(2,1)S(1)}, u32[]{:S(2)}, u32[]{:S(2)}) collective-permute-start(bf16[2,16,16,128]{3,1,0,2:T(8,128)(2,1)S(1)} %copy.81), channel_id=1, source_target_pairs={{0,16},{4,20},{8,24},{12,28},{16,0},{20,4},{24,8},{28,12},{1,17},{... | collective-permute-start | bytes 393224 | tf_op jit(solution)/shard_map/ppermute | solution.py:650
  177.5 12.7 %copy-start.5 = (bf16[2,16,16,128]{3,2,1,0:T(8,128)(2,1)S(1)}, bf16[2,16,16,128]{3,2,1,0:T(8,128)(2,1)}, u32[]{:S(2)}) copy-start(bf16[2,16,16,128]{3,2,1,0:T(8,128)(2,1)} %get-tuple-element.58) | copy-start | bytes 393220
  177.5 12.8 %copy-start.4 = (bf16[2,16,16,128]{3,2,1,0:T(8,128)(2,1)S(1)}, bf16[2,16,16,128]{3,2,1,0:T(8,128)(2,1)}, u32[]{:S(2)}) copy-start(bf16[2,16,16,128]{3,2,1,0:T(8,128)(2,1)} %get-tuple-element.59) | copy-start | bytes 393220
  177.5 12.8 %copy-start.3 = (bf16[2,16,16,128]{3,2,1,0:T(8,128)(2,1)S(1)}, bf16[2,16,16,128]{3,2,1,0:T(8,128)(2,1)}, u32[]{:S(2)}) copy-start(bf16[2,16,16,128]{3,2,1,0:T(8,128)(2,1)} %get-tuple-element.60) | copy-start | bytes 393220
  177.5 27.5 %copy-start.2 = (bf16[2,16,16,128]{3,2,1,0:T(8,128)(2,1)S(1)}, bf16[2,16,16,128]{3,2,1,0:T(8,128)(2,1)}, u32[]{:S(2)}) copy-start(bf16[2,16,16,128]{3,2,1,0:T(8,128)(2,1)} %get-tuple-element.61) | copy-start | bytes 393220
  177.5 44.3 %copy-start.1 = (bf16[2,16,16,128]{3,2,1,0:T(8,128)(2,1)S(1)}, bf16[2,16,16,128]{3,2,1,0:T(8,128)(2,1)}, u32[]{:S(2)}) copy-start(bf16[2,16,16,128]{3,2,1,0:T(8,128)(2,1)} %get-tuple-element.53) | copy-start | bytes 393220
  177.6 14.9 %collective-permute-start.28 = (bf16[2,16,16,128]{3,1,0,2:T(8,128)(2,1)S(1)}, bf16[2,16,16,128]{3,1,0,2:T(8,128)(2,1)S(1)}, u32[]{:S(2)}, u32[]{:S(2)}) collective-permute-start(bf16[2,16,16,128]{3,1,0,2:T(8,128)(2,1)S(1)} %copy.82), channel_id=1, source_target_pairs={{0,20},{4,16},{8,28},{12,24},{16,4},{20,0},{24,12},{28,8},{1,21},{... | collective-permute-start | bytes 393224 | tf_op jit(solution)/shard_map/ppermute | solution.py:650
  180.9 11.6 %collective-permute-start.29 = (bf16[2,16,16,128]{3,1,0,2:T(8,128)(2,1)S(1)}, bf16[2,16,16,128]{3,1,0,2:T(8,128)(2,1)S(1)}, u32[]{:S(2)}, u32[]{:S(2)}) collective-permute-start(bf16[2,16,16,128]{3,1,0,2:T(8,128)(2,1)S(1)} %copy.83), channel_id=1, source_target_pairs={{0,24},{4,28},{8,16},{12,20},{16,8},{20,12},{24,0},{28,4},{1,25},{... | collective-permute-start | bytes 393224 | tf_op jit(solution)/shard_map/ppermute | solution.py:650
  182.5 13.7 %collective-permute-start.30 = (bf16[2,16,16,128]{3,1,0,2:T(8,128)(2,1)S(1)}, bf16[2,16,16,128]{3,1,0,2:T(8,128)(2,1)S(1)}, u32[]{:S(2)}, u32[]{:S(2)}) collective-permute-start(bf16[2,16,16,128]{3,1,0,2:T(8,128)(2,1)S(1)} %copy.84), channel_id=1, source_target_pairs={{0,28},{4,24},{8,20},{12,16},{16,12},{20,8},{24,4},{28,0},{1,29},{... | collective-permute-start | bytes 393224 | tf_op jit(solution)/shard_map/ppermute | solution.py:650
  184.8 16.5 %collective-permute-start.17 = (bf16[2,16,16,128]{3,1,0,2:T(8,128)(2,1)S(1)}, bf16[2,16,16,128]{3,1,0,2:T(8,128)(2,1)S(1)}, u32[]{:S(2)}, u32[]{:S(2)}) collective-permute-start(bf16[2,16,16,128]{3,1,0,2:T(8,128)(2,1)S(1)} %copy.69), channel_id=1, source_target_pairs={{0,4},{4,0},{8,12},{12,8},{16,20},{20,16},{24,28},{28,24},{1,5},{5... | collective-permute-start | bytes 393224 | tf_op jit(solution)/shard_map/ppermute | solution.py:650
  186.3 16.0 %collective-permute-start.18 = (bf16[2,16,16,128]{3,1,0,2:T(8,128)(2,1)S(1)}, bf16[2,16,16,128]{3,1,0,2:T(8,128)(2,1)S(1)}, u32[]{:S(2)}, u32[]{:S(2)}) collective-permute-start(bf16[2,16,16,128]{3,1,0,2:T(8,128)(2,1)S(1)} %copy.70), channel_id=1, source_target_pairs={{0,8},{4,12},{8,0},{12,4},{16,24},{20,28},{24,16},{28,20},{1,9},{5... | collective-permute-start | bytes 393224 | tf_op jit(solution)/shard_map/ppermute | solution.py:650
  192.5 12.7 %collective-permute-start.19 = (bf16[2,16,16,128]{3,1,0,2:T(8,128)(2,1)S(1)}, bf16[2,16,16,128]{3,1,0,2:T(8,128)(2,1)S(1)}, u32[]{:S(2)}, u32[]{:S(2)}) collective-permute-start(bf16[2,16,16,128]{3,1,0,2:T(8,128)(2,1)S(1)} %copy.71), channel_id=1, source_target_pairs={{0,12},{4,8},{8,4},{12,0},{16,28},{20,24},{24,20},{28,16},{1,13},{... | collective-permute-start | bytes 393224 | tf_op jit(solution)/shard_map/ppermute | solution.py:650
  192.5 18.6 %collective-permute-start.20 = (bf16[2,16,16,128]{3,1,0,2:T(8,128)(2,1)S(1)}, bf16[2,16,16,128]{3,1,0,2:T(8,128)(2,1)S(1)}, u32[]{:S(2)}, u32[]{:S(2)}) collective-permute-start(bf16[2,16,16,128]{3,1,0,2:T(8,128)(2,1)S(1)} %copy.72), channel_id=1, source_target_pairs={{0,16},{4,20},{8,24},{12,28},{16,0},{20,4},{24,8},{28,12},{1,17},{... | collective-permute-start | bytes 393224 | tf_op jit(solution)/shard_map/ppermute | solution.py:650
  196.2 18.7 %collective-permute-start.21 = (bf16[2,16,16,128]{3,1,0,2:T(8,128)(2,1)S(1)}, bf16[2,16,16,128]{3,1,0,2:T(8,128)(2,1)S(1)}, u32[]{:S(2)}, u32[]{:S(2)}) collective-permute-start(bf16[2,16,16,128]{3,1,0,2:T(8,128)(2,1)S(1)} %copy.73), channel_id=1, source_target_pairs={{0,20},{4,16},{8,28},{12,24},{16,4},{20,0},{24,12},{28,8},{1,21},{... | collective-permute-start | bytes 393224 | tf_op jit(solution)/shard_map/ppermute | solution.py:650
  201.3 13.6 %collective-permute-start.22 = (bf16[2,16,16,128]{3,1,0,2:T(8,128)(2,1)S(1)}, bf16[2,16,16,128]{3,1,0,2:T(8,128)(2,1)S(1)}, u32[]{:S(2)}, u32[]{:S(2)}) collective-permute-start(bf16[2,16,16,128]{3,1,0,2:T(8,128)(2,1)S(1)} %copy.74), channel_id=1, source_target_pairs={{0,24},{4,28},{8,16},{12,20},{16,8},{20,12},{24,0},{28,4},{1,25},{... | collective-permute-start | bytes 393224 | tf_op jit(solution)/shard_map/ppermute | solution.py:650
  202.3 16.4 %collective-permute-start.23 = (bf16[2,16,16,128]{3,1,0,2:T(8,128)(2,1)S(1)}, bf16[2,16,16,128]{3,1,0,2:T(8,128)(2,1)S(1)}, u32[]{:S(2)}, u32[]{:S(2)}) collective-permute-start(bf16[2,16,16,128]{3,1,0,2:T(8,128)(2,1)S(1)} %copy.75), channel_id=1, source_target_pairs={{0,28},{4,24},{8,20},{12,16},{16,12},{20,8},{24,4},{28,0},{1,29},{... | collective-permute-start | bytes 393224 | tf_op jit(solution)/shard_map/ppermute | solution.py:650
  205.2 16.7 %collective-permute-start.34 = (bf16[4,32,128]{2,1,0:T(8,128)(2,1)S(1)}, bf16[4,32,128]{2,1,0:T(8,128)(2,1)S(1)}, u32[]{:S(2)}, u32[]{:S(2)}) collective-permute-start(bf16[4,32,128]{2,1,0:T(8,128)(2,1)S(1)} %get-tuple-element.76), channel_id=1, source_target_pairs={{0,4},{4,0},{8,12},{12,8},{16,20},{20,16},{24,28},{28,24},{1,5},{5... | collective-permute-start | bytes 98312 | tf_op jit(solution)/shard_map/ppermute | solution.py:650
  211.1 12.0 %collective-permute-start.35 = (bf16[4,32,128]{2,1,0:T(8,128)(2,1)S(1)}, bf16[4,32,128]{2,1,0:T(8,128)(2,1)S(1)}, u32[]{:S(2)}, u32[]{:S(2)}) collective-permute-start(bf16[4,32,128]{2,1,0:T(8,128)(2,1)S(1)} %get-tuple-element.82), channel_id=1, source_target_pairs={{0,8},{4,12},{8,0},{12,4},{16,24},{20,28},{24,16},{28,20},{1,9},{5... | collective-permute-start | bytes 98312 | tf_op jit(solution)/shard_map/ppermute | solution.py:650
  215.0 10.9 %collective-permute-start.36 = (bf16[4,32,128]{2,1,0:T(8,128)(2,1)S(1)}, bf16[4,32,128]{2,1,0:T(8,128)(2,1)S(1)}, u32[]{:S(2)}, u32[]{:S(2)}) collective-permute-start(bf16[4,32,128]{2,1,0:T(8,128)(2,1)S(1)} %get-tuple-element.81), channel_id=1, source_target_pairs={{0,12},{4,8},{8,4},{12,0},{16,28},{20,24},{24,20},{28,16},{1,13},{... | collective-permute-start | bytes 98312 | tf_op jit(solution)/shard_map/ppermute | solution.py:650
  215.0 11.0 %collective-permute-start.37 = (bf16[4,32,128]{2,1,0:T(8,128)(2,1)S(1)}, bf16[4,32,128]{2,1,0:T(8,128)(2,1)S(1)}, u32[]{:S(2)}, u32[]{:S(2)}) collective-permute-start(bf16[4,32,128]{2,1,0:T(8,128)(2,1)S(1)} %get-tuple-element.80), channel_id=1, source_target_pairs={{0,16},{4,20},{8,24},{12,28},{16,0},{20,4},{24,8},{28,12},{1,17},{... | collective-permute-start | bytes 98312 | tf_op jit(solution)/shard_map/ppermute | solution.py:650
  218.7 8.7 %collective-permute-start.38 = (bf16[4,32,128]{2,1,0:T(8,128)(2,1)S(1)}, bf16[4,32,128]{2,1,0:T(8,128)(2,1)S(1)}, u32[]{:S(2)}, u32[]{:S(2)}) collective-permute-start(bf16[4,32,128]{2,1,0:T(8,128)(2,1)S(1)} %get-tuple-element.79), channel_id=1, source_target_pairs={{0,20},{4,16},{8,28},{12,24},{16,4},{20,0},{24,12},{28,8},{1,21},{... | collective-permute-start | bytes 98312 | tf_op jit(solution)/shard_map/ppermute | solution.py:650
  222.0 5.9 %collective-permute-start.39 = (bf16[4,32,128]{2,1,0:T(8,128)(2,1)S(1)}, bf16[4,32,128]{2,1,0:T(8,128)(2,1)S(1)}, u32[]{:S(2)}, u32[]{:S(2)}) collective-permute-start(bf16[4,32,128]{2,1,0:T(8,128)(2,1)S(1)} %get-tuple-element.78), channel_id=1, source_target_pairs={{0,24},{4,28},{8,16},{12,20},{16,8},{20,12},{24,0},{28,4},{1,25},{... | collective-permute-start | bytes 98312 | tf_op jit(solution)/shard_map/ppermute | solution.py:650
  223.1 6.6 %collective-permute-start.40 = (bf16[4,32,128]{2,1,0:T(8,128)(2,1)S(1)}, bf16[4,32,128]{2,1,0:T(8,128)(2,1)S(1)}, u32[]{:S(2)}, u32[]{:S(2)}) collective-permute-start(bf16[4,32,128]{2,1,0:T(8,128)(2,1)S(1)} %get-tuple-element.77), channel_id=1, source_target_pairs={{0,28},{4,24},{8,20},{12,16},{16,12},{20,8},{24,4},{28,0},{1,29},{... | collective-permute-start | bytes 98312 | tf_op jit(solution)/shard_map/ppermute | solution.py:650
  225.9 5.2 %collective-permute-start.31 = (bf16[4,2,32,128]{3,2,1,0:T(8,128)(2,1)S(1)}, bf16[4,2,32,128]{3,2,1,0:T(8,128)(2,1)S(1)}, u32[]{:S(2)}, u32[]{:S(2)}) collective-permute-start(bf16[4,2,32,128]{3,2,1,0:T(8,128)(2,1)S(1)} %get-tuple-element.85), channel_id=1, source_target_pairs={{0,1},{1,0},{2,3},{3,2},{4,5},{5,4},{6,7},{7,6},{8,9},{9,8},{10,11... | collective-permute-start | bytes 196616 | tf_op jit(solution)/shard_map/ppermute | solution.py:650
  226.0 5.2 %collective-permute-start.32 = (bf16[4,2,32,128]{3,2,1,0:T(8,128)(2,1)S(1)}, bf16[4,2,32,128]{3,2,1,0:T(8,128)(2,1)S(1)}, u32[]{:S(2)}, u32[]{:S(2)}) collective-permute-start(bf16[4,2,32,128]{3,2,1,0:T(8,128)(2,1)S(1)} %get-tuple-element.87), channel_id=1, source_target_pairs={{0,2},{1,3},{2,0},{3,1},{4,6},{5,7},{6,4},{7,5},{8,10},{9,11},{10,... | collective-permute-start | bytes 196616 | tf_op jit(solution)/shard_map/ppermute | solution.py:650
  227.5 4.1 %collective-permute-start.33 = (bf16[4,2,32,128]{3,2,1,0:T(8,128)(2,1)S(1)}, bf16[4,2,32,128]{3,2,1,0:T(8,128)(2,1)S(1)}, u32[]{:S(2)}, u32[]{:S(2)}) collective-permute-start(bf16[4,2,32,128]{3,2,1,0:T(8,128)(2,1)S(1)} %get-tuple-element.86), channel_id=1, source_target_pairs={{0,3},{1,2},{2,1},{3,0},{4,7},{5,6},{6,5},{7,4},{8,11},{9,10},{10,... | collective-permute-start | bytes 196616 | tf_op jit(solution)/shard_map/ppermute | solution.py:650
  (13 other events, 71.4 us)

commit v2 on v1

--- a/solution.py
+++ b/solution.py
@@ -136,10 +136,9 @@
     return pl.CostEstimate(flops=int(micros * 1.1e9), bytes_accessed=0, transcendentals=0)
 
 
-def forward_x_kernel(sel, pot, section, last, *rest):
-    *outs, cos_ref, sin_ref, twisted = rest
-    fields = len(outs)
-    lanes = cos_ref.shape[2]
+def forward_x_kernel(sel, pot, section, last, out, cos_ref, sin_ref, twisted):
+    fields = out.shape[0]
+    lanes = out.shape[3]
     half = section.shape[1] // 2
 
     def chunk(t, carry):
@@ -167,10 +166,9 @@
         twisted[:, A + m * SUB : A + (m + 1) * SUB, :] = imag.astype(BF).reshape(
             2 * fields, SUB, lanes
         )
-    for o in range(fields):
-        d = sel[1] ^ o
-        lines = twisted[pl.ds(2 * d, 2)].reshape(4 * A, lanes)
-        outs[o][0] = dot(last[0, d], lines).astype(BF)
+    for d in range(fields):
+        lines = twisted[2 * d : 2 * d + 2].reshape(4 * A, lanes)
+        out[d, 0] = dot(last[0, d], lines).astype(BF)
 
 
 def forward_x(sel, pot, section, last, fields, part):
@@ -187,28 +185,27 @@
                 pl.BlockSpec((1,) + section.shape[1:], lambda i, s: (s[0], 0, 0)),
                 pl.BlockSpec((1,) + last.shape[1:], lambda i, s: (s[0], 0, 0, 0)),
             ],
-            out_specs=[pl.BlockSpec((1, ROWS, lanes), lambda i, s: (i, 0, 0))] * fields,
+            out_specs=pl.BlockSpec((fields, 1, ROWS, lanes), lambda i, s: (0, i, 0, 0)),
             scratch_shapes=[
                 pltpu.VMEM((A, A, lanes), BF),
                 pltpu.VMEM((A, A, lanes), BF),
                 pltpu.VMEM((2 * fields, 2 * A, lanes), BF),
             ],
         ),
-        out_shape=[jax.ShapeDtypeStruct((steps, ROWS, lanes), BF)] * fields,
+        out_shape=jax.ShapeDtypeStruct((fields, steps, ROWS, lanes), BF),
         compiler_params=pltpu.CompilerParams(vmem_limit_bytes=VMEM),
         cost_estimate=cost(9),
         name="forward_x",
     )(sel, pot.reshape(groups, HIGH, SUB, N), section, last)
 
 
-def section_step(sel, groups, section, gathered, twisted, start):
+def section_step(lines, section, gathered, twisted, start):
     chunk_rows = 16 * SUB
-    for g, group in enumerate(groups):
-        block = group[0].astype(F32)
+    for g in range(lines.shape[0]):
+        block = lines[g, 0].astype(F32)
         zeros = jnp.zeros((LANES - PART, LANES), F32)
         both = jnp.concatenate([block[:PART], zeros, block[PART:], zeros], axis=0)
-        spot = pl.multiple_of(sel[g] * LANES, LANES)
-        gathered[:, pl.ds(spot, LANES)] = both.astype(BF)
+        gathered[:, g * LANES : (g + 1) * LANES] = both.astype(BF)
     values = gathered[...]
     for c in range(A // 16):
         rows = slice(c * chunk_rows, (c + 1) * chunk_rows)
@@ -223,40 +220,37 @@
         twisted[spot, 1, pl.ds(start, SUB), :] = imag.astype(BF).reshape(16, SUB, LANES)
 
 
-def forward_y_first_kernel(sel, *refs):
-    *groups, section, twisted, gathered = refs
+def forward_y_first_kernel(lines, section, twisted, gathered):
     start = pl.multiple_of(pl.program_id(0) * SUB, SUB)
-    section_step(sel, groups, section, gathered, twisted, start)
-
-
-def forward_y_first(sel, groups, section):
-    steps = HIGH // PARTS
+    section_step(lines, section, gathered, twisted, start)
+
+
+def forward_y_first(lines, section):
+    groups, steps = lines.shape[:2]
     return pl.pallas_call(
         forward_y_first_kernel,
-        grid_spec=pltpu.PrefetchScalarGridSpec(
-            num_scalar_prefetch=1,
-            grid=(steps,),
-            in_specs=[pl.BlockSpec((1, ROWS, LANES), lambda i, s: (i, 0, 0))] * len(groups)
-            + [pl.BlockSpec(section.shape, lambda i, s: (0, 0))],
-            out_specs=pl.BlockSpec((A, 2, A // PARTS, LANES), lambda i, s: (0, 0, 0, 0)),
-            scratch_shapes=[pltpu.VMEM((2 * LANES, A * SUB), BF)],
-        ),
+        grid=(steps,),
+        in_specs=[
+            pl.BlockSpec((groups, 1, ROWS, LANES), lambda i: (0, i, 0, 0)),
+            pl.BlockSpec(section.shape, lambda i: (0, 0)),
+        ],
+        out_specs=pl.BlockSpec((A, 2, A // PARTS, LANES), lambda i: (0, 0, 0, 0)),
         out_shape=jax.ShapeDtypeStruct((A, 2, A // PARTS, LANES), BF),
+        scratch_shapes=[pltpu.VMEM((2 * LANES, A * SUB), BF)],
         compiler_params=pltpu.CompilerParams(vmem_limit_bytes=VMEM),
-        cost_estimate=cost(4),
+        cost_estimate=cost(7),
         name="forward_y_first",
-    )(sel, *groups, section)
-
-
-def forward_y_kernel(steps, sel, *refs):
-    *groups, section, earlier, last, out, gathered, twisted = refs
+    )(lines, section)
+
+
+def forward_y_kernel(steps, lines, section, earlier, last, after, out, gathered, twisted):
     step = pl.program_id(0)
     first = HIGH // PARTS
 
     @pl.when(step < first)
     def _():
         start = pl.multiple_of(step * SUB, SUB)
-        section_step(sel, groups, section, gathered, twisted, start)
+        section_step(lines, section, gathered, twisted, start)
 
     @pl.when(step >= first)
     def _():
@@ -271,42 +265,40 @@
             out[q] = dot(last[q], jnp.concatenate(rows, axis=0)).astype(BF)
 
 
-def forward_y(sel, groups, section, earlier, last):
+def forward_y(lines, section, earlier, last, after):
+    groups, first = lines.shape[:2]
     steps = 2
-    first = HIGH // PARTS
     count = PAIRS // steps
 
-    def late(i, s):
+    def late(i):
         return (jnp.maximum(i - first, 0), 0, 0)
 
     return pl.pallas_call(
         functools.partial(forward_y_kernel, steps),
-        grid_spec=pltpu.PrefetchScalarGridSpec(
-            num_scalar_prefetch=1,
-            grid=(first + steps,),
-            in_specs=[
-                pl.BlockSpec((1, ROWS, LANES), lambda i, s: (jnp.minimum(i, first - 1), 0, 0))
-            ]
-            * len(groups)
-            + [
-                pl.BlockSpec(section.shape, lambda i, s: (0, 0)),
-                pl.BlockSpec(earlier.shape, lambda i, s: (0, 0, 0, 0)),
-                pl.BlockSpec((count, ROWS, 4 * A), late),
-            ],
-            out_specs=pl.BlockSpec((count, ROWS, LANES), late),
-            scratch_shapes=[
-                pltpu.VMEM((2 * LANES, A * SUB), BF),
-                pltpu.VMEM((A, 2, A // PARTS, LANES), BF),
-            ],
-        ),
+        grid=(first + steps,),
+        in_specs=[
+            pl.BlockSpec(
+                (groups, 1, ROWS, LANES), lambda i: (0, jnp.minimum(i, first - 1), 0, 0)
+            ),
+            pl.BlockSpec(section.shape, lambda i: (0, 0)),
+            pl.BlockSpec(earlier.shape, lambda i: (0, 0, 0, 0)),
+            pl.BlockSpec((count, ROWS, 4 * A), late),
+            pl.BlockSpec(memory_space=pl.ANY),
+        ],
+        out_specs=pl.BlockSpec((count, ROWS, LANES), late),
         out_shape=jax.ShapeDtypeStruct((PAIRS, ROWS, LANES), BF),
+        scratch_shapes=[
+            pltpu.VMEM((2 * LANES, A * SUB), BF),
+            pltpu.VMEM((A, 2, A // PARTS, LANES), BF),
+        ],
         compiler_params=pltpu.CompilerParams(vmem_limit_bytes=VMEM),
-        cost_estimate=cost(8),
+        cost_estimate=cost(10),
         name="forward_y",
-    )(sel, *groups, section, earlier, last)
-
-
-def inverse_kernel(steps, sel, spec, freq_y, square_x, table_y, table_x, after, out, mid):
+    )(lines, section, earlier, last, after)
+
+
+def inverse_kernel(steps, which, sel, spec, freq_y, square_x, table_y, table_x, *rest):
+    out, mid = rest[-2:]
     step = pl.program_id(0)
     count = PAIRS // steps
     each = HALF // steps
@@ -316,9 +308,9 @@
     def _():
         def pair(q, carry):
             pair_id = step * count + q
-            offset = (2 * pair_id + sel[2]).astype(F32)
+            offset = (2 * pair_id + sel[3 * which + 2]).astype(F32)
             row_freq = freq_y[...] + offset
-            inside = row_freq * row_freq + square_x[...] <= limit
+            inside = row_freq * row_freq + square_x[0] <= limit
             values = jnp.where(inside, spec[q].astype(F32), 0.0).astype(BF)
             mixed = dot(table_y[q], values)
             for e in range(2):
@@ -351,7 +343,7 @@
         lax.fori_loop(0, each, line, 0, unroll=4)
 
 
-def inverse(sel, spec, freq_y, square_x, table_y, table_x, after):
+def inverse(which, sel, spec, freq_y, square_x, table_y, table_x, after):
     steps = 2
     count = PAIRS // steps
     each = HALF // steps
@@ -360,18 +352,18 @@
         return jnp.minimum(i, steps - 1)
 
     return pl.pallas_call(
-        functools.partial(inverse_kernel, steps),
+        functools.partial(inverse_kernel, steps, which),
         grid_spec=pltpu.PrefetchScalarGridSpec(
             num_scalar_prefetch=1,
             grid=(2 * steps,),
             in_specs=[
                 pl.BlockSpec((count, ROWS, LANES), lambda i, s: (early(i, s), 0, 0)),
                 pl.BlockSpec((ROWS, LANES), lambda i, s: (0, 0)),
-                pl.BlockSpec((1, LANES), lambda i, s: (0, 0)),
+                pl.BlockSpec((1, 1, LANES), lambda i, s: (which, 0, 0)),
                 pl.BlockSpec((count, 4 * A, ROWS), lambda i, s: (early(i, s), 0, 0)),
-                pl.BlockSpec((1, 1) + table_x.shape[2:], lambda i, s: (s[0], s[1], 0, 0)),
-                pl.BlockSpec(memory_space=pl.ANY),
-            ],
+                pl.BlockSpec((1, 1) + table_x.shape[2:], lambda i, s: (s[3 * which], s[3 * which + 1], 0, 0)),
+            ]
+            + [pl.BlockSpec(memory_space=pl.ANY)] * len(after),
             out_specs=pl.BlockSpec(
                 (each, 2 * A, 2 * LANES), lambda i, s: (jnp.maximum(i - steps, 0), 0, 0)
             ),
@@ -381,51 +373,58 @@
         compiler_params=pltpu.CompilerParams(vmem_limit_bytes=VMEM),
         cost_estimate=cost(8.5),
         name="inverse",
-    )(sel, spec, freq_y, square_x, table_y, table_x, after)
-
-
-def collect_kernel(sheet_count, *refs):
-    sheets, weights, outs = refs[:sheet_count], refs[sheet_count], refs[sheet_count + 1 :]
-    tiles = weights.shape[0] // 4
-    group = tiles // len(outs)
+    )(sel, spec, freq_y, square_x, table_y, table_x, *after)
+
+
+def collect_kernel(near, added, *refs):
+    sheets, weights, out = refs[:near], refs[near], refs[-1]
+    tiles = weights.shape[1] // 4
+    fields = out.shape[0]
     lane = lax.broadcasted_iota(jnp.int32, (tiles, LANES), 1)
     lower = lane < A
 
     def line(i, carry):
         stacked = sheets[0][i]
-        if len(sheets) > 1:
+        if near > 1:
             stacked = jnp.concatenate([sheet[i] for sheet in sheets], axis=0)
-        sums = dot(weights[...], stacked)
+        sums = dot(weights[0], stacked)
         for part in range(2):
             even = sums[2 * part * tiles : (2 * part + 1) * tiles]
             odd = sums[(2 * part + 1) * tiles : (2 * part + 2) * tiles]
             keep = jnp.where(lower, even[:, :LANES], odd[:, LANES:])
             move = jnp.where(lower, even[:, LANES:], odd[:, :LANES])
-            total = (keep + pltpu.roll(move, A, 1)).astype(BF)
-            for o, out in enumerate(outs):
-                out[part, i] = total[o * group : (o + 1) * group]
+            total = keep + pltpu.roll(move, A, 1)
+            total = total.reshape(fields, tiles // fields, LANES)
+            for a in range(added):
+                total = total + refs[near + 1 + a][:, part, i].astype(F32)
+            out[:, part, i] = total.astype(BF)
         return carry
 
-    lax.fori_loop(0, outs[0].shape[1], line, 0, unroll=2)
-
-
-def collect(sheets, weights, fields, part):
-    tiles = weights.shape[0] // 4
+    lax.fori_loop(0, out.shape[2], line, 0, unroll=2)
+
+
+def collect(which, sheets, weights, fields, part, added, after):
+    near = len(sheets)
+    tiles = weights.shape[1] // 4
     group = tiles // fields
     lines = HALF // PARTS
     steps = 2
     each = lines // steps
     sheet_spec = pl.BlockSpec((each, 2 * A, 2 * LANES), lambda i: (part * steps + i, 0, 0))
+    block = pl.BlockSpec((fields, 2, each, group, LANES), lambda i: (0, 0, i, 0, 0))
     return pl.pallas_call(
-        functools.partial(collect_kernel, len(sheets)),
+        functools.partial(collect_kernel, near, len(added)),
         grid=(steps,),
-        in_specs=[sheet_spec] * len(sheets) + [pl.BlockSpec(weights.shape, lambda i: (0, 0))],
-        out_specs=[pl.BlockSpec((2, each, group, LANES), lambda i: (0, i, 0, 0))] * fields,
-        out_shape=[jax.ShapeDtypeStruct((2, lines, group, LANES), BF)] * fields,
+        in_specs=[sheet_spec] * near
+        + [pl.BlockSpec((1,) + weights.shape[1:], lambda i: (which, 0, 0))]
+        + [block] * len(added)
+        + [pl.BlockSpec(memory_space=pl.ANY)] * len(after),
+        out_specs=block,
+        out_shape=jax.ShapeDtypeStruct((fields, 2, lines, group, LANES), BF),
         compiler_params=pltpu.CompilerParams(vmem_limit_bytes=VMEM),
-        cost_estimate=cost(6),
+        cost_estimate=cost(5),
         name="collect",
-    )(*sheets, weights)
+    )(*sheets, weights, *added, *after)
 
 
 def crop_kernel(rows, cols, odd, mine, pot, after, out, held, sems):
@@ -641,89 +640,97 @@
     slot_count = tile_table.shape[1]
     own_slots = blocks_dev * slot_count
     table = tile_table.reshape(field_count, hold_count, own_slots)
-    others = field_pos ^ jnp.arange(field_count, dtype=jnp.int32)
-    mates = hold_pos ^ jnp.arange(hold_count, dtype=jnp.int32)
-
-    def trade(arrays, axis, count):
-        out = [arrays[0]]
-        for o in range(1, count):
-            out.append(lax.ppermute(arrays[o], axis, [(i, i ^ o) for i in range(count)]))
-        return out
-
-    sel = jnp.stack([share, field_pos]).astype(jnp.int32)
+
+    def trade(value, axis):
+        return lax.all_to_all(value, axis, split_axis=0, concat_axis=0, tiled=True)
+
+    sel = share.reshape(1).astype(jnp.int32)
     received = []
     for part in range(PARTS):
-        lines = forward_x(sel, pot_first, section_x, last_x, field_count, part)
-        lines = trade(lines, "beam", field_count)
-        if lines[0].shape[2] != LANES:
-            ratio = LANES // lines[0].shape[2]
-            stacked = jnp.stack(lines)[others]
-            stacked = stacked.reshape((field_count // ratio, ratio) + lines[0].shape)
-            stacked = stacked.transpose(0, 2, 3, 1, 4).reshape(
-                field_count // ratio, lines[0].shape[0], ROWS, LANES
-            )
-            lines = [stacked[g] for g in range(stacked.shape[0])]
-            places = jnp.arange(len(lines), dtype=jnp.int32)
-        else:
-            places = others
+        lines = trade(forward_x(sel, pot_first, section_x, last_x, field_count, part), "beam")
+        if lines.shape[3] != LANES:
+            ratio = LANES // lines.shape[3]
+            lines = lines.reshape((field_count // ratio, ratio) + lines.shape[1:])
+            lines = lines.transpose(0, 2, 3, 1, 4).reshape(-1, HIGH // PARTS, ROWS, LANES)
         received.append(lines)
-    earlier = forward_y_first(places, received[0], section_y)
-    spec = forward_y(places, received[1], section_y, earlier, last_y)
-    specs = [spec]
-    for x in range(1, sheets):
-        top = 1 << (x.bit_length() - 1)
-        bit, source = (top, 0) if x == top else (x ^ top, top)
-        swap = [(i, i ^ bit) for i in range(hold_count)]
-        specs.append(lax.ppermute(specs[source], "slab", swap))
-
-    ids = lax.dynamic_index_in_dim(table, hold_pos, 1, keepdims=False)[others].reshape(-1)
+    earlier = forward_y_first(received[0], section_y)
+
+    ids = lax.dynamic_index_in_dim(table, hold_pos, 1, keepdims=False).reshape(-1)
     tile_y, tile_x = ids // across, ids % across
     mine = (tile_y // band_tiles == field_pos).astype(jnp.int32)
     rows = jnp.clip(tile_y - field_pos * band_tiles, 0, band_tiles - 1)
-    crops = crop(rows, tile_x // 2, tile_x % 2, mine, pot_second, spec)
-    crops = crops.reshape(field_count, own_slots, HALF, LANES)
-    crops = trade([crops[o] for o in range(field_count)], "beam", field_count)
-    crop_total = functools.reduce(jnp.add, [c.astype(F32) for c in crops]).astype(BF)
-
-    beam_row = lax.dynamic_index_in_dim(beam_index, hold_pos, 0, keepdims=False)
-    pair_ids = share ^ jnp.arange(sheets, dtype=jnp.int32)
+    crops = crop(rows, tile_x // 2, tile_x % 2, mine, pot_second, earlier)
+    spec = forward_y(received[1], section_y, earlier, last_y, crops)
+    crops = trade(crops.reshape(field_count, own_slots, HALF, LANES), "beam")
+
+    near = min(sheets, 2)
+    far = sheets // near
+    pair_ids = share ^ jnp.arange(near, dtype=jnp.int32)
     k1_pairs = field_pos * width_k + 2 * pair_ids
-    ordered = table[others][:, mates].reshape(-1)
-    weights = tile_weights(ordered, beam_row, k1_pairs)
+    rows_of = beam_index[hold_pos ^ (near * jnp.arange(far, dtype=jnp.int32))]
+    weights = jnp.stack(
+        [tile_weights(tile_table.reshape(-1), rows_of[f], k1_pairs) for f in range(far)]
+    )
     row = np.arange(ROWS)
     base = (row // (2 * K2_COUNT)) + A * (K2_LOW + row % K2_COUNT)
     base = np.where(row < 4 * K2_COUNT, base, 0)
     freq_y = np.broadcast_to(base[:, None], (ROWS, LANES)).astype(np.float32)
-    lane = jnp.arange(LANES, dtype=jnp.int32)[None, None, :]
-    freq_x = (
-        k1_pairs[:, None, None]
-        + lane // K2_COUNT
-        + A * (K2_LOW + lane % K2_COUNT)
-        + F * beam_row[1]
-    )
-    square_x = jnp.where(lane < 2 * K2_COUNT, freq_x * freq_x, N * N).astype(F32)
-    waves = []
-    for x in range(sheets):
-        sel = jnp.stack([field_pos, pair_ids[x], F * beam_row[0]]).astype(jnp.int32)
-        after = crops[0] if x >= 2 else spec
-        waves.append(inverse(sel, specs[x], freq_y, square_x[x], inverse_y, inverse_x, after))
+    lane = np.arange(LANES)
+    base = np.where(lane < 2 * K2_COUNT, lane // K2_COUNT + A * (K2_LOW + lane % K2_COUNT), N)
+    freq_x = (k1_pairs[None, :] + F * rows_of[:, 1:]).reshape(far * near, 1, 1)
+    freq_x = freq_x + base.astype(np.int32)
+    square_x = (freq_x * freq_x).astype(F32)
+    scalars = jnp.stack(
+        jnp.broadcast_arrays(field_pos, pair_ids[None, :], F * rows_of[:, :1]), axis=-1
+    )
+    scalars = scalars.astype(jnp.int32).reshape(-1)
+
+    shards_x = [spec]
+    for x in range(1, near):
+        shards_x.append(lax.ppermute(spec, "slab", [(i, i ^ x) for i in range(hold_count)]))
+    passed = [[] for _ in range(PARTS)]
+    last_wave = []
+    for f in reversed(range(far)):
+        waves = []
+        for x in range(near):
+            waves.append(
+                inverse(
+                    f * near + x,
+                    scalars,
+                    shards_x[x],
+                    freq_y,
+                    square_x,
+                    inverse_y,
+                    inverse_x,
+                    last_wave,
+                )
+            )
+            last_wave = waves[-1:]
+        for part in range(PARTS):
+            after = [crops] if f == 0 and part == 0 else []
+            partial = collect(f, waves, weights, field_count, part, passed[part] * (f == 0), after)
+            if f:
+                swap = [(i, i ^ (f * near)) for i in range(hold_count)]
+                passed[part].append(lax.ppermute(partial, "slab", swap))
+                last_wave = [partial]
+            else:
+                passed[part] = partial
     halves = []
     for part in range(PARTS):
-        partial = trade(collect(waves, weights, field_count, part), "beam", field_count)
-        total = functools.reduce(jnp.add, [t.astype(F32) for t in partial])
-        halves.append(total.astype(BF).transpose(2, 0, 1, 3))
-    tiles = jnp.concatenate(halves, axis=2).reshape(hold_count, own_slots, 2, HALF, LANES)
-    fields = jnp.stack(trade([tiles[x] for x in range(hold_count)], "slab", hold_count))
+        total = jnp.sum(trade(passed[part], "beam").astype(F32), axis=0).astype(BF)
+        halves.append(total.transpose(2, 0, 1, 3))
+    tiles = trade(jnp.concatenate(halves, axis=2), "slab")
+    fields = tiles.reshape(hold_count, own_slots, 2, HALF, LANES)
+    crop_total = jnp.sum(crops.astype(F32), axis=0).astype(BF)
 
     own = lax.dynamic_index_in_dim(
         lax.dynamic_index_in_dim(table, field_pos, 0, keepdims=False), hold_pos, 0, keepdims=False
     )
-    beams = beam_index[mates]
-    alpha = coefficients(own, beams, aberration[mates]).reshape(2, beam_total, own_slots * G)
+    alpha = coefficients(own, beam_index, aberration).reshape(2, beam_total, own_slots * G)
     first_block = (field_pos * hold_count + hold_pos) * blocks_dev
     counts = lax.dynamic_slice_in_dim(tile_count, first_block, blocks_dev, 0)
     bins = detect_tables(beam_total)
-    sums = detect(alpha, counts, fields, crop_total, plane_waves(beams), *bins)
+    sums = detect(alpha, counts, fields, crop_total, plane_waves(beam_index), *bins)
     return jnp.sum(sums, axis=2).reshape(blocks_dev, slot_count, G, NDET)
 
 

time: 239 us -> 223 us (0.933)
  starting transfers between devices: 71.4 us -> 32.3 us
  waiting for transfers between devices: 30.5 us -> 67.5 us
  local copies, waits for them, and re-layouts: 21.3 us -> 10.6 us
  other arithmetic: 15.1 us -> 10.3 us
  Pallas kernels: 97.6 us -> 101 us
    ppermute x41 -> x3, starting transfers between devices: 71.4 us -> 3.04 us  [the longest x2 3.03 us: shards(): passed[part].append(lax.ppermute(partial, 'slab', swap))]
    all_to_all x0 -> x6, waiting for transfers between devices: none -> 38 us  [trade(): return lax.all_to_all(value, axis, split_axis=0, concat_axis=0, tiled=True)]
    all_to_all x0 -> x6, starting transfers between devices: none -> 29.3 us  [trade(): return lax.all_to_all(value, axis, split_axis=0, concat_axis=0, tiled=True)]
    pallas_call x14 -> x0, local copies, waits for them, and re-layouts: 7.73 us -> none  [collect(): pl.pallas_call(functools.partial(collect_kernel, len(sheets)), grid=(step...]
    another operation x5 -> x3, other arithmetic: 6.26 us -> 1.17 us  [the longest x2 3.81 us: shards(): sel = jnp.stack([field_pos, pair_ids[x], F * beam_row[0]]).astype(jnp.int32)]
    pallas_call x8 -> x10, Pallas kernels: 64.6 us -> 69.3 us  [the longest x4 33.6 us: inverse(): pl.pallas_call(functools.partial(inverse_kernel, steps, which), grid_spec...]
    gather x7 -> x1, local copies, waits for them, and re-layouts: 3.12 us -> 0.56 us  [shards(): rows_of = beam_index[hold_pos ^ near * jnp.arange(far, dtype=jnp.int32)]]
    ppermute x41 -> x3, waiting for transfers between devices: 30.5 us -> 29.6 us  [the longest x2 29.6 us: shards(): passed[part].append(lax.ppermute(partial, 'slab', swap))]
  transfers between devices with their start and end apart: 41 -> 9, of which waited for: 7 -> 6; matrix products, arithmetic and copies ran while one was open for 13% -> 7% of each run, Pallas kernels for 24% -> 33%
where the time goes in v2:
time: 223 us; the launch traced here: 222 us
  Pallas kernels  101 us (45%)
  waiting for transfers between devices  67.5 us (30%)
  starting transfers between devices  32.3 us (14%)
  local copies, waits for them, and re-layouts  10.6 us (5%)
  other arithmetic  10.3 us (5%)
    all_to_all x6, waiting for transfers between devices, trade(): return lax.all_to_all(value, axis, split_axis=0, concat_axis=0, tiled=True)  38 us
    pallas_call x4, Pallas kernels, inverse(): pl.pallas_call(functools.partial(inverse_kernel, steps, which), grid_spec...  33.6 us
    ppermute x2, waiting for transfers between devices, shards(): passed[part].append(lax.ppermute(partial, 'slab', swap))  29.6 us
    all_to_all x6, starting transfers between devices, trade(): return lax.all_to_all(value, axis, split_axis=0, concat_axis=0, tiled=True)  29.3 us
    pallas_call x4, Pallas kernels, collect(): pl.pallas_call(functools.partial(collect_kernel, near, len(added)), grid=...  20.9 us
    pallas_call x2, Pallas kernels, forward_x(): pl.pallas_call(forward_x_kernel, grid_spec=pltpu.PrefetchScalarGridSpec(n...  20.6 us
    pallas_call x1, Pallas kernels, forward_y(): pl.pallas_call(functools.partial(forward_y_kernel, steps), grid=(first +...  8.81 us
    pallas_call x1, Pallas kernels, crop(): pl.pallas_call(crop_kernel, in_specs=[pl.BlockSpec(memory_space=pltpu.SME...  7.11 us
  transfers between devices with their start and end apart: 9, of which 6 were waited for; matrix products, arithmetic and copies ran while one was open for 7% of the time, Pallas kernels for 33%

profile of v2, /device:TPU:0, one launch (start us, length us, event | category | flops | bytes accessed | tf_op | source)
XLA Modules:
  0.0 222.2 jit_solution(3984507678796184467)
XLA Ops:
  0.0 10.3 %forward_x.3 = bf16[8,2,208,128]{3,2,1,0:T(8,128)(2,1)} custom-call(s32[1]{0:T(128)} %bitcast.3.sel, bf16[8,4,16,4096]{3,2,1,0:T(8,128)(2,1)} %bitcast.44, bf16[4,512,1024]{2,1,0:T(8,128)(2,1)} %constant.262.clone.section, bf16[4,8,208,256]{3,2,1,0:T(8,128)(2,1)} %constant.263.clone.last), custom_call_target="tpu_custom_call" | custom-call | flops 9900000256 | tf_op jit(solution)/shard_map/forward_x/pallas_call | solution.py:178
  10.3 7.3 %all-to-all-start.1 = ((bf16[8,2,208,128]{3,2,1,0:T(8,128)(2,1)}), bf16[8,2,208,128]{3,2,1,0:T(8,128)(2,1)S(1)}, u32[]{:S(2)}, u32[]{:S(2)}) async-start(bf16[8,2,208,128]{3,2,1,0:T(8,128)(2,1)} %forward_x.3), calls=%async_computation.1 | async-start | bytes 1703936 | tf_op jit(solution)/shard_map/all_to_all | solution.py:645
  17.6 0.1 copy.50
  17.7 0.6 gather_fusion
  18.3 0.2 multiply_reduce_fusion
  18.5 0.7 fusion.29
  19.1 0.1 copy.52
  19.3 0.1 reshape.919
  19.4 0.6 broadcast_subtract_fusion.1
  20.1 1.9 broadcast_subtract_fusion
  22.0 0.1 copy.51
  22.3 0.6 compare_convert_fusion
  22.8 0.6 and_select_fusion.5
  23.6 0.5 negate_convert_fusion.1
  24.1 0.5 and_select_fusion.6
  24.7 0.5 negate_convert_fusion
  25.2 10.3 %forward_x.2 = bf16[8,2,208,128]{3,2,1,0:T(8,128)(2,1)} custom-call(s32[1]{0:T(128)} %bitcast.3.sel, bf16[8,4,16,4096]{3,2,1,0:T(8,128)(2,1)} %bitcast.45, bf16[4,512,1024]{2,1,0:T(8,128)(2,1)} %constant.262.clone.section, bf16[4,8,208,256]{3,2,1,0:T(8,128)(2,1)} %constant.263.clone.last), custom_call_target="tpu_custom_call" | custom-call | flops 9900000256 | tf_op jit(solution)/shard_map/forward_x/pallas_call | solution.py:178
  35.6 3.6 %all-to-all-done.1.lines = bf16[8,2,208,128]{3,2,1,0:T(8,128)(2,1)S(1)} async-done(((bf16[8,2,208,128]{3,2,1,0:T(8,128)(2,1)}), bf16[8,2,208,128]{3,2,1,0:T(8,128)(2,1)S(1)}, u32[]{:S(2)}, u32[]{:S(2)}) %all-to-all-start.1) | async-done | bytes 852000 | tf_op jit(solution)/shard_map/all_to_all | solution.py:645
  39.2 3.5 %all-to-all-start = ((bf16[8,2,208,128]{3,2,1,0:T(8,128)(2,1)}), bf16[8,2,208,128]{3,2,1,0:T(8,128)(2,1)S(1)}, u32[]{:S(2)}, u32[]{:S(2)}) async-start(bf16[8,2,208,128]{3,2,1,0:T(8,128)(2,1)} %forward_x.2), calls=%async_computation | async-start | bytes 1703936 | tf_op jit(solution)/shard_map/all_to_all | solution.py:645
  42.8 6.0 %forward_y_first.1.after.earlier = bf16[64,2,32,128]{3,2,1,0:T(8,128)(2,1)} custom-call(bf16[8,2,208,128]{3,2,1,0:T(8,128)(2,1)} %copy-done.3, bf16[2048,1024]{1,0:T(8,128)(2,1)} %constant.264.clone.section), custom_call_target="tpu_custom_call" | custom-call | flops 7699999744 | tf_op jit(solution)/shard_map/forward_y_first/pallas_call | solution.py:230
  48.9 7.1 %crop.1.after = bf16[32,32,128]{2,1,0:T(8,128)(2,1)} custom-call(s32[32]{0:T(128)} %get-tuple-element.49.rows, s32[32]{0:T(128)} %get-tuple-element.48.cols, s32[32]{0:T(128)} %get-tuple-element.13.odd, s32[32]{0:T(128)} %get-tuple-element.10.mine, bf16[512,4096]{1,0:T(8,128)(2,1)} %pot.1, bf16[64,2,32,128]{3,2,1,0:T(8,128)(2,1)} %forward_y_first.1.after.earlier), custom_call_target="tpu_custom_call" | custom-call | flops 7699999744 | tf_op jit(solution)/shard_map/crop/pallas_call | solution.py:462
  56.0 8.5 %all-to-all-done.lines = bf16[8,2,208,128]{3,2,1,0:T(8,128)(2,1)S(1)} async-done(((bf16[8,2,208,128]{3,2,1,0:T(8,128)(2,1)}), bf16[8,2,208,128]{3,2,1,0:T(8,128)(2,1)S(1)}, u32[]{:S(2)}, u32[]{:S(2)}) %all-to-all-start) | async-done | bytes 852000 | tf_op jit(solution)/shard_map/all_to_all | solution.py:645
  64.5 0.9 copy-done.4
  65.4 8.8 %forward_y.1.spec = bf16[32,208,128]{2,1,0:T(8,128)(2,1)} custom-call(bf16[8,2,208,128]{3,2,1,0:T(8,128)(2,1)} %copy-done.4, bf16[2048,1024]{1,0:T(8,128)(2,1)} %constant.264.clone.section, bf16[64,2,32,128]{3,2,1,0:T(8,128)(2,1)} %forward_y_first.1.after.earlier, bf16[32,208,256]{2,1,0:T(8,128)(2,1)} %constant.265.clone.last, bf16[32,32,128]{2,1,0:T(8,128)(2,1)} %crop.1.after), custom_call_target="tpu_custom_call" | custom-call | flops 11000000512 | tf_op jit(solution)/shard_map/forward_y/pallas_call | solution.py:276
  74.3 0.4 copy.59
  74.7 0.3 reshape.931
  75.1 0.4 copy.60
  75.5 0.3 reshape.932
  76.1 0.6 reshape.915.sel
  76.8 0.7 multiply_convert_fusion.square_x
  77.5 3.6 %all-to-all-start.2 = ((bf16[8,4,32,128]{3,2,1,0:T(8,128)(2,1)}), bf16[8,4,32,128]{3,2,1,0:T(8,128)(2,1)S(1)}, u32[]{:S(2)}, u32[]{:S(2)}) async-start(bf16[8,4,32,128]{3,2,1,0:T(8,128)(2,1)} %bitcast.13), calls=%async_computation.2 | async-start | bytes 524288 | tf_op jit(solution)/shard_map/all_to_all | solution.py:645
  81.1 8.4 %inverse.4.rest_0_.refs_0_ = bf16[32,128,256]{2,1,0:T(8,128)(2,1)} custom-call(s32[12]{0:T(128)} %reshape.915.sel, bf16[32,208,128]{2,1,0:T(8,128)(2,1)} %forward_y.1.spec, f32[208,128]{1,0:T(8,128)} %constant.267.clone.freq_y, f32[4,1,128]{2,1,0:T(1,128)} %multiply_convert_fusion.square_x, bf16[32,256,208]{2,1,0:T(8,128)(2,1)} %constant.268.clone.table_y, ...), custom_call_target="tpu_custom_call" | custom-call | flops 9349999616 | tf_op jit(solution)/shard_map/inverse/pallas_call | solution.py:354
  89.5 8.4 %inverse.5.refs_1_ = bf16[32,128,256]{2,1,0:T(8,128)(2,1)} custom-call(s32[12]{0:T(128)} %reshape.915.sel, bf16[32,208,128]{2,1,0:T(8,128)(2,1)} %collective-permute-done.spec, f32[208,128]{1,0:T(8,128)} %constant.267.clone.freq_y, f32[4,1,128]{2,1,0:T(1,128)} %multiply_convert_fusion.square_x, bf16[32,256,208]{2,1,0:T(8,128)(2,1)} %constant.268.clone.table_y, ...), custom_call_target="tpu_custom_call" | custom-call | flops 9349999616 | tf_op jit(solution)/shard_map/inverse/pallas_call | solution.py:354
  97.9 5.1 %collect.5 = bf16[8,2,16,16,128]{4,3,2,1,0:T(8,128)(2,1)} custom-call(bf16[32,128,256]{2,1,0:T(8,128)(2,1)} %inverse.4.rest_0_.refs_0_, bf16[32,128,256]{2,1,0:T(8,128)(2,1)} %inverse.5.refs_1_, bf16[2,512,256]{2,1,0:T(8,128)(2,1)} %copy-done.5), custom_call_target="tpu_custom_call" | custom-call | flops 5500000256 | tf_op jit(solution)/shard_map/collect/pallas_call | solution.py:415
  103.0 5.3 %collect.4.rest_0_ = bf16[8,2,16,16,128]{4,3,2,1,0:T(8,128)(2,1)} custom-call(bf16[32,128,256]{2,1,0:T(8,128)(2,1)} %inverse.4.rest_0_.refs_0_, bf16[32,128,256]{2,1,0:T(8,128)(2,1)} %inverse.5.refs_1_, bf16[2,512,256]{2,1,0:T(8,128)(2,1)} %copy-done.5), custom_call_target="tpu_custom_call" | custom-call | flops 5500000256 | tf_op jit(solution)/shard_map/collect/pallas_call | solution.py:415
  108.3 1.5 collective-permute-start.1
  109.8 8.4 %inverse.6.rest_0_.refs_0_ = bf16[32,128,256]{2,1,0:T(8,128)(2,1)} custom-call(s32[12]{0:T(128)} %reshape.915.sel, bf16[32,208,128]{2,1,0:T(8,128)(2,1)} %forward_y.1.spec, f32[208,128]{1,0:T(8,128)} %constant.267.clone.freq_y, f32[4,1,128]{2,1,0:T(1,128)} %multiply_convert_fusion.square_x, bf16[32,256,208]{2,1,0:T(8,128)(2,1)} %constant.268.clone.table_y, ...), custom_call_target="tpu_custom_call" | custom-call | flops 9349999616 | tf_op jit(solution)/shard_map/inverse/pallas_call | solution.py:354
  118.2 8.4 %inverse.7.refs_1_ = bf16[32,128,256]{2,1,0:T(8,128)(2,1)} custom-call(s32[12]{0:T(128)} %reshape.915.sel, bf16[32,208,128]{2,1,0:T(8,128)(2,1)} %collective-permute-done.spec, f32[208,128]{1,0:T(8,128)} %constant.267.clone.freq_y, f32[4,1,128]{2,1,0:T(1,128)} %multiply_convert_fusion.square_x, bf16[32,256,208]{2,1,0:T(8,128)(2,1)} %constant.268.clone.table_y, ...), custom_call_target="tpu_custom_call" | custom-call | flops 9349999616 | tf_op jit(solution)/shard_map/inverse/pallas_call | solution.py:354
  126.6 7.1 %collective-permute-done.1.refs_3_ = bf16[8,2,16,16,128]{4,3,2,1,0:T(8,128)(2,1)S(1)} collective-permute-done((bf16[8,2,16,16,128]{4,3,2,1,0:T(8,128)(2,1)S(1)}, bf16[8,2,16,16,128]{4,3,2,1,0:T(8,128)(2,1)S(1)}, u32[]{:S(2)}, u32[]{:S(2)}) %collective-permute-start.1) | collective-permute-done | bytes 1048608 | tf_op jit(solution)/shard_map/ppermute | solution.py:714
  133.7 1.0 copy-done.12
  134.7 5.3 %collect.6 = bf16[8,2,16,16,128]{4,3,2,1,0:T(8,128)(2,1)} custom-call(bf16[32,128,256]{2,1,0:T(8,128)(2,1)} %inverse.6.rest_0_.refs_0_, bf16[32,128,256]{2,1,0:T(8,128)(2,1)} %inverse.7.refs_1_, bf16[2,512,256]{2,1,0:T(8,128)(2,1)} %copy-done.5, bf16[8,2,16,16,128]{4,3,2,1,0:T(8,128)(2,1)} %copy-done.12, bf16[8,4,32,128]{3,2,1,0:T(8,128)(2,1)} %copy-done), custom_call_target="tpu_custom_call" | custom-call | flops 5500000256 | tf_op jit(solution)/shard_map/collect/pallas_call | solution.py:415
  139.9 5.6 %all-to-all-start.3 = ((bf16[8,2,16,16,128]{4,3,2,1,0:T(8,128)(2,1)}), bf16[8,2,16,16,128]{4,3,2,1,0:T(8,128)(2,1)S(1)}, u32[]{:S(2)}, u32[]{:S(2)}) async-start(bf16[8,2,16,16,128]{4,3,2,1,0:T(8,128)(2,1)} %collect.6), calls=%async_computation.3 | async-start | bytes 2097152 | tf_op jit(solution)/shard_map/all_to_all | solution.py:645
  145.6 1.5 collective-permute-start.2
  147.1 22.4 %collective-permute-done.2.refs_3_ = bf16[8,2,16,16,128]{4,3,2,1,0:T(8,128)(2,1)S(1)} collective-permute-done((bf16[8,2,16,16,128]{4,3,2,1,0:T(8,128)(2,1)S(1)}, bf16[8,2,16,16,128]{4,3,2,1,0:T(8,128)(2,1)S(1)}, u32[]{:S(2)}, u32[]{:S(2)}) %collective-permute-start.2) | collective-permute-done | bytes 1048608 | tf_op jit(solution)/shard_map/ppermute | solution.py:714
  169.6 1.0 copy-done.13
  170.6 5.3 %collect.7 = bf16[8,2,16,16,128]{4,3,2,1,0:T(8,128)(2,1)} custom-call(bf16[32,128,256]{2,1,0:T(8,128)(2,1)} %inverse.6.rest_0_.refs_0_, bf16[32,128,256]{2,1,0:T(8,128)(2,1)} %inverse.7.refs_1_, bf16[2,512,256]{2,1,0:T(8,128)(2,1)} %copy-done.5, bf16[8,2,16,16,128]{4,3,2,1,0:T(8,128)(2,1)} %copy-done.13), custom_call_target="tpu_custom_call" | custom-call | flops 5500000256 | tf_op jit(solution)/shard_map/collect/pallas_call | solution.py:415
  175.8 5.9 %all-to-all-start.4 = ((bf16[8,2,16,16,128]{4,3,2,1,0:T(8,128)(2,1)}), bf16[8,2,16,16,128]{4,3,2,1,0:T(8,128)(2,1)S(1)}, u32[]{:S(2)}, u32[]{:S(2)}) async-start(bf16[8,2,16,16,128]{4,3,2,1,0:T(8,128)(2,1)} %collect.7), calls=%async_computation.4 | async-start | bytes 2097152 | tf_op jit(solution)/shard_map/all_to_all | solution.py:645
  181.7 0.2 dynamic-slice_reduce_fusion
  182.4 0.7 dynamic_slice.14.counts
  183.1 0.1 fusion.28
  183.3 0.3 fusion.14
  183.6 0.1 reduce_sum.45
  183.8 21.7 %all-to-all-done.4 = bf16[8,2,16,16,128]{4,3,2,1,0:T(8,128)(2,1)S(1)} async-done(((bf16[8,2,16,16,128]{4,3,2,1,0:T(8,128)(2,1)}), bf16[8,2,16,16,128]{4,3,2,1,0:T(8,128)(2,1)S(1)}, u32[]{:S(2)}, u32[]{:S(2)}) %all-to-all-start.4) | async-done | bytes 1048608 | tf_op jit(solution)/shard_map/all_to_all | solution.py:645
  205.5 0.1 reduce_sum.46
  205.7 0.8 copy.57
  206.4 3.4 %all-to-all-start.5 = ((bf16[16,2,32,128]{3,2,1,0:T(8,128)(2,1)}), bf16[16,2,32,128]{3,2,1,0:T(8,128)(2,1)S(1)}, u32[]{:S(2)}, u32[]{:S(2)}) async-start(bf16[16,2,32,128]{3,2,1,0:T(8,128)(2,1)} %copy.57), calls=%async_computation.5 | async-start | bytes 524288 | tf_op jit(solution)/shard_map/all_to_all | solution.py:645
  209.9 0.6 pad_maximum_fusion.4.alpha
  210.5 0.7 pad_maximum_fusion.3.plane
  211.1 0.6 reduce_sum.47.pot
  211.8 4.1 %all-to-all-done.5 = bf16[16,2,32,128]{3,2,1,0:T(8,128)(2,1)S(1)} async-done(((bf16[16,2,32,128]{3,2,1,0:T(8,128)(2,1)}), bf16[16,2,32,128]{3,2,1,0:T(8,128)(2,1)S(1)}, u32[]{:S(2)}, u32[]{:S(2)}) %all-to-all-start.5) | async-done | bytes 262176 | tf_op jit(solution)/shard_map/all_to_all | solution.py:645
  215.9 0.7 copy-done.2
  216.6 4.0 %detect.1 = f32[12,16,128]{2,1,0:T(8,128)} custom-call(f32[2,4,12]{2,1,0:T(4,128)} %pad_maximum_fusion.4.alpha, s32[1]{0:T(128)} %dynamic_slice.14.counts, bf16[4,4,2,32,128]{4,3,2,1,0:T(8,128)(2,1)} %bitcast.41, bf16[4,32,128]{2,1,0:T(8,128)(2,1)} %reduce_sum.47.pot, f32[4,2,32,128]{3,2,1,0:T(8,128)} %pad_maximum_fusion.3.plane, ...), custom_call_target="tpu_custom_call" | custom-call | tf_op jit(solution)/shard_map/detect/pallas_call | solution.py:521
  220.6 1.0 reduce_sum.48
  221.6 0.6 copy.58
  (68 shorter events, 1.5 us)
Async XLA Ops:
  0.0 17.6 %copy-start.6 = (s32[4,2]{0,1:T(2,128)S(1)}, s32[4,2]{0,1:T(2,128)}, u32[]{:S(2)}) copy-start(s32[4,2]{0,1:T(2,128)} %param.19) | copy-start | bytes 100
  0.0 19.1 %copy-start.7 = (s32[32,4]{0,1:T(4,128)S(1)}, s32[32,4]{0,1:T(4,128)}, u32[]{:S(2)}) copy-start(s32[32,4]{0,1:T(4,128)} %param.21) | copy-start | bytes 1540
  10.3 28.9 %all-to-all-start.1 = ((bf16[8,2,208,128]{3,2,1,0:T(8,128)(2,1)}), bf16[8,2,208,128]{3,2,1,0:T(8,128)(2,1)S(1)}, u32[]{:S(2)}, u32[]{:S(2)}) async-start(bf16[8,2,208,128]{3,2,1,0:T(8,128)(2,1)} %forward_x.3), calls=%async_computation.1 | async-start | bytes 1703936 | tf_op jit(solution)/shard_map/all_to_all | solution.py:645
  39.2 3.6 %copy-start.3 = (bf16[8,2,208,128]{3,2,1,0:T(8,128)(2,1)}, bf16[8,2,208,128]{3,2,1,0:T(8,128)(2,1)S(1)}, u32[]{:S(2)}) copy-start(bf16[8,2,208,128]{3,2,1,0:T(8,128)(2,1)S(1)} %all-to-all-done.1.lines) | copy-start | bytes 2555908
  39.2 25.3 %all-to-all-start = ((bf16[8,2,208,128]{3,2,1,0:T(8,128)(2,1)}), bf16[8,2,208,128]{3,2,1,0:T(8,128)(2,1)S(1)}, u32[]{:S(2)}, u32[]{:S(2)}) async-start(bf16[8,2,208,128]{3,2,1,0:T(8,128)(2,1)} %forward_x.2), calls=%async_computation | async-start | bytes 1703936 | tf_op jit(solution)/shard_map/all_to_all | solution.py:645
  64.5 0.9 copy-start.4
  74.2 2.6 %copy-start.8 = (s32[128]{0:T(128)S(1)}, s32[128]{0:T(128)}, u32[]{:S(2)}) copy-start(s32[128]{0:T(128)} %constant.266.clone) | copy-start | bytes 1540
  74.2 15.3 %collective-permute-start = (bf16[32,208,128]{2,1,0:T(8,128)(2,1)}, bf16[32,208,128]{2,1,0:T(8,128)(2,1)}, u32[]{:S(2)}, u32[]{:S(2)}) collective-permute-start(bf16[32,208,128]{2,1,0:T(8,128)(2,1)} %forward_y.1.spec), channel_id=1, source_target_pairs={{0,1},{1,0},{2,3},{3,2},{4,5},{5,4},{6,7},{7,6},{8,9},{9,8},{10,11... | collective-permute-start | bytes 5111816 | tf_op jit(solution)/shard_map/ppermute | solution.py:690
  76.8 12.7 %copy-start.5 = (bf16[2,512,256]{2,1,0:T(8,128)(2,1)}, bf16[2,512,256]{2,1,0:T(8,128)(2,1)S(1)}, u32[]{:S(2)}) copy-start(bf16[2,512,256]{2,1,0:T(8,128)(2,1)S(1)} %constant_dynamic-update-slice_fusion.refs_2_) | copy-start | bytes 1572868
  77.5 49.0 %all-to-all-start.2 = ((bf16[8,4,32,128]{3,2,1,0:T(8,128)(2,1)}), bf16[8,4,32,128]{3,2,1,0:T(8,128)(2,1)S(1)}, u32[]{:S(2)}, u32[]{:S(2)}) async-start(bf16[8,4,32,128]{3,2,1,0:T(8,128)(2,1)} %bitcast.13), calls=%async_computation.2 | async-start | bytes 524288 | tf_op jit(solution)/shard_map/all_to_all | solution.py:645
  103.0 5.3 %copy-start.11 = (bf16[8,2,16,16,128]{4,3,2,1,0:T(8,128)(2,1)S(1)}, bf16[8,2,16,16,128]{4,3,2,1,0:T(8,128)(2,1)}, u32[]{:S(2)}) copy-start(bf16[8,2,16,16,128]{4,3,2,1,0:T(8,128)(2,1)} %collect.5) | copy-start | bytes 3145732
  108.3 25.4 %collective-permute-start.1 = (bf16[8,2,16,16,128]{4,3,2,1,0:T(8,128)(2,1)S(1)}, bf16[8,2,16,16,128]{4,3,2,1,0:T(8,128)(2,1)S(1)}, u32[]{:S(2)}, u32[]{:S(2)}) collective-permute-start(bf16[8,2,16,16,128]{4,3,2,1,0:T(8,128)(2,1)S(1)} %copy-done.11), channel_id=1, source_target_pairs={{0,2},{1,3},{2,0},{3,1},{4,6},{5,7},{6,4},{7,5},{8,10},{9,11},{10,... | collective-permute-start | bytes 3145736 | tf_op jit(solution)/shard_map/ppermute | solution.py:714
  126.6 19.0 %copy-start.10 = (bf16[8,2,16,16,128]{4,3,2,1,0:T(8,128)(2,1)S(1)}, bf16[8,2,16,16,128]{4,3,2,1,0:T(8,128)(2,1)}, u32[]{:S(2)}) copy-start(bf16[8,2,16,16,128]{4,3,2,1,0:T(8,128)(2,1)} %collect.4.rest_0_) | copy-start | bytes 3145732
  126.6 7.1 %copy-start = (bf16[8,4,32,128]{3,2,1,0:T(8,128)(2,1)}, bf16[8,4,32,128]{3,2,1,0:T(8,128)(2,1)S(1)}, u32[]{:S(2)}) copy-start(bf16[8,4,32,128]{3,2,1,0:T(8,128)(2,1)S(1)} %all-to-all-done.2.refs_4_) | copy-start | bytes 786436
  133.7 1.0 copy-start.12
  139.9 35.9 %all-to-all-start.3 = ((bf16[8,2,16,16,128]{4,3,2,1,0:T(8,128)(2,1)}), bf16[8,2,16,16,128]{4,3,2,1,0:T(8,128)(2,1)S(1)}, u32[]{:S(2)}, u32[]{:S(2)}) async-start(bf16[8,2,16,16,128]{4,3,2,1,0:T(8,128)(2,1)} %collect.6), calls=%async_computation.3 | async-start | bytes 2097152 | tf_op jit(solution)/shard_map/all_to_all | solution.py:645
  145.6 36.9 %copy-start.14 = (s32[32]{0:T(128)S(1)}, s32[32]{0:T(128)}, u32[]{:S(2)}) copy-start(s32[32]{0:T(128)} %param.22) | copy-start | bytes 388
  145.6 37.5 %copy-start.9 = (f32[4]{0:T(128)S(1)}, f32[4]{0:T(128)}, u32[]{:S(2)}) copy-start(f32[4]{0:T(128)} %param.20) | copy-start | bytes 52
  145.6 24.0 %collective-permute-start.2 = (bf16[8,2,16,16,128]{4,3,2,1,0:T(8,128)(2,1)S(1)}, bf16[8,2,16,16,128]{4,3,2,1,0:T(8,128)(2,1)S(1)}, u32[]{:S(2)}, u32[]{:S(2)}) collective-permute-start(bf16[8,2,16,16,128]{4,3,2,1,0:T(8,128)(2,1)S(1)} %copy-done.10), channel_id=1, source_target_pairs={{0,2},{1,3},{2,0},{3,1},{4,6},{5,7},{6,4},{7,5},{8,10},{9,11},{10,... | collective-permute-start | bytes 3145736 | tf_op jit(solution)/shard_map/ppermute | solution.py:714
  169.6 1.0 copy-start.13
  175.8 35.3 %copy-start.1 = (bf16[8,4,32,128]{3,2,1,0:T(8,128)(2,1)S(1)}, bf16[8,4,32,128]{3,2,1,0:T(8,128)(2,1)}, u32[]{:S(2)}) copy-start(bf16[8,4,32,128]{3,2,1,0:T(8,128)(2,1)} %copy-done) | copy-start | bytes 786436
  175.8 29.7 %all-to-all-start.4 = ((bf16[8,2,16,16,128]{4,3,2,1,0:T(8,128)(2,1)}), bf16[8,2,16,16,128]{4,3,2,1,0:T(8,128)(2,1)S(1)}, u32[]{:S(2)}, u32[]{:S(2)}) async-start(bf16[8,2,16,16,128]{4,3,2,1,0:T(8,128)(2,1)} %collect.7), calls=%async_computation.4 | async-start | bytes 2097152 | tf_op jit(solution)/shard_map/all_to_all | solution.py:645
  206.4 9.4 %all-to-all-start.5 = ((bf16[16,2,32,128]{3,2,1,0:T(8,128)(2,1)}), bf16[16,2,32,128]{3,2,1,0:T(8,128)(2,1)S(1)}, u32[]{:S(2)}, u32[]{:S(2)}) async-start(bf16[16,2,32,128]{3,2,1,0:T(8,128)(2,1)} %copy.57), calls=%async_computation.5 | async-start | bytes 524288 | tf_op jit(solution)/shard_map/all_to_all | solution.py:645
  215.9 0.7 copy-start.2

commit v3 on v2

--- a/solution.py
+++ b/solution.py
@@ -143,7 +143,7 @@
 
     def chunk(t, carry):
         block = pot[:, 0, :, pl.ds(pl.multiple_of(t * LANES, LANES), LANES)]
-        values = block.reshape(lanes, LANES).astype(F32).T
+        values = block.reshape(lanes, LANES).T.astype(F32)
         sine, cosine = sine_cosine(values)
         cos_ref[pl.ds(2 * t, 2)] = cosine.astype(BF).reshape(2, A, lanes)
         sin_ref[pl.ds(2 * t, 2)] = sine.astype(BF).reshape(2, A, lanes)
@@ -297,6 +297,21 @@
     )(lines, section, earlier, last, after)
 
 
+def order_kernel(value, after, out):
+    pass
+
+
+def order(value, after):
+    return pl.pallas_call(
+        order_kernel,
+        in_specs=[pl.BlockSpec(memory_space=pl.ANY)] * 2,
+        out_specs=pl.BlockSpec(memory_space=pl.ANY),
+        out_shape=jax.ShapeDtypeStruct(value.shape, value.dtype),
+        input_output_aliases={0: 0},
+        name="order",
+    )(value, after)
+
+
 def inverse_kernel(steps, which, sel, spec, freq_y, square_x, table_y, table_x, *rest):
     out, mid = rest[-2:]
     step = pl.program_id(0)
@@ -371,15 +386,17 @@
         ),
         out_shape=jax.ShapeDtypeStruct((HALF, 2 * A, 2 * LANES), BF),
         compiler_params=pltpu.CompilerParams(vmem_limit_bytes=VMEM),
-        cost_estimate=cost(8.5),
+        cost_estimate=cost(3),
         name="inverse",
     )(sel, spec, freq_y, square_x, table_y, table_x, *after)
 
 
 def collect_kernel(near, added, *refs):
-    sheets, weights, out = refs[:near], refs[near], refs[-1]
-    tiles = weights.shape[1] // 4
-    fields = out.shape[0]
+    sheets, weights = refs[:near], refs[near]
+    out, held = refs[-2:]
+    devices, _, slots, lines, _ = out.shape
+    tiles = devices * slots
+    pitch = lines + 1
     lane = lax.broadcasted_iota(jnp.int32, (tiles, LANES), 1)
     lower = lane < A
 
@@ -394,37 +411,44 @@
             keep = jnp.where(lower, even[:, :LANES], odd[:, LANES:])
             move = jnp.where(lower, even[:, LANES:], odd[:, :LANES])
             total = keep + pltpu.roll(move, A, 1)
-            total = total.reshape(fields, tiles // fields, LANES)
-            for a in range(added):
-                total = total + refs[near + 1 + a][:, part, i].astype(F32)
-            out[:, part, i] = total.astype(BF)
+            held[pl.ds(part * tiles * pitch + i, tiles, stride=pitch), :] = total
         return carry
 
-    lax.fori_loop(0, out.shape[2], line, 0, unroll=2)
-
-
-def collect(which, sheets, weights, fields, part, added, after):
+    lax.fori_loop(0, lines, line, 0, unroll=4)
+
+    def device(d, carry):
+        for part in range(2):
+            for slot in range(slots):
+                start = (part * tiles + d * slots + slot) * pitch
+                total = held[pl.ds(start, lines), :]
+                for a in range(added):
+                    total = total + refs[near + 1 + a][d, part, slot].astype(F32)
+                out[d, part, slot] = total.astype(BF)
+        return carry
+
+    lax.fori_loop(0, devices, device, 0, unroll=4)
+
+
+def collect(which, sheets, weights, devices, part, added):
     near = len(sheets)
     tiles = weights.shape[1] // 4
-    group = tiles // fields
     lines = HALF // PARTS
-    steps = 2
-    each = lines // steps
-    sheet_spec = pl.BlockSpec((each, 2 * A, 2 * LANES), lambda i: (part * steps + i, 0, 0))
-    block = pl.BlockSpec((fields, 2, each, group, LANES), lambda i: (0, 0, i, 0, 0))
+    shape = (devices, 2, tiles // devices, lines, LANES)
+    sheet_spec = pl.BlockSpec((lines, 2 * A, 2 * LANES), lambda i: (part, 0, 0))
+    block = pl.BlockSpec(shape, lambda i: (0, 0, 0, 0, 0))
     return pl.pallas_call(
         functools.partial(collect_kernel, near, len(added)),
-        grid=(steps,),
+        grid=(1,),
         in_specs=[sheet_spec] * near
         + [pl.BlockSpec((1,) + weights.shape[1:], lambda i: (which, 0, 0))]
-        + [block] * len(added)
-        + [pl.BlockSpec(memory_space=pl.ANY)] * len(after),
+        + [block] * len(added),
         out_specs=block,
-        out_shape=jax.ShapeDtypeStruct((fields, 2, lines, group, LANES), BF),
+        out_shape=jax.ShapeDtypeStruct(shape, BF),
+        scratch_shapes=[pltpu.VMEM((2 * tiles * (lines + 1), LANES), F32)],
         compiler_params=pltpu.CompilerParams(vmem_limit_bytes=VMEM),
-        cost_estimate=cost(5),
+        cost_estimate=cost(1.5),
         name="collect",
-    )(*sheets, weights, *added, *after)
+    )(*sheets, weights, *added)
 
 
 def crop_kernel(rows, cols, odd, mine, pot, after, out, held, sems):
@@ -472,12 +496,17 @@
     )(rows, cols, odd, mine, pot, after)
 
 
-def detect_kernel(alpha, counts, fields, pot, plane, across, down, bins, out, lines):
-    beams, slots = fields.shape[0], fields.shape[1]
+def detect_kernel(parts, alpha, counts, *refs):
+    fields = refs[:parts]
+    pot, plane, across, down, bins, out, lines, held = refs[parts:]
+    beams, _, slots = fields[0].shape[:3]
     for s in range(slots):
         waves = []
         for j in range(beams):
-            re, im = fields[j, s, 0].astype(F32), fields[j, s, 1].astype(F32)
+            re, im = (
+                jnp.concatenate([half[j, part, s] for half in fields], axis=0).astype(F32)
+                for part in range(2)
+            )
             cos, sin = plane[j, 0], plane[j, 1]
             waves.append((re * cos - im * sin, re * sin + im * cos))
         turned, level = sine_cosine(pot[s].astype(F32))
@@ -511,22 +540,27 @@
         sums = jnp.sum(power[None] * bins[...], axis=1)
         block, slot = divmod(i // G, slots // counts.shape[0])
         active = slot < counts[block]
-        out[i] = jnp.where(active, sums, 0.0)
+        held[i * NDET : (i + 1) * NDET, :] = jnp.where(active, sums, 0.0)
+    out[...] = jnp.sum(held[...].T, axis=0, keepdims=True)
 
 
 def detect(alpha, counts, fields, pot, plane, across, down, bins):
-    slots = fields.shape[1]
+    slots = fields[0].shape[2]
+    rows = -(-slots * G * NDET // LANES) * LANES
     smem = pl.BlockSpec(memory_space=pltpu.SMEM)
     vmem = pl.BlockSpec(memory_space=pltpu.VMEM)
     return pl.pallas_call(
-        detect_kernel,
-        in_specs=[smem, smem] + [vmem] * 6,
+        functools.partial(detect_kernel, len(fields)),
+        in_specs=[smem, smem] + [vmem] * (5 + len(fields)),
         out_specs=vmem,
-        out_shape=jax.ShapeDtypeStruct((slots * G, NDET, LANES), F32),
-        scratch_shapes=[pltpu.VMEM((2 * slots * G, HALF, LANES), BF)],
+        out_shape=jax.ShapeDtypeStruct((1, rows), F32),
+        scratch_shapes=[
+            pltpu.VMEM((2 * slots * G, HALF, LANES), BF),
+            pltpu.VMEM((rows, LANES), F32),
+        ],
         compiler_params=pltpu.CompilerParams(vmem_limit_bytes=VMEM),
         name="detect",
-    )(alpha, counts, fields, pot, plane, across, down, bins)
+    )(alpha, counts, *fields, pot, plane, across, down, bins)
 
 
 def detect_tables(beam_total):
@@ -661,7 +695,7 @@
     rows = jnp.clip(tile_y - field_pos * band_tiles, 0, band_tiles - 1)
     crops = crop(rows, tile_x // 2, tile_x % 2, mine, pot_second, earlier)
     spec = forward_y(received[1], section_y, earlier, last_y, crops)
-    crops = trade(crops.reshape(field_count, own_slots, HALF, LANES), "beam")
+    crops = crops.reshape(field_count, own_slots, HALF, LANES)
 
     near = min(sheets, 2)
     far = sheets // near
@@ -707,20 +741,23 @@
             )
             last_wave = waves[-1:]
         for part in range(PARTS):
-            after = [crops] if f == 0 and part == 0 else []
-            partial = collect(f, waves, weights, field_count, part, passed[part] * (f == 0), after)
+            partial = collect(
+                f, waves, weights, field_count * hold_count, part, passed[part] * (f == 0)
+            )
             if f:
                 swap = [(i, i ^ (f * near)) for i in range(hold_count)]
                 passed[part].append(lax.ppermute(partial, "slab", swap))
                 last_wave = [partial]
             else:
                 passed[part] = partial
-    halves = []
+        if f:
+            crops = order(crops, last_wave[0])
+    crops = trade(crops, "beam")
+    fields = []
     for part in range(PARTS):
-        total = jnp.sum(trade(passed[part], "beam").astype(F32), axis=0).astype(BF)
-        halves.append(total.transpose(2, 0, 1, 3))
-    tiles = trade(jnp.concatenate(halves, axis=2), "slab")
-    fields = tiles.reshape(hold_count, own_slots, 2, HALF, LANES)
+        tiles = trade(passed[part], ("beam", "slab"))
+        tiles = tiles.reshape((field_count, hold_count) + tiles.shape[1:]).astype(F32)
+        fields.append(jnp.sum(tiles, axis=0).astype(BF))
     crop_total = jnp.sum(crops.astype(F32), axis=0).astype(BF)
 
     own = lax.dynamic_index_in_dim(
@@ -731,7 +768,7 @@
     counts = lax.dynamic_slice_in_dim(tile_count, first_block, blocks_dev, 0)
     bins = detect_tables(beam_total)
     sums = detect(alpha, counts, fields, crop_total, plane_waves(beam_index), *bins)
-    return jnp.sum(sums, axis=2).reshape(blocks_dev, slot_count, G, NDET)
+    return sums[0, : own_slots * G * NDET].reshape(blocks_dev, slot_count, G, NDET)
 
 
 def solution(mesh):

time: 223 us -> 219 us (0.982)
  starting transfers between devices: 32.3 us -> 27.4 us
    all_to_all x6 -> x5, starting transfers between devices: 29.3 us -> 24.1 us  [trade(): return lax.all_to_all(value, axis, split_axis=0, concat_axis=0, tiled=True)]
    ppermute x2, waiting for transfers between devices: 29.6 us -> 34.7 us  [shards(): passed[part].append(lax.ppermute(partial, 'slab', swap))]
    all_to_all x6 -> x5, waiting for transfers between devices: 38 us -> 34.7 us  [trade(): return lax.all_to_all(value, axis, split_axis=0, concat_axis=0, tiled=True)]
  transfers between devices with their start and end apart: 9 -> 8, of which waited for: 6 -> 4; matrix products, arithmetic and copies ran while one was open for 7% -> 7% of each run, Pallas kernels for 33% -> 29%
where the time goes in v3:
time: 219 us; the launch traced here: 218 us
  Pallas kernels  99.7 us (46%)
  waiting for transfers between devices  69.4 us (32%)
  starting transfers between devices  27.4 us (13%)
  local copies, waits for them, and re-layouts  11 us (5%)
  other arithmetic  10.6 us (5%)
    all_to_all x5, waiting for transfers between devices, trade(): return lax.all_to_all(value, axis, split_axis=0, concat_axis=0, tiled=True)  34.7 us
    ppermute x2, waiting for transfers between devices, shards(): passed[part].append(lax.ppermute(partial, 'slab', swap))  34.7 us
    pallas_call x4, Pallas kernels, inverse(): pl.pallas_call(functools.partial(inverse_kernel, steps, which), grid_spec...  33.6 us
    all_to_all x5, starting transfers between devices, trade(): return lax.all_to_all(value, axis, split_axis=0, concat_axis=0, tiled=True)  24.1 us
    pallas_call x2, Pallas kernels, forward_x(): pl.pallas_call(forward_x_kernel, grid_spec=pltpu.PrefetchScalarGridSpec(n...  20.2 us
    pallas_call x4, Pallas kernels, collect(): pl.pallas_call(functools.partial(collect_kernel, near, len(added)), grid=...  20 us
    pallas_call x1, Pallas kernels, forward_y(): pl.pallas_call(functools.partial(forward_y_kernel, steps), grid=(first +...  8.81 us
    pallas_call x1, Pallas kernels, crop(): pl.pallas_call(crop_kernel, in_specs=[pl.BlockSpec(memory_space=pltpu.SME...  7.1 us
  transfers between devices with their start and end apart: 8, of which 4 were waited for; matrix products, arithmetic and copies ran while one was open for 7% of the time, Pallas kernels for 29%

profile of v3, /device:TPU:0, one launch (start us, length us, event | category | flops | bytes accessed | tf_op | source)
XLA Modules:
  0.0 218.5 jit_solution(18250831871355279217)
XLA Ops:
  0.0 10.1 %forward_x.3 = bf16[8,2,208,128]{3,2,1,0:T(8,128)(2,1)} custom-call(s32[1]{0:T(128)} %bitcast.3.sel, bf16[8,4,16,4096]{3,2,1,0:T(8,128)(2,1)} %bitcast.43, bf16[4,512,1024]{2,1,0:T(8,128)(2,1)} %constant.261.clone.section, bf16[4,8,208,256]{3,2,1,0:T(8,128)(2,1)} %constant.262.clone.last), custom_call_target="tpu_custom_call" | custom-call | flops 9900000256 | tf_op jit(solution)/shard_map/forward_x/pallas_call | solution.py:178
  10.1 7.3 %all-to-all-start.1 = ((bf16[8,2,208,128]{3,2,1,0:T(8,128)(2,1)}), bf16[8,2,208,128]{3,2,1,0:T(8,128)(2,1)S(1)}, u32[]{:S(2)}, u32[]{:S(2)}) async-start(bf16[8,2,208,128]{3,2,1,0:T(8,128)(2,1)} %forward_x.3), calls=%async_computation.1 | async-start | bytes 1703936 | tf_op jit(solution)/shard_map/all_to_all | solution.py:679
  17.4 0.1 copy.32
  17.5 0.6 gather_fusion
  18.1 0.2 multiply_reduce_fusion
  18.3 0.7 fusion.29
  19.0 0.1 copy.34
  19.2 0.1 copy.33
  19.4 0.5 compare_convert_fusion
  19.9 0.1 reshape.919
  20.1 0.7 broadcast_subtract_fusion.1
  20.8 1.8 broadcast_subtract_fusion
  22.7 0.5 and_select_fusion.5
  23.2 0.5 negate_convert_fusion
  23.8 10.1 %forward_x.2 = bf16[8,2,208,128]{3,2,1,0:T(8,128)(2,1)} custom-call(s32[1]{0:T(128)} %bitcast.3.sel, bf16[8,4,16,4096]{3,2,1,0:T(8,128)(2,1)} %bitcast.44, bf16[4,512,1024]{2,1,0:T(8,128)(2,1)} %constant.261.clone.section, bf16[4,8,208,256]{3,2,1,0:T(8,128)(2,1)} %constant.262.clone.last), custom_call_target="tpu_custom_call" | custom-call | flops 9900000256 | tf_op jit(solution)/shard_map/forward_x/pallas_call | solution.py:178
  33.9 5.2 %all-to-all-done.1.lines = bf16[8,2,208,128]{3,2,1,0:T(8,128)(2,1)S(1)} async-done(((bf16[8,2,208,128]{3,2,1,0:T(8,128)(2,1)}), bf16[8,2,208,128]{3,2,1,0:T(8,128)(2,1)S(1)}, u32[]{:S(2)}, u32[]{:S(2)}) %all-to-all-start.1) | async-done | bytes 852000 | tf_op jit(solution)/shard_map/all_to_all | solution.py:679
  39.0 3.5 %all-to-all-start = ((bf16[8,2,208,128]{3,2,1,0:T(8,128)(2,1)}), bf16[8,2,208,128]{3,2,1,0:T(8,128)(2,1)S(1)}, u32[]{:S(2)}, u32[]{:S(2)}) async-start(bf16[8,2,208,128]{3,2,1,0:T(8,128)(2,1)} %forward_x.2), calls=%async_computation | async-start | bytes 1703936 | tf_op jit(solution)/shard_map/all_to_all | solution.py:679
  42.6 0.6 and_select_fusion.6
  43.2 6.0 %forward_y_first.1.after.earlier = bf16[64,2,32,128]{3,2,1,0:T(8,128)(2,1)} custom-call(bf16[8,2,208,128]{3,2,1,0:T(8,128)(2,1)} %copy-done.5, bf16[2048,1024]{1,0:T(8,128)(2,1)} %constant.263.clone.section), custom_call_target="tpu_custom_call" | custom-call | flops 7699999744 | tf_op jit(solution)/shard_map/forward_y_first/pallas_call | solution.py:230
  49.2 7.1 %crop.1.after = bf16[32,32,128]{2,1,0:T(8,128)(2,1)} custom-call(s32[32]{0:T(128)} %get-tuple-element.49.rows, s32[32]{0:T(128)} %get-tuple-element.48.cols, s32[32]{0:T(128)} %get-tuple-element.13.odd, s32[32]{0:T(128)} %get-tuple-element.10.mine, bf16[512,4096]{1,0:T(8,128)(2,1)} %pot.1, bf16[64,2,32,128]{3,2,1,0:T(8,128)(2,1)} %forward_y_first.1.after.earlier), custom_call_target="tpu_custom_call" | custom-call | flops 7699999744 | tf_op jit(solution)/shard_map/crop/pallas_call | solution.py:486
  56.3 8.0 %all-to-all-done.lines = bf16[8,2,208,128]{3,2,1,0:T(8,128)(2,1)S(1)} async-done(((bf16[8,2,208,128]{3,2,1,0:T(8,128)(2,1)}), bf16[8,2,208,128]{3,2,1,0:T(8,128)(2,1)S(1)}, u32[]{:S(2)}, u32[]{:S(2)}) %all-to-all-start) | async-done | bytes 852000 | tf_op jit(solution)/shard_map/all_to_all | solution.py:679
  64.3 0.9 copy-done.6
  65.2 8.8 %forward_y.1.spec = bf16[32,208,128]{2,1,0:T(8,128)(2,1)} custom-call(bf16[8,2,208,128]{3,2,1,0:T(8,128)(2,1)} %copy-done.6, bf16[2048,1024]{1,0:T(8,128)(2,1)} %constant.263.clone.section, bf16[64,2,32,128]{3,2,1,0:T(8,128)(2,1)} %forward_y_first.1.after.earlier, bf16[32,208,256]{2,1,0:T(8,128)(2,1)} %constant.264.clone.last, bf16[32,32,128]{2,1,0:T(8,128)(2,1)} %crop.1.after), custom_call_target="tpu_custom_call" | custom-call | flops 11000000512 | tf_op jit(solution)/shard_map/forward_y/pallas_call | solution.py:276
  74.3 0.6 reshape.915.sel
  75.0 0.4 copy.41
  75.4 0.3 reshape.932
  75.8 0.5 negate_convert_fusion.1
  76.4 0.4 copy.40
  76.8 0.3 reshape.931
  77.2 0.7 multiply_convert_fusion.square_x
  78.0 8.4 %inverse.4.rest_0_.refs_0_ = bf16[32,128,256]{2,1,0:T(8,128)(2,1)} custom-call(s32[12]{0:T(128)} %reshape.915.sel, bf16[32,208,128]{2,1,0:T(8,128)(2,1)} %forward_y.1.spec, f32[208,128]{1,0:T(8,128)} %constant.266.clone.freq_y, f32[4,1,128]{2,1,0:T(1,128)} %multiply_convert_fusion.square_x, bf16[32,256,208]{2,1,0:T(8,128)(2,1)} %constant.267.clone.table_y, ...), custom_call_target="tpu_custom_call" | custom-call | flops 3300000000 | tf_op jit(solution)/shard_map/inverse/pallas_call | solution.py:369
  86.4 1.2 copy-done
  87.5 8.4 %inverse.5.refs_1_ = bf16[32,128,256]{2,1,0:T(8,128)(2,1)} custom-call(s32[12]{0:T(128)} %reshape.915.sel, bf16[32,208,128]{2,1,0:T(8,128)(2,1)} %copy-done, f32[208,128]{1,0:T(8,128)} %constant.266.clone.freq_y, f32[4,1,128]{2,1,0:T(1,128)} %multiply_convert_fusion.square_x, bf16[32,256,208]{2,1,0:T(8,128)(2,1)} %constant.267.clone.table_y, ...), custom_call_target="tpu_custom_call" | custom-call | flops 3300000000 | tf_op jit(solution)/shard_map/inverse/pallas_call | solution.py:369
  95.9 4.8 %collect.5 = bf16[32,2,4,16,128]{4,3,2,1,0:T(8,128)(2,1)} custom-call(bf16[32,128,256]{2,1,0:T(8,128)(2,1)} %inverse.4.rest_0_.refs_0_, bf16[32,128,256]{2,1,0:T(8,128)(2,1)} %inverse.5.refs_1_, bf16[2,512,256]{2,1,0:T(8,128)(2,1)} %copy-done.1), custom_call_target="tpu_custom_call" | custom-call | flops 1650000000 | tf_op jit(solution)/shard_map/collect/pallas_call | solution.py:439
  100.7 1.5 collective-permute-start.1
  102.2 4.8 %collect.4.rest_0_.after = bf16[32,2,4,16,128]{4,3,2,1,0:T(8,128)(2,1)} custom-call(bf16[32,128,256]{2,1,0:T(8,128)(2,1)} %inverse.4.rest_0_.refs_0_, bf16[32,128,256]{2,1,0:T(8,128)(2,1)} %inverse.5.refs_1_, bf16[2,512,256]{2,1,0:T(8,128)(2,1)} %copy-done.1), custom_call_target="tpu_custom_call" | custom-call | flops 1650000000 | tf_op jit(solution)/shard_map/collect/pallas_call | solution.py:439
  107.0 3.6 %all-to-all-start.4 = ((bf16[8,4,32,128]{3,2,1,0:T(8,128)(2,1)}), bf16[8,4,32,128]{3,2,1,0:T(8,128)(2,1)S(1)}, u32[]{:S(2)}, u32[]{:S(2)}) async-start(bf16[8,4,32,128]{3,2,1,0:T(8,128)(2,1)} %order.1), calls=%async_computation.4 | async-start | bytes 524288 | tf_op jit(solution)/shard_map/all_to_all | solution.py:679
  110.6 8.4 %inverse.6.rest_0_.refs_0_ = bf16[32,128,256]{2,1,0:T(8,128)(2,1)} custom-call(s32[12]{0:T(128)} %reshape.915.sel, bf16[32,208,128]{2,1,0:T(8,128)(2,1)} %forward_y.1.spec, f32[208,128]{1,0:T(8,128)} %constant.266.clone.freq_y, f32[4,1,128]{2,1,0:T(1,128)} %multiply_convert_fusion.square_x, bf16[32,256,208]{2,1,0:T(8,128)(2,1)} %constant.267.clone.table_y, ...), custom_call_target="tpu_custom_call" | custom-call | flops 3300000000 | tf_op jit(solution)/shard_map/inverse/pallas_call | solution.py:369
  119.0 8.4 %inverse.7.refs_1_ = bf16[32,128,256]{2,1,0:T(8,128)(2,1)} custom-call(s32[12]{0:T(128)} %reshape.915.sel, bf16[32,208,128]{2,1,0:T(8,128)(2,1)} %copy-done, f32[208,128]{1,0:T(8,128)} %constant.266.clone.freq_y, f32[4,1,128]{2,1,0:T(1,128)} %multiply_convert_fusion.square_x, bf16[32,256,208]{2,1,0:T(8,128)(2,1)} %constant.267.clone.table_y, ...), custom_call_target="tpu_custom_call" | custom-call | flops 3300000000 | tf_op jit(solution)/shard_map/inverse/pallas_call | solution.py:369
  127.4 1.0 copy-done.3
  128.4 5.2 %collect.6 = bf16[32,2,4,16,128]{4,3,2,1,0:T(8,128)(2,1)} custom-call(bf16[32,128,256]{2,1,0:T(8,128)(2,1)} %inverse.6.rest_0_.refs_0_, bf16[32,128,256]{2,1,0:T(8,128)(2,1)} %inverse.7.refs_1_, bf16[2,512,256]{2,1,0:T(8,128)(2,1)} %copy-done.1, bf16[32,2,4,16,128]{4,3,2,1,0:T(8,128)(2,1)} %copy-done.3), custom_call_target="tpu_custom_call" | custom-call | flops 1650000000 | tf_op jit(solution)/shard_map/collect/pallas_call | solution.py:439
  133.6 5.1 %all-to-all-start.2 = ((bf16[32,2,4,16,128]{4,3,2,1,0:T(8,128)(2,1)}), bf16[32,2,4,16,128]{4,3,2,1,0:T(8,128)(2,1)S(1)}, u32[]{:S(2)}, u32[]{:S(2)}) async-start(bf16[32,2,4,16,128]{4,3,2,1,0:T(8,128)(2,1)} %collect.6), calls=%async_computation.2 | async-start | bytes 2097152 | tf_op jit(solution)/shard_map/all_to_all | solution.py:679
  138.7 1.8 collective-permute-start.2
  140.5 34.7 %collective-permute-done.2.refs_3_ = bf16[32,2,4,16,128]{4,3,2,1,0:T(8,128)(2,1)S(1)} collective-permute-done((bf16[32,2,4,16,128]{4,3,2,1,0:T(8,128)(2,1)S(1)}, bf16[32,2,4,16,128]{4,3,2,1,0:T(8,128)(2,1)S(1)}, u32[]{:S(2)}, u32[]{:S(2)}) %collective-permute-start.2) | collective-permute-done | bytes 1048608 | tf_op jit(solution)/shard_map/ppermute | solution.py:749
  175.2 1.0 copy-done.4
  176.2 5.2 %collect.7 = bf16[32,2,4,16,128]{4,3,2,1,0:T(8,128)(2,1)} custom-call(bf16[32,128,256]{2,1,0:T(8,128)(2,1)} %inverse.6.rest_0_.refs_0_, bf16[32,128,256]{2,1,0:T(8,128)(2,1)} %inverse.7.refs_1_, bf16[2,512,256]{2,1,0:T(8,128)(2,1)} %copy-done.1, bf16[32,2,4,16,128]{4,3,2,1,0:T(8,128)(2,1)} %copy-done.4), custom_call_target="tpu_custom_call" | custom-call | flops 1650000000 | tf_op jit(solution)/shard_map/collect/pallas_call | solution.py:439
  181.4 4.6 %all-to-all-start.3 = ((bf16[32,2,4,16,128]{4,3,2,1,0:T(8,128)(2,1)}), bf16[32,2,4,16,128]{4,3,2,1,0:T(8,128)(2,1)S(1)}, u32[]{:S(2)}, u32[]{:S(2)}) async-start(bf16[32,2,4,16,128]{4,3,2,1,0:T(8,128)(2,1)} %collect.7), calls=%async_computation.3 | async-start | bytes 2097152 | tf_op jit(solution)/shard_map/all_to_all | solution.py:679
  186.1 0.1 add.516
  186.2 0.2 dynamic-slice_reduce_fusion
  186.5 0.1 add.523
  186.6 0.1 add.514
  186.7 0.7 dynamic_slice.14.counts
  187.4 0.1 fusion.28
  187.5 0.6 pad_maximum_fusion.3.alpha
  188.2 0.3 fusion.14
  188.5 0.7 pad_maximum_fusion.2.refs_3_
  189.2 0.6 reduce_sum.38.refs_2_
  189.8 0.8 reduce_sum.36.refs_0_
  190.7 21.5 %all-to-all-done.3 = bf16[32,2,4,16,128]{4,3,2,1,0:T(8,128)(2,1)S(1)} async-done(((bf16[32,2,4,16,128]{4,3,2,1,0:T(8,128)(2,1)}), bf16[32,2,4,16,128]{4,3,2,1,0:T(8,128)(2,1)S(1)}, u32[]{:S(2)}, u32[]{:S(2)}) %all-to-all-start.3) | async-done | bytes 1048608 | tf_op jit(solution)/shard_map/all_to_all | solution.py:679
  212.2 0.8 reduce_sum.37.refs_1_
  213.0 4.1 %detect.1 = f32[1,256]{1,0:T(1,128)} custom-call(f32[2,4,12]{2,1,0:T(4,128)} %pad_maximum_fusion.3.alpha, s32[1]{0:T(128)} %dynamic_slice.14.counts, bf16[4,2,4,16,128]{4,3,2,1,0:T(8,128)(2,1)} %reduce_sum.36.refs_0_, bf16[4,2,4,16,128]{4,3,2,1,0:T(8,128)(2,1)} %reduce_sum.37.refs_1_, bf16[4,32,128]{2,1,0:T(8,128)(2,1)} %reduce_sum.38.refs_2_, ...), custom_call_target="tpu_custom_call" | custom-call | tf_op jit(solution)/shard_map/detect/pallas_call | solution.py:552
  217.1 0.7 slice_reduce_fusion
  217.8 0.1 reshape_squeeze.3
  217.9 0.6 copy.39
  (59 shorter events, 1.2 us)
Async XLA Ops:
  0.0 17.4 %copy-start.7 = (s32[4,2]{0,1:T(2,128)S(1)}, s32[4,2]{0,1:T(2,128)}, u32[]{:S(2)}) copy-start(s32[4,2]{0,1:T(2,128)} %param.19) | copy-start | bytes 100
  0.0 18.9 %copy-start.8 = (s32[32,4]{0,1:T(4,128)S(1)}, s32[32,4]{0,1:T(4,128)}, u32[]{:S(2)}) copy-start(s32[32,4]{0,1:T(4,128)} %param.21) | copy-start | bytes 1540
  10.1 28.9 %all-to-all-start.1 = ((bf16[8,2,208,128]{3,2,1,0:T(8,128)(2,1)}), bf16[8,2,208,128]{3,2,1,0:T(8,128)(2,1)S(1)}, u32[]{:S(2)}, u32[]{:S(2)}) async-start(bf16[8,2,208,128]{3,2,1,0:T(8,128)(2,1)} %forward_x.3), calls=%async_computation.1 | async-start | bytes 1703936 | tf_op jit(solution)/shard_map/all_to_all | solution.py:679
  39.0 4.2 %copy-start.5 = (bf16[8,2,208,128]{3,2,1,0:T(8,128)(2,1)}, bf16[8,2,208,128]{3,2,1,0:T(8,128)(2,1)S(1)}, u32[]{:S(2)}) copy-start(bf16[8,2,208,128]{3,2,1,0:T(8,128)(2,1)S(1)} %all-to-all-done.1.lines) | copy-start | bytes 2555908
  39.0 25.3 %all-to-all-start = ((bf16[8,2,208,128]{3,2,1,0:T(8,128)(2,1)}), bf16[8,2,208,128]{3,2,1,0:T(8,128)(2,1)S(1)}, u32[]{:S(2)}, u32[]{:S(2)}) async-start(bf16[8,2,208,128]{3,2,1,0:T(8,128)(2,1)} %forward_x.2), calls=%async_computation | async-start | bytes 1703936 | tf_op jit(solution)/shard_map/all_to_all | solution.py:679
  64.3 0.9 copy-start.6
  74.0 3.2 %copy-start.9 = (s32[128]{0:T(128)S(1)}, s32[128]{0:T(128)}, u32[]{:S(2)}) copy-start(s32[128]{0:T(128)} %constant.265.clone) | copy-start | bytes 1540
  74.0 12.3 %collective-permute-start = (bf16[32,208,128]{2,1,0:T(8,128)(2,1)}, bf16[32,208,128]{2,1,0:T(8,128)(2,1)S(1)}, u32[]{:S(2)}, u32[]{:S(2)}) collective-permute-start(bf16[32,208,128]{2,1,0:T(8,128)(2,1)} %forward_y.1.spec), channel_id=1, source_target_pairs={{0,1},{1,0},{2,3},{3,2},{4,5},{5,4},{6,7},{7,6},{8,9},{9,8},{10,11... | collective-permute-start | bytes 5111816 | tf_op jit(solution)/shard_map/ppermute | solution.py:724
  77.2 9.1 %copy-start.1 = (bf16[2,512,256]{2,1,0:T(8,128)(2,1)}, bf16[2,512,256]{2,1,0:T(8,128)(2,1)S(1)}, u32[]{:S(2)}) copy-start(bf16[2,512,256]{2,1,0:T(8,128)(2,1)S(1)} %constant_dynamic-update-slice_fusion.refs_2_) | copy-start | bytes 1572868
  86.4 1.2 copy-start
  100.7 26.7 %collective-permute-start.1 = (bf16[32,2,4,16,128]{4,3,2,1,0:T(8,128)(2,1)}, bf16[32,2,4,16,128]{4,3,2,1,0:T(8,128)(2,1)S(1)}, u32[]{:S(2)}, u32[]{:S(2)}) collective-permute-start(bf16[32,2,4,16,128]{4,3,2,1,0:T(8,128)(2,1)} %collect.5), channel_id=1, source_target_pairs={{0,2},{1,3},{2,0},{3,1},{4,6},{5,7},{6,4},{7,5},{8,10},{9,11},{10,... | collective-permute-start | bytes 3145736 | tf_op jit(solution)/shard_map/ppermute | solution.py:749
  107.0 26.5 %all-to-all-start.4 = ((bf16[8,4,32,128]{3,2,1,0:T(8,128)(2,1)}), bf16[8,4,32,128]{3,2,1,0:T(8,128)(2,1)S(1)}, u32[]{:S(2)}, u32[]{:S(2)}) async-start(bf16[8,4,32,128]{3,2,1,0:T(8,128)(2,1)} %order.1), calls=%async_computation.4 | async-start | bytes 524288 | tf_op jit(solution)/shard_map/all_to_all | solution.py:679
  127.4 11.3 %copy-start.2 = (bf16[32,2,4,16,128]{4,3,2,1,0:T(8,128)(2,1)S(1)}, bf16[32,2,4,16,128]{4,3,2,1,0:T(8,128)(2,1)}, u32[]{:S(2)}) copy-start(bf16[32,2,4,16,128]{4,3,2,1,0:T(8,128)(2,1)} %collect.4.rest_0_.after) | copy-start | bytes 3145732
  127.4 1.0 copy-start.3
  133.6 47.8 %all-to-all-start.2 = ((bf16[32,2,4,16,128]{4,3,2,1,0:T(8,128)(2,1)}), bf16[32,2,4,16,128]{4,3,2,1,0:T(8,128)(2,1)S(1)}, u32[]{:S(2)}, u32[]{:S(2)}) async-start(bf16[32,2,4,16,128]{4,3,2,1,0:T(8,128)(2,1)} %collect.6), calls=%async_computation.2 | async-start | bytes 2097152 | tf_op jit(solution)/shard_map/all_to_all | solution.py:679
  138.7 48.1 %copy-start.11 = (s32[32]{0:T(128)S(1)}, s32[32]{0:T(128)}, u32[]{:S(2)}) copy-start(s32[32]{0:T(128)} %param.22) | copy-start | bytes 388
  138.7 48.7 %copy-start.10 = (f32[4]{0:T(128)S(1)}, f32[4]{0:T(128)}, u32[]{:S(2)}) copy-start(f32[4]{0:T(128)} %param.20) | copy-start | bytes 52
  138.7 36.5 %collective-permute-start.2 = (bf16[32,2,4,16,128]{4,3,2,1,0:T(8,128)(2,1)S(1)}, bf16[32,2,4,16,128]{4,3,2,1,0:T(8,128)(2,1)S(1)}, u32[]{:S(2)}, u32[]{:S(2)}) collective-permute-start(bf16[32,2,4,16,128]{4,3,2,1,0:T(8,128)(2,1)S(1)} %copy-done.2), channel_id=1, source_target_pairs={{0,2},{1,3},{2,0},{3,1},{4,6},{5,7},{6,4},{7,5},{8,10},{9,11},{10,... | collective-permute-start | bytes 3145736 | tf_op jit(solution)/shard_map/ppermute | solution.py:749
  175.2 1.0 copy-start.4
  181.4 30.8 %all-to-all-start.3 = ((bf16[32,2,4,16,128]{4,3,2,1,0:T(8,128)(2,1)}), bf16[32,2,4,16,128]{4,3,2,1,0:T(8,128)(2,1)S(1)}, u32[]{:S(2)}, u32[]{:S(2)}) async-start(bf16[32,2,4,16,128]{4,3,2,1,0:T(8,128)(2,1)} %collect.7), calls=%async_computation.3 | async-start | bytes 2097152 | tf_op jit(solution)/shard_map/all_to_all | solution.py:679

commit v4 on v3

--- a/solution.py
+++ b/solution.py
@@ -27,6 +27,7 @@
 HALF = A // 2
 PAIRS = A // 2
 PARTS = 2
+BLOCKS = 4
 VMEM = 60 * 1024 * 1024
 PITCH = A + 1
 BF = jnp.bfloat16
@@ -78,7 +79,7 @@
     for e, k1 in enumerate(k1_pair):
         freq = k1 + A * digits_k2()
         table = np.conj(turn(freq[:, None] * n2[None, :], N)) / A
-        out[e * 2 * K2_COUNT : (e + 1) * 2 * K2_COUNT, e] = real_rows(table)
+        out[e * PART : e * PART + 2 * K2_COUNT, e] = real_rows(table)
     return low(out.reshape(ROWS, 4 * A))
 
 
@@ -89,10 +90,10 @@
 
 
 def first_inverse_y(k1_pair):
-    out = np.zeros((2, 2 * A, ROWS))
+    out = np.zeros((2, 2 * A, PART))
     for e, k1 in enumerate(k1_pair):
-        out[e, :, e * 2 * K2_COUNT : (e + 1) * 2 * K2_COUNT] = real_rows(first_inverse(k1))
-    return low(out.reshape(4 * A, ROWS))
+        out[e, :, : 2 * K2_COUNT] = real_rows(first_inverse(k1))
+    return low(out)
 
 
 def first_inverse_x(k1_pair):
@@ -199,63 +200,83 @@
     )(sel, pot.reshape(groups, HIGH, SUB, N), section, last)
 
 
-def section_step(lines, section, gathered, twisted, start):
-    chunk_rows = 16 * SUB
+def gather_lines(lines, gathered):
+    steps = lines.shape[1]
+    zeros = jnp.zeros((LANES - PART, LANES), F32)
     for g in range(lines.shape[0]):
-        block = lines[g, 0].astype(F32)
-        zeros = jnp.zeros((LANES - PART, LANES), F32)
-        both = jnp.concatenate([block[:PART], zeros, block[PART:], zeros], axis=0)
-        gathered[:, g * LANES : (g + 1) * LANES] = both.astype(BF)
+        for h in range(steps):
+            block = lines[g, h].astype(F32)
+            both = jnp.concatenate([block[:PART], zeros, block[PART:], zeros], axis=0)
+            rows = slice(2 * h * LANES, 2 * (h + 1) * LANES)
+            gathered[rows, g * LANES : (g + 1) * LANES] = both.astype(BF)
+
+
+def section_step(steps, section, gathered, twisted):
+    count = section.shape[1] // SUB
+    dims = (((1,), (1,)), ((), ()))
     values = gathered[...]
-    for c in range(A // 16):
-        rows = slice(c * chunk_rows, (c + 1) * chunk_rows)
-        turned = slice(A * SUB + c * chunk_rows, A * SUB + (c + 1) * chunk_rows)
-        dims = (((1,), (1,)), ((), ()))
-        by_cos = lax.dot_general(section[rows, :], values, dims, preferred_element_type=F32)
-        by_sin = lax.dot_general(section[turned, :], values, dims, preferred_element_type=F32)
-        real = by_cos[:, :LANES] - by_sin[:, LANES:]
-        imag = by_cos[:, LANES:] + by_sin[:, :LANES]
-        spot = slice(c * 16, (c + 1) * 16)
-        twisted[spot, 0, pl.ds(start, SUB), :] = real.astype(BF).reshape(16, SUB, LANES)
-        twisted[spot, 1, pl.ds(start, SUB), :] = imag.astype(BF).reshape(16, SUB, LANES)
+    by_cos = lax.dot_general(section[0], values, dims, preferred_element_type=F32)
+    by_sin = lax.dot_general(section[1], values, dims, preferred_element_type=F32)
+    for h in range(steps):
+        re = slice(2 * h * LANES, (2 * h + 1) * LANES)
+        im = slice((2 * h + 1) * LANES, (2 * h + 2) * LANES)
+        real = by_cos[:, re] - by_sin[:, im]
+        imag = by_cos[:, im] + by_sin[:, re]
+        span = slice(h * SUB, (h + 1) * SUB)
+        yield span, real.astype(BF).reshape(count, SUB, LANES), imag.astype(BF).reshape(
+            count, SUB, LANES
+        )
 
 
 def forward_y_first_kernel(lines, section, twisted, gathered):
-    start = pl.multiple_of(pl.program_id(0) * SUB, SUB)
-    section_step(lines, section, gathered, twisted, start)
+    @pl.when(pl.program_id(0) == 0)
+    def _():
+        gather_lines(lines, gathered)
+
+    for span, real, imag in section_step(lines.shape[1], section, gathered, twisted):
+        twisted[:, 0, span, :] = real
+        twisted[:, 1, span, :] = imag
 
 
 def forward_y_first(lines, section):
-    groups, steps = lines.shape[:2]
+    steps = lines.shape[1]
+    count = A // BLOCKS
     return pl.pallas_call(
         forward_y_first_kernel,
-        grid=(steps,),
+        grid=(BLOCKS,),
         in_specs=[
-            pl.BlockSpec((groups, 1, ROWS, LANES), lambda i: (0, i, 0, 0)),
-            pl.BlockSpec(section.shape, lambda i: (0, 0)),
+            pl.BlockSpec(lines.shape, lambda i: (0, 0, 0, 0)),
+            pl.BlockSpec((2, count * SUB, A * SUB), lambda i: (0, i, 0)),
         ],
-        out_specs=pl.BlockSpec((A, 2, A // PARTS, LANES), lambda i: (0, 0, 0, 0)),
+        out_specs=pl.BlockSpec((count, 2, A // PARTS, LANES), lambda i: (i, 0, 0, 0)),
         out_shape=jax.ShapeDtypeStruct((A, 2, A // PARTS, LANES), BF),
-        scratch_shapes=[pltpu.VMEM((2 * LANES, A * SUB), BF)],
+        scratch_shapes=[pltpu.VMEM((2 * steps * LANES, A * SUB), BF)],
         compiler_params=pltpu.CompilerParams(vmem_limit_bytes=VMEM),
-        cost_estimate=cost(7),
+        cost_estimate=cost(6),
         name="forward_y_first",
     )(lines, section)
 
 
-def forward_y_kernel(steps, lines, section, earlier, last, after, out, gathered, twisted):
+def forward_y_kernel(lines, section, earlier, last, *rest):
+    out, gathered, twisted = rest[-3:]
     step = pl.program_id(0)
-    first = HIGH // PARTS
-
-    @pl.when(step < first)
+
+    @pl.when(step == 0)
     def _():
-        start = pl.multiple_of(step * SUB, SUB)
-        section_step(lines, section, gathered, twisted, start)
-
-    @pl.when(step >= first)
+        gather_lines(lines, gathered)
+
+    @pl.when(step < BLOCKS)
     def _():
-        count = PAIRS // steps
-        base = (step - first) * count
+        count = A // BLOCKS
+        spot = pl.ds(step * count, count)
+        for span, real, imag in section_step(lines.shape[1], section, gathered, twisted):
+            twisted[spot, 0, span, :] = real
+            twisted[spot, 1, span, :] = imag
+
+    @pl.when(step >= BLOCKS)
+    def _():
+        count = out.shape[0]
+        base = (step - BLOCKS) * count
         for q in range(count):
             rows = []
             for e in range(2):
@@ -266,58 +287,61 @@
 
 
 def forward_y(lines, section, earlier, last, after):
-    groups, first = lines.shape[:2]
     steps = 2
     count = PAIRS // steps
 
     def late(i):
-        return (jnp.maximum(i - first, 0), 0, 0)
+        return (jnp.maximum(i - BLOCKS, 0), 0, 0)
 
     return pl.pallas_call(
-        functools.partial(forward_y_kernel, steps),
-        grid=(first + steps,),
+        forward_y_kernel,
+        grid=(BLOCKS + steps,),
         in_specs=[
+            pl.BlockSpec(lines.shape, lambda i: (0, 0, 0, 0)),
             pl.BlockSpec(
-                (groups, 1, ROWS, LANES), lambda i: (0, jnp.minimum(i, first - 1), 0, 0)
+                (2, A // BLOCKS * SUB, A * SUB), lambda i: (0, jnp.minimum(i, BLOCKS - 1), 0)
             ),
-            pl.BlockSpec(section.shape, lambda i: (0, 0)),
             pl.BlockSpec(earlier.shape, lambda i: (0, 0, 0, 0)),
             pl.BlockSpec((count, ROWS, 4 * A), late),
-            pl.BlockSpec(memory_space=pl.ANY),
-        ],
+        ]
+        + [pl.BlockSpec(memory_space=pl.ANY)] * len(after),
         out_specs=pl.BlockSpec((count, ROWS, LANES), late),
         out_shape=jax.ShapeDtypeStruct((PAIRS, ROWS, LANES), BF),
         scratch_shapes=[
-            pltpu.VMEM((2 * LANES, A * SUB), BF),
+            pltpu.VMEM((2 * lines.shape[1] * LANES, A * SUB), BF),
             pltpu.VMEM((A, 2, A // PARTS, LANES), BF),
         ],
         compiler_params=pltpu.CompilerParams(vmem_limit_bytes=VMEM),
-        cost_estimate=cost(10),
+        cost_estimate=cost(8),
         name="forward_y",
-    )(lines, section, earlier, last, after)
-
-
-def order_kernel(value, after, out):
+    )(lines, section, earlier, last, *after)
+
+
+def order_kernel(value, *rest):
     pass
 
 
 def order(value, after):
     return pl.pallas_call(
         order_kernel,
-        in_specs=[pl.BlockSpec(memory_space=pl.ANY)] * 2,
+        in_specs=[pl.BlockSpec(memory_space=pl.ANY)] * (1 + len(after)),
         out_specs=pl.BlockSpec(memory_space=pl.ANY),
         out_shape=jax.ShapeDtypeStruct(value.shape, value.dtype),
         input_output_aliases={0: 0},
         name="order",
-    )(value, after)
-
-
-def inverse_kernel(steps, which, sel, spec, freq_y, square_x, table_y, table_x, *rest):
-    out, mid = rest[-2:]
+    )(value, *after)
+
+
+def inverse_kernel(steps, which, near, sel, *refs):
+    specs = refs[:near]
+    freq_y, square_x, table_y = refs[near : near + 3]
+    tables_x = refs[near + 3 : 2 * near + 3]
+    out, mid = refs[-2:]
     step = pl.program_id(0)
     count = PAIRS // steps
     each = HALF // steps
     limit = F32(LIMIT * LIMIT)
+    whole = 2 * A * PITCH
 
     @pl.when(step < steps)
     def _():
@@ -325,14 +349,21 @@
             pair_id = step * count + q
             offset = (2 * pair_id + sel[3 * which + 2]).astype(F32)
             row_freq = freq_y[...] + offset
-            inside = row_freq * row_freq + square_x[0] <= limit
-            values = jnp.where(inside, spec[q].astype(F32), 0.0).astype(BF)
-            mixed = dot(table_y[q], values)
+            row_square = row_freq * row_freq
+            values = []
+            for x in range(near):
+                inside = row_square + square_x[x] <= limit
+                values.append(jnp.where(inside, specs[x][q].astype(F32), 0.0))
             for e in range(2):
-                for part in range(2):
-                    rows = slice((2 * e + part) * A, (2 * e + part + 1) * A)
-                    spot = part * A * PITCH + 2 * pair_id + e
-                    mid[pl.ds(spot, A, stride=PITCH), :] = mixed[rows]
+                half = [v[e * PART : (e + 1) * PART].astype(BF) for v in values]
+                half = half[0] if near == 1 else jnp.concatenate(half, axis=1)
+                mixed = dot(table_y[q, e], half)
+                for x in range(near):
+                    for part in range(2):
+                        spot = x * whole + part * A * PITCH + 2 * pair_id + e
+                        mid[pl.ds(spot, A, stride=PITCH), :] = mixed[
+                            part * A : (part + 1) * A, x * LANES : (x + 1) * LANES
+                        ]
             return carry
 
         lax.fori_loop(0, count, pair, 0, unroll=4)
@@ -341,24 +372,29 @@
     def _():
         def line(i, carry):
             by = (step - steps) * each + i
-            rows = []
-            for b in range(2):
-                for part in range(2):
-                    start = part * A * PITCH + (by + b * HALF) * PITCH
-                    rows.append(mid[pl.ds(start, A), :].astype(BF))
-            product = dot(jnp.concatenate(rows, axis=0), table_x[0, 0])
-            for b in range(2):
-                re = product[2 * b * A : (2 * b + 1) * A]
-                im = product[(2 * b + 1) * A : (2 * b + 2) * A]
-                span = slice(b * LANES, (b + 1) * LANES)
-                out[i, :A, span] = (re[:, :LANES] - im[:, LANES:]).astype(BF)
-                out[i, A:, span] = (re[:, LANES:] + im[:, :LANES]).astype(BF)
+            for x in range(near):
+                rows = []
+                for b in range(2):
+                    for part in range(2):
+                        start = x * whole + part * A * PITCH + (by + b * HALF) * PITCH
+                        rows.append(mid[pl.ds(start, A), :].astype(BF))
+                product = dot(jnp.concatenate(rows, axis=0), tables_x[x][0, 0])
+                low_row = 2 * A * x
+                for b in range(2):
+                    re = product[2 * b * A : (2 * b + 1) * A]
+                    im = product[(2 * b + 1) * A : (2 * b + 2) * A]
+                    span = slice(b * LANES, (b + 1) * LANES)
+                    real = re[:, :LANES] - im[:, LANES:]
+                    imag = re[:, LANES:] + im[:, :LANES]
+                    out[i, low_row : low_row + A, span] = real.astype(BF)
+                    out[i, low_row + A : low_row + 2 * A, span] = imag.astype(BF)
             return carry
 
         lax.fori_loop(0, each, line, 0, unroll=4)
 
 
-def inverse(which, sel, spec, freq_y, square_x, table_y, table_x, after):
+def inverse(which, sel, specs, freq_y, square_x, table_y, table_x, after):
+    near = len(specs)
     steps = 2
     count = PAIRS // steps
     each = HALF // steps
@@ -366,34 +402,39 @@
     def early(i, s):
         return jnp.minimum(i, steps - 1)
 
+    def table_spec(x):
+        return pl.BlockSpec(
+            (1, 1) + table_x.shape[2:],
+            lambda i, s: (s[3 * (which + x)], s[3 * (which + x) + 1], 0, 0),
+        )
+
     return pl.pallas_call(
-        functools.partial(inverse_kernel, steps, which),
+        functools.partial(inverse_kernel, steps, which, near),
         grid_spec=pltpu.PrefetchScalarGridSpec(
             num_scalar_prefetch=1,
             grid=(2 * steps,),
-            in_specs=[
-                pl.BlockSpec((count, ROWS, LANES), lambda i, s: (early(i, s), 0, 0)),
+            in_specs=[pl.BlockSpec((count, ROWS, LANES), lambda i, s: (early(i, s), 0, 0))] * near
+            + [
                 pl.BlockSpec((ROWS, LANES), lambda i, s: (0, 0)),
-                pl.BlockSpec((1, 1, LANES), lambda i, s: (which, 0, 0)),
-                pl.BlockSpec((count, 4 * A, ROWS), lambda i, s: (early(i, s), 0, 0)),
-                pl.BlockSpec((1, 1) + table_x.shape[2:], lambda i, s: (s[3 * which], s[3 * which + 1], 0, 0)),
+                pl.BlockSpec((near, 1, LANES), lambda i, s: (which // near, 0, 0)),
+                pl.BlockSpec((count, 2, 2 * A, PART), lambda i, s: (early(i, s), 0, 0, 0)),
             ]
+            + [table_spec(x) for x in range(near)]
             + [pl.BlockSpec(memory_space=pl.ANY)] * len(after),
             out_specs=pl.BlockSpec(
-                (each, 2 * A, 2 * LANES), lambda i, s: (jnp.maximum(i - steps, 0), 0, 0)
+                (each, 2 * A * near, 2 * LANES), lambda i, s: (jnp.maximum(i - steps, 0), 0, 0)
             ),
-            scratch_shapes=[pltpu.VMEM((2 * A * PITCH, LANES), F32)],
+            scratch_shapes=[pltpu.VMEM((near * 2 * A * PITCH, LANES), F32)],
         ),
-        out_shape=jax.ShapeDtypeStruct((HALF, 2 * A, 2 * LANES), BF),
+        out_shape=jax.ShapeDtypeStruct((HALF, 2 * A * near, 2 * LANES), BF),
         compiler_params=pltpu.CompilerParams(vmem_limit_bytes=VMEM),
-        cost_estimate=cost(3),
+        cost_estimate=cost(6),
         name="inverse",
-    )(sel, spec, freq_y, square_x, table_y, table_x, *after)
-
-
-def collect_kernel(near, added, *refs):
-    sheets, weights = refs[:near], refs[near]
-    out, held = refs[-2:]
+    )(sel, *specs, freq_y, square_x, table_y, *[table_x] * near, *after)
+
+
+def collect_kernel(*refs):
+    *sheets, weights, out, held = refs
     devices, _, slots, lines, _ = out.shape
     tiles = devices * slots
     pitch = lines + 1
@@ -402,9 +443,9 @@
 
     def line(i, carry):
         stacked = sheets[0][i]
-        if near > 1:
+        if len(sheets) > 1:
             stacked = jnp.concatenate([sheet[i] for sheet in sheets], axis=0)
-        sums = dot(weights[0], stacked)
+        sums = dot(weights[...], stacked)
         for part in range(2):
             even = sums[2 * part * tiles : (2 * part + 1) * tiles]
             odd = sums[(2 * part + 1) * tiles : (2 * part + 2) * tiles]
@@ -421,34 +462,29 @@
             for slot in range(slots):
                 start = (part * tiles + d * slots + slot) * pitch
                 total = held[pl.ds(start, lines), :]
-                for a in range(added):
-                    total = total + refs[near + 1 + a][d, part, slot].astype(F32)
                 out[d, part, slot] = total.astype(BF)
         return carry
 
     lax.fori_loop(0, devices, device, 0, unroll=4)
 
 
-def collect(which, sheets, weights, devices, part, added):
-    near = len(sheets)
-    tiles = weights.shape[1] // 4
+def collect(sheets, weights, devices, part):
+    tiles = weights.shape[0] // 4
     lines = HALF // PARTS
     shape = (devices, 2, tiles // devices, lines, LANES)
-    sheet_spec = pl.BlockSpec((lines, 2 * A, 2 * LANES), lambda i: (part, 0, 0))
+    sheet_spec = pl.BlockSpec((lines,) + sheets[0].shape[1:], lambda i: (part, 0, 0))
     block = pl.BlockSpec(shape, lambda i: (0, 0, 0, 0, 0))
     return pl.pallas_call(
-        functools.partial(collect_kernel, near, len(added)),
+        collect_kernel,
         grid=(1,),
-        in_specs=[sheet_spec] * near
-        + [pl.BlockSpec((1,) + weights.shape[1:], lambda i: (which, 0, 0))]
-        + [block] * len(added),
+        in_specs=[sheet_spec] * len(sheets) + [pl.BlockSpec(weights.shape, lambda i: (0, 0))],
         out_specs=block,
         out_shape=jax.ShapeDtypeStruct(shape, BF),
         scratch_shapes=[pltpu.VMEM((2 * tiles * (lines + 1), LANES), F32)],
         compiler_params=pltpu.CompilerParams(vmem_limit_bytes=VMEM),
         cost_estimate=cost(1.5),
         name="collect",
-    )(*sheets, weights, *added)
+    )(*sheets, weights)
 
 
 def crop_kernel(rows, cols, odd, mine, pot, after, out, held, sems):
@@ -655,7 +691,7 @@
             for t in range(sheets)
         ]
     )
-    section_y = section_forward(np.arange(A))
+    section_y = section_forward(np.arange(A)).reshape(2, A * SUB, A * SUB)
     last_y = np.stack([last_forward_y([2 * q, 2 * q + 1]) for q in range(PAIRS)])
     inverse_y = np.stack([first_inverse_y([2 * q, 2 * q + 1]) for q in range(PAIRS)])
     inverse_x = np.stack(
@@ -678,87 +714,73 @@
     def trade(value, axis):
         return lax.all_to_all(value, axis, split_axis=0, concat_axis=0, tiled=True)
 
+    near = min(sheets, 2)
+    far = sheets // near
+
+    def swap(value, x):
+        return lax.ppermute(value, "slab", [(i, i ^ x) for i in range(hold_count)])
+
+    ids = lax.dynamic_index_in_dim(table, hold_pos, 1, keepdims=False).reshape(-1)
+    tile_y, tile_x = ids // across, ids % across
+    mine = (tile_y // band_tiles == field_pos).astype(jnp.int32)
+    rows = jnp.clip(tile_y - field_pos * band_tiles, 0, band_tiles - 1)
+
+    beam_row = lax.dynamic_index_in_dim(beam_index, hold_pos, 0, keepdims=False)
+    pair_ids = share ^ jnp.arange(sheets, dtype=jnp.int32)
+    k1_pairs = field_pos * width_k + 2 * pair_ids
+    weights = tile_weights(tile_table.reshape(-1), beam_row, k1_pairs)
+    row = np.arange(ROWS)
+    base = row // PART + A * (K2_LOW + row % PART % K2_COUNT)
+    freq_y = np.broadcast_to(base[:, None], (ROWS, LANES)).astype(np.float32)
+    lane = np.arange(LANES)
+    base = np.where(lane < 2 * K2_COUNT, lane // K2_COUNT + A * (K2_LOW + lane % K2_COUNT), N)
+    freq_x = (k1_pairs + F * beam_row[1])[:, None, None] + base.astype(np.int32)
+    square_x = (freq_x * freq_x).astype(F32)
+    scalars = jnp.stack(
+        jnp.broadcast_arrays(field_pos, pair_ids, F * beam_row[0]), axis=-1
+    )
+    scalars = scalars.astype(jnp.int32).reshape(-1)
+
     sel = share.reshape(1).astype(jnp.int32)
-    received = []
+    received = [[] for _ in range(far)]
+    earlier = []
     for part in range(PARTS):
         lines = trade(forward_x(sel, pot_first, section_x, last_x, field_count, part), "beam")
         if lines.shape[3] != LANES:
             ratio = LANES // lines.shape[3]
             lines = lines.reshape((field_count // ratio, ratio) + lines.shape[1:])
             lines = lines.transpose(0, 2, 3, 1, 4).reshape(-1, HIGH // PARTS, ROWS, LANES)
-        received.append(lines)
-    earlier = forward_y_first(received[0], section_y)
-
-    ids = lax.dynamic_index_in_dim(table, hold_pos, 1, keepdims=False).reshape(-1)
-    tile_y, tile_x = ids // across, ids % across
-    mine = (tile_y // band_tiles == field_pos).astype(jnp.int32)
-    rows = jnp.clip(tile_y - field_pos * band_tiles, 0, band_tiles - 1)
-    crops = crop(rows, tile_x // 2, tile_x % 2, mine, pot_second, earlier)
-    spec = forward_y(received[1], section_y, earlier, last_y, crops)
-    crops = crops.reshape(field_count, own_slots, HALF, LANES)
-
-    near = min(sheets, 2)
-    far = sheets // near
-    pair_ids = share ^ jnp.arange(near, dtype=jnp.int32)
-    k1_pairs = field_pos * width_k + 2 * pair_ids
-    rows_of = beam_index[hold_pos ^ (near * jnp.arange(far, dtype=jnp.int32))]
-    weights = jnp.stack(
-        [tile_weights(tile_table.reshape(-1), rows_of[f], k1_pairs) for f in range(far)]
-    )
-    row = np.arange(ROWS)
-    base = (row // (2 * K2_COUNT)) + A * (K2_LOW + row % K2_COUNT)
-    base = np.where(row < 4 * K2_COUNT, base, 0)
-    freq_y = np.broadcast_to(base[:, None], (ROWS, LANES)).astype(np.float32)
-    lane = np.arange(LANES)
-    base = np.where(lane < 2 * K2_COUNT, lane // K2_COUNT + A * (K2_LOW + lane % K2_COUNT), N)
-    freq_x = (k1_pairs[None, :] + F * rows_of[:, 1:]).reshape(far * near, 1, 1)
-    freq_x = freq_x + base.astype(np.int32)
-    square_x = (freq_x * freq_x).astype(F32)
-    scalars = jnp.stack(
-        jnp.broadcast_arrays(field_pos, pair_ids[None, :], F * rows_of[:, :1]), axis=-1
-    )
-    scalars = scalars.astype(jnp.int32).reshape(-1)
-
-    shards_x = [spec]
-    for x in range(1, near):
-        shards_x.append(lax.ppermute(spec, "slab", [(i, i ^ x) for i in range(hold_count)]))
-    passed = [[] for _ in range(PARTS)]
-    last_wave = []
-    for f in reversed(range(far)):
-        waves = []
-        for x in range(near):
-            waves.append(
-                inverse(
-                    f * near + x,
-                    scalars,
-                    shards_x[x],
-                    freq_y,
-                    square_x,
-                    inverse_y,
-                    inverse_x,
-                    last_wave,
-                )
+        if part:
+            crops = crop(rows, tile_x // 2, tile_x % 2, mine, pot_second, earlier[0])
+            lines = order(lines, [crops, weights, square_x])
+        for f in range(far):
+            received[f].append(swap(lines, f * near) if f else lines)
+        if part == 0:
+            earlier = [forward_y_first(received[f][0], section_y) for f in range(far)]
+    crops = lax.psum_scatter(
+        crops.reshape(field_count, own_slots * HALF, LANES), "beam", scatter_dimension=0
+    ).reshape(own_slots, HALF, LANES)
+
+    waves = []
+    ready = []
+    token = []
+    for f in range(far):
+        spec = forward_y(received[f][1], section_y, earlier[f], last_y, token + earlier[1:])
+        ready.append([spec] + [swap(spec, x) for x in range(1, near)])
+        token = [spec]
+    for f in range(far):
+        waves.append(
+            inverse(
+                f * near, scalars, ready[f], freq_y, square_x, inverse_y, inverse_x, token
             )
-            last_wave = waves[-1:]
-        for part in range(PARTS):
-            partial = collect(
-                f, waves, weights, field_count * hold_count, part, passed[part] * (f == 0)
-            )
-            if f:
-                swap = [(i, i ^ (f * near)) for i in range(hold_count)]
-                passed[part].append(lax.ppermute(partial, "slab", swap))
-                last_wave = [partial]
-            else:
-                passed[part] = partial
-        if f:
-            crops = order(crops, last_wave[0])
-    crops = trade(crops, "beam")
+        )
+        token = waves[-1:]
     fields = []
     for part in range(PARTS):
-        tiles = trade(passed[part], ("beam", "slab"))
+        tiles = collect(waves, weights, field_count * hold_count, part)
+        tiles = trade(tiles, ("beam", "slab"))
         tiles = tiles.reshape((field_count, hold_count) + tiles.shape[1:]).astype(F32)
         fields.append(jnp.sum(tiles, axis=0).astype(BF))
-    crop_total = jnp.sum(crops.astype(F32), axis=0).astype(BF)
 
     own = lax.dynamic_index_in_dim(
         lax.dynamic_index_in_dim(table, field_pos, 0, keepdims=False), hold_pos, 0, keepdims=False
@@ -767,7 +789,7 @@
     first_block = (field_pos * hold_count + hold_pos) * blocks_dev
     counts = lax.dynamic_slice_in_dim(tile_count, first_block, blocks_dev, 0)
     bins = detect_tables(beam_total)
-    sums = detect(alpha, counts, fields, crop_total, plane_waves(beam_index), *bins)
+    sums = detect(alpha, counts, fields, crops, plane_waves(beam_index), *bins)
     return sums[0, : own_slots * G * NDET].reshape(blocks_dev, slot_count, G, NDET)
 
 

time: 219 us -> 246 us (1.12)
  waiting for transfers between devices: 69.4 us -> 93.3 us
  between operations: 0.3 us -> 14.9 us
  starting transfers between devices: 27.4 us -> 22.9 us
  Pallas kernels: 99.7 us -> 95.4 us
    reduce_scatter x0 -> x1, waiting for transfers between devices: none -> 38.8 us  [shards(): lax.psum_scatter(crops.reshape(field_count, own_slots * HALF, LANES), 'be...]
    ppermute x3 -> x4, waiting for transfers between devices: 34.7 us -> 1.99 us  [swap(): return lax.ppermute(value, 'slab', [(i, i ^ x) for i in range(hold_count)])]
    all_to_all x5 -> x4, waiting for transfers between devices: 34.7 us -> 52.5 us  [trade(): return lax.all_to_all(value, axis, split_axis=0, concat_axis=0, tiled=True)]
    pallas_call x10 -> x8, Pallas kernels: 68.3 us -> 64.1 us  [the longest x2 20.2 us: inverse(): pl.pallas_call(functools.partial(inverse_kernel, steps, which, near), gri...]
    all_to_all x5 -> x4, starting transfers between devices: 24.1 us -> 19.9 us  [trade(): return lax.all_to_all(value, axis, split_axis=0, concat_axis=0, tiled=True)]
  transfers between devices with their start and end apart: 8 -> 9, of which waited for: 4 -> 6; matrix products, arithmetic and copies ran while one was open for 7% -> 6% of each run, Pallas kernels for 29% -> 26%
where the time goes in v4:
time: 246 us; the launch traced here: 245 us
  Pallas kernels  95.4 us (39%)
  waiting for transfers between devices  93.3 us (38%)
  starting transfers between devices  22.9 us (9%)
  between operations  14.9 us (6%)
  local copies, waits for them, and re-layouts  9.85 us (4%)
  other arithmetic  8.33 us (3%)
    all_to_all x4, waiting for transfers between devices, trade(): return lax.all_to_all(value, axis, split_axis=0, concat_axis=0, tiled=True)  52.5 us
    reduce_scatter x1, waiting for transfers between devices, shards(): lax.psum_scatter(crops.reshape(field_count, own_slots * HALF, LANES), 'be...  38.8 us
    pallas_call x2, Pallas kernels, inverse(): pl.pallas_call(functools.partial(inverse_kernel, steps, which, near), gri...  20.2 us
    pallas_call x2, Pallas kernels, forward_x(): pl.pallas_call(forward_x_kernel, grid_spec=pltpu.PrefetchScalarGridSpec(n...  20.1 us
    all_to_all x4, starting transfers between devices, trade(): return lax.all_to_all(value, axis, split_axis=0, concat_axis=0, tiled=True)  19.9 us
    pallas_call x2, Pallas kernels, forward_y(): pl.pallas_call(forward_y_kernel, grid=(BLOCKS + steps,), in_specs=[pl.Blo...  18.5 us
    pallas_call x2, Pallas kernels, collect(): pl.pallas_call(collect_kernel, grid=(1,), in_specs=[sheet_spec] * len(she...  13.2 us
    pallas_call x2, Pallas kernels, forward_y_first(): pl.pallas_call(forward_y_first_kernel, grid=(BLOCKS,), in_specs=[pl.Block...  12.2 us
  transfers between devices with their start and end apart: 9, of which 6 were waited for; matrix products, arithmetic and copies ran while one was open for 6% of the time, Pallas kernels for 26%

profile of v4, /device:TPU:0, one launch (start us, length us, event | category | flops | bytes accessed | tf_op | source)
XLA Modules:
  0.0 244.7 jit_solution(5448075117340122814)
XLA Ops:
  6.5 10.1 %forward_x.3 = bf16[8,2,208,128]{3,2,1,0:T(8,128)(2,1)} custom-call(s32[1]{0:T(128)} %bitcast.3.sel, bf16[8,4,16,4096]{3,2,1,0:T(8,128)(2,1)} %bitcast.38, bf16[4,512,1024]{2,1,0:T(8,128)(2,1)} %constant.252.clone.section, bf16[4,8,208,256]{3,2,1,0:T(8,128)(2,1)} %constant.253.clone.last), custom_call_target="tpu_custom_call" | custom-call | flops 9900000256 | tf_op jit(solution)/shard_map/forward_x/pallas_call | solution.py:179
  16.6 7.4 %all-to-all-start.1 = ((bf16[8,2,208,128]{3,2,1,0:T(8,128)(2,1)}), bf16[8,2,208,128]{3,2,1,0:T(8,128)(2,1)S(1)}, u32[]{:S(2)}, u32[]{:S(2)}) async-start(bf16[8,2,208,128]{3,2,1,0:T(8,128)(2,1)} %forward_x.3), calls=%async_computation.1 | async-start | bytes 1703936 | tf_op jit(solution)/shard_map/all_to_all | solution.py:715
  24.0 0.1 reshape.766
  24.1 0.1 copy.30
  24.2 0.1 constant_dynamic-slice_fusion.1
  24.3 0.5 fusion.25
  25.5 0.1 constant_dynamic-slice_fusion
  25.6 0.1 copy.29
  25.7 0.1 reshape.770
  25.8 0.1 reshape.771
  25.9 1.3 fusion.23
  27.2 0.1 broadcast_multiply_fusion
  27.3 1.1 negate_convert_fusion
  28.5 0.8 copy.36
  29.3 1.4 reshape.775.rest_1_.refs_2_
  30.7 0.5 compare_convert_fusion
  31.2 0.5 and_select_fusion.5
  31.7 0.7 multiply_convert_fusion.rest_2_.refs_3_
  32.4 10.1 %forward_x.2 = bf16[8,2,208,128]{3,2,1,0:T(8,128)(2,1)} custom-call(s32[1]{0:T(128)} %bitcast.3.sel, bf16[8,4,16,4096]{3,2,1,0:T(8,128)(2,1)} %bitcast.39, bf16[4,512,1024]{2,1,0:T(8,128)(2,1)} %constant.252.clone.section, bf16[4,8,208,256]{3,2,1,0:T(8,128)(2,1)} %constant.253.clone.last), custom_call_target="tpu_custom_call" | custom-call | flops 9900000256 | tf_op jit(solution)/shard_map/forward_x/pallas_call | solution.py:179
  42.4 3.2 %all-to-all-done.1.lines = bf16[8,2,208,128]{3,2,1,0:T(8,128)(2,1)S(1)} async-done(((bf16[8,2,208,128]{3,2,1,0:T(8,128)(2,1)}), bf16[8,2,208,128]{3,2,1,0:T(8,128)(2,1)S(1)}, u32[]{:S(2)}, u32[]{:S(2)}) %all-to-all-start.1) | async-done | bytes 852000 | tf_op jit(solution)/shard_map/all_to_all | solution.py:715
  45.7 3.5 %all-to-all-start = ((bf16[8,2,208,128]{3,2,1,0:T(8,128)(2,1)}), bf16[8,2,208,128]{3,2,1,0:T(8,128)(2,1)S(1)}, u32[]{:S(2)}, u32[]{:S(2)}) async-start(bf16[8,2,208,128]{3,2,1,0:T(8,128)(2,1)} %forward_x.2), calls=%async_computation | async-start | bytes 1703936 | tf_op jit(solution)/shard_map/all_to_all | solution.py:715
  49.2 0.5 and_select_fusion.6
  49.7 1.5 collective-permute-start
  51.2 6.1 %forward_y_first.2.after.earlier = bf16[64,2,32,128]{3,2,1,0:T(8,128)(2,1)} custom-call(bf16[8,2,208,128]{3,2,1,0:T(8,128)(2,1)} %copy-done.1, bf16[2,1024,1024]{2,1,0:T(8,128)(2,1)} %constant.254.clone.section), custom_call_target="tpu_custom_call" | custom-call | flops 6600000000 | tf_op jit(solution)/shard_map/forward_y_first/pallas_call | solution.py:244
  57.3 7.1 %crop.1.rest_0_ = bf16[32,32,128]{2,1,0:T(8,128)(2,1)} custom-call(s32[32]{0:T(128)} %get-tuple-element.35.rows, s32[32]{0:T(128)} %get-tuple-element.34.cols, s32[32]{0:T(128)} %get-tuple-element.10.odd, s32[32]{0:T(128)} %get-tuple-element.7.mine, bf16[512,4096]{1,0:T(8,128)(2,1)} %pot.1, bf16[64,2,32,128]{3,2,1,0:T(8,128)(2,1)} %forward_y_first.2.after.earlier), custom_call_target="tpu_custom_call" | custom-call | flops 7699999744 | tf_op jit(solution)/shard_map/crop/pallas_call | solution.py:522
  64.5 6.5 %all-to-all-done.value = bf16[8,2,208,128]{3,2,1,0:T(8,128)(2,1)S(1)} async-done(((bf16[8,2,208,128]{3,2,1,0:T(8,128)(2,1)}), bf16[8,2,208,128]{3,2,1,0:T(8,128)(2,1)S(1)}, u32[]{:S(2)}, u32[]{:S(2)}) %all-to-all-start) | async-done | bytes 852000 | tf_op jit(solution)/shard_map/all_to_all | solution.py:715
  70.9 0.9 copy-done
  71.8 1.5 collective-permute-start.2
  73.3 0.9 copy-done.7
  74.3 6.1 %forward_y_first.3.rest_0_.earlier.rest_1_ = bf16[64,2,32,128]{3,2,1,0:T(8,128)(2,1)} custom-call(bf16[8,2,208,128]{3,2,1,0:T(8,128)(2,1)} %copy-done.7, bf16[2,1024,1024]{2,1,0:T(8,128)(2,1)} %constant.254.clone.section), custom_call_target="tpu_custom_call" | custom-call | flops 6600000000 | tf_op jit(solution)/shard_map/forward_y_first/pallas_call | solution.py:244
  80.4 9.2 %forward_y.2.rest_0_.refs_0_ = bf16[32,208,128]{2,1,0:T(8,128)(2,1)} custom-call(bf16[8,2,208,128]{3,2,1,0:T(8,128)(2,1)} %order.1.lines, bf16[2,1024,1024]{2,1,0:T(8,128)(2,1)} %constant.254.clone.section, bf16[64,2,32,128]{3,2,1,0:T(8,128)(2,1)} %forward_y_first.2.after.earlier, bf16[32,208,256]{2,1,0:T(8,128)(2,1)} %constant.255.clone.last, ...), custom_call_target="tpu_custom_call" | custom-call | flops 8800000000 | tf_op jit(solution)/shard_map/forward_y/pallas_call | solution.py:296
  89.6 2.0 collective-permute-done.2.lines
  91.6 9.2 %forward_y.3.refs_7_.refs_0_ = bf16[32,208,128]{2,1,0:T(8,128)(2,1)} custom-call(bf16[8,2,208,128]{3,2,1,0:T(8,128)(2,1)} %collective-permute-done.2.lines, bf16[2,1024,1024]{2,1,0:T(8,128)(2,1)} %constant.254.clone.section, bf16[64,2,32,128]{3,2,1,0:T(8,128)(2,1)} %forward_y_first.3.rest_0_.earlier.rest_1_, bf16[32,208,256]{2,1,0:T(8,128)(2,1)} %constant.255.clone.last, ...), custom_call_target="tpu_custom_call" | custom-call | flops 8800000000 | tf_op jit(solution)/shard_map/forward_y/pallas_call | solution.py:296
  101.5 0.1 pad.10.clone
  101.6 0.1 add_add_fusion
  101.7 0.7 reshape.767.sel
  102.3 1.2 copy-done.6
  103.5 10.1 %inverse.2.refs_7_.refs_0_ = bf16[32,256,256]{2,1,0:T(8,128)(2,1)} custom-call(s32[12]{0:T(128)} %reshape.767.sel, bf16[32,208,128]{2,1,0:T(8,128)(2,1)} %forward_y.2.rest_0_.refs_0_, bf16[32,208,128]{2,1,0:T(8,128)(2,1)} %copy-done.6, f32[208,128]{1,0:T(8,128)} %constant.256.clone.refs_2_, f32[4,1,128]{2,1,0:T(1,128)} %multiply_convert_fusion.rest_2_.refs_3_, ...), custom_call_target="tpu_custom_call" | custom-call | flops 6600000000 | tf_op jit(solution)/shard_map/inverse/pallas_call | solution.py:411
  113.6 10.1 %inverse.3.refs_1_ = bf16[32,256,256]{2,1,0:T(8,128)(2,1)} custom-call(s32[12]{0:T(128)} %reshape.767.sel, bf16[32,208,128]{2,1,0:T(8,128)(2,1)} %forward_y.3.refs_7_.refs_0_, bf16[32,208,128]{2,1,0:T(8,128)(2,1)} %collective-permute-done.3.refs_1_, f32[208,128]{1,0:T(8,128)} %constant.256.clone.refs_2_, f32[4,1,128]{2,1,0:T(1,128)} %multiply_convert_fusion.rest_2_.refs_3_, ...), custom_call_target="tpu_custom_call" | custom-call | flops 6600000000 | tf_op jit(solution)/shard_map/inverse/pallas_call | solution.py:411
  123.7 6.6 %collect.2 = bf16[32,2,4,16,128]{4,3,2,1,0:T(8,128)(2,1)} custom-call(bf16[32,256,256]{2,1,0:T(8,128)(2,1)} %inverse.2.refs_7_.refs_0_, bf16[32,256,256]{2,1,0:T(8,128)(2,1)} %inverse.3.refs_1_, bf16[512,512]{1,0:T(8,128)(2,1)} %reshape.775.rest_1_.refs_2_), custom_call_target="tpu_custom_call" | custom-call | flops 1650000000 | tf_op jit(solution)/shard_map/collect/pallas_call | solution.py:477
  130.3 5.3 %all-to-all-start.2 = ((bf16[32,2,4,16,128]{4,3,2,1,0:T(8,128)(2,1)}), bf16[32,2,4,16,128]{4,3,2,1,0:T(8,128)(2,1)S(1)}, u32[]{:S(2)}, u32[]{:S(2)}) async-start(bf16[32,2,4,16,128]{4,3,2,1,0:T(8,128)(2,1)} %collect.2), calls=%async_computation.2 | async-start | bytes 2097152 | tf_op jit(solution)/shard_map/all_to_all | solution.py:715
  135.6 6.6 %collect.3 = bf16[32,2,4,16,128]{4,3,2,1,0:T(8,128)(2,1)} custom-call(bf16[32,256,256]{2,1,0:T(8,128)(2,1)} %inverse.2.refs_7_.refs_0_, bf16[32,256,256]{2,1,0:T(8,128)(2,1)} %inverse.3.refs_1_, bf16[512,512]{1,0:T(8,128)(2,1)} %reshape.775.rest_1_.refs_2_), custom_call_target="tpu_custom_call" | custom-call | flops 1650000000 | tf_op jit(solution)/shard_map/collect/pallas_call | solution.py:477
  142.2 19.4 %all-to-all-done.2 = bf16[32,2,4,16,128]{4,3,2,1,0:T(8,128)(2,1)S(1)} async-done(((bf16[32,2,4,16,128]{4,3,2,1,0:T(8,128)(2,1)}), bf16[32,2,4,16,128]{4,3,2,1,0:T(8,128)(2,1)S(1)}, u32[]{:S(2)}, u32[]{:S(2)}) %all-to-all-start.2) | async-done | bytes 1048608 | tf_op jit(solution)/shard_map/all_to_all | solution.py:715
  161.6 3.6 %all-to-all-start.3 = ((bf16[32,2,4,16,128]{4,3,2,1,0:T(8,128)(2,1)}), bf16[32,2,4,16,128]{4,3,2,1,0:T(8,128)(2,1)S(1)}, u32[]{:S(2)}, u32[]{:S(2)}) async-start(bf16[32,2,4,16,128]{4,3,2,1,0:T(8,128)(2,1)} %collect.3), calls=%async_computation.3 | async-start | bytes 2097152 | tf_op jit(solution)/shard_map/all_to_all | solution.py:715
  165.3 0.1 add.447
  165.4 0.1 add.438
  165.5 0.2 dynamic-slice_reduce_fusion
  165.8 0.1 add.444
  165.8 0.1 add.445
  165.9 0.1 add.435
  166.0 0.1 add.436
  166.1 0.6 dynamic_slice.18.counts
  166.7 0.1 fusion.24
  166.8 0.6 pad_maximum_fusion.2.alpha
  167.5 0.3 fusion.9
  167.8 0.7 pad_maximum_fusion.1.refs_3_
  168.5 0.9 reduce_sum.24.refs_0_
  169.4 23.4 %all-to-all-done.3 = bf16[32,2,4,16,128]{4,3,2,1,0:T(8,128)(2,1)S(1)} async-done(((bf16[32,2,4,16,128]{4,3,2,1,0:T(8,128)(2,1)}), bf16[32,2,4,16,128]{4,3,2,1,0:T(8,128)(2,1)S(1)}, u32[]{:S(2)}, u32[]{:S(2)}) %all-to-all-start.3) | async-done | bytes 1048608 | tf_op jit(solution)/shard_map/all_to_all | solution.py:715
  192.8 0.8 reduce_sum.25.refs_1_
  193.6 38.8 %reduce-scatter.2.cloned.1.call-done = bf16[1,128,128]{2,1,0:T(8,128)(2,1)} async-done(((bf16[8,128,128]{2,1,0:T(8,128)(2,1)}), bf16[1,128,128]{2,1,0:T(8,128)(2,1)}) %reduce-scatter.2.cloned.1.call-update) | async-done | bytes 32784 | tf_op jit(solution)/shard_map/reduce_scatter | solution.py:760
  232.5 4.1 %detect.1 = f32[1,256]{1,0:T(1,128)} custom-call(f32[2,4,12]{2,1,0:T(4,128)} %pad_maximum_fusion.2.alpha, s32[1]{0:T(128)} %dynamic_slice.18.counts, bf16[4,2,4,16,128]{4,3,2,1,0:T(8,128)(2,1)} %reduce_sum.24.refs_0_, bf16[4,2,4,16,128]{4,3,2,1,0:T(8,128)(2,1)} %reduce_sum.25.refs_1_, bf16[4,32,128]{2,1,0:T(8,128)(2,1)} %bitcast.37, ...), custom_call_target="tpu_custom_call" | custom-call | tf_op jit(solution)/shard_map/detect/pallas_call | solution.py:588
  236.5 0.7 slice_reduce_fusion
  237.2 0.1 reshape_squeeze.3
  237.3 0.6 copy.35
  (39 shorter events, 0.3 us)
Async XLA Ops:
  6.5 17.5 %copy-start.3 = (s32[32,4]{0,1:T(4,128)S(1)}, s32[32,4]{0,1:T(4,128)}, u32[]{:S(2)}) copy-start(s32[32,4]{0,1:T(4,128)} %param.21) | copy-start | bytes 1540
  6.5 17.7 %copy-start.2 = (s32[4,2]{0,1:T(2,128)S(1)}, s32[4,2]{0,1:T(2,128)}, u32[]{:S(2)}) copy-start(s32[4,2]{0,1:T(2,128)} %param.19) | copy-start | bytes 100
  16.6 15.1 %copy-start.4 = (s32[128]{0:T(128)S(1)}, s32[128]{0:T(128)}, u32[]{:S(2)}) copy-start(s32[128]{0:T(128)} %constant.251.clone) | copy-start | bytes 1540
  16.6 29.0 %all-to-all-start.1 = ((bf16[8,2,208,128]{3,2,1,0:T(8,128)(2,1)}), bf16[8,2,208,128]{3,2,1,0:T(8,128)(2,1)S(1)}, u32[]{:S(2)}, u32[]{:S(2)}) async-start(bf16[8,2,208,128]{3,2,1,0:T(8,128)(2,1)} %forward_x.3), calls=%async_computation.1 | async-start | bytes 1703936 | tf_op jit(solution)/shard_map/all_to_all | solution.py:715
  45.7 5.6 %copy-start.1 = (bf16[8,2,208,128]{3,2,1,0:T(8,128)(2,1)}, bf16[8,2,208,128]{3,2,1,0:T(8,128)(2,1)S(1)}, u32[]{:S(2)}) copy-start(bf16[8,2,208,128]{3,2,1,0:T(8,128)(2,1)S(1)} %all-to-all-done.1.lines) | copy-start | bytes 2555908
  45.7 25.3 %all-to-all-start = ((bf16[8,2,208,128]{3,2,1,0:T(8,128)(2,1)}), bf16[8,2,208,128]{3,2,1,0:T(8,128)(2,1)S(1)}, u32[]{:S(2)}, u32[]{:S(2)}) async-start(bf16[8,2,208,128]{3,2,1,0:T(8,128)(2,1)} %forward_x.2), calls=%async_computation | async-start | bytes 1703936 | tf_op jit(solution)/shard_map/all_to_all | solution.py:715
  49.7 23.6 %collective-permute-start = (bf16[8,2,208,128]{3,2,1,0:T(8,128)(2,1)S(1)}, bf16[8,2,208,128]{3,2,1,0:T(8,128)(2,1)S(1)}, u32[]{:S(2)}, u32[]{:S(2)}) collective-permute-start(bf16[8,2,208,128]{3,2,1,0:T(8,128)(2,1)S(1)} %all-to-all-done.1.lines), channel_id=1, source_target_pairs={{0,2},{1,3},{2,0},{3,1},{4,6},{5,7},{6,4},{7,5},{8,10},{9,11},{10,... | collective-permute-start | bytes 2555912 | tf_op jit(solution)/shard_map/ppermute | solution.py:721
  70.9 0.9 copy-start
  71.8 19.8 %collective-permute-start.2 = (bf16[8,2,208,128]{3,2,1,0:T(8,128)(2,1)}, bf16[8,2,208,128]{3,2,1,0:T(8,128)(2,1)}, u32[]{:S(2)}, u32[]{:S(2)}) collective-permute-start(bf16[8,2,208,128]{3,2,1,0:T(8,128)(2,1)} %order.1.lines), channel_id=1, source_target_pairs={{0,2},{1,3},{2,0},{3,1},{4,6},{5,7},{6,4},{7,5},{8,10},{9,11},{10,... | collective-permute-start | bytes 2555912 | tf_op jit(solution)/shard_map/ppermute | solution.py:721
  73.3 0.9 copy-start.7
  89.6 12.7 %collective-permute-start.1 = (bf16[32,208,128]{2,1,0:T(8,128)(2,1)}, bf16[32,208,128]{2,1,0:T(8,128)(2,1)S(1)}, u32[]{:S(2)}, u32[]{:S(2)}) collective-permute-start(bf16[32,208,128]{2,1,0:T(8,128)(2,1)} %forward_y.2.rest_0_.refs_0_), channel_id=1, source_target_pairs={{0,1},{1,0},{2,3},{3,2},{4,5},{5,4},{6,7},{7,6},{8,9},{9,8},{10,11... | collective-permute-start | bytes 5111816 | tf_op jit(solution)/shard_map/ppermute | solution.py:721
  100.8 12.7 %collective-permute-start.3 = (bf16[32,208,128]{2,1,0:T(8,128)(2,1)}, bf16[32,208,128]{2,1,0:T(8,128)(2,1)}, u32[]{:S(2)}, u32[]{:S(2)}) collective-permute-start(bf16[32,208,128]{2,1,0:T(8,128)(2,1)} %forward_y.3.refs_7_.refs_0_), channel_id=1, source_target_pairs={{0,1},{1,0},{2,3},{3,2},{4,5},{5,4},{6,7},{7,6},{8,9},{9,8},{10,11... | collective-permute-start | bytes 5111816 | tf_op jit(solution)/shard_map/ppermute | solution.py:721
  102.3 1.2 copy-start.6
  130.3 31.4 %all-to-all-start.2 = ((bf16[32,2,4,16,128]{4,3,2,1,0:T(8,128)(2,1)}), bf16[32,2,4,16,128]{4,3,2,1,0:T(8,128)(2,1)S(1)}, u32[]{:S(2)}, u32[]{:S(2)}) async-start(bf16[32,2,4,16,128]{4,3,2,1,0:T(8,128)(2,1)} %collect.2), calls=%async_computation.2 | async-start | bytes 2097152 | tf_op jit(solution)/shard_map/all_to_all | solution.py:715
  135.6 30.5 %copy-start.8 = (s32[32]{0:T(128)S(1)}, s32[32]{0:T(128)}, u32[]{:S(2)}) copy-start(s32[32]{0:T(128)} %param.22) | copy-start | bytes 388
  135.6 31.1 %copy-start.5 = (f32[4]{0:T(128)S(1)}, f32[4]{0:T(128)}, u32[]{:S(2)}) copy-start(f32[4]{0:T(128)} %param.20) | copy-start | bytes 52
  161.6 31.2 %all-to-all-start.3 = ((bf16[32,2,4,16,128]{4,3,2,1,0:T(8,128)(2,1)}), bf16[32,2,4,16,128]{4,3,2,1,0:T(8,128)(2,1)S(1)}, u32[]{:S(2)}, u32[]{:S(2)}) async-start(bf16[32,2,4,16,128]{4,3,2,1,0:T(8,128)(2,1)} %collect.3), calls=%async_computation.3 | async-start | bytes 2097152 | tf_op jit(solution)/shard_map/all_to_all | solution.py:715
  165.2 67.2 %reduce-scatter.2.cloned.1.call-start = ((), (), s32[]{:S(2)}) async-start(), calls=%async_computation.5 | async-start | bytes 294912 | tf_op jit(solution)/shard_map/reduce_scatter | solution.py:760
Sparse Core Ops, SparseCore 0:
  169.4 63.0 reduce-scatter.1

commit v5 on v4

--- a/solution.py
+++ b/solution.py
@@ -207,25 +207,21 @@
         for h in range(steps):
             block = lines[g, h].astype(F32)
             both = jnp.concatenate([block[:PART], zeros, block[PART:], zeros], axis=0)
-            rows = slice(2 * h * LANES, 2 * (h + 1) * LANES)
-            gathered[rows, g * LANES : (g + 1) * LANES] = both.astype(BF)
-
-
-def section_step(steps, section, gathered, twisted):
-    count = section.shape[1] // SUB
-    dims = (((1,), (1,)), ((), ()))
-    values = gathered[...]
-    by_cos = lax.dot_general(section[0], values, dims, preferred_element_type=F32)
-    by_sin = lax.dot_general(section[1], values, dims, preferred_element_type=F32)
+            columns = slice(2 * h * LANES, 2 * (h + 1) * LANES)
+            gathered[g * LANES : (g + 1) * LANES, columns] = both.astype(BF).T
+
+
+def section_step(steps, section, gathered):
+    rows = section.shape[1]
+    both = dot(section[...].reshape(2 * rows, section.shape[2]), gathered[...])
     for h in range(steps):
         re = slice(2 * h * LANES, (2 * h + 1) * LANES)
         im = slice((2 * h + 1) * LANES, (2 * h + 2) * LANES)
-        real = by_cos[:, re] - by_sin[:, im]
-        imag = by_cos[:, im] + by_sin[:, re]
+        real = both[:rows, re] - both[rows:, im]
+        imag = both[:rows, im] + both[rows:, re]
+        shape = (rows // SUB, SUB, LANES)
         span = slice(h * SUB, (h + 1) * SUB)
-        yield span, real.astype(BF).reshape(count, SUB, LANES), imag.astype(BF).reshape(
-            count, SUB, LANES
-        )
+        yield span, real.astype(BF).reshape(shape), imag.astype(BF).reshape(shape)
 
 
 def forward_y_first_kernel(lines, section, twisted, gathered):
@@ -233,7 +229,7 @@
     def _():
         gather_lines(lines, gathered)
 
-    for span, real, imag in section_step(lines.shape[1], section, gathered, twisted):
+    for span, real, imag in section_step(lines.shape[1], section, gathered):
         twisted[:, 0, span, :] = real
         twisted[:, 1, span, :] = imag
 
@@ -250,7 +246,7 @@
         ],
         out_specs=pl.BlockSpec((count, 2, A // PARTS, LANES), lambda i: (i, 0, 0, 0)),
         out_shape=jax.ShapeDtypeStruct((A, 2, A // PARTS, LANES), BF),
-        scratch_shapes=[pltpu.VMEM((2 * steps * LANES, A * SUB), BF)],
+        scratch_shapes=[pltpu.VMEM((A * SUB, 2 * steps * LANES), BF)],
         compiler_params=pltpu.CompilerParams(vmem_limit_bytes=VMEM),
         cost_estimate=cost(6),
         name="forward_y_first",
@@ -269,7 +265,7 @@
     def _():
         count = A // BLOCKS
         spot = pl.ds(step * count, count)
-        for span, real, imag in section_step(lines.shape[1], section, gathered, twisted):
+        for span, real, imag in section_step(lines.shape[1], section, gathered):
             twisted[spot, 0, span, :] = real
             twisted[spot, 1, span, :] = imag
 
@@ -308,7 +304,7 @@
         out_specs=pl.BlockSpec((count, ROWS, LANES), late),
         out_shape=jax.ShapeDtypeStruct((PAIRS, ROWS, LANES), BF),
         scratch_shapes=[
-            pltpu.VMEM((2 * lines.shape[1] * LANES, A * SUB), BF),
+            pltpu.VMEM((A * SUB, 2 * lines.shape[1] * LANES), BF),
             pltpu.VMEM((A, 2, A // PARTS, LANES), BF),
         ],
         compiler_params=pltpu.CompilerParams(vmem_limit_bytes=VMEM),
@@ -445,7 +441,7 @@
         stacked = sheets[0][i]
         if len(sheets) > 1:
             stacked = jnp.concatenate([sheet[i] for sheet in sheets], axis=0)
-        sums = dot(weights[...], stacked)
+        sums = dot(weights[0], stacked)
         for part in range(2):
             even = sums[2 * part * tiles : (2 * part + 1) * tiles]
             odd = sums[(2 * part + 1) * tiles : (2 * part + 2) * tiles]
@@ -468,21 +464,21 @@
     lax.fori_loop(0, devices, device, 0, unroll=4)
 
 
-def collect(sheets, weights, devices, part):
-    tiles = weights.shape[0] // 4
-    lines = HALF // PARTS
+def collect(sheets, weights, devices, which):
+    tiles = weights.shape[1] // 4
+    lines = HALF
     shape = (devices, 2, tiles // devices, lines, LANES)
-    sheet_spec = pl.BlockSpec((lines,) + sheets[0].shape[1:], lambda i: (part, 0, 0))
+    sheet_spec = pl.BlockSpec(sheets[0].shape, lambda i: (0, 0, 0))
     block = pl.BlockSpec(shape, lambda i: (0, 0, 0, 0, 0))
     return pl.pallas_call(
         collect_kernel,
         grid=(1,),
-        in_specs=[sheet_spec] * len(sheets) + [pl.BlockSpec(weights.shape, lambda i: (0, 0))],
+        in_specs=[sheet_spec] * len(sheets) + [pl.BlockSpec((1,) + weights.shape[1:], lambda i: (which, 0, 0))],
         out_specs=block,
         out_shape=jax.ShapeDtypeStruct(shape, BF),
         scratch_shapes=[pltpu.VMEM((2 * tiles * (lines + 1), LANES), F32)],
         compiler_params=pltpu.CompilerParams(vmem_limit_bytes=VMEM),
-        cost_estimate=cost(1.5),
+        cost_estimate=cost(6),
         name="collect",
     )(*sheets, weights)
 
@@ -728,7 +724,10 @@
     beam_row = lax.dynamic_index_in_dim(beam_index, hold_pos, 0, keepdims=False)
     pair_ids = share ^ jnp.arange(sheets, dtype=jnp.int32)
     k1_pairs = field_pos * width_k + 2 * pair_ids
-    weights = tile_weights(tile_table.reshape(-1), beam_row, k1_pairs)
+    parity = field_pos % 2
+    sets = table.reshape(field_count // 2, 2, hold_count, own_slots)
+    sets = [lax.dynamic_index_in_dim(sets, pos, 1, keepdims=False) for pos in (1 - parity, parity)]
+    weights = jnp.stack([tile_weights(t.reshape(-1), beam_row, k1_pairs) for t in sets])
     row = np.arange(ROWS)
     base = row // PART + A * (K2_LOW + row % PART % K2_COUNT)
     freq_y = np.broadcast_to(base[:, None], (ROWS, LANES)).astype(np.float32)
@@ -757,16 +756,15 @@
             received[f].append(swap(lines, f * near) if f else lines)
         if part == 0:
             earlier = [forward_y_first(received[f][0], section_y) for f in range(far)]
-    crops = lax.psum_scatter(
-        crops.reshape(field_count, own_slots * HALF, LANES), "beam", scatter_dimension=0
-    ).reshape(own_slots, HALF, LANES)
-
     waves = []
     ready = []
     token = []
     for f in range(far):
         spec = forward_y(received[f][1], section_y, earlier[f], last_y, token + earlier[1:])
         ready.append([spec] + [swap(spec, x) for x in range(1, near)])
+        if f == 0:
+            crops = order(crops.reshape(field_count, own_slots, HALF, LANES), [spec])
+            crops = trade(crops, "beam")
         token = [spec]
     for f in range(far):
         waves.append(
@@ -774,13 +772,27 @@
                 f * near, scalars, ready[f], freq_y, square_x, inverse_y, inverse_x, token
             )
         )
-        token = waves[-1:]
-    fields = []
-    for part in range(PARTS):
-        tiles = collect(waves, weights, field_count * hold_count, part)
-        tiles = trade(tiles, ("beam", "slab"))
-        tiles = tiles.reshape((field_count, hold_count) + tiles.shape[1:]).astype(F32)
-        fields.append(jnp.sum(tiles, axis=0).astype(BF))
+        token = waves[-1:] + [crops]
+    owners = field_count // 2 * hold_count
+    partial = collect(waves, weights, owners, 0)
+    partial = lax.ppermute(partial, "beam", [(i, i ^ 1) for i in range(field_count)])
+    tiles = collect(waves, weights, owners, 1)
+    tiles = (tiles.astype(F32) + partial.astype(F32)).astype(BF)
+    groups = [
+        [b * hold_count + h for b in range(g, field_count, 2) for h in range(hold_count)]
+        for g in range(2)
+    ]
+    tiles = lax.all_to_all(
+        tiles,
+        ("beam", "slab"),
+        split_axis=0,
+        concat_axis=0,
+        axis_index_groups=groups,
+        tiled=True,
+    )
+    tiles = tiles.reshape((field_count // 2, hold_count) + tiles.shape[1:]).astype(F32)
+    fields = [jnp.sum(tiles, axis=0).astype(BF)]
+    crops = jnp.sum(crops.astype(F32), axis=0).astype(BF)
 
     own = lax.dynamic_index_in_dim(
         lax.dynamic_index_in_dim(table, field_pos, 0, keepdims=False), hold_pos, 0, keepdims=False

time: 246 us -> 198 us (0.80)
  waiting for transfers between devices: 93.3 us -> 43.2 us
  between operations: 14.9 us -> 1.58 us
  starting transfers between devices: 22.9 us -> 28.2 us
  other arithmetic: 8.33 us -> 12.9 us
  Pallas kernels: 95.4 us -> 99.5 us
    all_to_all x4 -> x3, waiting for transfers between devices: 52.5 us -> 7.02 us  [trade(): return lax.all_to_all(value, axis, split_axis=0, concat_axis=0, tiled=True)]
    reduce_scatter x1 -> x0, waiting for transfers between devices: 38.8 us -> none  [shards(): lax.psum_scatter(crops.reshape(field_count, own_slots * HALF, LANES), 'be...]
    all_to_all x0 -> x1, waiting for transfers between devices: none -> 19.1 us  [shards(): lax.all_to_all(tiles, ('beam', 'slab'), split_axis=0, concat_axis=0, axis...]
    ppermute x0 -> x1, waiting for transfers between devices: none -> 14.8 us  [shards(): lax.ppermute(partial, 'beam', [(i, i ^ 1) for i in range(field_count)])]
    all_to_all x0 -> x1, starting transfers between devices: none -> 5.97 us  [shards(): lax.all_to_all(tiles, ('beam', 'slab'), split_axis=0, concat_axis=0, axis...]
    pallas_call x2, Pallas kernels: 13.2 us -> 17.4 us  [collect(): pl.pallas_call(collect_kernel, grid=(1,), in_specs=[sheet_spec] * len(she...]
    all_to_all x4 -> x3, starting transfers between devices: 19.9 us -> 17.1 us  [trade(): return lax.all_to_all(value, axis, split_axis=0, concat_axis=0, tiled=True)]
    convert_element_type x0 -> x1, other arithmetic: none -> 2.7 us  [shards(): tiles = (tiles.astype(F32) + partial.astype(F32)).astype(BF)]
  transfers between devices with their start and end apart: 9 -> 9, of which waited for: 6 -> 5; matrix products, arithmetic and copies ran while one was open for 6% -> 7% of each run, Pallas kernels for 26% -> 34%
where the time goes in v5:
time: 198 us; the launch traced here: 196 us
  Pallas kernels  99.5 us (50%)
  waiting for transfers between devices  43.2 us (22%)
  starting transfers between devices  28.2 us (14%)
  other arithmetic  12.9 us (7%)
  local copies, waits for them, and re-layouts  10.4 us (5%)
    pallas_call x2, Pallas kernels, inverse(): pl.pallas_call(functools.partial(inverse_kernel, steps, which, near), gri...  20.2 us
    pallas_call x2, Pallas kernels, forward_x(): pl.pallas_call(forward_x_kernel, grid_spec=pltpu.PrefetchScalarGridSpec(n...  20.1 us
    all_to_all x1, waiting for transfers between devices, shards(): lax.all_to_all(tiles, ('beam', 'slab'), split_axis=0, concat_axis=0, axis...  19.1 us
    pallas_call x2, Pallas kernels, forward_y(): pl.pallas_call(forward_y_kernel, grid=(BLOCKS + steps,), in_specs=[pl.Blo...  18.4 us
    pallas_call x2, Pallas kernels, collect(): pl.pallas_call(collect_kernel, grid=(1,), in_specs=[sheet_spec] * len(she...  17.4 us
    all_to_all x3, starting transfers between devices, trade(): return lax.all_to_all(value, axis, split_axis=0, concat_axis=0, tiled=True)  17.1 us
    ppermute x1, waiting for transfers between devices, shards(): lax.ppermute(partial, 'beam', [(i, i ^ 1) for i in range(field_count)])  14.8 us
    pallas_call x2, Pallas kernels, forward_y_first(): pl.pallas_call(forward_y_first_kernel, grid=(BLOCKS,), in_specs=[pl.Block...  12.2 us
  transfers between devices with their start and end apart: 9, of which 5 were waited for; matrix products, arithmetic and copies ran while one was open for 7% of the time, Pallas kernels for 34%

profile of v5, /device:TPU:0, one launch (start us, length us, event | category | flops | bytes accessed | tf_op | source)
XLA Modules:
  0.0 195.8 jit_solution(16373153588104357708)
XLA Ops:
  0.0 10.1 %forward_x.3 = bf16[8,2,208,128]{3,2,1,0:T(8,128)(2,1)} custom-call(s32[1]{0:T(128)} %bitcast.3.sel, bf16[8,4,16,4096]{3,2,1,0:T(8,128)(2,1)} %bitcast.44, bf16[4,512,1024]{2,1,0:T(8,128)(2,1)} %constant.286.clone.section, bf16[4,8,208,256]{3,2,1,0:T(8,128)(2,1)} %constant.287.clone.last), custom_call_target="tpu_custom_call" | custom-call | flops 9900000256 | tf_op jit(solution)/shard_map/forward_x/pallas_call | solution.py:179
  10.1 7.3 %all-to-all-start.1 = ((bf16[8,2,208,128]{3,2,1,0:T(8,128)(2,1)}), bf16[8,2,208,128]{3,2,1,0:T(8,128)(2,1)S(1)}, u32[]{:S(2)}, u32[]{:S(2)}) async-start(bf16[8,2,208,128]{3,2,1,0:T(8,128)(2,1)} %forward_x.3), calls=%async_computation.1 | async-start | bytes 1703936 | tf_op jit(solution)/shard_map/all_to_all | solution.py:711
  17.4 0.1 reshape_reshape.3
  17.6 0.6 fusion.32
  18.3 0.1 copy.28
  18.5 0.6 compare_convert_fusion
  19.1 0.5 and_select_fusion.7
  19.6 0.1 copy.29
  19.8 0.1 reshape.918
  19.9 0.1 copy.31
  20.0 0.1 reshape.919
  20.7 1.3 fusion.29
  22.2 1.2 negate_convert_fusion.1
  23.4 0.1 maximum_bitcast_fusion
  23.6 0.1 pad_maximum_fusion
  23.7 0.5 copy.30
  24.2 0.3 convert_element_type.110
  24.6 1.2 negate_convert_fusion
  25.9 0.1 maximum_bitcast_fusion.2
  26.0 0.1 pad_maximum_fusion.1
  26.1 0.6 and_select_fusion.8
  26.7 0.7 multiply_convert_fusion.rest_2_.refs_3_
  27.4 10.1 %forward_x.2 = bf16[8,2,208,128]{3,2,1,0:T(8,128)(2,1)} custom-call(s32[1]{0:T(128)} %bitcast.3.sel, bf16[8,4,16,4096]{3,2,1,0:T(8,128)(2,1)} %bitcast.45, bf16[4,512,1024]{2,1,0:T(8,128)(2,1)} %constant.286.clone.section, bf16[4,8,208,256]{3,2,1,0:T(8,128)(2,1)} %constant.287.clone.last), custom_call_target="tpu_custom_call" | custom-call | flops 9900000256 | tf_op jit(solution)/shard_map/forward_x/pallas_call | solution.py:179
  37.4 1.6 all-to-all-done.1.lines
  39.0 4.4 %all-to-all-start = ((bf16[8,2,208,128]{3,2,1,0:T(8,128)(2,1)}), bf16[8,2,208,128]{3,2,1,0:T(8,128)(2,1)S(1)}, u32[]{:S(2)}, u32[]{:S(2)}) async-start(bf16[8,2,208,128]{3,2,1,0:T(8,128)(2,1)} %forward_x.2), calls=%async_computation | async-start | bytes 1703936 | tf_op jit(solution)/shard_map/all_to_all | solution.py:711
  43.5 0.5 copy.32
  44.0 0.3 convert_element_type.112
  44.4 1.6 collective-permute-start
  45.9 6.1 %forward_y_first.2.after.earlier = bf16[64,2,32,128]{3,2,1,0:T(8,128)(2,1)} custom-call(bf16[8,2,208,128]{3,2,1,0:T(8,128)(2,1)} %copy-done.4, bf16[2,1024,1024]{2,1,0:T(8,128)(2,1)} %constant.288.clone.section), custom_call_target="tpu_custom_call" | custom-call | flops 6600000000 | tf_op jit(solution)/shard_map/forward_y_first/pallas_call | solution.py:240
  52.0 7.1 %crop.1.rest_0_ = bf16[32,32,128]{2,1,0:T(8,128)(2,1)} custom-call(s32[32]{0:T(128)} %get-tuple-element.46.rows, s32[32]{0:T(128)} %get-tuple-element.45.cols, s32[32]{0:T(128)} %get-tuple-element.10.odd, s32[32]{0:T(128)} %get-tuple-element.7.mine, bf16[512,4096]{1,0:T(8,128)(2,1)} %pot.1, bf16[64,2,32,128]{3,2,1,0:T(8,128)(2,1)} %forward_y_first.2.after.earlier), custom_call_target="tpu_custom_call" | custom-call | flops 7699999744 | tf_op jit(solution)/shard_map/crop/pallas_call | solution.py:518
  59.2 5.5 %all-to-all-done.value = bf16[8,2,208,128]{3,2,1,0:T(8,128)(2,1)S(1)} async-done(((bf16[8,2,208,128]{3,2,1,0:T(8,128)(2,1)}), bf16[8,2,208,128]{3,2,1,0:T(8,128)(2,1)S(1)}, u32[]{:S(2)}, u32[]{:S(2)}) %all-to-all-start) | async-done | bytes 852000 | tf_op jit(solution)/shard_map/all_to_all | solution.py:711
  64.6 0.9 copy-done
  65.5 1.5 collective-permute-start.2
  67.0 6.1 %forward_y_first.3.rest_0_.earlier.rest_1_ = bf16[64,2,32,128]{3,2,1,0:T(8,128)(2,1)} custom-call(bf16[8,2,208,128]{3,2,1,0:T(8,128)(2,1)} %collective-permute-done.lines, bf16[2,1024,1024]{2,1,0:T(8,128)(2,1)} %constant.288.clone.section), custom_call_target="tpu_custom_call" | custom-call | flops 6600000000 | tf_op jit(solution)/shard_map/forward_y_first/pallas_call | solution.py:240
  73.1 9.2 %forward_y.2.rest_0_.refs_0_ = bf16[32,208,128]{2,1,0:T(8,128)(2,1)} custom-call(bf16[8,2,208,128]{3,2,1,0:T(8,128)(2,1)} %order.2.lines, bf16[2,1024,1024]{2,1,0:T(8,128)(2,1)} %constant.288.clone.section, bf16[64,2,32,128]{3,2,1,0:T(8,128)(2,1)} %forward_y_first.2.after.earlier, bf16[32,208,256]{2,1,0:T(8,128)(2,1)} %constant.289.clone.last, ...), custom_call_target="tpu_custom_call" | custom-call | flops 8800000000 | tf_op jit(solution)/shard_map/forward_y/pallas_call | solution.py:292
  82.4 2.3 %collective-permute-done.2.lines = bf16[8,2,208,128]{3,2,1,0:T(8,128)(2,1)S(1)} collective-permute-done((bf16[8,2,208,128]{3,2,1,0:T(8,128)(2,1)}, bf16[8,2,208,128]{3,2,1,0:T(8,128)(2,1)S(1)}, u32[]{:S(2)}, u32[]{:S(2)}) %collective-permute-start.2) | collective-permute-done | bytes 852000 | tf_op jit(solution)/shard_map/ppermute | solution.py:717
  84.6 0.9 copy-done.11
  85.5 9.2 %forward_y.3.refs_7_.refs_0_ = bf16[32,208,128]{2,1,0:T(8,128)(2,1)} custom-call(bf16[8,2,208,128]{3,2,1,0:T(8,128)(2,1)} %copy-done.11, bf16[2,1024,1024]{2,1,0:T(8,128)(2,1)} %constant.288.clone.section, bf16[64,2,32,128]{3,2,1,0:T(8,128)(2,1)} %forward_y_first.3.rest_0_.earlier.rest_1_, bf16[32,208,256]{2,1,0:T(8,128)(2,1)} %constant.289.clone.last, ...), custom_call_target="tpu_custom_call" | custom-call | flops 8800000000 | tf_op jit(solution)/shard_map/forward_y/pallas_call | solution.py:292
  95.5 0.6 reshape.914.sel
  96.1 5.4 %all-to-all-start.2 = ((bf16[8,4,32,128]{3,2,1,0:T(8,128)(2,1)}), bf16[8,4,32,128]{3,2,1,0:T(8,128)(2,1)S(1)}, u32[]{:S(2)}, u32[]{:S(2)}) async-start(bf16[8,4,32,128]{3,2,1,0:T(8,128)(2,1)} %order.3), calls=%async_computation.2 | async-start | bytes 524288 | tf_op jit(solution)/shard_map/all_to_all | solution.py:711
  101.6 10.1 %inverse.2.refs_7_.refs_0_ = bf16[32,256,256]{2,1,0:T(8,128)(2,1)} custom-call(s32[12]{0:T(128)} %reshape.914.sel, bf16[32,208,128]{2,1,0:T(8,128)(2,1)} %forward_y.2.rest_0_.refs_0_, bf16[32,208,128]{2,1,0:T(8,128)(2,1)} %collective-permute-done.1.refs_1_, f32[208,128]{1,0:T(8,128)} %constant.290.clone.refs_2_, ...), custom_call_target="tpu_custom_call" | custom-call | flops 6600000000 | tf_op jit(solution)/shard_map/inverse/pallas_call | solution.py:407
  111.7 0.7 copy-done.2
  112.4 1.2 copy-done.10
  113.5 10.1 %inverse.3.refs_1_ = bf16[32,256,256]{2,1,0:T(8,128)(2,1)} custom-call(s32[12]{0:T(128)} %reshape.914.sel, bf16[32,208,128]{2,1,0:T(8,128)(2,1)} %forward_y.3.refs_7_.refs_0_, bf16[32,208,128]{2,1,0:T(8,128)(2,1)} %copy-done.10, f32[208,128]{1,0:T(8,128)} %constant.290.clone.refs_2_, f32[4,1,128]{2,1,0:T(1,128)} %multiply_convert_fusion.rest_2_.refs_3_, ...), custom_call_target="tpu_custom_call" | custom-call | flops 6600000000 | tf_op jit(solution)/shard_map/inverse/pallas_call | solution.py:407
  123.7 8.7 %collect.3 = bf16[16,2,4,32,128]{4,3,2,1,0:T(8,128)(2,1)} custom-call(bf16[32,256,256]{2,1,0:T(8,128)(2,1)} %inverse.2.refs_7_.refs_0_, bf16[32,256,256]{2,1,0:T(8,128)(2,1)} %inverse.3.refs_1_, bf16[2,256,512]{2,1,0:T(8,128)(2,1)} %copy-done.1), custom_call_target="tpu_custom_call" | custom-call | flops 6600000000 | tf_op jit(solution)/shard_map/collect/pallas_call | solution.py:473
  132.4 2.0 %collective-permute-start.4 = (bf16[16,2,4,32,128]{4,3,2,1,0:T(8,128)(2,1)}, bf16[16,2,4,32,128]{4,3,2,1,0:T(8,128)(2,1)S(1)}, u32[]{:S(2)}, u32[]{:S(2)}) collective-permute-start(bf16[16,2,4,32,128]{4,3,2,1,0:T(8,128)(2,1)} %collect.3), channel_id=1, source_target_pairs={{0,4},{4,0},{8,12},{12,8},{16,20},{20,16},{24,28},{28,24},{1,5},{5... | collective-permute-start | bytes 3145736 | tf_op jit(solution)/shard_map/ppermute | solution.py:778
  134.4 8.7 %collect.2 = bf16[16,2,4,32,128]{4,3,2,1,0:T(8,128)(2,1)} custom-call(bf16[32,256,256]{2,1,0:T(8,128)(2,1)} %inverse.2.refs_7_.refs_0_, bf16[32,256,256]{2,1,0:T(8,128)(2,1)} %inverse.3.refs_1_, bf16[2,256,512]{2,1,0:T(8,128)(2,1)} %copy-done.1), custom_call_target="tpu_custom_call" | custom-call | flops 6600000000 | tf_op jit(solution)/shard_map/collect/pallas_call | solution.py:473
  143.1 14.8 %collective-permute-done.4 = bf16[16,2,4,32,128]{4,3,2,1,0:T(8,128)(2,1)S(1)} collective-permute-done((bf16[16,2,4,32,128]{4,3,2,1,0:T(8,128)(2,1)}, bf16[16,2,4,32,128]{4,3,2,1,0:T(8,128)(2,1)S(1)}, u32[]{:S(2)}, u32[]{:S(2)}) %collective-permute-start.4) | collective-permute-done | bytes 1048608 | tf_op jit(solution)/shard_map/ppermute | solution.py:778
  157.9 2.7 %add_convert_fusion = bf16[16,2,4,32,128]{4,3,2,1,0:T(8,128)(2,1)} fusion(bf16[16,2,4,32,128]{4,3,2,1,0:T(8,128)(2,1)S(1)} %collective-permute-done.4, bf16[16,2,4,32,128]{4,3,2,1,0:T(8,128)(2,1)} %collect.2), kind=kLoop, calls=%fused_computation | loop fusion | flops 2097152 | bytes 3145728 | tf_op jit(solution)/shard_map/convert_element_type | solution.py:780
  160.6 6.0 %all-to-all-start.3 = ((bf16[16,2,4,32,128]{4,3,2,1,0:T(8,128)(2,1)}), bf16[16,2,4,32,128]{4,3,2,1,0:T(8,128)(2,1)S(1)}, u32[]{:S(2)}, u32[]{:S(2)}) async-start(bf16[16,2,4,32,128]{4,3,2,1,0:T(8,128)(2,1)} %add_convert_fusion), calls=%async_computation.3 | async-start | bytes 2097152 | tf_op jit(solution)/shard_map/all_to_all | solution.py:785
  166.6 0.2 dynamic-slice_reduce_fusion
  166.9 0.1 add.526
  167.4 0.6 dynamic_slice.25.counts
  168.0 0.1 fusion.31
  168.1 0.6 pad_maximum_fusion.3.alpha
  168.7 0.3 fusion.14
  169.1 0.7 pad_maximum_fusion.2.refs_2_
  169.7 0.6 reduce_sum.25.refs_1_
  170.4 19.1 %all-to-all-done.3 = bf16[16,2,4,32,128]{4,3,2,1,0:T(8,128)(2,1)S(1)} async-done(((bf16[16,2,4,32,128]{4,3,2,1,0:T(8,128)(2,1)}), bf16[16,2,4,32,128]{4,3,2,1,0:T(8,128)(2,1)S(1)}, u32[]{:S(2)}, u32[]{:S(2)}) %all-to-all-start.3) | async-done | bytes 1048608 | tf_op jit(solution)/shard_map/all_to_all | solution.py:785
  189.5 0.9 reduce_sum.24.refs_0_
  190.4 4.0 %detect.1 = f32[1,256]{1,0:T(1,128)} custom-call(f32[2,4,12]{2,1,0:T(4,128)} %pad_maximum_fusion.3.alpha, s32[1]{0:T(128)} %dynamic_slice.25.counts, bf16[4,2,4,32,128]{4,3,2,1,0:T(8,128)(2,1)} %reduce_sum.24.refs_0_, bf16[4,32,128]{2,1,0:T(8,128)(2,1)} %reduce_sum.25.refs_1_, f32[4,2,32,128]{3,2,1,0:T(8,128)} %pad_maximum_fusion.2.refs_2_, ...), custom_call_target="tpu_custom_call" | custom-call | tf_op jit(solution)/shard_map/detect/pallas_call | solution.py:584
  194.4 0.7 slice_reduce_fusion
  195.1 0.1 reshape_squeeze.3
  195.2 0.6 copy.33
  (60 shorter events, 1.3 us)
Async XLA Ops:
  0.0 17.4 %copy-start.7 = (s32[32,4]{0,1:T(4,128)S(1)}, s32[32,4]{0,1:T(4,128)}, u32[]{:S(2)}) copy-start(s32[32,4]{0,1:T(4,128)} %param.21) | copy-start | bytes 1540
  0.0 17.5 %copy-start.5 = (s32[4,2]{0,1:T(2,128)S(1)}, s32[4,2]{0,1:T(2,128)}, u32[]{:S(2)}) copy-start(s32[4,2]{0,1:T(2,128)} %param.19) | copy-start | bytes 100
  10.1 28.9 %all-to-all-start.1 = ((bf16[8,2,208,128]{3,2,1,0:T(8,128)(2,1)}), bf16[8,2,208,128]{3,2,1,0:T(8,128)(2,1)S(1)}, u32[]{:S(2)}, u32[]{:S(2)}) async-start(bf16[8,2,208,128]{3,2,1,0:T(8,128)(2,1)} %forward_x.3), calls=%async_computation.1 | async-start | bytes 1703936 | tf_op jit(solution)/shard_map/all_to_all | solution.py:711
  23.7 3.0 %copy-start.8 = (s32[128]{0:T(128)S(1)}, s32[128]{0:T(128)}, u32[]{:S(2)}) copy-start(s32[128]{0:T(128)} %constant.285.clone) | copy-start | bytes 1540
  39.0 5.4 %copy-start.4 = (bf16[8,2,208,128]{3,2,1,0:T(8,128)(2,1)}, bf16[8,2,208,128]{3,2,1,0:T(8,128)(2,1)S(1)}, u32[]{:S(2)}) copy-start(bf16[8,2,208,128]{3,2,1,0:T(8,128)(2,1)S(1)} %all-to-all-done.1.lines) | copy-start | bytes 2555908
  39.0 25.6 %all-to-all-start = ((bf16[8,2,208,128]{3,2,1,0:T(8,128)(2,1)}), bf16[8,2,208,128]{3,2,1,0:T(8,128)(2,1)S(1)}, u32[]{:S(2)}, u32[]{:S(2)}) async-start(bf16[8,2,208,128]{3,2,1,0:T(8,128)(2,1)} %forward_x.2), calls=%async_computation | async-start | bytes 1703936 | tf_op jit(solution)/shard_map/all_to_all | solution.py:711
  44.4 7.7 %copy-start.1 = (bf16[2,256,512]{2,1,0:T(8,128)(2,1)}, bf16[2,256,512]{2,1,0:T(8,128)(2,1)S(1)}, u32[]{:S(2)}) copy-start(bf16[2,256,512]{2,1,0:T(8,128)(2,1)S(1)} %constant_dynamic-update-slice_fusion.rest_1_.refs_2_) | copy-start | bytes 1572868
  44.4 22.7 %collective-permute-start = (bf16[8,2,208,128]{3,2,1,0:T(8,128)(2,1)S(1)}, bf16[8,2,208,128]{3,2,1,0:T(8,128)(2,1)}, u32[]{:S(2)}, u32[]{:S(2)}) collective-permute-start(bf16[8,2,208,128]{3,2,1,0:T(8,128)(2,1)S(1)} %all-to-all-done.1.lines), channel_id=1, source_target_pairs={{0,2},{1,3},{2,0},{3,1},{4,6},{5,7},{6,4},{7,5},{8,10},{9,11},{10,... | collective-permute-start | bytes 2555912 | tf_op jit(solution)/shard_map/ppermute | solution.py:717
  64.6 0.9 copy-start
  65.5 19.1 %collective-permute-start.2 = (bf16[8,2,208,128]{3,2,1,0:T(8,128)(2,1)}, bf16[8,2,208,128]{3,2,1,0:T(8,128)(2,1)S(1)}, u32[]{:S(2)}, u32[]{:S(2)}) collective-permute-start(bf16[8,2,208,128]{3,2,1,0:T(8,128)(2,1)} %order.2.lines), channel_id=1, source_target_pairs={{0,2},{1,3},{2,0},{3,1},{4,6},{5,7},{6,4},{7,5},{8,10},{9,11},{10,... | collective-permute-start | bytes 2555912 | tf_op jit(solution)/shard_map/ppermute | solution.py:717
  82.4 19.2 %collective-permute-start.1 = (bf16[32,208,128]{2,1,0:T(8,128)(2,1)}, bf16[32,208,128]{2,1,0:T(8,128)(2,1)}, u32[]{:S(2)}, u32[]{:S(2)}) collective-permute-start(bf16[32,208,128]{2,1,0:T(8,128)(2,1)} %forward_y.2.rest_0_.refs_0_), channel_id=1, source_target_pairs={{0,1},{1,0},{2,3},{3,2},{4,5},{5,4},{6,7},{7,6},{8,9},{9,8},{10,11... | collective-permute-start | bytes 5111816 | tf_op jit(solution)/shard_map/ppermute | solution.py:717
  84.6 0.9 copy-start.11
  94.7 16.9 %collective-permute-start.3 = (bf16[32,208,128]{2,1,0:T(8,128)(2,1)}, bf16[32,208,128]{2,1,0:T(8,128)(2,1)S(1)}, u32[]{:S(2)}, u32[]{:S(2)}) collective-permute-start(bf16[32,208,128]{2,1,0:T(8,128)(2,1)} %forward_y.3.refs_7_.refs_0_), channel_id=1, source_target_pairs={{0,1},{1,0},{2,3},{3,2},{4,5},{5,4},{6,7},{7,6},{8,9},{9,8},{10,11... | collective-permute-start | bytes 5111816 | tf_op jit(solution)/shard_map/ppermute | solution.py:717
  96.1 15.5 %all-to-all-start.2 = ((bf16[8,4,32,128]{3,2,1,0:T(8,128)(2,1)}), bf16[8,4,32,128]{3,2,1,0:T(8,128)(2,1)S(1)}, u32[]{:S(2)}, u32[]{:S(2)}) async-start(bf16[8,4,32,128]{3,2,1,0:T(8,128)(2,1)} %order.3), calls=%async_computation.2 | async-start | bytes 524288 | tf_op jit(solution)/shard_map/all_to_all | solution.py:711
  111.6 0.7 copy-start.2
  112.3 1.2 copy-start.10
  132.4 25.5 %collective-permute-start.4 = (bf16[16,2,4,32,128]{4,3,2,1,0:T(8,128)(2,1)}, bf16[16,2,4,32,128]{4,3,2,1,0:T(8,128)(2,1)S(1)}, u32[]{:S(2)}, u32[]{:S(2)}) collective-permute-start(bf16[16,2,4,32,128]{4,3,2,1,0:T(8,128)(2,1)} %collect.3), channel_id=1, source_target_pairs={{0,4},{4,0},{8,12},{12,8},{16,20},{20,16},{24,28},{28,24},{1,5},{5... | collective-permute-start | bytes 3145736 | tf_op jit(solution)/shard_map/ppermute | solution.py:778
  143.1 23.7 %copy-start.6 = (s32[4,2]{0,1:T(2,128)S(1)}, s32[4,2]{0,1:T(2,128)}, u32[]{:S(2)}) copy-start(s32[4,2]{0,1:T(2,128)} %param.19) | copy-start | bytes 100
  143.1 24.3 %copy-start.12 = (s32[32]{0:T(128)S(1)}, s32[32]{0:T(128)}, u32[]{:S(2)}) copy-start(s32[32]{0:T(128)} %param.22) | copy-start | bytes 388
  143.1 24.9 %copy-start.9 = (f32[4]{0:T(128)S(1)}, f32[4]{0:T(128)}, u32[]{:S(2)}) copy-start(f32[4]{0:T(128)} %param.20) | copy-start | bytes 52
  160.6 9.2 %copy-start.3 = (bf16[8,4,32,128]{3,2,1,0:T(8,128)(2,1)S(1)}, bf16[8,4,32,128]{3,2,1,0:T(8,128)(2,1)}, u32[]{:S(2)}) copy-start(bf16[8,4,32,128]{3,2,1,0:T(8,128)(2,1)} %copy-done.2) | copy-start | bytes 786436
  160.6 28.9 %all-to-all-start.3 = ((bf16[16,2,4,32,128]{4,3,2,1,0:T(8,128)(2,1)}), bf16[16,2,4,32,128]{4,3,2,1,0:T(8,128)(2,1)S(1)}, u32[]{:S(2)}, u32[]{:S(2)}) async-start(bf16[16,2,4,32,128]{4,3,2,1,0:T(8,128)(2,1)} %add_convert_fusion), calls=%async_computation.3 | async-start | bytes 2097152 | tf_op jit(solution)/shard_map/all_to_all | solution.py:785

commit v6 on v5

--- a/solution.py
+++ b/solution.py
@@ -23,13 +23,14 @@
 ROWS = 2 * PART
 LANES = 128
 SUB = 16
+FEW = 4
 HIGH = A // SUB
 HALF = A // 2
 PAIRS = A // 2
 PARTS = 2
-BLOCKS = 4
 VMEM = 60 * 1024 * 1024
 PITCH = A + 1
+PITCH_Y = A // PARTS + 1
 BF = jnp.bfloat16
 F32 = jnp.float32
 
@@ -46,11 +47,9 @@
     return K2_LOW + np.arange(K2_COUNT)
 
 
-def spread(table):
+def spread(table, sub):
     both = np.stack([table.real, table.imag])
-    eye = np.eye(SUB)
-    out = both[:, :, None, :, None] * eye[None, None, :, None, :]
-    return low(out.reshape(2 * table.shape[0] * SUB, table.shape[1] * SUB))
+    return both[:, :, None, :, None] * np.eye(sub)[None, None, :, None, :]
 
 
 def real_rows(table):
@@ -59,7 +58,23 @@
 
 def section_forward(k1):
     n1 = np.arange(A)
-    return spread(np.conj(turn(k1[:, None] * n1[None, :], A)) / A)
+    return np.conj(turn(k1[:, None] * n1[None, :], A)) / A
+
+
+def first_forward_x(k1):
+    return low(spread(section_forward(k1), SUB).reshape(2 * len(k1) * SUB, A * SUB))
+
+
+def first_forward_y():
+    table = spread(section_forward(np.arange(A)), FEW).transpose(0, 2, 1, 3, 4)
+    return low(table.reshape(2 * A * FEW, A * FEW))
+
+
+def line_order(lanes):
+    order = np.arange(lanes).reshape(-1, SUB // FEW, FEW).transpose(1, 0, 2).reshape(-1)
+    out = np.zeros((lanes, lanes))
+    out[order, np.arange(lanes)] = 1
+    return low(out)
 
 
 def last_forward_x(k1_pair):
@@ -97,12 +112,15 @@
 
 
 def first_inverse_x(k1_pair):
-    out = np.zeros((LANES, 2, 2, A))
+    out = np.zeros((2, LANES, 2, 2, A))
     for ks, k1 in enumerate(k1_pair):
         table = first_inverse(k1).T
-        out[ks * K2_COUNT : (ks + 1) * K2_COUNT, 0, ks] = table.real
-        out[ks * K2_COUNT : (ks + 1) * K2_COUNT, 1, ks] = table.imag
-    return low(out.reshape(LANES, 4 * A))
+        rows = slice(ks * K2_COUNT, (ks + 1) * K2_COUNT)
+        out[0, rows, 0, ks] = table.real
+        out[0, rows, 1, ks] = table.imag
+        out[1, rows, 0, ks] = -table.imag
+        out[1, rows, 1, ks] = table.real
+    return low(out.reshape(2 * LANES, 4 * A))
 
 
 def sine_cosine(x):
@@ -137,7 +155,7 @@
     return pl.CostEstimate(flops=int(micros * 1.1e9), bytes_accessed=0, transcendentals=0)
 
 
-def forward_x_kernel(sel, pot, section, last, out, cos_ref, sin_ref, twisted):
+def forward_x_kernel(sel, pot, section, last, perm, out, cos_ref, sin_ref, twisted):
     fields = out.shape[0]
     lanes = out.shape[3]
     half = section.shape[1] // 2
@@ -169,7 +187,7 @@
         )
     for d in range(fields):
         lines = twisted[2 * d : 2 * d + 2].reshape(4 * A, lanes)
-        out[d, 0] = dot(last[0, d], lines).astype(BF)
+        out[d, 0] = dot(dot(last[0, d], lines).astype(BF), perm[...]).astype(BF)
 
 
 def forward_x(sel, pot, section, last, fields, part):
@@ -185,6 +203,7 @@
                 pl.BlockSpec((groups, 1, SUB, N), lambda i, s: (0, part * steps + i, 0, 0)),
                 pl.BlockSpec((1,) + section.shape[1:], lambda i, s: (s[0], 0, 0)),
                 pl.BlockSpec((1,) + last.shape[1:], lambda i, s: (s[0], 0, 0, 0)),
+                pl.BlockSpec((lanes, lanes), lambda i, s: (0, 0)),
             ],
             out_specs=pl.BlockSpec((fields, 1, ROWS, lanes), lambda i, s: (0, i, 0, 0)),
             scratch_shapes=[
@@ -197,88 +216,92 @@
         compiler_params=pltpu.CompilerParams(vmem_limit_bytes=VMEM),
         cost_estimate=cost(9),
         name="forward_x",
-    )(sel, pot.reshape(groups, HIGH, SUB, N), section, last)
-
-
-def gather_lines(lines, gathered):
-    steps = lines.shape[1]
+    )(sel, pot.reshape(groups, HIGH, SUB, N), section, last, line_order(lanes))
+
+
+def first_section_y(lines, section, gathered, held):
+    groups, steps = lines.shape[:2]
+    span = LANES * FEW // SUB
     zeros = jnp.zeros((LANES - PART, LANES), F32)
-    for g in range(lines.shape[0]):
+    for g in range(groups):
         for h in range(steps):
             block = lines[g, h].astype(F32)
             both = jnp.concatenate([block[:PART], zeros, block[PART:], zeros], axis=0)
+            turned = both.astype(BF).T
             columns = slice(2 * h * LANES, 2 * (h + 1) * LANES)
-            gathered[g * LANES : (g + 1) * LANES, columns] = both.astype(BF).T
-
-
-def section_step(steps, section, gathered):
-    rows = section.shape[1]
-    both = dot(section[...].reshape(2 * rows, section.shape[2]), gathered[...])
-    for h in range(steps):
-        re = slice(2 * h * LANES, (2 * h + 1) * LANES)
-        im = slice((2 * h + 1) * LANES, (2 * h + 2) * LANES)
-        real = both[:rows, re] - both[rows:, im]
-        imag = both[:rows, im] + both[rows:, re]
-        shape = (rows // SUB, SUB, LANES)
-        span = slice(h * SUB, (h + 1) * SUB)
-        yield span, real.astype(BF).reshape(shape), imag.astype(BF).reshape(shape)
-
-
-def forward_y_first_kernel(lines, section, twisted, gathered):
-    @pl.when(pl.program_id(0) == 0)
-    def _():
-        gather_lines(lines, gathered)
-
-    for span, real, imag in section_step(lines.shape[1], section, gathered):
-        twisted[:, 0, span, :] = real
-        twisted[:, 1, span, :] = imag
+            for a in range(SUB // FEW):
+                gathered[a, g * span : (g + 1) * span, columns] = turned[a * span : (a + 1) * span]
+    half = A * FEW
+    for a in range(SUB // FEW):
+        both = dot(section[...], gathered[a])
+        for h in range(steps):
+            re = slice(2 * h * LANES, (2 * h + 1) * LANES)
+            im = slice((2 * h + 1) * LANES, (2 * h + 2) * LANES)
+            real = both[:half, re] - both[half:, im]
+            imag = both[:half, im] + both[half:, re]
+            for b in range(FEW):
+                n2 = h * SUB + a * FEW + b
+                rows = slice(b * A, (b + 1) * A)
+                held[pl.ds(n2, A, stride=PITCH_Y), :] = real[rows]
+                held[pl.ds(A * PITCH_Y + n2, A, stride=PITCH_Y), :] = imag[rows]
+
+
+def first_section_scratch(lines):
+    return [
+        pltpu.VMEM((SUB // FEW, A * FEW, 2 * lines.shape[1] * LANES), BF),
+        pltpu.VMEM(((2 * A + 1) * PITCH_Y, LANES), F32),
+    ]
+
+
+def forward_y_first_kernel(lines, section, twisted, gathered, held):
+    first_section_y(lines, section, gathered, held)
+
+    def digit(k, carry):
+        for part in range(2):
+            start = (part * A + k) * PITCH_Y
+            twisted[k, part] = held[pl.ds(start, A // PARTS), :].astype(BF)
+        return carry
+
+    lax.fori_loop(0, A, digit, 0, unroll=8)
 
 
 def forward_y_first(lines, section):
-    steps = lines.shape[1]
-    count = A // BLOCKS
     return pl.pallas_call(
         forward_y_first_kernel,
-        grid=(BLOCKS,),
+        grid=(1,),
         in_specs=[
             pl.BlockSpec(lines.shape, lambda i: (0, 0, 0, 0)),
-            pl.BlockSpec((2, count * SUB, A * SUB), lambda i: (0, i, 0)),
+            pl.BlockSpec(section.shape, lambda i: (0, 0)),
         ],
-        out_specs=pl.BlockSpec((count, 2, A // PARTS, LANES), lambda i: (i, 0, 0, 0)),
+        out_specs=pl.BlockSpec((A, 2, A // PARTS, LANES), lambda i: (0, 0, 0, 0)),
         out_shape=jax.ShapeDtypeStruct((A, 2, A // PARTS, LANES), BF),
-        scratch_shapes=[pltpu.VMEM((A * SUB, 2 * steps * LANES), BF)],
+        scratch_shapes=first_section_scratch(lines),
         compiler_params=pltpu.CompilerParams(vmem_limit_bytes=VMEM),
-        cost_estimate=cost(6),
+        cost_estimate=cost(4),
         name="forward_y_first",
     )(lines, section)
 
 
 def forward_y_kernel(lines, section, earlier, last, *rest):
-    out, gathered, twisted = rest[-3:]
+    out, gathered, held = rest[-3:]
     step = pl.program_id(0)
 
     @pl.when(step == 0)
     def _():
-        gather_lines(lines, gathered)
-
-    @pl.when(step < BLOCKS)
-    def _():
-        count = A // BLOCKS
-        spot = pl.ds(step * count, count)
-        for span, real, imag in section_step(lines.shape[1], section, gathered):
-            twisted[spot, 0, span, :] = real
-            twisted[spot, 1, span, :] = imag
-
-    @pl.when(step >= BLOCKS)
+        first_section_y(lines, section, gathered, held)
+
+    @pl.when(step > 0)
     def _():
         count = out.shape[0]
-        base = (step - BLOCKS) * count
+        base = (step - 1) * count
         for q in range(count):
             rows = []
             for e in range(2):
                 for part in range(2):
-                    rows.append(earlier[2 * (base + q) + e, part])
-                    rows.append(twisted[2 * (base + q) + e, part])
+                    k = 2 * (base + q) + e
+                    rows.append(earlier[k, part])
+                    start = (part * A + k) * PITCH_Y
+                    rows.append(held[pl.ds(start, A // PARTS), :].astype(BF))
             out[q] = dot(last[q], jnp.concatenate(rows, axis=0)).astype(BF)
 
 
@@ -287,28 +310,23 @@
     count = PAIRS // steps
 
     def late(i):
-        return (jnp.maximum(i - BLOCKS, 0), 0, 0)
+        return (jnp.maximum(i - 1, 0), 0, 0)
 
     return pl.pallas_call(
         forward_y_kernel,
-        grid=(BLOCKS + steps,),
+        grid=(1 + steps,),
         in_specs=[
             pl.BlockSpec(lines.shape, lambda i: (0, 0, 0, 0)),
-            pl.BlockSpec(
-                (2, A // BLOCKS * SUB, A * SUB), lambda i: (0, jnp.minimum(i, BLOCKS - 1), 0)
-            ),
+            pl.BlockSpec(section.shape, lambda i: (0, 0)),
             pl.BlockSpec(earlier.shape, lambda i: (0, 0, 0, 0)),
             pl.BlockSpec((count, ROWS, 4 * A), late),
         ]
         + [pl.BlockSpec(memory_space=pl.ANY)] * len(after),
         out_specs=pl.BlockSpec((count, ROWS, LANES), late),
         out_shape=jax.ShapeDtypeStruct((PAIRS, ROWS, LANES), BF),
-        scratch_shapes=[
-            pltpu.VMEM((A * SUB, 2 * lines.shape[1] * LANES), BF),
-            pltpu.VMEM((A, 2, A // PARTS, LANES), BF),
-        ],
+        scratch_shapes=first_section_scratch(lines),
         compiler_params=pltpu.CompilerParams(vmem_limit_bytes=VMEM),
-        cost_estimate=cost(8),
+        cost_estimate=cost(6),
         name="forward_y",
     )(lines, section, earlier, last, *after)
 
@@ -371,19 +389,17 @@
             for x in range(near):
                 rows = []
                 for b in range(2):
+                    start = x * whole + (by + b * HALF) * PITCH
+                    real = mid[pl.ds(start, A), :].astype(BF)
+                    imag = mid[pl.ds(start + A * PITCH, A), :].astype(BF)
+                    rows.append(jnp.concatenate([real, imag], axis=1))
+                product = dot(jnp.concatenate(rows, axis=0), tables_x[x][0, 0]).astype(BF)
+                for b in range(2):
                     for part in range(2):
-                        start = x * whole + part * A * PITCH + (by + b * HALF) * PITCH
-                        rows.append(mid[pl.ds(start, A), :].astype(BF))
-                product = dot(jnp.concatenate(rows, axis=0), tables_x[x][0, 0])
-                low_row = 2 * A * x
-                for b in range(2):
-                    re = product[2 * b * A : (2 * b + 1) * A]
-                    im = product[(2 * b + 1) * A : (2 * b + 2) * A]
-                    span = slice(b * LANES, (b + 1) * LANES)
-                    real = re[:, :LANES] - im[:, LANES:]
-                    imag = re[:, LANES:] + im[:, :LANES]
-                    out[i, low_row : low_row + A, span] = real.astype(BF)
-                    out[i, low_row + A : low_row + 2 * A, span] = imag.astype(BF)
+                        low_row = 2 * A * x + A * part
+                        out[i, low_row : low_row + A, b * LANES : (b + 1) * LANES] = product[
+                            b * A : (b + 1) * A, part * LANES : (part + 1) * LANES
+                        ]
             return carry
 
         lax.fori_loop(0, each, line, 0, unroll=4)
@@ -420,7 +436,7 @@
             out_specs=pl.BlockSpec(
                 (each, 2 * A * near, 2 * LANES), lambda i, s: (jnp.maximum(i - steps, 0), 0, 0)
             ),
-            scratch_shapes=[pltpu.VMEM((near * 2 * A * PITCH, LANES), F32)],
+            scratch_shapes=[pltpu.VMEM(((near * 2 * A + 1) * PITCH, LANES), F32)],
         ),
         out_shape=jax.ShapeDtypeStruct((HALF, 2 * A * near, 2 * LANES), BF),
         compiler_params=pltpu.CompilerParams(vmem_limit_bytes=VMEM),
@@ -432,6 +448,8 @@
 def collect_kernel(*refs):
     *sheets, weights, out, held = refs
     devices, _, slots, lines, _ = out.shape
+    each = sheets[0].shape[0]
+    step = pl.program_id(0)
     tiles = devices * slots
     pitch = lines + 1
     lane = lax.broadcasted_iota(jnp.int32, (tiles, LANES), 1)
@@ -448,10 +466,11 @@
             keep = jnp.where(lower, even[:, :LANES], odd[:, LANES:])
             move = jnp.where(lower, even[:, LANES:], odd[:, :LANES])
             total = keep + pltpu.roll(move, A, 1)
-            held[pl.ds(part * tiles * pitch + i, tiles, stride=pitch), :] = total
+            spot = part * tiles * pitch + step * each + i
+            held[pl.ds(spot, tiles, stride=pitch), :] = total
         return carry
 
-    lax.fori_loop(0, lines, line, 0, unroll=4)
+    lax.fori_loop(0, each, line, 0, unroll=4)
 
     def device(d, carry):
         for part in range(2):
@@ -461,22 +480,25 @@
                 out[d, part, slot] = total.astype(BF)
         return carry
 
-    lax.fori_loop(0, devices, device, 0, unroll=4)
+    @pl.when(step == lines // each - 1)
+    def _():
+        lax.fori_loop(0, devices, device, 0, unroll=4)
 
 
 def collect(sheets, weights, devices, which):
     tiles = weights.shape[1] // 4
     lines = HALF
     shape = (devices, 2, tiles // devices, lines, LANES)
-    sheet_spec = pl.BlockSpec(sheets[0].shape, lambda i: (0, 0, 0))
+    steps = 4
+    sheet_spec = pl.BlockSpec((lines // steps,) + sheets[0].shape[1:], lambda i: (i, 0, 0))
     block = pl.BlockSpec(shape, lambda i: (0, 0, 0, 0, 0))
     return pl.pallas_call(
         collect_kernel,
-        grid=(1,),
+        grid=(steps,),
         in_specs=[sheet_spec] * len(sheets) + [pl.BlockSpec((1,) + weights.shape[1:], lambda i: (which, 0, 0))],
         out_specs=block,
         out_shape=jax.ShapeDtypeStruct(shape, BF),
-        scratch_shapes=[pltpu.VMEM((2 * tiles * (lines + 1), LANES), F32)],
+        scratch_shapes=[pltpu.VMEM(((2 * tiles + 1) * (lines + 1), LANES), F32)],
         compiler_params=pltpu.CompilerParams(vmem_limit_bytes=VMEM),
         cost_estimate=cost(6),
         name="collect",
@@ -668,7 +690,7 @@
 
     section_x = np.stack(
         [
-            section_forward(
+            first_forward_x(
                 np.array(
                     [width_k * p + 2 * t + ks for p in range(field_count) for ks in range(2)]
                 )
@@ -687,7 +709,7 @@
             for t in range(sheets)
         ]
     )
-    section_y = section_forward(np.arange(A)).reshape(2, A * SUB, A * SUB)
+    section_y = first_forward_y()
     last_y = np.stack([last_forward_y([2 * q, 2 * q + 1]) for q in range(PAIRS)])
     inverse_y = np.stack([first_inverse_y([2 * q, 2 * q + 1]) for q in range(PAIRS)])
     inverse_x = np.stack(
@@ -747,8 +769,10 @@
         lines = trade(forward_x(sel, pot_first, section_x, last_x, field_count, part), "beam")
         if lines.shape[3] != LANES:
             ratio = LANES // lines.shape[3]
-            lines = lines.reshape((field_count // ratio, ratio) + lines.shape[1:])
-            lines = lines.transpose(0, 2, 3, 1, 4).reshape(-1, HIGH // PARTS, ROWS, LANES)
+            lines = lines.reshape(
+                field_count // ratio, ratio, HIGH // PARTS, ROWS, SUB // FEW, -1
+            )
+            lines = lines.transpose(0, 2, 3, 4, 1, 5).reshape(-1, HIGH // PARTS, ROWS, LANES)
         if part:
             crops = crop(rows, tile_x // 2, tile_x % 2, mine, pot_second, earlier[0])
             lines = order(lines, [crops, weights, square_x])
@@ -765,14 +789,14 @@
         if f == 0:
             crops = order(crops.reshape(field_count, own_slots, HALF, LANES), [spec])
             crops = trade(crops, "beam")
-        token = [spec]
+        token = [spec, crops]
     for f in range(far):
         waves.append(
             inverse(
                 f * near, scalars, ready[f], freq_y, square_x, inverse_y, inverse_x, token
             )
         )
-        token = waves[-1:] + [crops]
+        token = waves[-1:]
     owners = field_count // 2 * hold_count
     partial = collect(waves, weights, owners, 0)
     partial = lax.ppermute(partial, "beam", [(i, i ^ 1) for i in range(field_count)])

time: 198 us -> 190 us (0.960)
  Pallas kernels: 99.5 us -> 85.2 us
  waiting for transfers between devices: 43.2 us -> 53.5 us
  starting transfers between devices: 28.2 us -> 23.8 us
    pallas_call x6, Pallas kernels: 48 us -> 33.9 us  [the longest x2 15 us: collect(): pl.pallas_call(collect_kernel, grid=(steps,), in_specs=[sheet_spec] * len...]
    all_to_all x3, waiting for transfers between devices: 7.02 us -> 12.9 us  [trade(): return lax.all_to_all(value, axis, split_axis=0, concat_axis=0, tiled=True)]
    ppermute x1, waiting for transfers between devices: 14.8 us -> 18.2 us  [shards(): lax.ppermute(partial, 'beam', [(i, i ^ 1) for i in range(field_count)])]
    all_to_all x1, starting transfers between devices: 5.97 us -> 3.65 us  [shards(): lax.all_to_all(tiles, ('beam', 'slab'), split_axis=0, concat_axis=0, axis...]
  transfers between devices with their start and end apart: 9 -> 9, of which waited for: 5 -> 6; matrix products, arithmetic and copies ran while one was open for 7% -> 8% of each run, Pallas kernels for 34% -> 28%
where the time goes in v6:
time: 190 us; the launch traced here: 188 us
  Pallas kernels  85.2 us (45%)
  waiting for transfers between devices  53.5 us (28%)
  starting transfers between devices  23.8 us (13%)
  other arithmetic  14.1 us (7%)
  local copies, waits for them, and re-layouts  9.56 us (5%)
    pallas_call x2, Pallas kernels, forward_x(): pl.pallas_call(forward_x_kernel, grid_spec=pltpu.PrefetchScalarGridSpec(n...  21.4 us
    all_to_all x1, waiting for transfers between devices, shards(): lax.all_to_all(tiles, ('beam', 'slab'), split_axis=0, concat_axis=0, axis...  19.1 us
    pallas_call x2, Pallas kernels, inverse(): pl.pallas_call(functools.partial(inverse_kernel, steps, which, near), gri...  18.8 us
    ppermute x1, waiting for transfers between devices, shards(): lax.ppermute(partial, 'beam', [(i, i ^ 1) for i in range(field_count)])  18.2 us
    all_to_all x3, starting transfers between devices, trade(): return lax.all_to_all(value, axis, split_axis=0, concat_axis=0, tiled=True)  17 us
    pallas_call x2, Pallas kernels, collect(): pl.pallas_call(collect_kernel, grid=(steps,), in_specs=[sheet_spec] * len...  15 us
    all_to_all x3, waiting for transfers between devices, trade(): return lax.all_to_all(value, axis, split_axis=0, concat_axis=0, tiled=True)  12.9 us
    pallas_call x2, Pallas kernels, forward_y(): pl.pallas_call(forward_y_kernel, grid=(1 + steps,), in_specs=[pl.BlockSpe...  12.2 us
  transfers between devices with their start and end apart: 9, of which 6 were waited for; matrix products, arithmetic and copies ran while one was open for 8% of the time, Pallas kernels for 28%

profile of v6, /device:TPU:0, one launch (start us, length us, event | category | flops | bytes accessed | tf_op | source)
XLA Modules:
  0.0 187.7 jit_solution(18186018022015794694)
XLA Ops:
  0.0 10.7 %forward_x.3 = bf16[8,2,208,128]{3,2,1,0:T(8,128)(2,1)} custom-call(s32[1]{0:T(128)} %bitcast.3.sel, bf16[8,4,16,4096]{3,2,1,0:T(8,128)(2,1)} %bitcast.44, bf16[4,512,1024]{2,1,0:T(8,128)(2,1)} %constant.288.clone.section, bf16[4,8,208,256]{3,2,1,0:T(8,128)(2,1)} %constant.289.clone.last, bf16[128,128]{1,0:T(8,128)(2,1)} %constant.290.clone.perm), custom_call_target="tpu_custom_call" | custom-call | flops 9900000256 | tf_op jit(solution)/shard_map/forward_x/pallas_call | solution.py:197
  10.7 7.3 %all-to-all-start.1 = ((bf16[8,2,208,128]{3,2,1,0:T(8,128)(2,1)}), bf16[8,2,208,128]{3,2,1,0:T(8,128)(2,1)S(1)}, u32[]{:S(2)}, u32[]{:S(2)}) async-start(bf16[8,2,208,128]{3,2,1,0:T(8,128)(2,1)} %forward_x.3), calls=%async_computation.1 | async-start | bytes 1703936 | tf_op jit(solution)/shard_map/all_to_all | solution.py:733
  18.1 0.1 reshape_reshape.3
  18.3 0.6 fusion.32
  19.5 0.5 broadcast_add_fusion
  20.1 0.1 copy.30
  20.3 0.6 compare_convert_fusion
  20.9 0.1 copy.33
  21.0 0.1 reshape.919
  21.1 0.1 copy.31
  21.2 0.1 reshape.918
  21.3 1.3 fusion.29
  22.8 1.2 negate_convert_fusion.1
  24.1 0.1 maximum_bitcast_fusion
  24.2 0.1 pad_maximum_fusion
  24.3 0.5 copy.32
  24.9 0.3 convert_element_type.110
  25.2 1.3 negate_convert_fusion
  26.5 0.1 maximum_bitcast_fusion.2
  26.6 0.1 pad_maximum_fusion.1
  26.7 0.6 and_select_fusion.7
  27.3 0.6 and_select_fusion.8
  27.9 10.7 %forward_x.2 = bf16[8,2,208,128]{3,2,1,0:T(8,128)(2,1)} custom-call(s32[1]{0:T(128)} %bitcast.3.sel, bf16[8,4,16,4096]{3,2,1,0:T(8,128)(2,1)} %bitcast.45, bf16[4,512,1024]{2,1,0:T(8,128)(2,1)} %constant.288.clone.section, bf16[4,8,208,256]{3,2,1,0:T(8,128)(2,1)} %constant.289.clone.last, bf16[128,128]{1,0:T(8,128)(2,1)} %constant.290.clone.perm), custom_call_target="tpu_custom_call" | custom-call | flops 9900000256 | tf_op jit(solution)/shard_map/forward_x/pallas_call | solution.py:197
  38.6 1.1 all-to-all-done.1.lines
  39.6 4.9 %all-to-all-start = ((bf16[8,2,208,128]{3,2,1,0:T(8,128)(2,1)}), bf16[8,2,208,128]{3,2,1,0:T(8,128)(2,1)S(1)}, u32[]{:S(2)}, u32[]{:S(2)}) async-start(bf16[8,2,208,128]{3,2,1,0:T(8,128)(2,1)} %forward_x.2), calls=%async_computation | async-start | bytes 1703936 | tf_op jit(solution)/shard_map/all_to_all | solution.py:733
  44.6 0.5 copy.34
  45.2 0.3 convert_element_type.112
  45.5 1.3 multiply_convert_fusion.rest_2_.refs_3_
  46.9 1.5 collective-permute-start
  48.3 3.3 %forward_y_first.2.after.earlier = bf16[64,2,32,128]{3,2,1,0:T(8,128)(2,1)} custom-call(bf16[8,2,208,128]{3,2,1,0:T(8,128)(2,1)} %copy-done.4, bf16[512,256]{1,0:T(8,128)(2,1)} %constant.291.clone.section), custom_call_target="tpu_custom_call" | custom-call | flops 4400000000 | tf_op jit(solution)/shard_map/forward_y_first/pallas_call | solution.py:269
  51.7 7.1 %crop.1.rest_0_ = bf16[32,32,128]{2,1,0:T(8,128)(2,1)} custom-call(s32[32]{0:T(128)} %get-tuple-element.46.rows, s32[32]{0:T(128)} %get-tuple-element.45.cols, s32[32]{0:T(128)} %get-tuple-element.10.odd, s32[32]{0:T(128)} %get-tuple-element.7.mine, bf16[512,4096]{1,0:T(8,128)(2,1)} %pot.1, bf16[64,2,32,128]{3,2,1,0:T(8,128)(2,1)} %forward_y_first.2.after.earlier), custom_call_target="tpu_custom_call" | custom-call | flops 7699999744 | tf_op jit(solution)/shard_map/crop/pallas_call | solution.py:540
  58.8 7.0 %all-to-all-done.value = bf16[8,2,208,128]{3,2,1,0:T(8,128)(2,1)S(1)} async-done(((bf16[8,2,208,128]{3,2,1,0:T(8,128)(2,1)}), bf16[8,2,208,128]{3,2,1,0:T(8,128)(2,1)S(1)}, u32[]{:S(2)}, u32[]{:S(2)}) %all-to-all-start) | async-done | bytes 852000 | tf_op jit(solution)/shard_map/all_to_all | solution.py:733
  65.8 0.9 copy-done
  66.7 1.5 collective-permute-start.2
  68.2 3.4 %forward_y_first.3.rest_0_.earlier.rest_2_ = bf16[64,2,32,128]{3,2,1,0:T(8,128)(2,1)} custom-call(bf16[8,2,208,128]{3,2,1,0:T(8,128)(2,1)} %collective-permute-done.lines, bf16[512,256]{1,0:T(8,128)(2,1)} %constant.291.clone.section), custom_call_target="tpu_custom_call" | custom-call | flops 4400000000 | tf_op jit(solution)/shard_map/forward_y_first/pallas_call | solution.py:269
  71.5 6.1 %forward_y.2.rest_0_.refs_0_ = bf16[32,208,128]{2,1,0:T(8,128)(2,1)} custom-call(bf16[8,2,208,128]{3,2,1,0:T(8,128)(2,1)} %order.2.lines, bf16[512,256]{1,0:T(8,128)(2,1)} %constant.291.clone.section, bf16[64,2,32,128]{3,2,1,0:T(8,128)(2,1)} %forward_y_first.2.after.earlier, bf16[32,208,256]{2,1,0:T(8,128)(2,1)} %constant.292.clone.last, ...), custom_call_target="tpu_custom_call" | custom-call | flops 6600000000 | tf_op jit(solution)/shard_map/forward_y/pallas_call | solution.py:315
  77.6 4.8 %all-to-all-start.2 = ((bf16[8,4,32,128]{3,2,1,0:T(8,128)(2,1)}), bf16[8,4,32,128]{3,2,1,0:T(8,128)(2,1)S(1)}, u32[]{:S(2)}, u32[]{:S(2)}) async-start(bf16[8,4,32,128]{3,2,1,0:T(8,128)(2,1)} %order.3), calls=%async_computation.2 | async-start | bytes 524288 | tf_op jit(solution)/shard_map/all_to_all | solution.py:733
  82.4 3.3 %collective-permute-done.2.lines = bf16[8,2,208,128]{3,2,1,0:T(8,128)(2,1)S(1)} collective-permute-done((bf16[8,2,208,128]{3,2,1,0:T(8,128)(2,1)}, bf16[8,2,208,128]{3,2,1,0:T(8,128)(2,1)S(1)}, u32[]{:S(2)}, u32[]{:S(2)}) %collective-permute-start.2) | collective-permute-done | bytes 852000 | tf_op jit(solution)/shard_map/ppermute | solution.py:739
  85.7 4.9 %all-to-all-done.2.rest_1_.refs_8_ = bf16[8,4,32,128]{3,2,1,0:T(8,128)(2,1)S(1)} async-done(((bf16[8,4,32,128]{3,2,1,0:T(8,128)(2,1)}), bf16[8,4,32,128]{3,2,1,0:T(8,128)(2,1)S(1)}, u32[]{:S(2)}, u32[]{:S(2)}) %all-to-all-start.2) | async-done | bytes 262176 | tf_op jit(solution)/shard_map/all_to_all | solution.py:733
  90.6 0.7 copy-done.2
  91.4 6.1 %forward_y.3.refs_7_.refs_0_ = bf16[32,208,128]{2,1,0:T(8,128)(2,1)} custom-call(bf16[8,2,208,128]{3,2,1,0:T(8,128)(2,1)} %copy-done.10, bf16[512,256]{1,0:T(8,128)(2,1)} %constant.291.clone.section, bf16[64,2,32,128]{3,2,1,0:T(8,128)(2,1)} %forward_y_first.3.rest_0_.earlier.rest_2_, bf16[32,208,256]{2,1,0:T(8,128)(2,1)} %constant.292.clone.last, ...), custom_call_target="tpu_custom_call" | custom-call | flops 6600000000 | tf_op jit(solution)/shard_map/forward_y/pallas_call | solution.py:315
  98.3 0.6 reshape.914.sel
  98.9 1.2 copy-done.9
  100.1 9.3 %inverse.2.refs_7_.refs_0_ = bf16[32,256,256]{2,1,0:T(8,128)(2,1)} custom-call(s32[12]{0:T(128)} %reshape.914.sel, bf16[32,208,128]{2,1,0:T(8,128)(2,1)} %forward_y.2.rest_0_.refs_0_, bf16[32,208,128]{2,1,0:T(8,128)(2,1)} %copy-done.9, f32[208,128]{1,0:T(8,128)} %constant.293.clone.refs_2_, f32[4,1,128]{2,1,0:T(1,128)} %multiply_convert_fusion.rest_2_.refs_3_, ...), custom_call_target="tpu_custom_call" | custom-call | flops 6600000000 | tf_op jit(solution)/shard_map/inverse/pallas_call | solution.py:423
  109.4 9.4 %inverse.3.refs_1_ = bf16[32,256,256]{2,1,0:T(8,128)(2,1)} custom-call(s32[12]{0:T(128)} %reshape.914.sel, bf16[32,208,128]{2,1,0:T(8,128)(2,1)} %forward_y.3.refs_7_.refs_0_, bf16[32,208,128]{2,1,0:T(8,128)(2,1)} %collective-permute-done.3.refs_1_, f32[208,128]{1,0:T(8,128)} %constant.293.clone.refs_2_, f32[4,1,128]{2,1,0:T(1,128)} %multiply_convert_fusion.rest_2_.refs_3_, ...), custom_call_target="tpu_custom_call" | custom-call | flops 6600000000 | tf_op jit(solution)/shard_map/inverse/pallas_call | solution.py:423
  118.9 7.5 %collect.3 = bf16[16,2,4,32,128]{4,3,2,1,0:T(8,128)(2,1)} custom-call(bf16[32,256,256]{2,1,0:T(8,128)(2,1)} %inverse.2.refs_7_.refs_0_, bf16[32,256,256]{2,1,0:T(8,128)(2,1)} %inverse.3.refs_1_, bf16[2,256,512]{2,1,0:T(8,128)(2,1)} %copy-done.1), custom_call_target="tpu_custom_call" | custom-call | flops 6600000000 | tf_op jit(solution)/shard_map/collect/pallas_call | solution.py:495
  126.4 0.2 collective-permute-start.4
  126.6 7.5 %collect.2 = bf16[16,2,4,32,128]{4,3,2,1,0:T(8,128)(2,1)} custom-call(bf16[32,256,256]{2,1,0:T(8,128)(2,1)} %inverse.2.refs_7_.refs_0_, bf16[32,256,256]{2,1,0:T(8,128)(2,1)} %inverse.3.refs_1_, bf16[2,256,512]{2,1,0:T(8,128)(2,1)} %copy-done.1), custom_call_target="tpu_custom_call" | custom-call | flops 6600000000 | tf_op jit(solution)/shard_map/collect/pallas_call | solution.py:495
  134.1 18.2 %collective-permute-done.4 = bf16[16,2,4,32,128]{4,3,2,1,0:T(8,128)(2,1)S(1)} collective-permute-done((bf16[16,2,4,32,128]{4,3,2,1,0:T(8,128)(2,1)}, bf16[16,2,4,32,128]{4,3,2,1,0:T(8,128)(2,1)S(1)}, u32[]{:S(2)}, u32[]{:S(2)}) %collective-permute-start.4) | collective-permute-done | bytes 1048608 | tf_op jit(solution)/shard_map/ppermute | solution.py:802
  152.2 2.6 %add_convert_fusion = bf16[16,2,4,32,128]{4,3,2,1,0:T(8,128)(2,1)} fusion(bf16[16,2,4,32,128]{4,3,2,1,0:T(8,128)(2,1)S(1)} %collective-permute-done.4, bf16[16,2,4,32,128]{4,3,2,1,0:T(8,128)(2,1)} %collect.2), kind=kLoop, calls=%fused_computation | loop fusion | flops 2097152 | bytes 3145728 | tf_op jit(solution)/shard_map/convert_element_type | solution.py:804
  154.8 3.7 %all-to-all-start.3 = ((bf16[16,2,4,32,128]{4,3,2,1,0:T(8,128)(2,1)}), bf16[16,2,4,32,128]{4,3,2,1,0:T(8,128)(2,1)S(1)}, u32[]{:S(2)}, u32[]{:S(2)}) async-start(bf16[16,2,4,32,128]{4,3,2,1,0:T(8,128)(2,1)} %add_convert_fusion), calls=%async_computation.3 | async-start | bytes 2097152 | tf_op jit(solution)/shard_map/all_to_all | solution.py:809
  158.7 0.2 dynamic-slice_reduce_fusion
  159.3 0.6 dynamic_slice.25.counts
  159.9 0.1 fusion.31
  160.0 0.6 pad_maximum_fusion.3.alpha
  160.6 0.3 fusion.14
  161.0 0.7 pad_maximum_fusion.2.refs_2_
  161.7 0.6 reduce_sum.25.refs_1_
  162.3 19.1 %all-to-all-done.3 = bf16[16,2,4,32,128]{4,3,2,1,0:T(8,128)(2,1)S(1)} async-done(((bf16[16,2,4,32,128]{4,3,2,1,0:T(8,128)(2,1)}), bf16[16,2,4,32,128]{4,3,2,1,0:T(8,128)(2,1)S(1)}, u32[]{:S(2)}, u32[]{:S(2)}) %all-to-all-start.3) | async-done | bytes 1048608 | tf_op jit(solution)/shard_map/all_to_all | solution.py:809
  181.4 0.9 reduce_sum.24.refs_0_
  182.3 4.0 %detect.1 = f32[1,256]{1,0:T(1,128)} custom-call(f32[2,4,12]{2,1,0:T(4,128)} %pad_maximum_fusion.3.alpha, s32[1]{0:T(128)} %dynamic_slice.25.counts, bf16[4,2,4,32,128]{4,3,2,1,0:T(8,128)(2,1)} %reduce_sum.24.refs_0_, bf16[4,32,128]{2,1,0:T(8,128)(2,1)} %reduce_sum.25.refs_1_, f32[4,2,32,128]{3,2,1,0:T(8,128)} %pad_maximum_fusion.2.refs_2_, ...), custom_call_target="tpu_custom_call" | custom-call | tf_op jit(solution)/shard_map/detect/pallas_call | solution.py:606
  186.3 0.7 slice_reduce_fusion
  187.0 0.1 reshape_squeeze.3
  187.1 0.6 copy.35
  (58 shorter events, 1.3 us)
Async XLA Ops:
  0.0 18.0 %copy-start.7 = (s32[32,4]{0,1:T(4,128)S(1)}, s32[32,4]{0,1:T(4,128)}, u32[]{:S(2)}) copy-start(s32[32,4]{0,1:T(4,128)} %param.23) | copy-start | bytes 1540
  0.0 18.2 %copy-start.5 = (s32[4,2]{0,1:T(2,128)S(1)}, s32[4,2]{0,1:T(2,128)}, u32[]{:S(2)}) copy-start(s32[4,2]{0,1:T(2,128)} %param.21) | copy-start | bytes 100
  10.7 28.9 %all-to-all-start.1 = ((bf16[8,2,208,128]{3,2,1,0:T(8,128)(2,1)}), bf16[8,2,208,128]{3,2,1,0:T(8,128)(2,1)S(1)}, u32[]{:S(2)}, u32[]{:S(2)}) async-start(bf16[8,2,208,128]{3,2,1,0:T(8,128)(2,1)} %forward_x.3), calls=%async_computation.1 | async-start | bytes 1703936 | tf_op jit(solution)/shard_map/all_to_all | solution.py:733
  39.6 8.7 %copy-start.4 = (bf16[8,2,208,128]{3,2,1,0:T(8,128)(2,1)}, bf16[8,2,208,128]{3,2,1,0:T(8,128)(2,1)S(1)}, u32[]{:S(2)}) copy-start(bf16[8,2,208,128]{3,2,1,0:T(8,128)(2,1)S(1)} %all-to-all-done.1.lines) | copy-start | bytes 2555908
  39.6 26.1 %all-to-all-start = ((bf16[8,2,208,128]{3,2,1,0:T(8,128)(2,1)}), bf16[8,2,208,128]{3,2,1,0:T(8,128)(2,1)S(1)}, u32[]{:S(2)}, u32[]{:S(2)}) async-start(bf16[8,2,208,128]{3,2,1,0:T(8,128)(2,1)} %forward_x.2), calls=%async_computation | async-start | bytes 1703936 | tf_op jit(solution)/shard_map/all_to_all | solution.py:733
  45.5 6.2 %copy-start.1 = (bf16[2,256,512]{2,1,0:T(8,128)(2,1)}, bf16[2,256,512]{2,1,0:T(8,128)(2,1)S(1)}, u32[]{:S(2)}) copy-start(bf16[2,256,512]{2,1,0:T(8,128)(2,1)S(1)} %constant_dynamic-update-slice_fusion.rest_1_.refs_2_) | copy-start | bytes 1572868
  46.9 21.3 %collective-permute-start = (bf16[8,2,208,128]{3,2,1,0:T(8,128)(2,1)S(1)}, bf16[8,2,208,128]{3,2,1,0:T(8,128)(2,1)}, u32[]{:S(2)}, u32[]{:S(2)}) collective-permute-start(bf16[8,2,208,128]{3,2,1,0:T(8,128)(2,1)S(1)} %all-to-all-done.1.lines), channel_id=1, source_target_pairs={{0,2},{1,3},{2,0},{3,1},{4,6},{5,7},{6,4},{7,5},{8,10},{9,11},{10,... | collective-permute-start | bytes 2555912 | tf_op jit(solution)/shard_map/ppermute | solution.py:739
  65.8 0.9 copy-start
  66.7 19.1 %collective-permute-start.2 = (bf16[8,2,208,128]{3,2,1,0:T(8,128)(2,1)}, bf16[8,2,208,128]{3,2,1,0:T(8,128)(2,1)S(1)}, u32[]{:S(2)}, u32[]{:S(2)}) collective-permute-start(bf16[8,2,208,128]{3,2,1,0:T(8,128)(2,1)} %order.2.lines), channel_id=1, source_target_pairs={{0,2},{1,3},{2,0},{3,1},{4,6},{5,7},{6,4},{7,5},{8,10},{9,11},{10,... | collective-permute-start | bytes 2555912 | tf_op jit(solution)/shard_map/ppermute | solution.py:739
  77.6 13.0 %all-to-all-start.2 = ((bf16[8,4,32,128]{3,2,1,0:T(8,128)(2,1)}), bf16[8,4,32,128]{3,2,1,0:T(8,128)(2,1)S(1)}, u32[]{:S(2)}, u32[]{:S(2)}) async-start(bf16[8,4,32,128]{3,2,1,0:T(8,128)(2,1)} %order.3), calls=%async_computation.2 | async-start | bytes 524288 | tf_op jit(solution)/shard_map/all_to_all | solution.py:733
  82.4 16.5 %collective-permute-start.1 = (bf16[32,208,128]{2,1,0:T(8,128)(2,1)}, bf16[32,208,128]{2,1,0:T(8,128)(2,1)S(1)}, u32[]{:S(2)}, u32[]{:S(2)}) collective-permute-start(bf16[32,208,128]{2,1,0:T(8,128)(2,1)} %forward_y.2.rest_0_.refs_0_), channel_id=1, source_target_pairs={{0,1},{1,0},{2,3},{3,2},{4,5},{5,4},{6,7},{7,6},{8,9},{9,8},{10,11... | collective-permute-start | bytes 5111816 | tf_op jit(solution)/shard_map/ppermute | solution.py:739
  85.7 4.9 %copy-start.10 = (bf16[8,2,208,128]{3,2,1,0:T(8,128)(2,1)}, bf16[8,2,208,128]{3,2,1,0:T(8,128)(2,1)S(1)}, u32[]{:S(2)}) copy-start(bf16[8,2,208,128]{3,2,1,0:T(8,128)(2,1)S(1)} %collective-permute-done.2.lines) | copy-start | bytes 2555908
  90.6 0.7 copy-start.2
  97.4 12.0 %collective-permute-start.3 = (bf16[32,208,128]{2,1,0:T(8,128)(2,1)}, bf16[32,208,128]{2,1,0:T(8,128)(2,1)}, u32[]{:S(2)}, u32[]{:S(2)}) collective-permute-start(bf16[32,208,128]{2,1,0:T(8,128)(2,1)} %forward_y.3.refs_7_.refs_0_), channel_id=1, source_target_pairs={{0,1},{1,0},{2,3},{3,2},{4,5},{5,4},{6,7},{7,6},{8,9},{9,8},{10,11... | collective-permute-start | bytes 5111816 | tf_op jit(solution)/shard_map/ppermute | solution.py:739
  98.9 1.2 copy-start.9
  126.4 25.8 %collective-permute-start.4 = (bf16[16,2,4,32,128]{4,3,2,1,0:T(8,128)(2,1)}, bf16[16,2,4,32,128]{4,3,2,1,0:T(8,128)(2,1)S(1)}, u32[]{:S(2)}, u32[]{:S(2)}) collective-permute-start(bf16[16,2,4,32,128]{4,3,2,1,0:T(8,128)(2,1)} %collect.3), channel_id=1, source_target_pairs={{0,4},{4,0},{8,12},{12,8},{16,20},{20,16},{24,28},{28,24},{1,5},{5... | collective-permute-start | bytes 3145736 | tf_op jit(solution)/shard_map/ppermute | solution.py:802
  134.0 24.9 %copy-start.6 = (s32[4,2]{0,1:T(2,128)S(1)}, s32[4,2]{0,1:T(2,128)}, u32[]{:S(2)}) copy-start(s32[4,2]{0,1:T(2,128)} %param.21) | copy-start | bytes 100
  134.0 25.2 %copy-start.11 = (s32[32]{0:T(128)S(1)}, s32[32]{0:T(128)}, u32[]{:S(2)}) copy-start(s32[32]{0:T(128)} %param.24) | copy-start | bytes 388
  134.0 25.8 %copy-start.8 = (f32[4]{0:T(128)S(1)}, f32[4]{0:T(128)}, u32[]{:S(2)}) copy-start(f32[4]{0:T(128)} %param.22) | copy-start | bytes 52
  134.0 27.6 %copy-start.3 = (bf16[8,4,32,128]{3,2,1,0:T(8,128)(2,1)S(1)}, bf16[8,4,32,128]{3,2,1,0:T(8,128)(2,1)}, u32[]{:S(2)}) copy-start(bf16[8,4,32,128]{3,2,1,0:T(8,128)(2,1)} %copy-done.2) | copy-start | bytes 786436
  154.8 26.6 %all-to-all-start.3 = ((bf16[16,2,4,32,128]{4,3,2,1,0:T(8,128)(2,1)}), bf16[16,2,4,32,128]{4,3,2,1,0:T(8,128)(2,1)S(1)}, u32[]{:S(2)}, u32[]{:S(2)}) async-start(bf16[16,2,4,32,128]{4,3,2,1,0:T(8,128)(2,1)} %add_convert_fusion), calls=%async_computation.3 | async-start | bytes 2097152 | tf_op jit(solution)/shard_map/all_to_all | solution.py:809

commit v7 on v6

--- a/solution.py
+++ b/solution.py
@@ -445,8 +445,9 @@
     )(sel, *specs, freq_y, square_x, table_y, *[table_x] * near, *after)
 
 
-def collect_kernel(*refs):
-    *sheets, weights, out, held = refs
+def collect_kernel(count, *refs):
+    sheets, weights = refs[:count], refs[count]
+    out, held = refs[-2:]
     devices, _, slots, lines, _ = out.shape
     each = sheets[0].shape[0]
     step = pl.program_id(0)
@@ -485,24 +486,27 @@
         lax.fori_loop(0, devices, device, 0, unroll=4)
 
 
-def collect(sheets, weights, devices, which):
+def collect(sheets, weights, devices, which, part, after):
     tiles = weights.shape[1] // 4
-    lines = HALF
+    lines = HALF // PARTS
     shape = (devices, 2, tiles // devices, lines, LANES)
     steps = 4
-    sheet_spec = pl.BlockSpec((lines // steps,) + sheets[0].shape[1:], lambda i: (i, 0, 0))
+    sheet_spec = pl.BlockSpec(
+        (lines // steps,) + sheets[0].shape[1:], lambda i: (part * steps + i, 0, 0)
+    )
     block = pl.BlockSpec(shape, lambda i: (0, 0, 0, 0, 0))
     return pl.pallas_call(
-        collect_kernel,
+        functools.partial(collect_kernel, len(sheets)),
         grid=(steps,),
-        in_specs=[sheet_spec] * len(sheets) + [pl.BlockSpec((1,) + weights.shape[1:], lambda i: (which, 0, 0))],
+        in_specs=[sheet_spec] * len(sheets) + [pl.BlockSpec((1,) + weights.shape[1:], lambda i: (which, 0, 0))]
+        + [pl.BlockSpec(memory_space=pl.ANY)] * len(after),
         out_specs=block,
         out_shape=jax.ShapeDtypeStruct(shape, BF),
         scratch_shapes=[pltpu.VMEM(((2 * tiles + 1) * (lines + 1), LANES), F32)],
         compiler_params=pltpu.CompilerParams(vmem_limit_bytes=VMEM),
-        cost_estimate=cost(6),
+        cost_estimate=cost(0.05),
         name="collect",
-    )(*sheets, weights)
+    )(*sheets, weights, *after)
 
 
 def crop_kernel(rows, cols, odd, mine, pot, after, out, held, sems):
@@ -780,15 +784,15 @@
             received[f].append(swap(lines, f * near) if f else lines)
         if part == 0:
             earlier = [forward_y_first(received[f][0], section_y) for f in range(far)]
+    crops = order(crops.reshape(field_count, own_slots, HALF, LANES), received[0][1:])
+    crops = trade(crops, "beam")
+
     waves = []
     ready = []
     token = []
     for f in range(far):
         spec = forward_y(received[f][1], section_y, earlier[f], last_y, token + earlier[1:])
         ready.append([spec] + [swap(spec, x) for x in range(1, near)])
-        if f == 0:
-            crops = order(crops.reshape(field_count, own_slots, HALF, LANES), [spec])
-            crops = trade(crops, "beam")
         token = [spec, crops]
     for f in range(far):
         waves.append(
@@ -798,24 +802,30 @@
         )
         token = waves[-1:]
     owners = field_count // 2 * hold_count
-    partial = collect(waves, weights, owners, 0)
-    partial = lax.ppermute(partial, "beam", [(i, i ^ 1) for i in range(field_count)])
-    tiles = collect(waves, weights, owners, 1)
-    tiles = (tiles.astype(F32) + partial.astype(F32)).astype(BF)
     groups = [
         [b * hold_count + h for b in range(g, field_count, 2) for h in range(hold_count)]
         for g in range(2)
     ]
-    tiles = lax.all_to_all(
-        tiles,
-        ("beam", "slab"),
-        split_axis=0,
-        concat_axis=0,
-        axis_index_groups=groups,
-        tiled=True,
-    )
-    tiles = tiles.reshape((field_count // 2, hold_count) + tiles.shape[1:]).astype(F32)
-    fields = [jnp.sum(tiles, axis=0).astype(BF)]
+    token = []
+    partial = []
+    for which in range(2):
+        for part in range(PARTS):
+            partial.append(collect(waves, weights, owners, which, part, token))
+            token = partial[-1:]
+    fields = []
+    for part in range(PARTS):
+        passed = lax.ppermute(partial[part], "beam", [(i, i ^ 1) for i in range(field_count)])
+        tiles = (partial[PARTS + part].astype(F32) + passed.astype(F32)).astype(BF)
+        tiles = lax.all_to_all(
+            tiles,
+            ("beam", "slab"),
+            split_axis=0,
+            concat_axis=0,
+            axis_index_groups=groups,
+            tiled=True,
+        )
+        tiles = tiles.reshape((field_count // 2, hold_count) + tiles.shape[1:]).astype(F32)
+        fields.append(jnp.sum(tiles, axis=0).astype(BF))
     crops = jnp.sum(crops.astype(F32), axis=0).astype(BF)
 
     own = lax.dynamic_index_in_dim(

time: 190 us -> 188 us (0.989)
  waiting for transfers between devices: 53.5 us -> 37.5 us
  starting transfers between devices: 23.8 us -> 33.6 us
  Pallas kernels: 85.2 us -> 90.1 us
    all_to_all x1 -> x2, waiting for transfers between devices: 19.1 us -> 11.5 us  [shards(): lax.all_to_all(tiles, ('beam', 'slab'), split_axis=0, concat_axis=0, axis...]
    all_to_all x1 -> x2, starting transfers between devices: 3.65 us -> 10.5 us  [shards(): lax.all_to_all(tiles, ('beam', 'slab'), split_axis=0, concat_axis=0, axis...]
    all_to_all x3, waiting for transfers between devices: 12.9 us -> 7.76 us  [trade(): return lax.all_to_all(value, axis, split_axis=0, concat_axis=0, tiled=True)]
    pallas_call x2 -> x4, Pallas kernels: 15 us -> 20 us  [collect(): pl.pallas_call(functools.partial(collect_kernel, len(sheets)), grid=(step...]
    ppermute x1 -> x2, waiting for transfers between devices: 18.2 us -> 13.7 us  [shards(): lax.ppermute(partial[part], 'beam', [(i, i ^ 1) for i in range(field_coun...]
    ppermute x1 -> x2, starting transfers between devices: 0.18 us -> 4.12 us  [shards(): lax.ppermute(partial[part], 'beam', [(i, i ^ 1) for i in range(field_coun...]
  transfers between devices with their start and end apart: 9 -> 11, of which waited for: 6 -> 6; matrix products, arithmetic and copies ran while one was open for 8% -> 10% of each run, Pallas kernels for 28% -> 30%
where the time goes in v7:
time: 188 us; the launch traced here: 187 us
  Pallas kernels  90.1 us (48%)
  waiting for transfers between devices  37.5 us (20%)
  starting transfers between devices  33.6 us (18%)
  other arithmetic  15.4 us (8%)
  local copies, waits for them, and re-layouts  8.75 us (5%)
    pallas_call x2, Pallas kernels, forward_x(): pl.pallas_call(forward_x_kernel, grid_spec=pltpu.PrefetchScalarGridSpec(n...  21.4 us
    pallas_call x4, Pallas kernels, collect(): pl.pallas_call(functools.partial(collect_kernel, len(sheets)), grid=(step...  20 us
    pallas_call x2, Pallas kernels, inverse(): pl.pallas_call(functools.partial(inverse_kernel, steps, which, near), gri...  18.8 us
    all_to_all x3, starting transfers between devices, trade(): return lax.all_to_all(value, axis, split_axis=0, concat_axis=0, tiled=True)  16 us
    ppermute x2, waiting for transfers between devices, shards(): lax.ppermute(partial[part], 'beam', [(i, i ^ 1) for i in range(field_coun...  13.7 us
    pallas_call x2, Pallas kernels, forward_y(): pl.pallas_call(forward_y_kernel, grid=(1 + steps,), in_specs=[pl.BlockSpe...  12.2 us
    all_to_all x2, waiting for transfers between devices, shards(): lax.all_to_all(tiles, ('beam', 'slab'), split_axis=0, concat_axis=0, axis...  11.5 us
    all_to_all x2, starting transfers between devices, shards(): lax.all_to_all(tiles, ('beam', 'slab'), split_axis=0, concat_axis=0, axis...  10.5 us
  transfers between devices with their start and end apart: 11, of which 6 were waited for; matrix products, arithmetic and copies ran while one was open for 10% of the time, Pallas kernels for 30%

profile of v7, /device:TPU:0, one launch (start us, length us, event | category | flops | bytes accessed | tf_op | source)
XLA Modules:
  0.0 187.1 jit_solution(4399597669235866115)
XLA Ops:
  0.0 10.7 %forward_x.3 = bf16[8,2,208,128]{3,2,1,0:T(8,128)(2,1)} custom-call(s32[1]{0:T(128)} %bitcast.3.sel, bf16[8,4,16,4096]{3,2,1,0:T(8,128)(2,1)} %bitcast.46, bf16[4,512,1024]{2,1,0:T(8,128)(2,1)} %constant.289.clone.section, bf16[4,8,208,256]{3,2,1,0:T(8,128)(2,1)} %constant.290.clone.last, bf16[128,128]{1,0:T(8,128)(2,1)} %constant.291.clone.perm), custom_call_target="tpu_custom_call" | custom-call | flops 9900000256 | tf_op jit(solution)/shard_map/forward_x/pallas_call | solution.py:197
  10.7 7.3 %all-to-all-start.1 = ((bf16[8,2,208,128]{3,2,1,0:T(8,128)(2,1)}), bf16[8,2,208,128]{3,2,1,0:T(8,128)(2,1)S(1)}, u32[]{:S(2)}, u32[]{:S(2)}) async-start(bf16[8,2,208,128]{3,2,1,0:T(8,128)(2,1)} %forward_x.3), calls=%async_computation.1 | async-start | bytes 1703936 | tf_op jit(solution)/shard_map/all_to_all | solution.py:737
  18.3 0.6 fusion.32
  19.5 0.6 broadcast_add_fusion
  20.2 0.1 copy.30
  20.4 0.6 compare_convert_fusion
  21.0 0.1 copy.33
  21.2 0.1 copy.31
  21.4 1.4 fusion.29
  23.0 1.2 negate_convert_fusion.1
  24.4 0.1 pad_maximum_fusion
  24.5 0.5 copy.32
  25.1 0.3 convert_element_type.121
  25.4 1.3 negate_convert_fusion
  26.7 0.1 maximum_bitcast_fusion.2
  26.8 0.1 pad_maximum_fusion.1
  26.9 0.6 and_select_fusion.7
  27.5 0.6 and_select_fusion.8
  28.1 10.7 %forward_x.2 = bf16[8,2,208,128]{3,2,1,0:T(8,128)(2,1)} custom-call(s32[1]{0:T(128)} %bitcast.3.sel, bf16[8,4,16,4096]{3,2,1,0:T(8,128)(2,1)} %bitcast.47, bf16[4,512,1024]{2,1,0:T(8,128)(2,1)} %constant.289.clone.section, bf16[4,8,208,256]{3,2,1,0:T(8,128)(2,1)} %constant.290.clone.last, bf16[128,128]{1,0:T(8,128)(2,1)} %constant.291.clone.perm), custom_call_target="tpu_custom_call" | custom-call | flops 9900000256 | tf_op jit(solution)/shard_map/forward_x/pallas_call | solution.py:197
  38.8 0.8 all-to-all-done.1.lines
  39.6 5.2 %all-to-all-start = ((bf16[8,2,208,128]{3,2,1,0:T(8,128)(2,1)}), bf16[8,2,208,128]{3,2,1,0:T(8,128)(2,1)S(1)}, u32[]{:S(2)}, u32[]{:S(2)}) async-start(bf16[8,2,208,128]{3,2,1,0:T(8,128)(2,1)} %forward_x.2), calls=%async_computation | async-start | bytes 1703936 | tf_op jit(solution)/shard_map/all_to_all | solution.py:737
  44.8 0.5 copy.34
  45.3 0.3 convert_element_type.123
  45.7 1.4 multiply_convert_fusion.rest_2_.refs_3_
  47.1 1.5 collective-permute-start
  48.6 3.3 %forward_y_first.2.after.earlier = bf16[64,2,32,128]{3,2,1,0:T(8,128)(2,1)} custom-call(bf16[8,2,208,128]{3,2,1,0:T(8,128)(2,1)} %copy-done.6, bf16[512,256]{1,0:T(8,128)(2,1)} %constant.292.clone.section), custom_call_target="tpu_custom_call" | custom-call | flops 4400000000 | tf_op jit(solution)/shard_map/forward_y_first/pallas_call | solution.py:269
  51.9 7.1 %crop.1.rest_0_ = bf16[32,32,128]{2,1,0:T(8,128)(2,1)} custom-call(s32[32]{0:T(128)} %get-tuple-element.46.rows, s32[32]{0:T(128)} %get-tuple-element.45.cols, s32[32]{0:T(128)} %get-tuple-element.10.odd, s32[32]{0:T(128)} %get-tuple-element.7.mine, bf16[512,4096]{1,0:T(8,128)(2,1)} %pot.1, bf16[64,2,32,128]{3,2,1,0:T(8,128)(2,1)} %forward_y_first.2.after.earlier), custom_call_target="tpu_custom_call" | custom-call | flops 7699999744 | tf_op jit(solution)/shard_map/crop/pallas_call | solution.py:544
  59.0 6.9 %all-to-all-done.value = bf16[8,2,208,128]{3,2,1,0:T(8,128)(2,1)S(1)} async-done(((bf16[8,2,208,128]{3,2,1,0:T(8,128)(2,1)}), bf16[8,2,208,128]{3,2,1,0:T(8,128)(2,1)S(1)}, u32[]{:S(2)}, u32[]{:S(2)}) %all-to-all-start) | async-done | bytes 852000 | tf_op jit(solution)/shard_map/all_to_all | solution.py:737
  65.9 0.9 copy-done.1
  66.9 1.5 collective-permute-start.2
  68.3 3.6 %all-to-all-start.2 = ((bf16[8,4,32,128]{3,2,1,0:T(8,128)(2,1)}), bf16[8,4,32,128]{3,2,1,0:T(8,128)(2,1)S(1)}, u32[]{:S(2)}, u32[]{:S(2)}) async-start(bf16[8,4,32,128]{3,2,1,0:T(8,128)(2,1)} %order.3), calls=%async_computation.2 | async-start | bytes 524288 | tf_op jit(solution)/shard_map/all_to_all | solution.py:737
  72.0 3.4 %forward_y_first.3.rest_0_.earlier.rest_2_ = bf16[64,2,32,128]{3,2,1,0:T(8,128)(2,1)} custom-call(bf16[8,2,208,128]{3,2,1,0:T(8,128)(2,1)} %collective-permute-done.lines, bf16[512,256]{1,0:T(8,128)(2,1)} %constant.292.clone.section), custom_call_target="tpu_custom_call" | custom-call | flops 4400000000 | tf_op jit(solution)/shard_map/forward_y_first/pallas_call | solution.py:269
  75.3 6.1 %forward_y.2.rest_0_.refs_0_ = bf16[32,208,128]{2,1,0:T(8,128)(2,1)} custom-call(bf16[8,2,208,128]{3,2,1,0:T(8,128)(2,1)} %order.2.lines.rest_0_, bf16[512,256]{1,0:T(8,128)(2,1)} %constant.292.clone.section, bf16[64,2,32,128]{3,2,1,0:T(8,128)(2,1)} %forward_y_first.2.after.earlier, bf16[32,208,256]{2,1,0:T(8,128)(2,1)} %constant.293.clone.last, ...), custom_call_target="tpu_custom_call" | custom-call | flops 6600000000 | tf_op jit(solution)/shard_map/forward_y/pallas_call | solution.py:315
  81.4 4.6 %collective-permute-done.2.lines = bf16[8,2,208,128]{3,2,1,0:T(8,128)(2,1)} collective-permute-done((bf16[8,2,208,128]{3,2,1,0:T(8,128)(2,1)}, bf16[8,2,208,128]{3,2,1,0:T(8,128)(2,1)}, u32[]{:S(2)}, u32[]{:S(2)}) %collective-permute-start.2) | collective-permute-done | bytes 852000 | tf_op jit(solution)/shard_map/ppermute | solution.py:743
  86.0 6.1 %forward_y.3.refs_7_.refs_0_ = bf16[32,208,128]{2,1,0:T(8,128)(2,1)} custom-call(bf16[8,2,208,128]{3,2,1,0:T(8,128)(2,1)} %collective-permute-done.2.lines, bf16[512,256]{1,0:T(8,128)(2,1)} %constant.292.clone.section, bf16[64,2,32,128]{3,2,1,0:T(8,128)(2,1)} %forward_y_first.3.rest_0_.earlier.rest_2_, bf16[32,208,256]{2,1,0:T(8,128)(2,1)} %constant.293.clone.last, ...), custom_call_target="tpu_custom_call" | custom-call | flops 6600000000 | tf_op jit(solution)/shard_map/forward_y/pallas_call | solution.py:315
  93.0 0.6 reshape.917.sel
  93.6 1.2 copy-done.11
  94.8 9.4 %inverse.2.refs_7_.refs_0_ = bf16[32,256,256]{2,1,0:T(8,128)(2,1)} custom-call(s32[12]{0:T(128)} %reshape.917.sel, bf16[32,208,128]{2,1,0:T(8,128)(2,1)} %forward_y.2.rest_0_.refs_0_, bf16[32,208,128]{2,1,0:T(8,128)(2,1)} %copy-done.11, f32[208,128]{1,0:T(8,128)} %constant.294.clone.refs_2_, f32[4,1,128]{2,1,0:T(1,128)} %multiply_convert_fusion.rest_2_.refs_3_, ...), custom_call_target="tpu_custom_call" | custom-call | flops 6600000000 | tf_op jit(solution)/shard_map/inverse/pallas_call | solution.py:423
  104.1 9.4 %inverse.3.refs_1_ = bf16[32,256,256]{2,1,0:T(8,128)(2,1)} custom-call(s32[12]{0:T(128)} %reshape.917.sel, bf16[32,208,128]{2,1,0:T(8,128)(2,1)} %forward_y.3.refs_7_.refs_0_, bf16[32,208,128]{2,1,0:T(8,128)(2,1)} %collective-permute-done.3.refs_1_, f32[208,128]{1,0:T(8,128)} %constant.294.clone.refs_2_, f32[4,1,128]{2,1,0:T(1,128)} %multiply_convert_fusion.rest_2_.refs_3_, ...), custom_call_target="tpu_custom_call" | custom-call | flops 6600000000 | tf_op jit(solution)/shard_map/inverse/pallas_call | solution.py:423
  113.6 5.0 %collect.4.refs_3_ = bf16[16,2,4,16,128]{4,3,2,1,0:T(8,128)(2,1)} custom-call(bf16[32,256,256]{2,1,0:T(8,128)(2,1)} %inverse.2.refs_7_.refs_0_, bf16[32,256,256]{2,1,0:T(8,128)(2,1)} %inverse.3.refs_1_, bf16[2,256,512]{2,1,0:T(8,128)(2,1)} %copy-done), custom_call_target="tpu_custom_call" | custom-call | flops 55000000 | tf_op jit(solution)/shard_map/collect/pallas_call | solution.py:498
  118.6 5.0 %collect.5.refs_3_ = bf16[16,2,4,16,128]{4,3,2,1,0:T(8,128)(2,1)} custom-call(bf16[32,256,256]{2,1,0:T(8,128)(2,1)} %inverse.2.refs_7_.refs_0_, bf16[32,256,256]{2,1,0:T(8,128)(2,1)} %inverse.3.refs_1_, bf16[2,256,512]{2,1,0:T(8,128)(2,1)} %copy-done, bf16[16,2,4,16,128]{4,3,2,1,0:T(8,128)(2,1)} %collect.4.refs_3_), custom_call_target="tpu_custom_call" | custom-call | flops 55000000 | tf_op jit(solution)/shard_map/collect/pallas_call | solution.py:498
  123.6 2.3 %collective-permute-start.5 = (bf16[16,2,4,16,128]{4,3,2,1,0:T(8,128)(2,1)}, bf16[16,2,4,16,128]{4,3,2,1,0:T(8,128)(2,1)S(1)}, u32[]{:S(2)}, u32[]{:S(2)}) collective-permute-start(bf16[16,2,4,16,128]{4,3,2,1,0:T(8,128)(2,1)} %collect.5.refs_3_), channel_id=1, source_target_pairs={{0,4},{4,0},{8,12},{12,8},{16,20},{20,16},{24,28},{28,24},{1,5},{5... | collective-permute-start | bytes 1572872 | tf_op jit(solution)/shard_map/ppermute | solution.py:817
  125.9 5.0 %collect.6.refs_3_ = bf16[16,2,4,16,128]{4,3,2,1,0:T(8,128)(2,1)} custom-call(bf16[32,256,256]{2,1,0:T(8,128)(2,1)} %inverse.2.refs_7_.refs_0_, bf16[32,256,256]{2,1,0:T(8,128)(2,1)} %inverse.3.refs_1_, bf16[2,256,512]{2,1,0:T(8,128)(2,1)} %copy-done, bf16[16,2,4,16,128]{4,3,2,1,0:T(8,128)(2,1)} %collect.5.refs_3_), custom_call_target="tpu_custom_call" | custom-call | flops 55000000 | tf_op jit(solution)/shard_map/collect/pallas_call | solution.py:498
  130.8 5.1 %collect.7 = bf16[16,2,4,16,128]{4,3,2,1,0:T(8,128)(2,1)} custom-call(bf16[32,256,256]{2,1,0:T(8,128)(2,1)} %inverse.2.refs_7_.refs_0_, bf16[32,256,256]{2,1,0:T(8,128)(2,1)} %inverse.3.refs_1_, bf16[2,256,512]{2,1,0:T(8,128)(2,1)} %copy-done, bf16[16,2,4,16,128]{4,3,2,1,0:T(8,128)(2,1)} %collect.6.refs_3_), custom_call_target="tpu_custom_call" | custom-call | flops 55000000 | tf_op jit(solution)/shard_map/collect/pallas_call | solution.py:498
  135.9 2.7 %collective-permute-done.5 = bf16[16,2,4,16,128]{4,3,2,1,0:T(8,128)(2,1)S(1)} collective-permute-done((bf16[16,2,4,16,128]{4,3,2,1,0:T(8,128)(2,1)}, bf16[16,2,4,16,128]{4,3,2,1,0:T(8,128)(2,1)S(1)}, u32[]{:S(2)}, u32[]{:S(2)}) %collective-permute-start.5) | collective-permute-done | bytes 524320 | tf_op jit(solution)/shard_map/ppermute | solution.py:817
  138.7 2.1 %add_convert_fusion = bf16[16,2,4,16,128]{4,3,2,1,0:T(8,128)(2,1)} fusion(bf16[16,2,4,16,128]{4,3,2,1,0:T(8,128)(2,1)S(1)} %collective-permute-done.5, bf16[16,2,4,16,128]{4,3,2,1,0:T(8,128)(2,1)} %collect.7), kind=kLoop, calls=%fused_computation | loop fusion | flops 1048576 | bytes 1572864 | tf_op jit(solution)/shard_map/convert_element_type | solution.py:818
  140.7 4.7 %all-to-all-start.4 = ((bf16[16,2,4,16,128]{4,3,2,1,0:T(8,128)(2,1)}), bf16[16,2,4,16,128]{4,3,2,1,0:T(8,128)(2,1)S(1)}, u32[]{:S(2)}, u32[]{:S(2)}) async-start(bf16[16,2,4,16,128]{4,3,2,1,0:T(8,128)(2,1)} %add_convert_fusion), calls=%async_computation.4 | async-start | bytes 1048576 | tf_op jit(solution)/shard_map/all_to_all | solution.py:819
  145.5 1.8 collective-permute-start.4
  147.5 0.2 dynamic-slice_reduce_fusion
  148.1 0.6 dynamic_slice.25.counts
  148.7 0.1 fusion.31
  148.8 11.0 %collective-permute-done.4 = bf16[16,2,4,16,128]{4,3,2,1,0:T(8,128)(2,1)S(1)} collective-permute-done((bf16[16,2,4,16,128]{4,3,2,1,0:T(8,128)(2,1)S(1)}, bf16[16,2,4,16,128]{4,3,2,1,0:T(8,128)(2,1)S(1)}, u32[]{:S(2)}, u32[]{:S(2)}) %collective-permute-start.4) | collective-permute-done | bytes 524320 | tf_op jit(solution)/shard_map/ppermute | solution.py:817
  159.8 1.0 add_convert_fusion.1
  160.8 5.8 %all-to-all-start.3 = ((bf16[16,2,4,16,128]{4,3,2,1,0:T(8,128)(2,1)}), bf16[16,2,4,16,128]{4,3,2,1,0:T(8,128)(2,1)S(1)}, u32[]{:S(2)}, u32[]{:S(2)}) async-start(bf16[16,2,4,16,128]{4,3,2,1,0:T(8,128)(2,1)} %add_convert_fusion.1), calls=%async_computation.3 | async-start | bytes 1048576 | tf_op jit(solution)/shard_map/all_to_all | solution.py:819
  166.6 0.6 pad_maximum_fusion.3.alpha
  167.2 0.3 fusion.14
  167.6 0.7 pad_maximum_fusion.2.refs_3_
  168.2 0.6 reduce_sum.38.refs_2_
  168.9 0.7 reduce_sum.37.refs_1_
  169.6 11.5 %all-to-all-done.3 = bf16[16,2,4,16,128]{4,3,2,1,0:T(8,128)(2,1)S(1)} async-done(((bf16[16,2,4,16,128]{4,3,2,1,0:T(8,128)(2,1)}), bf16[16,2,4,16,128]{4,3,2,1,0:T(8,128)(2,1)S(1)}, u32[]{:S(2)}, u32[]{:S(2)}) %all-to-all-start.3) | async-done | bytes 524320 | tf_op jit(solution)/shard_map/all_to_all | solution.py:819
  181.0 0.7 reduce_sum.36.refs_0_
  181.8 4.0 %detect.1 = f32[1,256]{1,0:T(1,128)} custom-call(f32[2,4,12]{2,1,0:T(4,128)} %pad_maximum_fusion.3.alpha, s32[1]{0:T(128)} %dynamic_slice.25.counts, bf16[4,2,4,16,128]{4,3,2,1,0:T(8,128)(2,1)} %reduce_sum.36.refs_0_, bf16[4,2,4,16,128]{4,3,2,1,0:T(8,128)(2,1)} %reduce_sum.37.refs_1_, bf16[4,32,128]{2,1,0:T(8,128)(2,1)} %reduce_sum.38.refs_2_, ...), custom_call_target="tpu_custom_call" | custom-call | tf_op jit(solution)/shard_map/detect/pallas_call | solution.py:610
  185.8 0.6 slice_reduce_fusion
  186.5 0.6 copy.35
  (68 shorter events, 1.8 us)
Async XLA Ops:
  0.0 18.0 %copy-start.9 = (s32[32,4]{0,1:T(4,128)S(1)}, s32[32,4]{0,1:T(4,128)}, u32[]{:S(2)}) copy-start(s32[32,4]{0,1:T(4,128)} %param.23) | copy-start | bytes 1540
  0.0 18.2 %copy-start.7 = (s32[4,2]{0,1:T(2,128)S(1)}, s32[4,2]{0,1:T(2,128)}, u32[]{:S(2)}) copy-start(s32[4,2]{0,1:T(2,128)} %param.21) | copy-start | bytes 100
  10.7 28.9 %all-to-all-start.1 = ((bf16[8,2,208,128]{3,2,1,0:T(8,128)(2,1)}), bf16[8,2,208,128]{3,2,1,0:T(8,128)(2,1)S(1)}, u32[]{:S(2)}, u32[]{:S(2)}) async-start(bf16[8,2,208,128]{3,2,1,0:T(8,128)(2,1)} %forward_x.3), calls=%async_computation.1 | async-start | bytes 1703936 | tf_op jit(solution)/shard_map/all_to_all | solution.py:737
  39.6 9.0 %copy-start.6 = (bf16[8,2,208,128]{3,2,1,0:T(8,128)(2,1)}, bf16[8,2,208,128]{3,2,1,0:T(8,128)(2,1)S(1)}, u32[]{:S(2)}) copy-start(bf16[8,2,208,128]{3,2,1,0:T(8,128)(2,1)S(1)} %all-to-all-done.1.lines) | copy-start | bytes 2555908
  39.6 26.3 %all-to-all-start = ((bf16[8,2,208,128]{3,2,1,0:T(8,128)(2,1)}), bf16[8,2,208,128]{3,2,1,0:T(8,128)(2,1)S(1)}, u32[]{:S(2)}, u32[]{:S(2)}) async-start(bf16[8,2,208,128]{3,2,1,0:T(8,128)(2,1)} %forward_x.2), calls=%async_computation | async-start | bytes 1703936 | tf_op jit(solution)/shard_map/all_to_all | solution.py:737
  45.7 6.2 %copy-start = (bf16[2,256,512]{2,1,0:T(8,128)(2,1)}, bf16[2,256,512]{2,1,0:T(8,128)(2,1)S(1)}, u32[]{:S(2)}) copy-start(bf16[2,256,512]{2,1,0:T(8,128)(2,1)S(1)} %constant_dynamic-update-slice_fusion.rest_1_.refs_2_) | copy-start | bytes 1572868
  47.1 24.8 %collective-permute-start = (bf16[8,2,208,128]{3,2,1,0:T(8,128)(2,1)S(1)}, bf16[8,2,208,128]{3,2,1,0:T(8,128)(2,1)}, u32[]{:S(2)}, u32[]{:S(2)}) collective-permute-start(bf16[8,2,208,128]{3,2,1,0:T(8,128)(2,1)S(1)} %all-to-all-done.1.lines), channel_id=1, source_target_pairs={{0,2},{1,3},{2,0},{3,1},{4,6},{5,7},{6,4},{7,5},{8,10},{9,11},{10,... | collective-permute-start | bytes 2555912 | tf_op jit(solution)/shard_map/ppermute | solution.py:743
  65.9 0.9 copy-start.1
  66.9 19.2 %collective-permute-start.2 = (bf16[8,2,208,128]{3,2,1,0:T(8,128)(2,1)}, bf16[8,2,208,128]{3,2,1,0:T(8,128)(2,1)}, u32[]{:S(2)}, u32[]{:S(2)}) collective-permute-start(bf16[8,2,208,128]{3,2,1,0:T(8,128)(2,1)} %order.2.lines.rest_0_), channel_id=1, source_target_pairs={{0,2},{1,3},{2,0},{3,1},{4,6},{5,7},{6,4},{7,5},{8,10},{9,11},{10,... | collective-permute-start | bytes 2555912 | tf_op jit(solution)/shard_map/ppermute | solution.py:743
  68.3 13.1 %all-to-all-start.2 = ((bf16[8,4,32,128]{3,2,1,0:T(8,128)(2,1)}), bf16[8,4,32,128]{3,2,1,0:T(8,128)(2,1)S(1)}, u32[]{:S(2)}, u32[]{:S(2)}) async-start(bf16[8,4,32,128]{3,2,1,0:T(8,128)(2,1)} %order.3), calls=%async_computation.2 | async-start | bytes 524288 | tf_op jit(solution)/shard_map/all_to_all | solution.py:737
  81.4 12.2 %collective-permute-start.1 = (bf16[32,208,128]{2,1,0:T(8,128)(2,1)}, bf16[32,208,128]{2,1,0:T(8,128)(2,1)S(1)}, u32[]{:S(2)}, u32[]{:S(2)}) collective-permute-start(bf16[32,208,128]{2,1,0:T(8,128)(2,1)} %forward_y.2.rest_0_.refs_0_), channel_id=1, source_target_pairs={{0,1},{1,0},{2,3},{3,2},{4,5},{5,4},{6,7},{7,6},{8,9},{9,8},{10,11... | collective-permute-start | bytes 5111816 | tf_op jit(solution)/shard_map/ppermute | solution.py:743
  81.4 4.6 %copy-start.4 = (bf16[8,4,32,128]{3,2,1,0:T(8,128)(2,1)}, bf16[8,4,32,128]{3,2,1,0:T(8,128)(2,1)S(1)}, u32[]{:S(2)}) copy-start(bf16[8,4,32,128]{3,2,1,0:T(8,128)(2,1)S(1)} %all-to-all-done.2.rest_1_.refs_8_) | copy-start | bytes 786436
  92.1 12.0 %collective-permute-start.3 = (bf16[32,208,128]{2,1,0:T(8,128)(2,1)}, bf16[32,208,128]{2,1,0:T(8,128)(2,1)}, u32[]{:S(2)}, u32[]{:S(2)}) collective-permute-start(bf16[32,208,128]{2,1,0:T(8,128)(2,1)} %forward_y.3.refs_7_.refs_0_), channel_id=1, source_target_pairs={{0,1},{1,0},{2,3},{3,2},{4,5},{5,4},{6,7},{7,6},{8,9},{9,8},{10,11... | collective-permute-start | bytes 5111816 | tf_op jit(solution)/shard_map/ppermute | solution.py:743
  93.6 1.2 copy-start.11
  123.6 15.1 %collective-permute-start.5 = (bf16[16,2,4,16,128]{4,3,2,1,0:T(8,128)(2,1)}, bf16[16,2,4,16,128]{4,3,2,1,0:T(8,128)(2,1)S(1)}, u32[]{:S(2)}, u32[]{:S(2)}) collective-permute-start(bf16[16,2,4,16,128]{4,3,2,1,0:T(8,128)(2,1)} %collect.5.refs_3_), channel_id=1, source_target_pairs={{0,4},{4,0},{8,12},{12,8},{16,20},{20,16},{24,28},{28,24},{1,5},{5... | collective-permute-start | bytes 1572872 | tf_op jit(solution)/shard_map/ppermute | solution.py:817
  130.8 14.7 %copy-start.3 = (bf16[16,2,4,16,128]{4,3,2,1,0:T(8,128)(2,1)S(1)}, bf16[16,2,4,16,128]{4,3,2,1,0:T(8,128)(2,1)}, u32[]{:S(2)}) copy-start(bf16[16,2,4,16,128]{4,3,2,1,0:T(8,128)(2,1)} %collect.4.refs_3_) | copy-start | bytes 1572868
  130.8 16.9 %copy-start.8 = (s32[4,2]{0,1:T(2,128)S(1)}, s32[4,2]{0,1:T(2,128)}, u32[]{:S(2)}) copy-start(s32[4,2]{0,1:T(2,128)} %param.21) | copy-start | bytes 100
  130.8 17.3 %copy-start.12 = (s32[32]{0:T(128)S(1)}, s32[32]{0:T(128)}, u32[]{:S(2)}) copy-start(s32[32]{0:T(128)} %param.24) | copy-start | bytes 388
  130.8 17.8 %copy-start.10 = (f32[4]{0:T(128)S(1)}, f32[4]{0:T(128)}, u32[]{:S(2)}) copy-start(f32[4]{0:T(128)} %param.22) | copy-start | bytes 52
  130.8 29.0 %copy-start.2 = (bf16[16,2,4,16,128]{4,3,2,1,0:T(8,128)(2,1)S(1)}, bf16[16,2,4,16,128]{4,3,2,1,0:T(8,128)(2,1)}, u32[]{:S(2)}) copy-start(bf16[16,2,4,16,128]{4,3,2,1,0:T(8,128)(2,1)} %collect.6.refs_3_) | copy-start | bytes 1572868
  135.9 32.3 %copy-start.5 = (bf16[8,4,32,128]{3,2,1,0:T(8,128)(2,1)S(1)}, bf16[8,4,32,128]{3,2,1,0:T(8,128)(2,1)}, u32[]{:S(2)}) copy-start(bf16[8,4,32,128]{3,2,1,0:T(8,128)(2,1)} %copy-done.4) | copy-start | bytes 786436
  140.7 20.1 %all-to-all-start.4 = ((bf16[16,2,4,16,128]{4,3,2,1,0:T(8,128)(2,1)}), bf16[16,2,4,16,128]{4,3,2,1,0:T(8,128)(2,1)S(1)}, u32[]{:S(2)}, u32[]{:S(2)}) async-start(bf16[16,2,4,16,128]{4,3,2,1,0:T(8,128)(2,1)} %add_convert_fusion), calls=%async_computation.4 | async-start | bytes 1048576 | tf_op jit(solution)/shard_map/all_to_all | solution.py:819
  145.5 14.3 %collective-permute-start.4 = (bf16[16,2,4,16,128]{4,3,2,1,0:T(8,128)(2,1)S(1)}, bf16[16,2,4,16,128]{4,3,2,1,0:T(8,128)(2,1)S(1)}, u32[]{:S(2)}, u32[]{:S(2)}) collective-permute-start(bf16[16,2,4,16,128]{4,3,2,1,0:T(8,128)(2,1)S(1)} %copy-done.3), channel_id=1, source_target_pairs={{0,4},{4,0},{8,12},{12,8},{16,20},{20,16},{24,28},{28,24},{1,5},{5... | collective-permute-start | bytes 1572872 | tf_op jit(solution)/shard_map/ppermute | solution.py:817
  160.8 20.2 %all-to-all-start.3 = ((bf16[16,2,4,16,128]{4,3,2,1,0:T(8,128)(2,1)}), bf16[16,2,4,16,128]{4,3,2,1,0:T(8,128)(2,1)S(1)}, u32[]{:S(2)}, u32[]{:S(2)}) async-start(bf16[16,2,4,16,128]{4,3,2,1,0:T(8,128)(2,1)} %add_convert_fusion.1), calls=%async_computation.3 | async-start | bytes 1048576 | tf_op jit(solution)/shard_map/all_to_all | solution.py:819

commit v8 on v7

--- a/solution.py
+++ b/solution.py
@@ -490,7 +490,7 @@
     tiles = weights.shape[1] // 4
     lines = HALF // PARTS
     shape = (devices, 2, tiles // devices, lines, LANES)
-    steps = 4
+    steps = 2
     sheet_spec = pl.BlockSpec(
         (lines // steps,) + sheets[0].shape[1:], lambda i: (part * steps + i, 0, 0)
     )
@@ -750,9 +750,10 @@
     beam_row = lax.dynamic_index_in_dim(beam_index, hold_pos, 0, keepdims=False)
     pair_ids = share ^ jnp.arange(sheets, dtype=jnp.int32)
     k1_pairs = field_pos * width_k + 2 * pair_ids
-    parity = field_pos % 2
-    sets = table.reshape(field_count // 2, 2, hold_count, own_slots)
-    sets = [lax.dynamic_index_in_dim(sets, pos, 1, keepdims=False) for pos in (1 - parity, parity)]
+    near_bit, far_bit = (jnp.stack([1 - v, v]) for v in (field_pos % 2, field_pos // 2 % 2))
+    corners = table.reshape(field_count // 4, 2, 2, hold_count, own_slots)
+    corners = corners.transpose(2, 1, 0, 3, 4)[near_bit][:, far_bit]
+    sets = [corners[0], corners[1], corners[:, 0], corners[:, 1]]
     weights = jnp.stack([tile_weights(t.reshape(-1), beam_row, k1_pairs) for t in sets])
     row = np.arange(ROWS)
     base = row // PART + A * (K2_LOW + row % PART % K2_COUNT)
@@ -802,30 +803,39 @@
         )
         token = waves[-1:]
     owners = field_count // 2 * hold_count
-    groups = [
-        [b * hold_count + h for b in range(g, field_count, 2) for h in range(hold_count)]
-        for g in range(2)
-    ]
     token = []
     partial = []
     for which in range(2):
         for part in range(PARTS):
-            partial.append(collect(waves, weights, owners, which, part, token))
+            index = 2 * part + which
+            partial.append(collect(waves, weights, owners, index, part, token))
             token = partial[-1:]
-    fields = []
+
+    def hop(value, bit):
+        pairs = [(i, i ^ (1 << bit)) for i in range(field_count)]
+        return lax.ppermute(value, "beam", pairs).astype(F32)
+
+    totals = []
+    arrived = [hop(partial[part], part) for part in range(PARTS)]
     for part in range(PARTS):
-        passed = lax.ppermute(partial[part], "beam", [(i, i ^ 1) for i in range(field_count)])
-        tiles = (partial[PARTS + part].astype(F32) + passed.astype(F32)).astype(BF)
-        tiles = lax.all_to_all(
-            tiles,
-            ("beam", "slab"),
-            split_axis=0,
-            concat_axis=0,
-            axis_index_groups=groups,
-            tiled=True,
-        )
-        tiles = tiles.reshape((field_count // 2, hold_count) + tiles.shape[1:]).astype(F32)
-        fields.append(jnp.sum(tiles, axis=0).astype(BF))
+        own = partial[PARTS + part].astype(F32) + arrived[part]
+        rest = own[: owners // 2].astype(BF)
+        totals.append(own[owners // 2 :] + hop(rest, 1 - part))
+    tiles = jnp.concatenate(totals, axis=3).astype(BF)
+    groups = [
+        [b * hold_count + h for b in range(g, field_count, 4) for h in range(hold_count)]
+        for g in range(4)
+    ]
+    tiles = lax.all_to_all(
+        tiles,
+        ("beam", "slab"),
+        split_axis=0,
+        concat_axis=0,
+        axis_index_groups=groups,
+        tiled=True,
+    )
+    tiles = tiles.reshape((field_count // 4, hold_count) + tiles.shape[1:]).astype(F32)
+    fields = [jnp.sum(tiles, axis=0).astype(BF)]
     crops = jnp.sum(crops.astype(F32), axis=0).astype(BF)
 
     own = lax.dynamic_index_in_dim(

time: 188 us -> 187 us (level)
  other arithmetic: 15.4 us -> 22 us
  waiting for transfers between devices: 37.5 us -> 32.2 us
  starting transfers between devices: 33.6 us -> 28.7 us
  local copies, waits for them, and re-layouts: 8.75 us -> 12.8 us
    all_to_all x2 -> x1, starting transfers between devices: 10.5 us -> 3.49 us  [shards(): lax.all_to_all(tiles, ('beam', 'slab'), split_axis=0, concat_axis=0, axis...]
    ppermute x2 -> x4, waiting for transfers between devices: 13.7 us -> 9.03 us  [hop(): return lax.ppermute(value, 'beam', pairs).astype(F32)]
    sub x1 -> x4, other arithmetic: 1.35 us -> 5.12 us  [tile_weights(): ty = tile_ids // across - beam_row[0]]
    convert_element_type x2 -> x0, other arithmetic: 3.08 us -> none  [shards(): tiles = (partial[PARTS + part].astype(F32) + passed.astype(F32)).astype(BF)]
    another operation x2 -> x6, other arithmetic: 2.51 us -> 5.16 us
    ppermute x2 -> x4, starting transfers between devices: 4.12 us -> 5.5 us  [hop(): return lax.ppermute(value, 'beam', pairs).astype(F32)]
    all_to_all x2 -> x1, waiting for transfers between devices: 11.5 us -> 12.4 us  [shards(): lax.all_to_all(tiles, ('beam', 'slab'), split_axis=0, concat_axis=0, axis...]
  transfers between devices with their start and end apart: 11 -> 12, of which waited for: 6 -> 6; matrix products, arithmetic and copies ran while one was open for 10% -> 15% of each run, Pallas kernels for 30% -> 30%
where the time goes in v8:
time: 187 us; the launch traced here: 186 us
  Pallas kernels  88.5 us (47%)
  waiting for transfers between devices  32.2 us (17%)
  starting transfers between devices  28.7 us (15%)
  other arithmetic  22 us (12%)
  local copies, waits for them, and re-layouts  12.8 us (7%)
    pallas_call x2, Pallas kernels, forward_x(): pl.pallas_call(forward_x_kernel, grid_spec=pltpu.PrefetchScalarGridSpec(n...  21.3 us
    pallas_call x2, Pallas kernels, inverse(): pl.pallas_call(functools.partial(inverse_kernel, steps, which, near), gri...  18.8 us
    pallas_call x4, Pallas kernels, collect(): pl.pallas_call(functools.partial(collect_kernel, len(sheets)), grid=(step...  18.3 us
    all_to_all x3, starting transfers between devices, trade(): return lax.all_to_all(value, axis, split_axis=0, concat_axis=0, tiled=True)  16.7 us
    all_to_all x1, waiting for transfers between devices, shards(): lax.all_to_all(tiles, ('beam', 'slab'), split_axis=0, concat_axis=0, axis...  12.4 us
    pallas_call x2, Pallas kernels, forward_y(): pl.pallas_call(forward_y_kernel, grid=(1 + steps,), in_specs=[pl.BlockSpe...  12.2 us
    ppermute x4, waiting for transfers between devices, hop(): return lax.ppermute(value, 'beam', pairs).astype(F32)  9.03 us
    pallas_call x1, Pallas kernels, crop(): pl.pallas_call(crop_kernel, in_specs=[pl.BlockSpec(memory_space=pltpu.SME...  7.1 us
  transfers between devices with their start and end apart: 12, of which 6 were waited for; matrix products, arithmetic and copies ran while one was open for 15% of the time, Pallas kernels for 30%

profile of v8, /device:TPU:0, one launch (start us, length us, event | category | flops | bytes accessed | tf_op | source)
XLA Modules:
  0.0 186.0 jit_solution(12577446964868367331)
XLA Ops:
  0.0 10.7 %forward_x.3 = bf16[8,2,208,128]{3,2,1,0:T(8,128)(2,1)} custom-call(s32[1]{0:T(128)} %bitcast.3.sel, bf16[8,4,16,4096]{3,2,1,0:T(8,128)(2,1)} %bitcast.69, bf16[4,512,1024]{2,1,0:T(8,128)(2,1)} %constant.330.clone.section, bf16[4,8,208,256]{3,2,1,0:T(8,128)(2,1)} %constant.331.clone.last, bf16[128,128]{1,0:T(8,128)(2,1)} %constant.332.clone.perm), custom_call_target="tpu_custom_call" | custom-call | flops 9900000256 | tf_op jit(solution)/shard_map/forward_x/pallas_call | solution.py:197
  10.7 7.3 %all-to-all-start.1 = ((bf16[8,2,208,128]{3,2,1,0:T(8,128)(2,1)}), bf16[8,2,208,128]{3,2,1,0:T(8,128)(2,1)S(1)}, u32[]{:S(2)}, u32[]{:S(2)}) async-start(bf16[8,2,208,128]{3,2,1,0:T(8,128)(2,1)} %forward_x.3), calls=%async_computation.1 | async-start | bytes 1703936 | tf_op jit(solution)/shard_map/all_to_all | solution.py:737
  18.4 0.6 gather_fusion
  19.0 0.6 gather_fusion.1
  19.7 0.5 fusion.52
  20.8 0.6 broadcast_add_fusion
  21.7 0.6 compare_convert_fusion
  22.7 1.3 fusion.45
  24.0 1.3 fusion.47
  25.2 1.3 fusion.48
  26.5 1.3 fusion.46
  28.2 1.2 negate_convert_fusion.3
  29.7 0.5 copy.33
  30.6 1.3 negate_convert_fusion.1
  32.1 0.5 copy.35
  32.9 1.3 negate_convert_fusion.2
  34.4 0.5 copy.34
  35.3 1.3 negate_convert_fusion
  36.9 1.1 and_select_fusion.11
  38.0 1.1 and_select_fusion.12
  39.1 10.7 %forward_x.2 = bf16[8,2,208,128]{3,2,1,0:T(8,128)(2,1)} custom-call(s32[1]{0:T(128)} %bitcast.3.sel, bf16[8,4,16,4096]{3,2,1,0:T(8,128)(2,1)} %bitcast.70, bf16[4,512,1024]{2,1,0:T(8,128)(2,1)} %constant.330.clone.section, bf16[4,8,208,256]{3,2,1,0:T(8,128)(2,1)} %constant.331.clone.last, bf16[128,128]{1,0:T(8,128)(2,1)} %constant.332.clone.perm), custom_call_target="tpu_custom_call" | custom-call | flops 9900000256 | tf_op jit(solution)/shard_map/forward_x/pallas_call | solution.py:197
  49.8 6.0 %all-to-all-start = ((bf16[8,2,208,128]{3,2,1,0:T(8,128)(2,1)}), bf16[8,2,208,128]{3,2,1,0:T(8,128)(2,1)S(1)}, u32[]{:S(2)}, u32[]{:S(2)}) async-start(bf16[8,2,208,128]{3,2,1,0:T(8,128)(2,1)} %forward_x.2), calls=%async_computation | async-start | bytes 1703936 | tf_op jit(solution)/shard_map/all_to_all | solution.py:737
  55.8 0.5 copy.36
  56.8 1.4 multiply_convert_fusion.rest_2_.refs_3_
  58.1 1.5 collective-permute-start
  59.6 3.3 %forward_y_first.2.after.earlier = bf16[64,2,32,128]{3,2,1,0:T(8,128)(2,1)} custom-call(bf16[8,2,208,128]{3,2,1,0:T(8,128)(2,1)} %copy-done.6, bf16[512,256]{1,0:T(8,128)(2,1)} %constant.333.clone.section), custom_call_target="tpu_custom_call" | custom-call | flops 4400000000 | tf_op jit(solution)/shard_map/forward_y_first/pallas_call | solution.py:269
  63.0 7.1 %crop.1.rest_0_ = bf16[32,32,128]{2,1,0:T(8,128)(2,1)} custom-call(s32[32]{0:T(128)} %get-tuple-element.64.rows, s32[32]{0:T(128)} %get-tuple-element.63.cols, s32[32]{0:T(128)} %get-tuple-element.10.odd, s32[32]{0:T(128)} %get-tuple-element.7.mine, bf16[512,4096]{1,0:T(8,128)(2,1)} %pot.1, bf16[64,2,32,128]{3,2,1,0:T(8,128)(2,1)} %forward_y_first.2.after.earlier), custom_call_target="tpu_custom_call" | custom-call | flops 7699999744 | tf_op jit(solution)/shard_map/crop/pallas_call | solution.py:544
  70.1 6.9 %all-to-all-done.value = bf16[8,2,208,128]{3,2,1,0:T(8,128)(2,1)S(1)} async-done(((bf16[8,2,208,128]{3,2,1,0:T(8,128)(2,1)}), bf16[8,2,208,128]{3,2,1,0:T(8,128)(2,1)S(1)}, u32[]{:S(2)}, u32[]{:S(2)}) %all-to-all-start) | async-done | bytes 852000 | tf_op jit(solution)/shard_map/all_to_all | solution.py:737
  77.0 0.9 copy-done.1
  77.9 1.5 collective-permute-start.2
  79.4 3.4 %all-to-all-start.2 = ((bf16[8,4,32,128]{3,2,1,0:T(8,128)(2,1)}), bf16[8,4,32,128]{3,2,1,0:T(8,128)(2,1)S(1)}, u32[]{:S(2)}, u32[]{:S(2)}) async-start(bf16[8,4,32,128]{3,2,1,0:T(8,128)(2,1)} %order.3), calls=%async_computation.2 | async-start | bytes 524288 | tf_op jit(solution)/shard_map/all_to_all | solution.py:737
  82.8 0.9 copy-done.12
  83.7 3.3 %forward_y_first.3.rest_0_.earlier.rest_2_ = bf16[64,2,32,128]{3,2,1,0:T(8,128)(2,1)} custom-call(bf16[8,2,208,128]{3,2,1,0:T(8,128)(2,1)} %copy-done.12, bf16[512,256]{1,0:T(8,128)(2,1)} %constant.333.clone.section), custom_call_target="tpu_custom_call" | custom-call | flops 4400000000 | tf_op jit(solution)/shard_map/forward_y_first/pallas_call | solution.py:269
  87.1 6.1 %forward_y.2.rest_0_.refs_0_ = bf16[32,208,128]{2,1,0:T(8,128)(2,1)} custom-call(bf16[8,2,208,128]{3,2,1,0:T(8,128)(2,1)} %order.2.lines.rest_0_, bf16[512,256]{1,0:T(8,128)(2,1)} %constant.333.clone.section, bf16[64,2,32,128]{3,2,1,0:T(8,128)(2,1)} %forward_y_first.2.after.earlier, bf16[32,208,256]{2,1,0:T(8,128)(2,1)} %constant.334.clone.last, ...), custom_call_target="tpu_custom_call" | custom-call | flops 6600000000 | tf_op jit(solution)/shard_map/forward_y/pallas_call | solution.py:315
  93.2 3.9 %collective-permute-done.2.lines = bf16[8,2,208,128]{3,2,1,0:T(8,128)(2,1)} collective-permute-done((bf16[8,2,208,128]{3,2,1,0:T(8,128)(2,1)}, bf16[8,2,208,128]{3,2,1,0:T(8,128)(2,1)}, u32[]{:S(2)}, u32[]{:S(2)}) %collective-permute-start.2) | collective-permute-done | bytes 852000 | tf_op jit(solution)/shard_map/ppermute | solution.py:743
  97.1 6.1 %forward_y.3.refs_7_.refs_0_ = bf16[32,208,128]{2,1,0:T(8,128)(2,1)} custom-call(bf16[8,2,208,128]{3,2,1,0:T(8,128)(2,1)} %collective-permute-done.2.lines, bf16[512,256]{1,0:T(8,128)(2,1)} %constant.333.clone.section, bf16[64,2,32,128]{3,2,1,0:T(8,128)(2,1)} %forward_y_first.3.rest_0_.earlier.rest_2_, bf16[32,208,256]{2,1,0:T(8,128)(2,1)} %constant.334.clone.last, ...), custom_call_target="tpu_custom_call" | custom-call | flops 6600000000 | tf_op jit(solution)/shard_map/forward_y/pallas_call | solution.py:315
  104.0 0.6 reshape.1348.sel
  104.6 1.2 copy-done.11
  105.8 9.4 %inverse.2.refs_7_.refs_0_ = bf16[32,256,256]{2,1,0:T(8,128)(2,1)} custom-call(s32[12]{0:T(128)} %reshape.1348.sel, bf16[32,208,128]{2,1,0:T(8,128)(2,1)} %forward_y.2.rest_0_.refs_0_, bf16[32,208,128]{2,1,0:T(8,128)(2,1)} %copy-done.11, f32[208,128]{1,0:T(8,128)} %constant.335.clone.refs_2_, f32[4,1,128]{2,1,0:T(1,128)} %multiply_convert_fusion.rest_2_.refs_3_, ...), custom_call_target="tpu_custom_call" | custom-call | flops 6600000000 | tf_op jit(solution)/shard_map/inverse/pallas_call | solution.py:423
  115.2 9.4 %inverse.3.refs_1_ = bf16[32,256,256]{2,1,0:T(8,128)(2,1)} custom-call(s32[12]{0:T(128)} %reshape.1348.sel, bf16[32,208,128]{2,1,0:T(8,128)(2,1)} %forward_y.3.refs_7_.refs_0_, bf16[32,208,128]{2,1,0:T(8,128)(2,1)} %collective-permute-done.3.refs_1_, f32[208,128]{1,0:T(8,128)} %constant.335.clone.refs_2_, f32[4,1,128]{2,1,0:T(1,128)} %multiply_convert_fusion.rest_2_.refs_3_, ...), custom_call_target="tpu_custom_call" | custom-call | flops 6600000000 | tf_op jit(solution)/shard_map/inverse/pallas_call | solution.py:423
  124.6 4.5 %collect.4.refs_3_ = bf16[16,2,4,16,128]{4,3,2,1,0:T(8,128)(2,1)} custom-call(bf16[32,256,256]{2,1,0:T(8,128)(2,1)} %inverse.2.refs_7_.refs_0_, bf16[32,256,256]{2,1,0:T(8,128)(2,1)} %inverse.3.refs_1_, bf16[4,256,512]{2,1,0:T(8,128)(2,1)} %copy-done), custom_call_target="tpu_custom_call" | custom-call | flops 55000000 | tf_op jit(solution)/shard_map/collect/pallas_call | solution.py:498
  129.2 4.6 %collect.5.refs_3_ = bf16[16,2,4,16,128]{4,3,2,1,0:T(8,128)(2,1)} custom-call(bf16[32,256,256]{2,1,0:T(8,128)(2,1)} %inverse.2.refs_7_.refs_0_, bf16[32,256,256]{2,1,0:T(8,128)(2,1)} %inverse.3.refs_1_, bf16[4,256,512]{2,1,0:T(8,128)(2,1)} %copy-done, bf16[16,2,4,16,128]{4,3,2,1,0:T(8,128)(2,1)} %collect.4.refs_3_), custom_call_target="tpu_custom_call" | custom-call | flops 55000000 | tf_op jit(solution)/shard_map/collect/pallas_call | solution.py:498
  133.8 1.2 collective-permute-start.6
  135.0 1.5 collective-permute-start.4
  137.2 4.5 %collect.6.refs_3_ = bf16[16,2,4,16,128]{4,3,2,1,0:T(8,128)(2,1)} custom-call(bf16[32,256,256]{2,1,0:T(8,128)(2,1)} %inverse.2.refs_7_.refs_0_, bf16[32,256,256]{2,1,0:T(8,128)(2,1)} %inverse.3.refs_1_, bf16[4,256,512]{2,1,0:T(8,128)(2,1)} %copy-done, bf16[16,2,4,16,128]{4,3,2,1,0:T(8,128)(2,1)} %collect.5.refs_3_), custom_call_target="tpu_custom_call" | custom-call | flops 55000000 | tf_op jit(solution)/shard_map/collect/pallas_call | solution.py:498
  141.8 4.6 %collect.7 = bf16[16,2,4,16,128]{4,3,2,1,0:T(8,128)(2,1)} custom-call(bf16[32,256,256]{2,1,0:T(8,128)(2,1)} %inverse.2.refs_7_.refs_0_, bf16[32,256,256]{2,1,0:T(8,128)(2,1)} %inverse.3.refs_1_, bf16[4,256,512]{2,1,0:T(8,128)(2,1)} %copy-done, bf16[16,2,4,16,128]{4,3,2,1,0:T(8,128)(2,1)} %collect.6.refs_3_), custom_call_target="tpu_custom_call" | custom-call | flops 55000000 | tf_op jit(solution)/shard_map/collect/pallas_call | solution.py:498
  146.4 2.0 %collective-permute-done.6 = bf16[16,2,4,16,128]{4,3,2,1,0:T(8,128)(2,1)S(1)} collective-permute-done((bf16[16,2,4,16,128]{4,3,2,1,0:T(8,128)(2,1)}, bf16[16,2,4,16,128]{4,3,2,1,0:T(8,128)(2,1)S(1)}, u32[]{:S(2)}, u32[]{:S(2)}) %collective-permute-start.6) | collective-permute-done | bytes 524320 | tf_op jit(solution)/shard_map/ppermute | solution.py:816
  148.3 1.2 convert_add_fusion
  149.6 2.4 %collective-permute-start.7 = (bf16[8,2,4,16,128]{4,3,2,1,0:T(8,128)(2,1)S(1)}, bf16[8,2,4,16,128]{4,3,2,1,0:T(8,128)(2,1)S(1)}, u32[]{:S(2)}, u32[]{:S(2)}) collective-permute-start(bf16[8,2,4,16,128]{4,3,2,1,0:T(8,128)(2,1)S(1)} %slice.98), channel_id=1, source_target_pairs={{0,4},{4,0},{8,12},{12,8},{16,20},{20,16},{24,28},{28,24},{1,5},{5... | collective-permute-start | bytes 786440 | tf_op jit(solution)/shard_map/ppermute | solution.py:816
  152.2 0.5 collective-permute-start.5
  152.8 5.4 %collective-permute-done.7 = bf16[8,2,4,16,128]{4,3,2,1,0:T(8,128)(2,1)S(1)} collective-permute-done((bf16[8,2,4,16,128]{4,3,2,1,0:T(8,128)(2,1)S(1)}, bf16[8,2,4,16,128]{4,3,2,1,0:T(8,128)(2,1)S(1)}, u32[]{:S(2)}, u32[]{:S(2)}) %collective-permute-start.7) | collective-permute-done | bytes 262176 | tf_op jit(solution)/shard_map/ppermute | solution.py:816
  158.2 1.7 collective-permute-done.5
  160.0 0.8 pad_maximum_fusion.4
  160.8 3.5 %all-to-all-start.3 = ((bf16[8,2,4,32,128]{4,3,2,1,0:T(8,128)(2,1)}), bf16[8,2,4,32,128]{4,3,2,1,0:T(8,128)(2,1)S(1)}, u32[]{:S(2)}, u32[]{:S(2)}) async-start(bf16[8,2,4,32,128]{4,3,2,1,0:T(8,128)(2,1)} %pad_maximum_fusion.4), calls=%async_computation.3 | async-start | bytes 1048576 | tf_op jit(solution)/shard_map/all_to_all | solution.py:829
  164.4 0.6 dynamic_slice.18.counts
  165.0 0.6 pad_maximum_fusion.6.alpha
  165.6 0.3 fusion.26
  166.0 0.7 pad_maximum_fusion.5.refs_2_
  166.6 0.7 reduce_sum.25.refs_1_
  167.3 12.4 %all-to-all-done.3 = bf16[8,2,4,32,128]{4,3,2,1,0:T(8,128)(2,1)S(1)} async-done(((bf16[8,2,4,32,128]{4,3,2,1,0:T(8,128)(2,1)}), bf16[8,2,4,32,128]{4,3,2,1,0:T(8,128)(2,1)S(1)}, u32[]{:S(2)}, u32[]{:S(2)}) %all-to-all-start.3) | async-done | bytes 524320 | tf_op jit(solution)/shard_map/all_to_all | solution.py:829
  179.7 0.8 reduce_sum.24.refs_0_
  180.5 4.1 %detect.1 = f32[1,256]{1,0:T(1,128)} custom-call(f32[2,4,12]{2,1,0:T(4,128)} %pad_maximum_fusion.6.alpha, s32[1]{0:T(128)} %dynamic_slice.18.counts, bf16[4,2,4,32,128]{4,3,2,1,0:T(8,128)(2,1)} %reduce_sum.24.refs_0_, bf16[4,32,128]{2,1,0:T(8,128)(2,1)} %reduce_sum.25.refs_1_, f32[4,2,32,128]{3,2,1,0:T(8,128)} %pad_maximum_fusion.5.refs_2_, ...), custom_call_target="tpu_custom_call" | custom-call | tf_op jit(solution)/shard_map/detect/pallas_call | solution.py:610
  184.6 0.7 slice_reduce_fusion
  185.4 0.6 copy.37
  (100 shorter events, 5.4 us)
Async XLA Ops:
  0.0 18.0 %copy-start.9 = (s32[32,4]{0,1:T(4,128)S(1)}, s32[32,4]{0,1:T(4,128)}, u32[]{:S(2)}) copy-start(s32[32,4]{0,1:T(4,128)} %param.23) | copy-start | bytes 1540
  0.0 19.6 %copy-start.7 = (s32[4,2]{0,1:T(2,128)S(1)}, s32[4,2]{0,1:T(2,128)}, u32[]{:S(2)}) copy-start(s32[4,2]{0,1:T(2,128)} %param.21) | copy-start | bytes 100
  10.7 39.1 %all-to-all-start.1 = ((bf16[8,2,208,128]{3,2,1,0:T(8,128)(2,1)}), bf16[8,2,208,128]{3,2,1,0:T(8,128)(2,1)S(1)}, u32[]{:S(2)}, u32[]{:S(2)}) async-start(bf16[8,2,208,128]{3,2,1,0:T(8,128)(2,1)} %forward_x.3), calls=%async_computation.1 | async-start | bytes 1703936 | tf_op jit(solution)/shard_map/all_to_all | solution.py:737
  49.8 6.0 %copy-start.6 = (bf16[8,2,208,128]{3,2,1,0:T(8,128)(2,1)}, bf16[8,2,208,128]{3,2,1,0:T(8,128)(2,1)S(1)}, u32[]{:S(2)}) copy-start(bf16[8,2,208,128]{3,2,1,0:T(8,128)(2,1)S(1)} %all-to-all-done.1.lines) | copy-start | bytes 2555908
  49.8 27.2 %all-to-all-start = ((bf16[8,2,208,128]{3,2,1,0:T(8,128)(2,1)}), bf16[8,2,208,128]{3,2,1,0:T(8,128)(2,1)S(1)}, u32[]{:S(2)}, u32[]{:S(2)}) async-start(bf16[8,2,208,128]{3,2,1,0:T(8,128)(2,1)} %forward_x.2), calls=%async_computation | async-start | bytes 1703936 | tf_op jit(solution)/shard_map/all_to_all | solution.py:737
  56.7 6.2 %copy-start = (bf16[4,256,512]{2,1,0:T(8,128)(2,1)}, bf16[4,256,512]{2,1,0:T(8,128)(2,1)S(1)}, u32[]{:S(2)}) copy-start(bf16[4,256,512]{2,1,0:T(8,128)(2,1)S(1)} %constant_dynamic-update-slice_fusion.rest_1_.refs_2_) | copy-start | bytes 3145732
  58.1 24.7 %collective-permute-start = (bf16[8,2,208,128]{3,2,1,0:T(8,128)(2,1)}, bf16[8,2,208,128]{3,2,1,0:T(8,128)(2,1)S(1)}, u32[]{:S(2)}, u32[]{:S(2)}) collective-permute-start(bf16[8,2,208,128]{3,2,1,0:T(8,128)(2,1)} %copy-done.6), channel_id=1, source_target_pairs={{0,2},{1,3},{2,0},{3,1},{4,6},{5,7},{6,4},{7,5},{8,10},{9,11},{10,... | collective-permute-start | bytes 2555912 | tf_op jit(solution)/shard_map/ppermute | solution.py:743
  77.0 0.9 copy-start.1
  77.9 19.2 %collective-permute-start.2 = (bf16[8,2,208,128]{3,2,1,0:T(8,128)(2,1)}, bf16[8,2,208,128]{3,2,1,0:T(8,128)(2,1)}, u32[]{:S(2)}, u32[]{:S(2)}) collective-permute-start(bf16[8,2,208,128]{3,2,1,0:T(8,128)(2,1)} %order.2.lines.rest_0_), channel_id=1, source_target_pairs={{0,2},{1,3},{2,0},{3,1},{4,6},{5,7},{6,4},{7,5},{8,10},{9,11},{10,... | collective-permute-start | bytes 2555912 | tf_op jit(solution)/shard_map/ppermute | solution.py:743
  79.4 13.8 %all-to-all-start.2 = ((bf16[8,4,32,128]{3,2,1,0:T(8,128)(2,1)}), bf16[8,4,32,128]{3,2,1,0:T(8,128)(2,1)S(1)}, u32[]{:S(2)}, u32[]{:S(2)}) async-start(bf16[8,4,32,128]{3,2,1,0:T(8,128)(2,1)} %order.3), calls=%async_computation.2 | async-start | bytes 524288 | tf_op jit(solution)/shard_map/all_to_all | solution.py:737
  82.8 0.9 copy-start.12
  93.2 11.4 %collective-permute-start.1 = (bf16[32,208,128]{2,1,0:T(8,128)(2,1)}, bf16[32,208,128]{2,1,0:T(8,128)(2,1)S(1)}, u32[]{:S(2)}, u32[]{:S(2)}) collective-permute-start(bf16[32,208,128]{2,1,0:T(8,128)(2,1)} %forward_y.2.rest_0_.refs_0_), channel_id=1, source_target_pairs={{0,1},{1,0},{2,3},{3,2},{4,5},{5,4},{6,7},{7,6},{8,9},{9,8},{10,11... | collective-permute-start | bytes 5111816 | tf_op jit(solution)/shard_map/ppermute | solution.py:743
  93.2 3.9 %copy-start.4 = (bf16[8,4,32,128]{3,2,1,0:T(8,128)(2,1)}, bf16[8,4,32,128]{3,2,1,0:T(8,128)(2,1)S(1)}, u32[]{:S(2)}) copy-start(bf16[8,4,32,128]{3,2,1,0:T(8,128)(2,1)S(1)} %all-to-all-done.2.rest_1_.refs_8_) | copy-start | bytes 786436
  103.2 12.0 %collective-permute-start.3 = (bf16[32,208,128]{2,1,0:T(8,128)(2,1)}, bf16[32,208,128]{2,1,0:T(8,128)(2,1)}, u32[]{:S(2)}, u32[]{:S(2)}) collective-permute-start(bf16[32,208,128]{2,1,0:T(8,128)(2,1)} %forward_y.3.refs_7_.refs_0_), channel_id=1, source_target_pairs={{0,1},{1,0},{2,3},{3,2},{4,5},{5,4},{6,7},{7,6},{8,9},{9,8},{10,11... | collective-permute-start | bytes 5111816 | tf_op jit(solution)/shard_map/ppermute | solution.py:743
  104.6 1.2 copy-start.11
  129.2 5.8 %copy-start.3 = (bf16[16,2,4,16,128]{4,3,2,1,0:T(8,128)(2,1)S(1)}, bf16[16,2,4,16,128]{4,3,2,1,0:T(8,128)(2,1)}, u32[]{:S(2)}) copy-start(bf16[16,2,4,16,128]{4,3,2,1,0:T(8,128)(2,1)} %collect.4.refs_3_) | copy-start | bytes 1572868
  129.2 7.7 %copy-start.8 = (s32[4,2]{0,1:T(2,128)S(1)}, s32[4,2]{0,1:T(2,128)}, u32[]{:S(2)}) copy-start(s32[4,2]{0,1:T(2,128)} %param.21) | copy-start | bytes 100
  133.8 14.5 %collective-permute-start.6 = (bf16[16,2,4,16,128]{4,3,2,1,0:T(8,128)(2,1)}, bf16[16,2,4,16,128]{4,3,2,1,0:T(8,128)(2,1)S(1)}, u32[]{:S(2)}, u32[]{:S(2)}) collective-permute-start(bf16[16,2,4,16,128]{4,3,2,1,0:T(8,128)(2,1)} %collect.5.refs_3_), channel_id=1, source_target_pairs={{0,8},{4,12},{8,0},{12,4},{16,24},{20,28},{24,16},{28,20},{1,9},{5... | collective-permute-start | bytes 1572872 | tf_op jit(solution)/shard_map/ppermute | solution.py:816
  135.0 17.0 %collective-permute-start.4 = (bf16[16,2,4,16,128]{4,3,2,1,0:T(8,128)(2,1)S(1)}, bf16[16,2,4,16,128]{4,3,2,1,0:T(8,128)(2,1)S(1)}, u32[]{:S(2)}, u32[]{:S(2)}) collective-permute-start(bf16[16,2,4,16,128]{4,3,2,1,0:T(8,128)(2,1)S(1)} %copy-done.3), channel_id=1, source_target_pairs={{0,4},{4,0},{8,12},{12,8},{16,20},{20,16},{24,28},{28,24},{1,5},{5... | collective-permute-start | bytes 1572872 | tf_op jit(solution)/shard_map/ppermute | solution.py:816
  141.8 10.2 %copy-start.2 = (bf16[16,2,4,16,128]{4,3,2,1,0:T(8,128)(2,1)S(1)}, bf16[16,2,4,16,128]{4,3,2,1,0:T(8,128)(2,1)}, u32[]{:S(2)}) copy-start(bf16[16,2,4,16,128]{4,3,2,1,0:T(8,128)(2,1)} %collect.6.refs_3_) | copy-start | bytes 1572868
  146.4 6.3 %copy-start.10 = (f32[4]{0:T(128)S(1)}, f32[4]{0:T(128)}, u32[]{:S(2)}) copy-start(f32[4]{0:T(128)} %param.22) | copy-start | bytes 52
  149.6 14.8 %copy-start.13 = (s32[32]{0:T(128)S(1)}, s32[32]{0:T(128)}, u32[]{:S(2)}) copy-start(s32[32]{0:T(128)} %param.24) | copy-start | bytes 388
  149.6 17.0 %copy-start.5 = (bf16[8,4,32,128]{3,2,1,0:T(8,128)(2,1)S(1)}, bf16[8,4,32,128]{3,2,1,0:T(8,128)(2,1)}, u32[]{:S(2)}) copy-start(bf16[8,4,32,128]{3,2,1,0:T(8,128)(2,1)} %copy-done.4) | copy-start | bytes 786436
  149.6 8.6 %collective-permute-start.7 = (bf16[8,2,4,16,128]{4,3,2,1,0:T(8,128)(2,1)S(1)}, bf16[8,2,4,16,128]{4,3,2,1,0:T(8,128)(2,1)S(1)}, u32[]{:S(2)}, u32[]{:S(2)}) collective-permute-start(bf16[8,2,4,16,128]{4,3,2,1,0:T(8,128)(2,1)S(1)} %slice.98), channel_id=1, source_target_pairs={{0,4},{4,0},{8,12},{12,8},{16,20},{20,16},{24,28},{28,24},{1,5},{5... | collective-permute-start | bytes 786440 | tf_op jit(solution)/shard_map/ppermute | solution.py:816
  152.2 7.7 %collective-permute-start.5 = (bf16[8,2,4,16,128]{4,3,2,1,0:T(8,128)(2,1)S(1)}, bf16[8,2,4,16,128]{4,3,2,1,0:T(8,128)(2,1)S(1)}, u32[]{:S(2)}, u32[]{:S(2)}) collective-permute-start(bf16[8,2,4,16,128]{4,3,2,1,0:T(8,128)(2,1)S(1)} %slice.99), channel_id=1, source_target_pairs={{0,8},{4,12},{8,0},{12,4},{16,24},{20,28},{24,16},{28,20},{1,9},{5... | collective-permute-start | bytes 786440 | tf_op jit(solution)/shard_map/ppermute | solution.py:816
  160.8 18.8 %all-to-all-start.3 = ((bf16[8,2,4,32,128]{4,3,2,1,0:T(8,128)(2,1)}), bf16[8,2,4,32,128]{4,3,2,1,0:T(8,128)(2,1)S(1)}, u32[]{:S(2)}, u32[]{:S(2)}) async-start(bf16[8,2,4,32,128]{4,3,2,1,0:T(8,128)(2,1)} %pad_maximum_fusion.4), calls=%async_computation.3 | async-start | bytes 1048576 | tf_op jit(solution)/shard_map/all_to_all | solution.py:829

commit v9 on v8

--- a/solution.py
+++ b/solution.py
@@ -123,15 +123,19 @@
     return low(out.reshape(2 * LANES, 4 * A))
 
 
+def cosine(u):
+    q = F32(COS_FIT[-1])
+    for c in COS_FIT[-2::-1]:
+        q = q * u + F32(c)
+    return q
+
+
 def sine_cosine(x):
     u = x * x
     s = F32(SIN_FIT[-1])
     for c in SIN_FIT[-2::-1]:
         s = s * u + F32(c)
-    q = F32(COS_FIT[-1])
-    for c in COS_FIT[-2::-1]:
-        q = q * u + F32(c)
-    return s * x, q
+    return s * x, cosine(u)
 
 
 def fit(function, degree):
@@ -445,22 +449,38 @@
     )(sel, *specs, freq_y, square_x, table_y, *[table_x] * near, *after)
 
 
-def collect_kernel(count, *refs):
-    sheets, weights = refs[:count], refs[count]
-    out, held = refs[-2:]
-    devices, _, slots, lines, _ = out.shape
+def collect_kernel(count, k1_pairs, *refs):
+    sheets, places = refs[:count], refs[count]
+    outs = refs[-2 - PARTS : -2]
+    weights, held = refs[-2:]
+    devices, _, slots, lines, _ = outs[0].shape
     each = sheets[0].shape[0]
-    step = pl.program_id(0)
+    steps = lines // each
+    step = pl.program_id(0) % steps
+    part_id = pl.program_id(0) // steps
     tiles = devices * slots
     pitch = lines + 1
     lane = lax.broadcasted_iota(jnp.int32, (tiles, LANES), 1)
     lower = lane < A
 
+    @pl.when(step == 0)
+    def _():
+        quarter = A // 4
+        base = places[0, 0, 0] * (lane % A) + quarter * (lane // A)
+        for x in range(weights.shape[1] // LANES):
+            for ks in range(2):
+                winding = base + places[0, 0, 1] * (k1_pairs[x] + ks)
+                for part in range(2):
+                    angle = ((winding - quarter * part) & (A - 1)) - A // 2
+                    angle = angle.astype(F32) * F32(2.0 * math.pi / A)
+                    rows = slice((2 * part + ks) * tiles, (2 * part + ks + 1) * tiles)
+                    weights[rows, x * LANES : (x + 1) * LANES] = (-cosine(angle * angle)).astype(BF)
+
     def line(i, carry):
         stacked = sheets[0][i]
         if len(sheets) > 1:
             stacked = jnp.concatenate([sheet[i] for sheet in sheets], axis=0)
-        sums = dot(weights[0], stacked)
+        sums = dot(weights[...], stacked)
         for part in range(2):
             even = sums[2 * part * tiles : (2 * part + 1) * tiles]
             odd = sums[(2 * part + 1) * tiles : (2 * part + 2) * tiles]
@@ -473,40 +493,51 @@
 
     lax.fori_loop(0, each, line, 0, unroll=4)
 
-    def device(d, carry):
-        for part in range(2):
-            for slot in range(slots):
-                start = (part * tiles + d * slots + slot) * pitch
-                total = held[pl.ds(start, lines), :]
-                out[d, part, slot] = total.astype(BF)
-        return carry
-
-    @pl.when(step == lines // each - 1)
-    def _():
-        lax.fori_loop(0, devices, device, 0, unroll=4)
-
-
-def collect(sheets, weights, devices, which, part, after):
-    tiles = weights.shape[1] // 4
+    for p, out in enumerate(outs):
+
+        def device(d, carry, out=out):
+            for part in range(2):
+                for slot in range(slots):
+                    start = (part * tiles + d * slots + slot) * pitch
+                    out[d, part, slot] = held[pl.ds(start, lines), :].astype(BF)
+            return carry
+
+        @pl.when((step == steps - 1) & (part_id == p))
+        def _(device=device):
+            lax.fori_loop(0, devices, device, 0, unroll=4)
+
+
+def collect(sheets, k1_pairs, places, devices, which, after):
+    tiles = places.shape[3]
     lines = HALF // PARTS
+    steps = 2
     shape = (devices, 2, tiles // devices, lines, LANES)
-    steps = 2
-    sheet_spec = pl.BlockSpec(
-        (lines // steps,) + sheets[0].shape[1:], lambda i: (part * steps + i, 0, 0)
-    )
-    block = pl.BlockSpec(shape, lambda i: (0, 0, 0, 0, 0))
+    depth = sum(sheet.shape[1] for sheet in sheets)
+    sheet_spec = pl.BlockSpec((lines // steps,) + sheets[0].shape[1:], lambda i, s: (i, 0, 0))
+    block = pl.BlockSpec(shape, lambda i, s: (0, 0, 0, 0, 0))
     return pl.pallas_call(
         functools.partial(collect_kernel, len(sheets)),
-        grid=(steps,),
-        in_specs=[sheet_spec] * len(sheets) + [pl.BlockSpec((1,) + weights.shape[1:], lambda i: (which, 0, 0))]
-        + [pl.BlockSpec(memory_space=pl.ANY)] * len(after),
-        out_specs=block,
-        out_shape=jax.ShapeDtypeStruct(shape, BF),
-        scratch_shapes=[pltpu.VMEM(((2 * tiles + 1) * (lines + 1), LANES), F32)],
+        grid_spec=pltpu.PrefetchScalarGridSpec(
+            num_scalar_prefetch=1,
+            grid=(PARTS * steps,),
+            in_specs=[sheet_spec] * len(sheets)
+            + [
+                pl.BlockSpec(
+                    (1, 1) + places.shape[2:], lambda i, s: (which, i // steps, 0, 0, 0)
+                )
+            ]
+            + [pl.BlockSpec(memory_space=pl.ANY)] * len(after),
+            out_specs=[block] * PARTS,
+            scratch_shapes=[
+                pltpu.VMEM((4 * tiles, depth), BF),
+                pltpu.VMEM(((2 * tiles + 1) * (lines + 1), LANES), F32),
+            ],
+        ),
+        out_shape=[jax.ShapeDtypeStruct(shape, BF)] * PARTS,
         compiler_params=pltpu.CompilerParams(vmem_limit_bytes=VMEM),
         cost_estimate=cost(0.05),
         name="collect",
-    )(*sheets, weights, *after)
+    )(k1_pairs, *sheets, places, *after)
 
 
 def crop_kernel(rows, cols, odd, mine, pot, after, out, held, sems):
@@ -651,24 +682,6 @@
     return jnp.stack([jnp.cos(phases), -jnp.sin(phases)])
 
 
-def tile_weights(tile_ids, beam_row, k1_pairs):
-    across = N // A
-    ty = tile_ids // across - beam_row[0]
-    tx = tile_ids % across - beam_row[1]
-    k1y = jnp.arange(A, dtype=jnp.int32)
-    k1x = k1_pairs[:, None] + jnp.arange(2, dtype=jnp.int32)[None, :]
-    winding = (
-        k1y[None, None, None, :] * ty[None, :, None, None]
-        + (k1x.T[:, None, :] * tx[None, :, None])[..., None]
-    )
-    angle = 2.0 * math.pi / A * (winding % A).astype(F32)
-    cos, sin = jnp.cos(angle), jnp.sin(angle)
-    upper = jnp.stack([cos, -sin], axis=3)
-    under = jnp.stack([sin, cos], axis=3)
-    both = jnp.stack([upper, under]).astype(BF)
-    return both.reshape(4 * tile_ids.shape[0], k1_pairs.shape[0] * 2 * A)
-
-
 def plane_waves(beam_index):
     by = jnp.arange(HALF, dtype=jnp.int32)[:, None] + HALF * (jnp.arange(LANES) // A)[None, :]
     bx = jnp.broadcast_to((jnp.arange(LANES, dtype=jnp.int32) % A)[None, :], by.shape)
@@ -753,8 +766,10 @@
     near_bit, far_bit = (jnp.stack([1 - v, v]) for v in (field_pos % 2, field_pos // 2 % 2))
     corners = table.reshape(field_count // 4, 2, 2, hold_count, own_slots)
     corners = corners.transpose(2, 1, 0, 3, 4)[near_bit][:, far_bit]
-    sets = [corners[0], corners[1], corners[:, 0], corners[:, 1]]
-    weights = jnp.stack([tile_weights(t.reshape(-1), beam_row, k1_pairs) for t in sets])
+    sets = jnp.stack([corners, corners.transpose(1, 0, 2, 3, 4)], axis=1)
+    sets = sets.reshape(2, PARTS, -1)
+    places = jnp.stack([sets // across - beam_row[0], sets % across - beam_row[1]], axis=2)
+    places = jnp.broadcast_to(places[..., None], places.shape + (LANES,))
     row = np.arange(ROWS)
     base = row // PART + A * (K2_LOW + row % PART % K2_COUNT)
     freq_y = np.broadcast_to(base[:, None], (ROWS, LANES)).astype(np.float32)
@@ -780,36 +795,29 @@
             lines = lines.transpose(0, 2, 3, 4, 1, 5).reshape(-1, HIGH // PARTS, ROWS, LANES)
         if part:
             crops = crop(rows, tile_x // 2, tile_x % 2, mine, pot_second, earlier[0])
-            lines = order(lines, [crops, weights, square_x])
+            lines = order(lines, [crops, square_x] + [r[0] for r in received[1:]])
         for f in range(far):
             received[f].append(swap(lines, f * near) if f else lines)
         if part == 0:
             earlier = [forward_y_first(received[f][0], section_y) for f in range(far)]
-    crops = order(crops.reshape(field_count, own_slots, HALF, LANES), received[0][1:])
-    crops = trade(crops, "beam")
-
     waves = []
-    ready = []
     token = []
     for f in range(far):
-        spec = forward_y(received[f][1], section_y, earlier[f], last_y, token + earlier[1:])
-        ready.append([spec] + [swap(spec, x) for x in range(1, near)])
-        token = [spec, crops]
-    for f in range(far):
+        spec = forward_y(received[f][1], section_y, earlier[f], last_y, token)
+        ready = [spec] + [swap(spec, x) for x in range(1, near)]
+        if f == 0:
+            token = [spec]
         waves.append(
             inverse(
-                f * near, scalars, ready[f], freq_y, square_x, inverse_y, inverse_x, token
+                f * near, scalars, ready, freq_y, square_x, inverse_y, inverse_x, token + earlier[1:]
             )
         )
         token = waves[-1:]
+    crops = order(crops.reshape(field_count, own_slots, HALF, LANES), [spec])
+    crops = trade(crops, "beam")
     owners = field_count // 2 * hold_count
-    token = []
-    partial = []
-    for which in range(2):
-        for part in range(PARTS):
-            index = 2 * part + which
-            partial.append(collect(waves, weights, owners, index, part, token))
-            token = partial[-1:]
+    other = collect(waves, k1_pairs, places, owners, 0, [crops])
+    partial = other + collect(waves, k1_pairs, places, owners, 1, other[:1])
 
     def hop(value, bit):
         pairs = [(i, i ^ (1 << bit)) for i in range(field_count)]

time: 187 us -> 186 us (level)
  waiting for transfers between devices: 32.2 us -> 43.7 us
  other arithmetic: 22 us -> 11 us
  local copies, waits for them, and re-layouts: 12.8 us -> 9.94 us
  starting transfers between devices: 28.7 us -> 31 us
    all_to_all x3, waiting for transfers between devices: 6.91 us -> 16.2 us  [trade(): return lax.all_to_all(value, axis, split_axis=0, concat_axis=0, tiled=True)]
    another operation x14 -> x3, other arithmetic: 6.06 us -> 0.15 us
    ppermute x4, waiting for transfers between devices: 3.9 us -> 8.26 us  [swap(): return lax.ppermute(value, 'slab', [(i, i ^ x) for i in range(hold_count)])]
    sub x4 -> x1, other arithmetic: 5.12 us -> 1.24 us  [shards(): sets // across - beam_row[0]]
    another operation x9 -> x4, local copies, waits for them, and re-layouts: 2.56 us -> 0.2 us  [the longest x3 0.19 us: shards(): sets = jnp.stack([corners, corners.transpose(1, 0, 2, 3, 4)], axis=1)]
    ppermute x4, waiting for transfers between devices: 9.03 us -> 6.71 us  [hop(): return lax.ppermute(value, 'beam', pairs).astype(F32)]
    pallas_call x4 -> x2, Pallas kernels: 18.3 us -> 17.3 us  [collect(): pl.pallas_call(functools.partial(collect_kernel, len(sheets)), grid_spec=...]
  transfers between devices with their start and end apart: 12 -> 12, of which waited for: 6 -> 8; matrix products, arithmetic and copies ran while one was open for 15% -> 8% of each run, Pallas kernels for 30% -> 28%
where the time goes in v9:
time: 186 us; the launch traced here: 185 us
  Pallas kernels  87.6 us (47%)
  waiting for transfers between devices  43.7 us (23%)
  starting transfers between devices  31 us (17%)
  other arithmetic  11 us (6%)
  local copies, waits for them, and re-layouts  9.94 us (5%)
    pallas_call x2, Pallas kernels, forward_x(): pl.pallas_call(forward_x_kernel, grid_spec=pltpu.PrefetchScalarGridSpec(n...  21.4 us
    pallas_call x2, Pallas kernels, inverse(): pl.pallas_call(functools.partial(inverse_kernel, steps, which, near), gri...  18.8 us
    pallas_call x2, Pallas kernels, collect(): pl.pallas_call(functools.partial(collect_kernel, len(sheets)), grid_spec=...  17.3 us
    all_to_all x3, starting transfers between devices, trade(): return lax.all_to_all(value, axis, split_axis=0, concat_axis=0, tiled=True)  16.6 us
    all_to_all x3, waiting for transfers between devices, trade(): return lax.all_to_all(value, axis, split_axis=0, concat_axis=0, tiled=True)  16.2 us
    all_to_all x1, waiting for transfers between devices, shards(): lax.all_to_all(tiles, ('beam', 'slab'), split_axis=0, concat_axis=0, axis...  12.5 us
    pallas_call x2, Pallas kernels, forward_y(): pl.pallas_call(forward_y_kernel, grid=(1 + steps,), in_specs=[pl.BlockSpe...  12.3 us
    ppermute x4, waiting for transfers between devices, swap(): return lax.ppermute(value, 'slab', [(i, i ^ x) for i in range(hold_count)])  8.26 us
  transfers between devices with their start and end apart: 12, of which 8 were waited for; matrix products, arithmetic and copies ran while one was open for 8% of the time, Pallas kernels for 28%

profile of v9, /device:TPU:0, one launch (start us, length us, event | category | flops | bytes accessed | tf_op | source)
XLA Modules:
  0.0 184.6 jit_solution(6478557650927219324)
XLA Ops:
  0.0 10.7 %forward_x.3 = bf16[8,2,208,128]{3,2,1,0:T(8,128)(2,1)} custom-call(s32[1]{0:T(128)} %bitcast.3.sel, bf16[8,4,16,4096]{3,2,1,0:T(8,128)(2,1)} %bitcast.44, bf16[4,512,1024]{2,1,0:T(8,128)(2,1)} %constant.270.clone.section, bf16[4,8,208,256]{3,2,1,0:T(8,128)(2,1)} %constant.271.clone.last, bf16[128,128]{1,0:T(8,128)(2,1)} %constant.272.clone.perm), custom_call_target="tpu_custom_call" | custom-call | flops 9900000256 | tf_op jit(solution)/shard_map/forward_x/pallas_call | solution.py:201
  10.7 7.3 %all-to-all-start.1 = ((bf16[8,2,208,128]{3,2,1,0:T(8,128)(2,1)}), bf16[8,2,208,128]{3,2,1,0:T(8,128)(2,1)S(1)}, u32[]{:S(2)}, u32[]{:S(2)}) async-start(bf16[8,2,208,128]{3,2,1,0:T(8,128)(2,1)} %forward_x.3), calls=%async_computation.1 | async-start | bytes 1703936 | tf_op jit(solution)/shard_map/all_to_all | solution.py:750
  18.1 0.1 copy.27
  18.4 0.6 compare_convert_fusion
  19.0 0.6 and_select_fusion.5
  19.6 0.6 and_select_fusion.6
  20.2 10.7 %forward_x.2 = bf16[8,2,208,128]{3,2,1,0:T(8,128)(2,1)} custom-call(s32[1]{0:T(128)} %bitcast.3.sel, bf16[8,4,16,4096]{3,2,1,0:T(8,128)(2,1)} %bitcast.45, bf16[4,512,1024]{2,1,0:T(8,128)(2,1)} %constant.270.clone.section, bf16[4,8,208,256]{3,2,1,0:T(8,128)(2,1)} %constant.271.clone.last, bf16[128,128]{1,0:T(8,128)(2,1)} %constant.272.clone.perm), custom_call_target="tpu_custom_call" | custom-call | flops 9900000256 | tf_op jit(solution)/shard_map/forward_x/pallas_call | solution.py:201
  30.9 8.8 %all-to-all-done.1.lines = bf16[8,2,208,128]{3,2,1,0:T(8,128)(2,1)S(1)} async-done(((bf16[8,2,208,128]{3,2,1,0:T(8,128)(2,1)}), bf16[8,2,208,128]{3,2,1,0:T(8,128)(2,1)S(1)}, u32[]{:S(2)}, u32[]{:S(2)}) %all-to-all-start.1) | async-done | bytes 852000 | tf_op jit(solution)/shard_map/all_to_all | solution.py:750
  39.6 3.5 %all-to-all-start = ((bf16[8,2,208,128]{3,2,1,0:T(8,128)(2,1)}), bf16[8,2,208,128]{3,2,1,0:T(8,128)(2,1)S(1)}, u32[]{:S(2)}, u32[]{:S(2)}) async-start(bf16[8,2,208,128]{3,2,1,0:T(8,128)(2,1)} %forward_x.2), calls=%async_computation | async-start | bytes 1703936 | tf_op jit(solution)/shard_map/all_to_all | solution.py:750
  43.2 0.6 fusion.24
  44.3 0.5 broadcast_add_fusion
  44.8 0.7 multiply_convert_fusion.rest_1_.refs_3_
  45.5 1.5 collective-permute-start
  47.0 3.3 %forward_y_first.2.after.earlier = bf16[64,2,32,128]{3,2,1,0:T(8,128)(2,1)} custom-call(bf16[8,2,208,128]{3,2,1,0:T(8,128)(2,1)} %copy-done.4, bf16[512,256]{1,0:T(8,128)(2,1)} %constant.273.clone.section), custom_call_target="tpu_custom_call" | custom-call | flops 4400000000 | tf_op jit(solution)/shard_map/forward_y_first/pallas_call | solution.py:273
  50.3 7.1 %crop.1.rest_0_ = bf16[32,32,128]{2,1,0:T(8,128)(2,1)} custom-call(s32[32]{0:T(128)} %get-tuple-element.38.rows, s32[32]{0:T(128)} %get-tuple-element.37.cols, s32[32]{0:T(128)} %get-tuple-element.18.odd, s32[32]{0:T(128)} %get-tuple-element.15.mine, bf16[512,4096]{1,0:T(8,128)(2,1)} %pot.1, bf16[64,2,32,128]{3,2,1,0:T(8,128)(2,1)} %forward_y_first.2.after.earlier), custom_call_target="tpu_custom_call" | custom-call | flops 7699999744 | tf_op jit(solution)/shard_map/crop/pallas_call | solution.py:575
  57.4 7.5 %all-to-all-done.value = bf16[8,2,208,128]{3,2,1,0:T(8,128)(2,1)S(1)} async-done(((bf16[8,2,208,128]{3,2,1,0:T(8,128)(2,1)}), bf16[8,2,208,128]{3,2,1,0:T(8,128)(2,1)S(1)}, u32[]{:S(2)}, u32[]{:S(2)}) %all-to-all-start) | async-done | bytes 852000 | tf_op jit(solution)/shard_map/all_to_all | solution.py:750
  64.9 1.1 collective-permute-done.rest_2_.lines
  66.0 0.9 copy-done.5
  66.9 6.2 %forward_y.2.refs_0_.refs_7_ = bf16[32,208,128]{2,1,0:T(8,128)(2,1)} custom-call(bf16[8,2,208,128]{3,2,1,0:T(8,128)(2,1)} %order.2.lines, bf16[512,256]{1,0:T(8,128)(2,1)} %constant.273.clone.section, bf16[64,2,32,128]{3,2,1,0:T(8,128)(2,1)} %forward_y_first.2.after.earlier, bf16[32,208,256]{2,1,0:T(8,128)(2,1)} %constant.274.clone.last), custom_call_target="tpu_custom_call" | custom-call | flops 6600000000 | tf_op jit(solution)/shard_map/forward_y/pallas_call | solution.py:319
  74.0 0.6 reshape.1008.sel
  74.6 1.5 collective-permute-start.2
  76.1 3.4 %forward_y_first.3.refs_8_.earlier = bf16[64,2,32,128]{3,2,1,0:T(8,128)(2,1)} custom-call(bf16[8,2,208,128]{3,2,1,0:T(8,128)(2,1)} %copy-done.5, bf16[512,256]{1,0:T(8,128)(2,1)} %constant.273.clone.section), custom_call_target="tpu_custom_call" | custom-call | flops 4400000000 | tf_op jit(solution)/shard_map/forward_y_first/pallas_call | solution.py:273
  79.4 9.4 %inverse.2.rest_0_.refs_7_.refs_0_ = bf16[32,256,256]{2,1,0:T(8,128)(2,1)} custom-call(s32[12]{0:T(128)} %reshape.1008.sel, bf16[32,208,128]{2,1,0:T(8,128)(2,1)} %forward_y.2.refs_0_.refs_7_, bf16[32,208,128]{2,1,0:T(8,128)(2,1)} %collective-permute-done.1.refs_1_, f32[208,128]{1,0:T(8,128)} %constant.275.clone.refs_2_, ...), custom_call_target="tpu_custom_call" | custom-call | flops 6600000000 | tf_op jit(solution)/shard_map/inverse/pallas_call | solution.py:427
  88.8 7.1 %collective-permute-done.2.lines = bf16[8,2,208,128]{3,2,1,0:T(8,128)(2,1)S(1)} collective-permute-done((bf16[8,2,208,128]{3,2,1,0:T(8,128)(2,1)S(1)}, bf16[8,2,208,128]{3,2,1,0:T(8,128)(2,1)S(1)}, u32[]{:S(2)}, u32[]{:S(2)}) %collective-permute-start.2) | collective-permute-done | bytes 852000 | tf_op jit(solution)/shard_map/ppermute | solution.py:756
  95.9 0.9 copy-done.11
  96.8 6.1 %forward_y.3.refs_0_.rest_0_ = bf16[32,208,128]{2,1,0:T(8,128)(2,1)} custom-call(bf16[8,2,208,128]{3,2,1,0:T(8,128)(2,1)} %copy-done.11, bf16[512,256]{1,0:T(8,128)(2,1)} %constant.273.clone.section, bf16[64,2,32,128]{3,2,1,0:T(8,128)(2,1)} %forward_y_first.3.refs_8_.earlier, bf16[32,208,256]{2,1,0:T(8,128)(2,1)} %constant.274.clone.last, ...), custom_call_target="tpu_custom_call" | custom-call | flops 6600000000 | tf_op jit(solution)/shard_map/forward_y/pallas_call | solution.py:319
  102.9 0.1 reshape_reshape.3
  103.0 0.1 copy.28
  103.3 0.6 gather_fusion
  103.9 0.6 gather_fusion.1
  104.4 0.1 stack.55
  104.5 0.1 stack.54
  104.6 1.2 fusion.15
  105.9 5.7 %all-to-all-start.2 = ((bf16[8,4,32,128]{3,2,1,0:T(8,128)(2,1)}), bf16[8,4,32,128]{3,2,1,0:T(8,128)(2,1)S(1)}, u32[]{:S(2)}, u32[]{:S(2)}) async-start(bf16[8,4,32,128]{3,2,1,0:T(8,128)(2,1)} %order.3), calls=%async_computation.2 | async-start | bytes 524288 | tf_op jit(solution)/shard_map/all_to_all | solution.py:750
  111.7 1.2 copy-done.10
  112.9 9.4 %inverse.3.refs_1_ = bf16[32,256,256]{2,1,0:T(8,128)(2,1)} custom-call(s32[12]{0:T(128)} %reshape.1008.sel, bf16[32,208,128]{2,1,0:T(8,128)(2,1)} %forward_y.3.refs_0_.rest_0_, bf16[32,208,128]{2,1,0:T(8,128)(2,1)} %copy-done.10, f32[208,128]{1,0:T(8,128)} %constant.275.clone.refs_2_, f32[4,1,128]{2,1,0:T(1,128)} %multiply_convert_fusion.rest_1_.refs_3_, ...), custom_call_target="tpu_custom_call" | custom-call | flops 6600000000 | tf_op jit(solution)/shard_map/inverse/pallas_call | solution.py:427
  122.3 0.8 broadcast_in_dim.2.refs_2_
  123.1 8.7 %collect.2 = (bf16[16,2,4,16,128]{4,3,2,1,0:T(8,128)(2,1)}, bf16[16,2,4,16,128]{4,3,2,1,0:T(8,128)(2,1)}) custom-call(s32[4]{0:T(128)} %get-tuple-element.14.k1_pairs, bf16[32,256,256]{2,1,0:T(8,128)(2,1)} %inverse.2.rest_0_.refs_7_.refs_0_, bf16[32,256,256]{2,1,0:T(8,128)(2,1)} %inverse.3.refs_1_, s32[2,2,2,64,128]{4,3,2,1,0:T(8,128)} %broadcast_in_dim.2.refs_2_, ...), custom_call_target="tpu_custom_call" | custom-call | flops 55000000 | tf_op jit(solution)/shard_map/collect/pallas_call | solution.py:518
  131.8 2.0 %collective-permute-start.6 = (bf16[16,2,4,16,128]{4,3,2,1,0:T(8,128)(2,1)}, bf16[16,2,4,16,128]{4,3,2,1,0:T(8,128)(2,1)S(1)}, u32[]{:S(2)}, u32[]{:S(2)}) collective-permute-start(bf16[16,2,4,16,128]{4,3,2,1,0:T(8,128)(2,1)} %get-tuple-element.12), channel_id=1, source_target_pairs={{0,8},{4,12},{8,0},{12,4},{16,24},{20,28},{24,16},{28,20},{1,9},{5... | collective-permute-start | bytes 1572872 | tf_op jit(solution)/shard_map/ppermute | solution.py:824
  133.8 0.2 dynamic-slice_reduce_fusion
  134.0 1.5 collective-permute-start.4
  135.9 0.1 add.406
  136.1 8.6 %collect.3 = (bf16[16,2,4,16,128]{4,3,2,1,0:T(8,128)(2,1)}, bf16[16,2,4,16,128]{4,3,2,1,0:T(8,128)(2,1)}) custom-call(s32[4]{0:T(128)} %get-tuple-element.14.k1_pairs, bf16[32,256,256]{2,1,0:T(8,128)(2,1)} %inverse.2.rest_0_.refs_7_.refs_0_, bf16[32,256,256]{2,1,0:T(8,128)(2,1)} %inverse.3.refs_1_, s32[2,2,2,64,128]{4,3,2,1,0:T(8,128)} %broadcast_in_dim.2.refs_2_, ...), custom_call_target="tpu_custom_call" | custom-call | flops 55000000 | tf_op jit(solution)/shard_map/collect/pallas_call | solution.py:518
  144.7 1.3 collective-permute-done.6
  146.1 1.2 convert_add_fusion
  147.3 1.8 collective-permute-start.7
  149.2 1.3 convert_add_fusion.1
  150.5 1.5 collective-permute-start.5
  152.0 0.1 fusion.23
  152.1 2.9 %collective-permute-done.7 = bf16[8,2,4,16,128]{4,3,2,1,0:T(8,128)(2,1)S(1)} collective-permute-done((bf16[8,2,4,16,128]{4,3,2,1,0:T(8,128)(2,1)S(1)}, bf16[8,2,4,16,128]{4,3,2,1,0:T(8,128)(2,1)S(1)}, u32[]{:S(2)}, u32[]{:S(2)}) %collective-permute-start.7) | collective-permute-done | bytes 262176 | tf_op jit(solution)/shard_map/ppermute | solution.py:824
  155.1 2.4 %collective-permute-done.5 = bf16[8,2,4,16,128]{4,3,2,1,0:T(8,128)(2,1)S(1)} collective-permute-done((bf16[8,2,4,16,128]{4,3,2,1,0:T(8,128)(2,1)S(1)}, bf16[8,2,4,16,128]{4,3,2,1,0:T(8,128)(2,1)S(1)}, u32[]{:S(2)}, u32[]{:S(2)}) %collective-permute-start.5) | collective-permute-done | bytes 262176 | tf_op jit(solution)/shard_map/ppermute | solution.py:824
  157.7 0.9 pad_maximum_fusion
  158.5 4.5 %all-to-all-start.3 = ((bf16[8,2,4,32,128]{4,3,2,1,0:T(8,128)(2,1)}), bf16[8,2,4,32,128]{4,3,2,1,0:T(8,128)(2,1)S(1)}, u32[]{:S(2)}, u32[]{:S(2)}) async-start(bf16[8,2,4,32,128]{4,3,2,1,0:T(8,128)(2,1)} %pad_maximum_fusion), calls=%async_computation.3 | async-start | bytes 1048576 | tf_op jit(solution)/shard_map/all_to_all | solution.py:837
  163.1 0.6 dynamic_slice.18.counts
  163.7 0.6 pad_maximum_fusion.2.alpha
  164.3 0.3 fusion.6
  164.7 0.7 pad_maximum_fusion.1.refs_2_
  165.3 0.6 reduce_sum.25.refs_1_
  166.0 12.5 %all-to-all-done.3 = bf16[8,2,4,32,128]{4,3,2,1,0:T(8,128)(2,1)S(1)} async-done(((bf16[8,2,4,32,128]{4,3,2,1,0:T(8,128)(2,1)}), bf16[8,2,4,32,128]{4,3,2,1,0:T(8,128)(2,1)S(1)}, u32[]{:S(2)}, u32[]{:S(2)}) %all-to-all-start.3) | async-done | bytes 524320 | tf_op jit(solution)/shard_map/all_to_all | solution.py:837
  178.4 0.8 reduce_sum.24.refs_0_
  179.3 4.0 %detect.1 = f32[1,256]{1,0:T(1,128)} custom-call(f32[2,4,12]{2,1,0:T(4,128)} %pad_maximum_fusion.2.alpha, s32[1]{0:T(128)} %dynamic_slice.18.counts, bf16[4,2,4,32,128]{4,3,2,1,0:T(8,128)(2,1)} %reduce_sum.24.refs_0_, bf16[4,32,128]{2,1,0:T(8,128)(2,1)} %reduce_sum.25.refs_1_, f32[4,2,32,128]{3,2,1,0:T(8,128)} %pad_maximum_fusion.1.refs_2_, ...), custom_call_target="tpu_custom_call" | custom-call | tf_op jit(solution)/shard_map/detect/pallas_call | solution.py:641
  183.3 0.7 slice_reduce_fusion
  184.0 0.1 reshape_squeeze.3
  184.0 0.6 copy.31
  (65 shorter events, 1.3 us)
Async XLA Ops:
  0.0 18.0 %copy-start.7 = (s32[32,4]{0,1:T(4,128)S(1)}, s32[32,4]{0,1:T(4,128)}, u32[]{:S(2)}) copy-start(s32[32,4]{0,1:T(4,128)} %param.23) | copy-start | bytes 1540
  0.0 18.9 %copy-start.6 = (s32[4,2]{0,1:T(2,128)S(1)}, s32[4,2]{0,1:T(2,128)}, u32[]{:S(2)}) copy-start(s32[4,2]{0,1:T(2,128)} %param.21) | copy-start | bytes 100
  10.7 28.9 %all-to-all-start.1 = ((bf16[8,2,208,128]{3,2,1,0:T(8,128)(2,1)}), bf16[8,2,208,128]{3,2,1,0:T(8,128)(2,1)S(1)}, u32[]{:S(2)}, u32[]{:S(2)}) async-start(bf16[8,2,208,128]{3,2,1,0:T(8,128)(2,1)} %forward_x.3), calls=%async_computation.1 | async-start | bytes 1703936 | tf_op jit(solution)/shard_map/all_to_all | solution.py:750
  20.2 24.7 %copy-start.8 = (s32[128]{0:T(128)S(1)}, s32[128]{0:T(128)}, u32[]{:S(2)}) copy-start(s32[128]{0:T(128)} %constant.269.clone) | copy-start | bytes 1540
  39.6 7.3 %copy-start.4 = (bf16[8,2,208,128]{3,2,1,0:T(8,128)(2,1)}, bf16[8,2,208,128]{3,2,1,0:T(8,128)(2,1)S(1)}, u32[]{:S(2)}) copy-start(bf16[8,2,208,128]{3,2,1,0:T(8,128)(2,1)S(1)} %all-to-all-done.1.lines) | copy-start | bytes 2555908
  39.6 25.3 %all-to-all-start = ((bf16[8,2,208,128]{3,2,1,0:T(8,128)(2,1)}), bf16[8,2,208,128]{3,2,1,0:T(8,128)(2,1)S(1)}, u32[]{:S(2)}, u32[]{:S(2)}) async-start(bf16[8,2,208,128]{3,2,1,0:T(8,128)(2,1)} %forward_x.2), calls=%async_computation | async-start | bytes 1703936 | tf_op jit(solution)/shard_map/all_to_all | solution.py:750
  45.5 20.5 %collective-permute-start = (bf16[8,2,208,128]{3,2,1,0:T(8,128)(2,1)S(1)}, bf16[8,2,208,128]{3,2,1,0:T(8,128)(2,1)S(1)}, u32[]{:S(2)}, u32[]{:S(2)}) collective-permute-start(bf16[8,2,208,128]{3,2,1,0:T(8,128)(2,1)S(1)} %all-to-all-done.1.lines), channel_id=1, source_target_pairs={{0,2},{1,3},{2,0},{3,1},{4,6},{5,7},{6,4},{7,5},{8,10},{9,11},{10,... | collective-permute-start | bytes 2555912 | tf_op jit(solution)/shard_map/ppermute | solution.py:756
  64.9 1.1 copy-start
  66.0 0.9 copy-start.5
  66.9 7.6 %copy-start.1 = (bf16[8,2,208,128]{3,2,1,0:T(8,128)(2,1)S(1)}, bf16[8,2,208,128]{3,2,1,0:T(8,128)(2,1)}, u32[]{:S(2)}) copy-start(bf16[8,2,208,128]{3,2,1,0:T(8,128)(2,1)} %order.2.lines) | copy-start | bytes 2555908
  73.1 6.3 %collective-permute-start.1 = (bf16[32,208,128]{2,1,0:T(8,128)(2,1)}, bf16[32,208,128]{2,1,0:T(8,128)(2,1)}, u32[]{:S(2)}, u32[]{:S(2)}) collective-permute-start(bf16[32,208,128]{2,1,0:T(8,128)(2,1)} %forward_y.2.refs_0_.refs_7_), channel_id=1, source_target_pairs={{0,1},{1,0},{2,3},{3,2},{4,5},{5,4},{6,7},{7,6},{8,9},{9,8},{10,11... | collective-permute-start | bytes 5111816 | tf_op jit(solution)/shard_map/ppermute | solution.py:756
  74.6 21.4 %collective-permute-start.2 = (bf16[8,2,208,128]{3,2,1,0:T(8,128)(2,1)S(1)}, bf16[8,2,208,128]{3,2,1,0:T(8,128)(2,1)S(1)}, u32[]{:S(2)}, u32[]{:S(2)}) collective-permute-start(bf16[8,2,208,128]{3,2,1,0:T(8,128)(2,1)S(1)} %copy-done.1), channel_id=1, source_target_pairs={{0,2},{1,3},{2,0},{3,1},{4,6},{5,7},{6,4},{7,5},{8,10},{9,11},{10,... | collective-permute-start | bytes 2555912 | tf_op jit(solution)/shard_map/ppermute | solution.py:756
  95.9 0.9 copy-start.11
  102.9 8.7 %collective-permute-start.3 = (bf16[32,208,128]{2,1,0:T(8,128)(2,1)}, bf16[32,208,128]{2,1,0:T(8,128)(2,1)S(1)}, u32[]{:S(2)}, u32[]{:S(2)}) collective-permute-start(bf16[32,208,128]{2,1,0:T(8,128)(2,1)} %forward_y.3.refs_0_.rest_0_), channel_id=1, source_target_pairs={{0,1},{1,0},{2,3},{3,2},{4,5},{5,4},{6,7},{7,6},{8,9},{9,8},{10,11... | collective-permute-start | bytes 5111816 | tf_op jit(solution)/shard_map/ppermute | solution.py:756
  105.9 16.4 %all-to-all-start.2 = ((bf16[8,4,32,128]{3,2,1,0:T(8,128)(2,1)}), bf16[8,4,32,128]{3,2,1,0:T(8,128)(2,1)S(1)}, u32[]{:S(2)}, u32[]{:S(2)}) async-start(bf16[8,4,32,128]{3,2,1,0:T(8,128)(2,1)} %order.3), calls=%async_computation.2 | async-start | bytes 524288 | tf_op jit(solution)/shard_map/all_to_all | solution.py:750
  111.7 1.2 copy-start.10
  122.3 0.8 copy-start.2
  131.8 14.3 %collective-permute-start.6 = (bf16[16,2,4,16,128]{4,3,2,1,0:T(8,128)(2,1)}, bf16[16,2,4,16,128]{4,3,2,1,0:T(8,128)(2,1)S(1)}, u32[]{:S(2)}, u32[]{:S(2)}) collective-permute-start(bf16[16,2,4,16,128]{4,3,2,1,0:T(8,128)(2,1)} %get-tuple-element.12), channel_id=1, source_target_pairs={{0,8},{4,12},{8,0},{12,4},{16,24},{20,28},{24,16},{28,20},{1,9},{5... | collective-permute-start | bytes 1572872 | tf_op jit(solution)/shard_map/ppermute | solution.py:824
  134.0 15.1 %collective-permute-start.4 = (bf16[16,2,4,16,128]{4,3,2,1,0:T(8,128)(2,1)}, bf16[16,2,4,16,128]{4,3,2,1,0:T(8,128)(2,1)S(1)}, u32[]{:S(2)}, u32[]{:S(2)}) collective-permute-start(bf16[16,2,4,16,128]{4,3,2,1,0:T(8,128)(2,1)} %get-tuple-element.9.refs_3_), channel_id=1, source_target_pairs={{0,4},{4,0},{8,12},{12,8},{16,20},{20,16},{24,28},{28,24},{1,5},{5... | collective-permute-start | bytes 1572872 | tf_op jit(solution)/shard_map/ppermute | solution.py:824
  144.7 7.2 %copy-start.9 = (f32[4]{0:T(128)S(1)}, f32[4]{0:T(128)}, u32[]{:S(2)}) copy-start(f32[4]{0:T(128)} %param.22) | copy-start | bytes 52
  147.3 7.7 %collective-permute-start.7 = (bf16[8,2,4,16,128]{4,3,2,1,0:T(8,128)(2,1)S(1)}, bf16[8,2,4,16,128]{4,3,2,1,0:T(8,128)(2,1)S(1)}, u32[]{:S(2)}, u32[]{:S(2)}) collective-permute-start(bf16[8,2,4,16,128]{4,3,2,1,0:T(8,128)(2,1)S(1)} %slice.72), channel_id=1, source_target_pairs={{0,4},{4,0},{8,12},{12,8},{16,20},{20,16},{24,28},{28,24},{1,5},{5... | collective-permute-start | bytes 786440 | tf_op jit(solution)/shard_map/ppermute | solution.py:824
  149.2 13.9 %copy-start.12 = (s32[32]{0:T(128)S(1)}, s32[32]{0:T(128)}, u32[]{:S(2)}) copy-start(s32[32]{0:T(128)} %param.24) | copy-start | bytes 388
  149.2 16.2 %copy-start.3 = (bf16[8,4,32,128]{3,2,1,0:T(8,128)(2,1)S(1)}, bf16[8,4,32,128]{3,2,1,0:T(8,128)(2,1)}, u32[]{:S(2)}) copy-start(bf16[8,4,32,128]{3,2,1,0:T(8,128)(2,1)} %copy-done.2) | copy-start | bytes 786436
  150.5 7.1 %collective-permute-start.5 = (bf16[8,2,4,16,128]{4,3,2,1,0:T(8,128)(2,1)S(1)}, bf16[8,2,4,16,128]{4,3,2,1,0:T(8,128)(2,1)S(1)}, u32[]{:S(2)}, u32[]{:S(2)}) collective-permute-start(bf16[8,2,4,16,128]{4,3,2,1,0:T(8,128)(2,1)S(1)} %slice.73), channel_id=1, source_target_pairs={{0,8},{4,12},{8,0},{12,4},{16,24},{20,28},{24,16},{28,20},{1,9},{5... | collective-permute-start | bytes 786440 | tf_op jit(solution)/shard_map/ppermute | solution.py:824
  158.5 19.9 %all-to-all-start.3 = ((bf16[8,2,4,32,128]{4,3,2,1,0:T(8,128)(2,1)}), bf16[8,2,4,32,128]{4,3,2,1,0:T(8,128)(2,1)S(1)}, u32[]{:S(2)}, u32[]{:S(2)}) async-start(bf16[8,2,4,32,128]{4,3,2,1,0:T(8,128)(2,1)} %pad_maximum_fusion), calls=%async_computation.3 | async-start | bytes 1048576 | tf_op jit(solution)/shard_map/all_to_all | solution.py:837

commit v10 on v9

--- a/solution.py
+++ b/solution.py
@@ -31,6 +31,7 @@
 VMEM = 60 * 1024 * 1024
 PITCH = A + 1
 PITCH_Y = A // PARTS + 1
+SMALL = pl.CostEstimate(flops=1 << 20, bytes_accessed=0, transcendentals=0)
 BF = jnp.bfloat16
 F32 = jnp.float32
 
@@ -153,10 +154,6 @@
 
 def dot(a, b):
     return jnp.dot(a, b, preferred_element_type=F32)
-
-
-def cost(micros):
-    return pl.CostEstimate(flops=int(micros * 1.1e9), bytes_accessed=0, transcendentals=0)
 
 
 def forward_x_kernel(sel, pot, section, last, perm, out, cos_ref, sin_ref, twisted):
@@ -218,7 +215,7 @@
         ),
         out_shape=jax.ShapeDtypeStruct((fields, steps, ROWS, lanes), BF),
         compiler_params=pltpu.CompilerParams(vmem_limit_bytes=VMEM),
-        cost_estimate=cost(9),
+        cost_estimate=SMALL,
         name="forward_x",
     )(sel, pot.reshape(groups, HIGH, SUB, N), section, last, line_order(lanes))
 
@@ -281,7 +278,7 @@
         out_shape=jax.ShapeDtypeStruct((A, 2, A // PARTS, LANES), BF),
         scratch_shapes=first_section_scratch(lines),
         compiler_params=pltpu.CompilerParams(vmem_limit_bytes=VMEM),
-        cost_estimate=cost(4),
+        cost_estimate=SMALL,
         name="forward_y_first",
     )(lines, section)
 
@@ -330,7 +327,7 @@
         out_shape=jax.ShapeDtypeStruct((PAIRS, ROWS, LANES), BF),
         scratch_shapes=first_section_scratch(lines),
         compiler_params=pltpu.CompilerParams(vmem_limit_bytes=VMEM),
-        cost_estimate=cost(6),
+        cost_estimate=SMALL,
         name="forward_y",
     )(lines, section, earlier, last, *after)
 
@@ -444,7 +441,7 @@
         ),
         out_shape=jax.ShapeDtypeStruct((HALF, 2 * A * near, 2 * LANES), BF),
         compiler_params=pltpu.CompilerParams(vmem_limit_bytes=VMEM),
-        cost_estimate=cost(6),
+        cost_estimate=SMALL,
         name="inverse",
     )(sel, *specs, freq_y, square_x, table_y, *[table_x] * near, *after)
 
@@ -535,7 +532,7 @@
         ),
         out_shape=[jax.ShapeDtypeStruct(shape, BF)] * PARTS,
         compiler_params=pltpu.CompilerParams(vmem_limit_bytes=VMEM),
-        cost_estimate=cost(0.05),
+        cost_estimate=SMALL,
         name="collect",
     )(k1_pairs, *sheets, places, *after)
 
@@ -580,7 +577,7 @@
         out_shape=jax.ShapeDtypeStruct((slots, HALF, LANES), BF),
         scratch_shapes=[pltpu.VMEM((slots, A, LANES), BF), pltpu.SemaphoreType.DMA((slots,))],
         compiler_params=pltpu.CompilerParams(vmem_limit_bytes=VMEM),
-        cost_estimate=cost(7),
+        cost_estimate=SMALL,
         name="crop",
     )(rows, cols, odd, mine, pot, after)
 
@@ -795,24 +792,20 @@
             lines = lines.transpose(0, 2, 3, 4, 1, 5).reshape(-1, HIGH // PARTS, ROWS, LANES)
         if part:
             crops = crop(rows, tile_x // 2, tile_x % 2, mine, pot_second, earlier[0])
-            lines = order(lines, [crops, square_x] + [r[0] for r in received[1:]])
+            lines = order(lines, [crops, square_x, places] + [r[0] for r in received[1:]])
         for f in range(far):
             received[f].append(swap(lines, f * near) if f else lines)
         if part == 0:
             earlier = [forward_y_first(received[f][0], section_y) for f in range(far)]
     waves = []
-    token = []
     for f in range(far):
-        spec = forward_y(received[f][1], section_y, earlier[f], last_y, token)
+        spec = forward_y(received[f][1], section_y, earlier[f], last_y, [])
         ready = [spec] + [swap(spec, x) for x in range(1, near)]
-        if f == 0:
-            token = [spec]
         waves.append(
             inverse(
-                f * near, scalars, ready, freq_y, square_x, inverse_y, inverse_x, token + earlier[1:]
+                f * near, scalars, ready, freq_y, square_x, inverse_y, inverse_x, waves[-1:]
             )
         )
-        token = waves[-1:]
     crops = order(crops.reshape(field_count, own_slots, HALF, LANES), [spec])
     crops = trade(crops, "beam")
     owners = field_count // 2 * hold_count

time: 186 us -> 184 us (0.989)
    all_to_all x3, waiting for transfers between devices: 16.2 us -> 13.1 us  [trade(): return lax.all_to_all(value, axis, split_axis=0, concat_axis=0, tiled=True)]
    ppermute x4, waiting for transfers between devices: 8.26 us -> 10.6 us  [swap(): return lax.ppermute(value, 'slab', [(i, i ^ x) for i in range(hold_count)])]
  transfers between devices with their start and end apart: 12 -> 12, of which waited for: 8 -> 8; matrix products, arithmetic and copies ran while one was open for 8% -> 8% of each run, Pallas kernels for 28% -> 35%
where the time goes in v10:
time: 184 us
  Pallas kernels  87.6 us (48%)
  waiting for transfers between devices  42.8 us (23%)
  starting transfers between devices  30.6 us (17%)
  other arithmetic  11.1 us (6%)
  local copies, waits for them, and re-layouts  9.93 us (5%)
    pallas_call x2, Pallas kernels, forward_x(): pl.pallas_call(forward_x_kernel, grid_spec=pltpu.PrefetchScalarGridSpec(n...  21.4 us
    pallas_call x2, Pallas kernels, inverse(): pl.pallas_call(functools.partial(inverse_kernel, steps, which, near), gri...  18.8 us
    pallas_call x2, Pallas kernels, collect(): pl.pallas_call(functools.partial(collect_kernel, len(sheets)), grid_spec=...  17.3 us
    all_to_all x3, starting transfers between devices, trade(): return lax.all_to_all(value, axis, split_axis=0, concat_axis=0, tiled=True)  16.3 us
    all_to_all x3, waiting for transfers between devices, trade(): return lax.all_to_all(value, axis, split_axis=0, concat_axis=0, tiled=True)  13.1 us
    all_to_all x1, waiting for transfers between devices, shards(): lax.all_to_all(tiles, ('beam', 'slab'), split_axis=0, concat_axis=0, axis...  12.5 us
    pallas_call x2, Pallas kernels, forward_y(): pl.pallas_call(forward_y_kernel, grid=(1 + steps,), in_specs=[pl.BlockSpe...  12.2 us
    ppermute x4, waiting for transfers between devices, swap(): return lax.ppermute(value, 'slab', [(i, i ^ x) for i in range(hold_count)])  10.6 us
  transfers between devices with their start and end apart: 12, of which 8 were waited for; matrix products, arithmetic and copies ran while one was open for 8% of the time, Pallas kernels for 35%

profile of v10, /device:TPU:0, one launch (start us, length us, event | category | flops | bytes accessed | tf_op | source)
XLA Modules:
  0.0 183.6 jit_solution(2664345668130905796)
XLA Ops:
  0.0 10.7 %forward_x.3 = bf16[8,2,208,128]{3,2,1,0:T(8,128)(2,1)} custom-call(s32[1]{0:T(128)} %bitcast.3.sel, bf16[8,4,16,4096]{3,2,1,0:T(8,128)(2,1)} %bitcast.40, bf16[4,512,1024]{2,1,0:T(8,128)(2,1)} %constant.270.clone.section, bf16[4,8,208,256]{3,2,1,0:T(8,128)(2,1)} %constant.271.clone.last, bf16[128,128]{1,0:T(8,128)(2,1)} %constant.272.clone.perm), custom_call_target="tpu_custom_call" | custom-call | flops 1048576 | tf_op jit(solution)/shard_map/forward_x/pallas_call | solution.py:198
  10.7 7.3 %all-to-all-start.1 = ((bf16[8,2,208,128]{3,2,1,0:T(8,128)(2,1)}), bf16[8,2,208,128]{3,2,1,0:T(8,128)(2,1)S(1)}, u32[]{:S(2)}, u32[]{:S(2)}) async-start(bf16[8,2,208,128]{3,2,1,0:T(8,128)(2,1)} %forward_x.3), calls=%async_computation.1 | async-start | bytes 1703936 | tf_op jit(solution)/shard_map/all_to_all | solution.py:747
  18.1 0.1 reshape_reshape.3
  18.2 0.1 copy.28
  18.4 0.6 gather_fusion
  19.0 0.6 gather_fusion.1
  19.6 0.1 stack.54
  19.7 10.7 %forward_x.2 = bf16[8,2,208,128]{3,2,1,0:T(8,128)(2,1)} custom-call(s32[1]{0:T(128)} %bitcast.3.sel, bf16[8,4,16,4096]{3,2,1,0:T(8,128)(2,1)} %bitcast.41, bf16[4,512,1024]{2,1,0:T(8,128)(2,1)} %constant.270.clone.section, bf16[4,8,208,256]{3,2,1,0:T(8,128)(2,1)} %constant.271.clone.last, bf16[128,128]{1,0:T(8,128)(2,1)} %constant.272.clone.perm), custom_call_target="tpu_custom_call" | custom-call | flops 1048576 | tf_op jit(solution)/shard_map/forward_x/pallas_call | solution.py:198
  30.5 0.5 fusion.24
  31.1 8.5 %all-to-all-done.1.lines = bf16[8,2,208,128]{3,2,1,0:T(8,128)(2,1)S(1)} async-done(((bf16[8,2,208,128]{3,2,1,0:T(8,128)(2,1)}), bf16[8,2,208,128]{3,2,1,0:T(8,128)(2,1)S(1)}, u32[]{:S(2)}, u32[]{:S(2)}) %all-to-all-start.1) | async-done | bytes 852000 | tf_op jit(solution)/shard_map/all_to_all | solution.py:747
  39.6 3.5 %all-to-all-start = ((bf16[8,2,208,128]{3,2,1,0:T(8,128)(2,1)}), bf16[8,2,208,128]{3,2,1,0:T(8,128)(2,1)S(1)}, u32[]{:S(2)}, u32[]{:S(2)}) async-start(bf16[8,2,208,128]{3,2,1,0:T(8,128)(2,1)} %forward_x.2), calls=%async_computation | async-start | bytes 1703936 | tf_op jit(solution)/shard_map/all_to_all | solution.py:747
  43.2 0.1 stack.55
  43.3 0.1 copy.27
  44.2 1.2 fusion.15
  45.5 0.6 broadcast_add_fusion
  46.1 1.5 collective-permute-start
  47.5 0.6 compare_convert_fusion
  48.1 0.6 and_select_fusion.5
  48.7 0.6 and_select_fusion.6
  49.3 0.7 multiply_convert_fusion.rest_1_.refs_3_
  49.9 3.3 %forward_y_first.2.after.earlier = bf16[64,2,32,128]{3,2,1,0:T(8,128)(2,1)} custom-call(bf16[8,2,208,128]{3,2,1,0:T(8,128)(2,1)} %copy-done.1, bf16[512,256]{1,0:T(8,128)(2,1)} %constant.273.clone.section), custom_call_target="tpu_custom_call" | custom-call | flops 1048576 | tf_op jit(solution)/shard_map/forward_y_first/pallas_call | solution.py:270
  53.3 7.1 %crop.1.rest_0_ = bf16[32,32,128]{2,1,0:T(8,128)(2,1)} custom-call(s32[32]{0:T(128)} %get-tuple-element.38.rows, s32[32]{0:T(128)} %get-tuple-element.37.cols, s32[32]{0:T(128)} %get-tuple-element.18.odd, s32[32]{0:T(128)} %get-tuple-element.15.mine, bf16[512,4096]{1,0:T(8,128)(2,1)} %pot.1, bf16[64,2,32,128]{3,2,1,0:T(8,128)(2,1)} %forward_y_first.2.after.earlier), custom_call_target="tpu_custom_call" | custom-call | flops 1048576 | tf_op jit(solution)/shard_map/crop/pallas_call | solution.py:572
  60.4 4.5 %all-to-all-done.value = bf16[8,2,208,128]{3,2,1,0:T(8,128)(2,1)S(1)} async-done(((bf16[8,2,208,128]{3,2,1,0:T(8,128)(2,1)}), bf16[8,2,208,128]{3,2,1,0:T(8,128)(2,1)S(1)}, u32[]{:S(2)}, u32[]{:S(2)}) %all-to-all-start) | async-done | bytes 852000 | tf_op jit(solution)/shard_map/all_to_all | solution.py:747
  64.9 1.7 collective-permute-done.rest_3_.lines
  66.6 1.0 broadcast_in_dim.2.rest_2_.refs_2_
  67.6 1.5 collective-permute-start.2
  69.1 6.1 %forward_y.2.refs_0_ = bf16[32,208,128]{2,1,0:T(8,128)(2,1)} custom-call(bf16[8,2,208,128]{3,2,1,0:T(8,128)(2,1)} %order.2.lines, bf16[512,256]{1,0:T(8,128)(2,1)} %constant.273.clone.section, bf16[64,2,32,128]{3,2,1,0:T(8,128)(2,1)} %forward_y_first.2.after.earlier, bf16[32,208,256]{2,1,0:T(8,128)(2,1)} %constant.274.clone.last), custom_call_target="tpu_custom_call" | custom-call | flops 1048576 | tf_op jit(solution)/shard_map/forward_y/pallas_call | solution.py:316
  75.2 3.4 %forward_y_first.3.earlier = bf16[64,2,32,128]{3,2,1,0:T(8,128)(2,1)} custom-call(bf16[8,2,208,128]{3,2,1,0:T(8,128)(2,1)} %copy-done.2, bf16[512,256]{1,0:T(8,128)(2,1)} %constant.273.clone.section), custom_call_target="tpu_custom_call" | custom-call | flops 1048576 | tf_op jit(solution)/shard_map/forward_y_first/pallas_call | solution.py:270
  78.6 8.9 %collective-permute-done.2.lines = bf16[8,2,208,128]{3,2,1,0:T(8,128)(2,1)S(1)} collective-permute-done((bf16[8,2,208,128]{3,2,1,0:T(8,128)(2,1)}, bf16[8,2,208,128]{3,2,1,0:T(8,128)(2,1)S(1)}, u32[]{:S(2)}, u32[]{:S(2)}) %collective-permute-start.2) | collective-permute-done | bytes 852000 | tf_op jit(solution)/shard_map/ppermute | solution.py:753
  87.5 0.9 copy-done.6
  88.4 6.1 %forward_y.3.refs_0_.rest_0_ = bf16[32,208,128]{2,1,0:T(8,128)(2,1)} custom-call(bf16[8,2,208,128]{3,2,1,0:T(8,128)(2,1)} %copy-done.6, bf16[512,256]{1,0:T(8,128)(2,1)} %constant.273.clone.section, bf16[64,2,32,128]{3,2,1,0:T(8,128)(2,1)} %forward_y_first.3.earlier, bf16[32,208,256]{2,1,0:T(8,128)(2,1)} %constant.274.clone.last), custom_call_target="tpu_custom_call" | custom-call | flops 1048576 | tf_op jit(solution)/shard_map/forward_y/pallas_call | solution.py:316
  94.5 5.5 %all-to-all-start.2 = ((bf16[8,4,32,128]{3,2,1,0:T(8,128)(2,1)}), bf16[8,4,32,128]{3,2,1,0:T(8,128)(2,1)S(1)}, u32[]{:S(2)}, u32[]{:S(2)}) async-start(bf16[8,4,32,128]{3,2,1,0:T(8,128)(2,1)} %order.3), calls=%async_computation.2 | async-start | bytes 524288 | tf_op jit(solution)/shard_map/all_to_all | solution.py:747
  100.7 0.7 reshape.1008.sel
  101.3 1.2 copy-done.5
  102.5 9.4 %inverse.2.refs_7_.refs_0_ = bf16[32,256,256]{2,1,0:T(8,128)(2,1)} custom-call(s32[12]{0:T(128)} %reshape.1008.sel, bf16[32,208,128]{2,1,0:T(8,128)(2,1)} %forward_y.2.refs_0_, bf16[32,208,128]{2,1,0:T(8,128)(2,1)} %copy-done.5, f32[208,128]{1,0:T(8,128)} %constant.275.clone.refs_2_, f32[4,1,128]{2,1,0:T(1,128)} %multiply_convert_fusion.rest_1_.refs_3_, ...), custom_call_target="tpu_custom_call" | custom-call | flops 1048576 | tf_op jit(solution)/shard_map/inverse/pallas_call | solution.py:424
  111.9 9.5 %inverse.3.refs_1_ = bf16[32,256,256]{2,1,0:T(8,128)(2,1)} custom-call(s32[12]{0:T(128)} %reshape.1008.sel, bf16[32,208,128]{2,1,0:T(8,128)(2,1)} %forward_y.3.refs_0_.rest_0_, bf16[32,208,128]{2,1,0:T(8,128)(2,1)} %collective-permute-done.3.refs_1_, f32[208,128]{1,0:T(8,128)} %constant.275.clone.refs_2_, f32[4,1,128]{2,1,0:T(1,128)} %multiply_convert_fusion.rest_1_.refs_3_, ...), custom_call_target="tpu_custom_call" | custom-call | flops 1048576 | tf_op jit(solution)/shard_map/inverse/pallas_call | solution.py:424
  121.4 0.7 copy-done.3
  122.1 8.7 %collect.2 = (bf16[16,2,4,16,128]{4,3,2,1,0:T(8,128)(2,1)}, bf16[16,2,4,16,128]{4,3,2,1,0:T(8,128)(2,1)}) custom-call(s32[4]{0:T(128)} %get-tuple-element.14.k1_pairs, bf16[32,256,256]{2,1,0:T(8,128)(2,1)} %inverse.2.refs_7_.refs_0_, bf16[32,256,256]{2,1,0:T(8,128)(2,1)} %inverse.3.refs_1_, s32[2,2,2,64,128]{4,3,2,1,0:T(8,128)} %broadcast_in_dim.2.rest_2_.refs_2_, ...), custom_call_target="tpu_custom_call" | custom-call | flops 1048576 | tf_op jit(solution)/shard_map/collect/pallas_call | solution.py:515
  130.8 2.0 %collective-permute-start.6 = (bf16[16,2,4,16,128]{4,3,2,1,0:T(8,128)(2,1)}, bf16[16,2,4,16,128]{4,3,2,1,0:T(8,128)(2,1)S(1)}, u32[]{:S(2)}, u32[]{:S(2)}) collective-permute-start(bf16[16,2,4,16,128]{4,3,2,1,0:T(8,128)(2,1)} %get-tuple-element.12), channel_id=1, source_target_pairs={{0,8},{4,12},{8,0},{12,4},{16,24},{20,28},{24,16},{28,20},{1,9},{5... | collective-permute-start | bytes 1572872 | tf_op jit(solution)/shard_map/ppermute | solution.py:817
  132.8 0.2 dynamic-slice_reduce_fusion
  133.0 1.5 collective-permute-start.4
  134.7 0.1 add.417
  135.0 8.6 %collect.3 = (bf16[16,2,4,16,128]{4,3,2,1,0:T(8,128)(2,1)}, bf16[16,2,4,16,128]{4,3,2,1,0:T(8,128)(2,1)}) custom-call(s32[4]{0:T(128)} %get-tuple-element.14.k1_pairs, bf16[32,256,256]{2,1,0:T(8,128)(2,1)} %inverse.2.refs_7_.refs_0_, bf16[32,256,256]{2,1,0:T(8,128)(2,1)} %inverse.3.refs_1_, s32[2,2,2,64,128]{4,3,2,1,0:T(8,128)} %broadcast_in_dim.2.rest_2_.refs_2_, ...), custom_call_target="tpu_custom_call" | custom-call | flops 1048576 | tf_op jit(solution)/shard_map/collect/pallas_call | solution.py:515
  143.6 1.3 collective-permute-done.6
  145.0 1.2 convert_add_fusion
  146.3 1.8 %collective-permute-start.7 = (bf16[8,2,4,16,128]{4,3,2,1,0:T(8,128)(2,1)S(1)}, bf16[8,2,4,16,128]{4,3,2,1,0:T(8,128)(2,1)S(1)}, u32[]{:S(2)}, u32[]{:S(2)}) collective-permute-start(bf16[8,2,4,16,128]{4,3,2,1,0:T(8,128)(2,1)S(1)} %slice.72), channel_id=1, source_target_pairs={{0,4},{4,0},{8,12},{12,8},{16,20},{20,16},{24,28},{28,24},{1,5},{5... | collective-permute-start | bytes 786440 | tf_op jit(solution)/shard_map/ppermute | solution.py:817
  148.1 1.3 convert_add_fusion.1
  149.4 1.5 collective-permute-start.5
  150.9 0.1 fusion.23
  151.0 2.9 %collective-permute-done.7 = bf16[8,2,4,16,128]{4,3,2,1,0:T(8,128)(2,1)S(1)} collective-permute-done((bf16[8,2,4,16,128]{4,3,2,1,0:T(8,128)(2,1)S(1)}, bf16[8,2,4,16,128]{4,3,2,1,0:T(8,128)(2,1)S(1)}, u32[]{:S(2)}, u32[]{:S(2)}) %collective-permute-start.7) | collective-permute-done | bytes 262176 | tf_op jit(solution)/shard_map/ppermute | solution.py:817
  154.0 2.5 %collective-permute-done.5 = bf16[8,2,4,16,128]{4,3,2,1,0:T(8,128)(2,1)S(1)} collective-permute-done((bf16[8,2,4,16,128]{4,3,2,1,0:T(8,128)(2,1)S(1)}, bf16[8,2,4,16,128]{4,3,2,1,0:T(8,128)(2,1)S(1)}, u32[]{:S(2)}, u32[]{:S(2)}) %collective-permute-start.5) | collective-permute-done | bytes 262176 | tf_op jit(solution)/shard_map/ppermute | solution.py:817
  156.6 0.9 pad_maximum_fusion
  157.5 4.5 %all-to-all-start.3 = ((bf16[8,2,4,32,128]{4,3,2,1,0:T(8,128)(2,1)}), bf16[8,2,4,32,128]{4,3,2,1,0:T(8,128)(2,1)S(1)}, u32[]{:S(2)}, u32[]{:S(2)}) async-start(bf16[8,2,4,32,128]{4,3,2,1,0:T(8,128)(2,1)} %pad_maximum_fusion), calls=%async_computation.3 | async-start | bytes 1048576 | tf_op jit(solution)/shard_map/all_to_all | solution.py:830
  161.9 0.6 dynamic_slice.18.counts
  162.6 0.6 pad_maximum_fusion.2.alpha
  163.2 0.3 fusion.6
  163.5 0.7 pad_maximum_fusion.1.refs_2_
  164.2 0.7 reduce_sum.25.refs_1_
  164.8 12.5 %all-to-all-done.3 = bf16[8,2,4,32,128]{4,3,2,1,0:T(8,128)(2,1)S(1)} async-done(((bf16[8,2,4,32,128]{4,3,2,1,0:T(8,128)(2,1)}), bf16[8,2,4,32,128]{4,3,2,1,0:T(8,128)(2,1)S(1)}, u32[]{:S(2)}, u32[]{:S(2)}) %all-to-all-start.3) | async-done | bytes 524320 | tf_op jit(solution)/shard_map/all_to_all | solution.py:830
  177.3 0.8 reduce_sum.24.refs_0_
  178.1 4.0 %detect.1 = f32[1,256]{1,0:T(1,128)} custom-call(f32[2,4,12]{2,1,0:T(4,128)} %pad_maximum_fusion.2.alpha, s32[1]{0:T(128)} %dynamic_slice.18.counts, bf16[4,2,4,32,128]{4,3,2,1,0:T(8,128)(2,1)} %reduce_sum.24.refs_0_, bf16[4,32,128]{2,1,0:T(8,128)(2,1)} %reduce_sum.25.refs_1_, f32[4,2,32,128]{3,2,1,0:T(8,128)} %pad_maximum_fusion.1.refs_2_, ...), custom_call_target="tpu_custom_call" | custom-call | tf_op jit(solution)/shard_map/detect/pallas_call | solution.py:638
  182.2 0.7 slice_reduce_fusion
  182.9 0.1 reshape_squeeze.3
  182.9 0.6 copy.31
  (63 shorter events, 1.3 us)
Async XLA Ops:
  0.0 18.0 %copy-start.8 = (s32[32,4]{0,1:T(4,128)S(1)}, s32[32,4]{0,1:T(4,128)}, u32[]{:S(2)}) copy-start(s32[32,4]{0,1:T(4,128)} %param.23) | copy-start | bytes 1540
  10.7 28.9 %all-to-all-start.1 = ((bf16[8,2,208,128]{3,2,1,0:T(8,128)(2,1)}), bf16[8,2,208,128]{3,2,1,0:T(8,128)(2,1)S(1)}, u32[]{:S(2)}, u32[]{:S(2)}) async-start(bf16[8,2,208,128]{3,2,1,0:T(8,128)(2,1)} %forward_x.3), calls=%async_computation.1 | async-start | bytes 1703936 | tf_op jit(solution)/shard_map/all_to_all | solution.py:747
  19.7 10.7 %copy-start.7 = (s32[4,2]{0,1:T(2,128)S(1)}, s32[4,2]{0,1:T(2,128)}, u32[]{:S(2)}) copy-start(s32[4,2]{0,1:T(2,128)} %param.21) | copy-start | bytes 100
  19.7 29.6 %copy-start.9 = (s32[128]{0:T(128)S(1)}, s32[128]{0:T(128)}, u32[]{:S(2)}) copy-start(s32[128]{0:T(128)} %constant.269.clone) | copy-start | bytes 1540
  39.6 10.3 %copy-start.1 = (bf16[8,2,208,128]{3,2,1,0:T(8,128)(2,1)}, bf16[8,2,208,128]{3,2,1,0:T(8,128)(2,1)S(1)}, u32[]{:S(2)}) copy-start(bf16[8,2,208,128]{3,2,1,0:T(8,128)(2,1)S(1)} %all-to-all-done.1.lines) | copy-start | bytes 2555908
  39.6 25.3 %all-to-all-start = ((bf16[8,2,208,128]{3,2,1,0:T(8,128)(2,1)}), bf16[8,2,208,128]{3,2,1,0:T(8,128)(2,1)S(1)}, u32[]{:S(2)}, u32[]{:S(2)}) async-start(bf16[8,2,208,128]{3,2,1,0:T(8,128)(2,1)} %forward_x.2), calls=%async_computation | async-start | bytes 1703936 | tf_op jit(solution)/shard_map/all_to_all | solution.py:747
  46.1 20.5 %collective-permute-start = (bf16[8,2,208,128]{3,2,1,0:T(8,128)(2,1)S(1)}, bf16[8,2,208,128]{3,2,1,0:T(8,128)(2,1)S(1)}, u32[]{:S(2)}, u32[]{:S(2)}) collective-permute-start(bf16[8,2,208,128]{3,2,1,0:T(8,128)(2,1)S(1)} %all-to-all-done.1.lines), channel_id=1, source_target_pairs={{0,2},{1,3},{2,0},{3,1},{4,6},{5,7},{6,4},{7,5},{8,10},{9,11},{10,... | collective-permute-start | bytes 2555912 | tf_op jit(solution)/shard_map/ppermute | solution.py:753
  64.9 2.7 %copy-start = (bf16[8,2,208,128]{3,2,1,0:T(8,128)(2,1)}, bf16[8,2,208,128]{3,2,1,0:T(8,128)(2,1)S(1)}, u32[]{:S(2)}) copy-start(bf16[8,2,208,128]{3,2,1,0:T(8,128)(2,1)S(1)} %all-to-all-done.value) | copy-start | bytes 2555908
  66.6 1.0 copy-start.2
  67.6 19.9 %collective-permute-start.2 = (bf16[8,2,208,128]{3,2,1,0:T(8,128)(2,1)}, bf16[8,2,208,128]{3,2,1,0:T(8,128)(2,1)S(1)}, u32[]{:S(2)}, u32[]{:S(2)}) collective-permute-start(bf16[8,2,208,128]{3,2,1,0:T(8,128)(2,1)} %order.2.lines), channel_id=1, source_target_pairs={{0,2},{1,3},{2,0},{3,1},{4,6},{5,7},{6,4},{7,5},{8,10},{9,11},{10,... | collective-permute-start | bytes 2555912 | tf_op jit(solution)/shard_map/ppermute | solution.py:753
  75.2 26.1 %collective-permute-start.1 = (bf16[32,208,128]{2,1,0:T(8,128)(2,1)}, bf16[32,208,128]{2,1,0:T(8,128)(2,1)S(1)}, u32[]{:S(2)}, u32[]{:S(2)}) collective-permute-start(bf16[32,208,128]{2,1,0:T(8,128)(2,1)} %forward_y.2.refs_0_), channel_id=1, source_target_pairs={{0,1},{1,0},{2,3},{3,2},{4,5},{5,4},{6,7},{7,6},{8,9},{9,8},{10,11... | collective-permute-start | bytes 5111816 | tf_op jit(solution)/shard_map/ppermute | solution.py:753
  87.5 0.9 copy-start.6
  94.5 17.4 %collective-permute-start.3 = (bf16[32,208,128]{2,1,0:T(8,128)(2,1)}, bf16[32,208,128]{2,1,0:T(8,128)(2,1)}, u32[]{:S(2)}, u32[]{:S(2)}) collective-permute-start(bf16[32,208,128]{2,1,0:T(8,128)(2,1)} %forward_y.3.refs_0_.rest_0_), channel_id=1, source_target_pairs={{0,1},{1,0},{2,3},{3,2},{4,5},{5,4},{6,7},{7,6},{8,9},{9,8},{10,11... | collective-permute-start | bytes 5111816 | tf_op jit(solution)/shard_map/ppermute | solution.py:753
  94.5 26.9 %all-to-all-start.2 = ((bf16[8,4,32,128]{3,2,1,0:T(8,128)(2,1)}), bf16[8,4,32,128]{3,2,1,0:T(8,128)(2,1)S(1)}, u32[]{:S(2)}, u32[]{:S(2)}) async-start(bf16[8,4,32,128]{3,2,1,0:T(8,128)(2,1)} %order.3), calls=%async_computation.2 | async-start | bytes 524288 | tf_op jit(solution)/shard_map/all_to_all | solution.py:747
  101.3 1.2 copy-start.5
  121.4 0.7 copy-start.3
  130.8 14.2 %collective-permute-start.6 = (bf16[16,2,4,16,128]{4,3,2,1,0:T(8,128)(2,1)}, bf16[16,2,4,16,128]{4,3,2,1,0:T(8,128)(2,1)S(1)}, u32[]{:S(2)}, u32[]{:S(2)}) collective-permute-start(bf16[16,2,4,16,128]{4,3,2,1,0:T(8,128)(2,1)} %get-tuple-element.12), channel_id=1, source_target_pairs={{0,8},{4,12},{8,0},{12,4},{16,24},{20,28},{24,16},{28,20},{1,9},{5... | collective-permute-start | bytes 1572872 | tf_op jit(solution)/shard_map/ppermute | solution.py:817
  133.0 15.1 %collective-permute-start.4 = (bf16[16,2,4,16,128]{4,3,2,1,0:T(8,128)(2,1)}, bf16[16,2,4,16,128]{4,3,2,1,0:T(8,128)(2,1)S(1)}, u32[]{:S(2)}, u32[]{:S(2)}) collective-permute-start(bf16[16,2,4,16,128]{4,3,2,1,0:T(8,128)(2,1)} %get-tuple-element.9.refs_3_), channel_id=1, source_target_pairs={{0,4},{4,0},{8,12},{12,8},{16,20},{20,16},{24,28},{28,24},{1,5},{5... | collective-permute-start | bytes 1572872 | tf_op jit(solution)/shard_map/ppermute | solution.py:817
  143.6 7.3 %copy-start.10 = (f32[4]{0:T(128)S(1)}, f32[4]{0:T(128)}, u32[]{:S(2)}) copy-start(f32[4]{0:T(128)} %param.22) | copy-start | bytes 52
  146.3 7.6 %collective-permute-start.7 = (bf16[8,2,4,16,128]{4,3,2,1,0:T(8,128)(2,1)S(1)}, bf16[8,2,4,16,128]{4,3,2,1,0:T(8,128)(2,1)S(1)}, u32[]{:S(2)}, u32[]{:S(2)}) collective-permute-start(bf16[8,2,4,16,128]{4,3,2,1,0:T(8,128)(2,1)S(1)} %slice.72), channel_id=1, source_target_pairs={{0,4},{4,0},{8,12},{12,8},{16,20},{20,16},{24,28},{28,24},{1,5},{5... | collective-permute-start | bytes 786440 | tf_op jit(solution)/shard_map/ppermute | solution.py:817
  148.1 13.8 %copy-start.11 = (s32[32]{0:T(128)S(1)}, s32[32]{0:T(128)}, u32[]{:S(2)}) copy-start(s32[32]{0:T(128)} %param.24) | copy-start | bytes 388
  148.1 16.1 %copy-start.4 = (bf16[8,4,32,128]{3,2,1,0:T(8,128)(2,1)S(1)}, bf16[8,4,32,128]{3,2,1,0:T(8,128)(2,1)}, u32[]{:S(2)}) copy-start(bf16[8,4,32,128]{3,2,1,0:T(8,128)(2,1)} %copy-done.3) | copy-start | bytes 786436
  149.4 7.1 %collective-permute-start.5 = (bf16[8,2,4,16,128]{4,3,2,1,0:T(8,128)(2,1)S(1)}, bf16[8,2,4,16,128]{4,3,2,1,0:T(8,128)(2,1)S(1)}, u32[]{:S(2)}, u32[]{:S(2)}) collective-permute-start(bf16[8,2,4,16,128]{4,3,2,1,0:T(8,128)(2,1)S(1)} %slice.73), channel_id=1, source_target_pairs={{0,8},{4,12},{8,0},{12,4},{16,24},{20,28},{24,16},{28,20},{1,9},{5... | collective-permute-start | bytes 786440 | tf_op jit(solution)/shard_map/ppermute | solution.py:817
  157.5 19.8 %all-to-all-start.3 = ((bf16[8,2,4,32,128]{4,3,2,1,0:T(8,128)(2,1)}), bf16[8,2,4,32,128]{4,3,2,1,0:T(8,128)(2,1)S(1)}, u32[]{:S(2)}, u32[]{:S(2)}) async-start(bf16[8,2,4,32,128]{4,3,2,1,0:T(8,128)(2,1)} %pad_maximum_fusion), calls=%async_computation.3 | async-start | bytes 1048576 | tf_op jit(solution)/shard_map/all_to_all | solution.py:830

commit v11 on v10

--- a/solution.py
+++ b/solution.py
@@ -381,7 +381,7 @@
                         ]
             return carry
 
-        lax.fori_loop(0, count, pair, 0, unroll=4)
+        lax.fori_loop(0, count, pair, 0, unroll=8)
 
     @pl.when(step >= steps)
     def _():
@@ -403,7 +403,7 @@
                         ]
             return carry
 
-        lax.fori_loop(0, each, line, 0, unroll=4)
+        lax.fori_loop(0, each, line, 0, unroll=8)
 
 
 def inverse(which, sel, specs, freq_y, square_x, table_y, table_x, after):
@@ -488,7 +488,7 @@
             held[pl.ds(spot, tiles, stride=pitch), :] = total
         return carry
 
-    lax.fori_loop(0, each, line, 0, unroll=4)
+    lax.fori_loop(0, each, line, 0, unroll=8)
 
     for p, out in enumerate(outs):
 
@@ -792,7 +792,7 @@
             lines = lines.transpose(0, 2, 3, 4, 1, 5).reshape(-1, HIGH // PARTS, ROWS, LANES)
         if part:
             crops = crop(rows, tile_x // 2, tile_x % 2, mine, pot_second, earlier[0])
-            lines = order(lines, [crops, square_x, places] + [r[0] for r in received[1:]])
+            lines = order(lines, [crops, square_x, places, scalars] + [r[0] for r in received[1:]])
         for f in range(far):
             received[f].append(swap(lines, f * near) if f else lines)
         if part == 0:
@@ -801,13 +801,14 @@
     for f in range(far):
         spec = forward_y(received[f][1], section_y, earlier[f], last_y, [])
         ready = [spec] + [swap(spec, x) for x in range(1, near)]
+        if f == 0:
+            crops = order(crops.reshape(field_count, own_slots, HALF, LANES), [spec])
+            crops = trade(crops, "beam")
         waves.append(
             inverse(
                 f * near, scalars, ready, freq_y, square_x, inverse_y, inverse_x, waves[-1:]
             )
         )
-    crops = order(crops.reshape(field_count, own_slots, HALF, LANES), [spec])
-    crops = trade(crops, "beam")
     owners = field_count // 2 * hold_count
     other = collect(waves, k1_pairs, places, owners, 0, [crops])
     partial = other + collect(waves, k1_pairs, places, owners, 1, other[:1])

time: 184 us -> 181 us (0.984)
  Pallas kernels: 87.6 us -> 83.4 us
    pallas_call x2, Pallas kernels: 18.8 us -> 16.1 us  [inverse(): pl.pallas_call(functools.partial(inverse_kernel, steps, which, near), gri...]
  transfers between devices with their start and end apart: 12 -> 12, of which waited for: 8 -> 8; matrix products, arithmetic and copies ran while one was open for 8% -> 8% of each run, Pallas kernels for 35% -> 34%
where the time goes in v11:
time: 181 us; the launch traced here: 180 us
  Pallas kernels  83.4 us (46%)
  waiting for transfers between devices  42.8 us (24%)
  starting transfers between devices  30.7 us (17%)
  other arithmetic  11.2 us (6%)
  local copies, waits for them, and re-layouts  10 us (6%)
    pallas_call x2, Pallas kernels, forward_x(): pl.pallas_call(forward_x_kernel, grid_spec=pltpu.PrefetchScalarGridSpec(n...  21.4 us
    all_to_all x3, starting transfers between devices, trade(): return lax.all_to_all(value, axis, split_axis=0, concat_axis=0, tiled=True)  16.3 us
    pallas_call x2, Pallas kernels, inverse(): pl.pallas_call(functools.partial(inverse_kernel, steps, which, near), gri...  16.1 us
    pallas_call x2, Pallas kernels, collect(): pl.pallas_call(functools.partial(collect_kernel, len(sheets)), grid_spec=...  15.8 us
    all_to_all x1, waiting for transfers between devices, shards(): lax.all_to_all(tiles, ('beam', 'slab'), split_axis=0, concat_axis=0, axis...  12.5 us
    pallas_call x2, Pallas kernels, forward_y(): pl.pallas_call(forward_y_kernel, grid=(1 + steps,), in_specs=[pl.BlockSpe...  12.2 us
    all_to_all x3, waiting for transfers between devices, trade(): return lax.all_to_all(value, axis, split_axis=0, concat_axis=0, tiled=True)  11.4 us
    ppermute x4, waiting for transfers between devices, swap(): return lax.ppermute(value, 'slab', [(i, i ^ x) for i in range(hold_count)])  11.4 us
  transfers between devices with their start and end apart: 12, of which 8 were waited for; matrix products, arithmetic and copies ran while one was open for 8% of the time, Pallas kernels for 34%

profile of v11, /device:TPU:0, one launch (start us, length us, event | category | flops | bytes accessed | tf_op | source)
XLA Modules:
  0.0 179.6 jit_solution(5703950164068751276)
XLA Ops:
  0.0 10.7 %forward_x.3 = bf16[8,2,208,128]{3,2,1,0:T(8,128)(2,1)} custom-call(s32[1]{0:T(128)} %bitcast.3.sel, bf16[8,4,16,4096]{3,2,1,0:T(8,128)(2,1)} %bitcast.40, bf16[4,512,1024]{2,1,0:T(8,128)(2,1)} %constant.270.clone.section, bf16[4,8,208,256]{3,2,1,0:T(8,128)(2,1)} %constant.271.clone.last, bf16[128,128]{1,0:T(8,128)(2,1)} %constant.272.clone.perm), custom_call_target="tpu_custom_call" | custom-call | flops 1048576 | tf_op jit(solution)/shard_map/forward_x/pallas_call | solution.py:198
  10.7 7.3 %all-to-all-start.1 = ((bf16[8,2,208,128]{3,2,1,0:T(8,128)(2,1)}), bf16[8,2,208,128]{3,2,1,0:T(8,128)(2,1)S(1)}, u32[]{:S(2)}, u32[]{:S(2)}) async-start(bf16[8,2,208,128]{3,2,1,0:T(8,128)(2,1)} %forward_x.3), calls=%async_computation.1 | async-start | bytes 1703936 | tf_op jit(solution)/shard_map/all_to_all | solution.py:747
  18.1 0.1 reshape_reshape.3
  18.3 0.6 fusion.24
  19.6 0.1 copy.28
  19.9 0.6 gather_fusion
  20.4 0.6 gather_fusion.1
  21.0 0.1 stack.54
  21.1 10.7 %forward_x.2 = bf16[8,2,208,128]{3,2,1,0:T(8,128)(2,1)} custom-call(s32[1]{0:T(128)} %bitcast.3.sel, bf16[8,4,16,4096]{3,2,1,0:T(8,128)(2,1)} %bitcast.41, bf16[4,512,1024]{2,1,0:T(8,128)(2,1)} %constant.270.clone.section, bf16[4,8,208,256]{3,2,1,0:T(8,128)(2,1)} %constant.271.clone.last, bf16[128,128]{1,0:T(8,128)(2,1)} %constant.272.clone.perm), custom_call_target="tpu_custom_call" | custom-call | flops 1048576 | tf_op jit(solution)/shard_map/forward_x/pallas_call | solution.py:198
  32.0 7.6 %all-to-all-done.1.lines = bf16[8,2,208,128]{3,2,1,0:T(8,128)(2,1)S(1)} async-done(((bf16[8,2,208,128]{3,2,1,0:T(8,128)(2,1)}), bf16[8,2,208,128]{3,2,1,0:T(8,128)(2,1)S(1)}, u32[]{:S(2)}, u32[]{:S(2)}) %all-to-all-start.1) | async-done | bytes 852000 | tf_op jit(solution)/shard_map/all_to_all | solution.py:747
  39.6 3.5 %all-to-all-start = ((bf16[8,2,208,128]{3,2,1,0:T(8,128)(2,1)}), bf16[8,2,208,128]{3,2,1,0:T(8,128)(2,1)S(1)}, u32[]{:S(2)}, u32[]{:S(2)}) async-start(bf16[8,2,208,128]{3,2,1,0:T(8,128)(2,1)} %forward_x.2), calls=%async_computation | async-start | bytes 1703936 | tf_op jit(solution)/shard_map/all_to_all | solution.py:747
  43.2 0.1 stack.55
  44.0 0.7 reshape.1008.rest_3_.sel
  44.7 0.1 copy.27
  44.9 1.4 fusion.15
  46.3 0.6 broadcast_add_fusion
  46.9 1.5 collective-permute-start
  48.4 0.5 compare_convert_fusion
  48.9 0.5 and_select_fusion.5
  49.4 0.6 and_select_fusion.6
  50.0 0.7 multiply_convert_fusion.rest_1_.refs_3_
  50.6 3.3 %forward_y_first.2.after.earlier = bf16[64,2,32,128]{3,2,1,0:T(8,128)(2,1)} custom-call(bf16[8,2,208,128]{3,2,1,0:T(8,128)(2,1)} %copy-done.1, bf16[512,256]{1,0:T(8,128)(2,1)} %constant.273.clone.section), custom_call_target="tpu_custom_call" | custom-call | flops 1048576 | tf_op jit(solution)/shard_map/forward_y_first/pallas_call | solution.py:270
  54.0 7.1 %crop.1.rest_0_ = bf16[32,32,128]{2,1,0:T(8,128)(2,1)} custom-call(s32[32]{0:T(128)} %get-tuple-element.38.rows, s32[32]{0:T(128)} %get-tuple-element.37.cols, s32[32]{0:T(128)} %get-tuple-element.18.odd, s32[32]{0:T(128)} %get-tuple-element.15.mine, bf16[512,4096]{1,0:T(8,128)(2,1)} %pot.1, bf16[64,2,32,128]{3,2,1,0:T(8,128)(2,1)} %forward_y_first.2.after.earlier), custom_call_target="tpu_custom_call" | custom-call | flops 1048576 | tf_op jit(solution)/shard_map/crop/pallas_call | solution.py:572
  61.1 3.8 %all-to-all-done.value = bf16[8,2,208,128]{3,2,1,0:T(8,128)(2,1)S(1)} async-done(((bf16[8,2,208,128]{3,2,1,0:T(8,128)(2,1)}), bf16[8,2,208,128]{3,2,1,0:T(8,128)(2,1)S(1)}, u32[]{:S(2)}, u32[]{:S(2)}) %all-to-all-start) | async-done | bytes 852000 | tf_op jit(solution)/shard_map/all_to_all | solution.py:747
  64.9 2.5 %collective-permute-done.rest_4_.lines = bf16[8,2,208,128]{3,2,1,0:T(8,128)(2,1)S(1)} collective-permute-done((bf16[8,2,208,128]{3,2,1,0:T(8,128)(2,1)S(1)}, bf16[8,2,208,128]{3,2,1,0:T(8,128)(2,1)S(1)}, u32[]{:S(2)}, u32[]{:S(2)}) %collective-permute-start) | collective-permute-done | bytes 852000 | tf_op jit(solution)/shard_map/ppermute | solution.py:753
  67.4 1.0 broadcast_in_dim.2.rest_2_.refs_2_
  68.4 1.5 collective-permute-start.2
  69.9 6.1 %forward_y.2.refs_0_.rest_0_ = bf16[32,208,128]{2,1,0:T(8,128)(2,1)} custom-call(bf16[8,2,208,128]{3,2,1,0:T(8,128)(2,1)} %order.2.lines, bf16[512,256]{1,0:T(8,128)(2,1)} %constant.273.clone.section, bf16[64,2,32,128]{3,2,1,0:T(8,128)(2,1)} %forward_y_first.2.after.earlier, bf16[32,208,256]{2,1,0:T(8,128)(2,1)} %constant.274.clone.last), custom_call_target="tpu_custom_call" | custom-call | flops 1048576 | tf_op jit(solution)/shard_map/forward_y/pallas_call | solution.py:316
  76.1 3.4 %forward_y_first.3.earlier = bf16[64,2,32,128]{3,2,1,0:T(8,128)(2,1)} custom-call(bf16[8,2,208,128]{3,2,1,0:T(8,128)(2,1)} %copy-done.2, bf16[512,256]{1,0:T(8,128)(2,1)} %constant.273.clone.section), custom_call_target="tpu_custom_call" | custom-call | flops 1048576 | tf_op jit(solution)/shard_map/forward_y_first/pallas_call | solution.py:270
  79.4 8.9 %collective-permute-done.2.lines = bf16[8,2,208,128]{3,2,1,0:T(8,128)(2,1)S(1)} collective-permute-done((bf16[8,2,208,128]{3,2,1,0:T(8,128)(2,1)}, bf16[8,2,208,128]{3,2,1,0:T(8,128)(2,1)S(1)}, u32[]{:S(2)}, u32[]{:S(2)}) %collective-permute-start.2) | collective-permute-done | bytes 852000 | tf_op jit(solution)/shard_map/ppermute | solution.py:753
  88.3 0.9 copy-done.6
  89.2 6.1 %forward_y.3.refs_0_ = bf16[32,208,128]{2,1,0:T(8,128)(2,1)} custom-call(bf16[8,2,208,128]{3,2,1,0:T(8,128)(2,1)} %copy-done.6, bf16[512,256]{1,0:T(8,128)(2,1)} %constant.273.clone.section, bf16[64,2,32,128]{3,2,1,0:T(8,128)(2,1)} %forward_y_first.3.earlier, bf16[32,208,256]{2,1,0:T(8,128)(2,1)} %constant.274.clone.last), custom_call_target="tpu_custom_call" | custom-call | flops 1048576 | tf_op jit(solution)/shard_map/forward_y/pallas_call | solution.py:316
  95.3 5.5 %all-to-all-start.2 = ((bf16[8,4,32,128]{3,2,1,0:T(8,128)(2,1)}), bf16[8,4,32,128]{3,2,1,0:T(8,128)(2,1)S(1)}, u32[]{:S(2)}, u32[]{:S(2)}) async-start(bf16[8,4,32,128]{3,2,1,0:T(8,128)(2,1)} %order.3), calls=%async_computation.2 | async-start | bytes 524288 | tf_op jit(solution)/shard_map/all_to_all | solution.py:747
  100.8 1.2 copy-done.5
  102.0 8.0 %inverse.2.refs_7_.refs_0_ = bf16[32,256,256]{2,1,0:T(8,128)(2,1)} custom-call(s32[12]{0:T(128)} %reshape.1008.rest_3_.sel, bf16[32,208,128]{2,1,0:T(8,128)(2,1)} %forward_y.2.refs_0_.rest_0_, bf16[32,208,128]{2,1,0:T(8,128)(2,1)} %copy-done.5, f32[208,128]{1,0:T(8,128)} %constant.275.clone.refs_2_, f32[4,1,128]{2,1,0:T(1,128)} %multiply_convert_fusion.rest_1_.refs_3_, ...), custom_call_target="tpu_custom_call" | custom-call | flops 1048576 | tf_op jit(solution)/shard_map/inverse/pallas_call | solution.py:424
  110.0 8.1 %inverse.3.refs_1_ = bf16[32,256,256]{2,1,0:T(8,128)(2,1)} custom-call(s32[12]{0:T(128)} %reshape.1008.rest_3_.sel, bf16[32,208,128]{2,1,0:T(8,128)(2,1)} %forward_y.3.refs_0_, bf16[32,208,128]{2,1,0:T(8,128)(2,1)} %collective-permute-done.3.refs_1_, f32[208,128]{1,0:T(8,128)} %constant.275.clone.refs_2_, f32[4,1,128]{2,1,0:T(1,128)} %multiply_convert_fusion.rest_1_.refs_3_, ...), custom_call_target="tpu_custom_call" | custom-call | flops 1048576 | tf_op jit(solution)/shard_map/inverse/pallas_call | solution.py:424
  118.1 0.7 copy-done.3
  118.8 7.9 %collect.2 = (bf16[16,2,4,16,128]{4,3,2,1,0:T(8,128)(2,1)}, bf16[16,2,4,16,128]{4,3,2,1,0:T(8,128)(2,1)}) custom-call(s32[4]{0:T(128)} %get-tuple-element.14.k1_pairs, bf16[32,256,256]{2,1,0:T(8,128)(2,1)} %inverse.2.refs_7_.refs_0_, bf16[32,256,256]{2,1,0:T(8,128)(2,1)} %inverse.3.refs_1_, s32[2,2,2,64,128]{4,3,2,1,0:T(8,128)} %broadcast_in_dim.2.rest_2_.refs_2_, ...), custom_call_target="tpu_custom_call" | custom-call | flops 1048576 | tf_op jit(solution)/shard_map/collect/pallas_call | solution.py:515
  126.8 2.0 %collective-permute-start.6 = (bf16[16,2,4,16,128]{4,3,2,1,0:T(8,128)(2,1)}, bf16[16,2,4,16,128]{4,3,2,1,0:T(8,128)(2,1)S(1)}, u32[]{:S(2)}, u32[]{:S(2)}) collective-permute-start(bf16[16,2,4,16,128]{4,3,2,1,0:T(8,128)(2,1)} %get-tuple-element.12), channel_id=1, source_target_pairs={{0,8},{4,12},{8,0},{12,4},{16,24},{20,28},{24,16},{28,20},{1,9},{5... | collective-permute-start | bytes 1572872 | tf_op jit(solution)/shard_map/ppermute | solution.py:818
  128.8 1.5 collective-permute-start.4
  130.3 0.1 add.417
  130.4 0.2 dynamic-slice_reduce_fusion
  131.0 7.9 %collect.3 = (bf16[16,2,4,16,128]{4,3,2,1,0:T(8,128)(2,1)}, bf16[16,2,4,16,128]{4,3,2,1,0:T(8,128)(2,1)}) custom-call(s32[4]{0:T(128)} %get-tuple-element.14.k1_pairs, bf16[32,256,256]{2,1,0:T(8,128)(2,1)} %inverse.2.refs_7_.refs_0_, bf16[32,256,256]{2,1,0:T(8,128)(2,1)} %inverse.3.refs_1_, s32[2,2,2,64,128]{4,3,2,1,0:T(8,128)} %broadcast_in_dim.2.rest_2_.refs_2_, ...), custom_call_target="tpu_custom_call" | custom-call | flops 1048576 | tf_op jit(solution)/shard_map/collect/pallas_call | solution.py:515
  138.9 2.1 %collective-permute-done.6 = bf16[16,2,4,16,128]{4,3,2,1,0:T(8,128)(2,1)S(1)} collective-permute-done((bf16[16,2,4,16,128]{4,3,2,1,0:T(8,128)(2,1)}, bf16[16,2,4,16,128]{4,3,2,1,0:T(8,128)(2,1)S(1)}, u32[]{:S(2)}, u32[]{:S(2)}) %collective-permute-start.6) | collective-permute-done | bytes 524320 | tf_op jit(solution)/shard_map/ppermute | solution.py:818
  141.0 1.2 convert_add_fusion
  142.3 1.8 %collective-permute-start.7 = (bf16[8,2,4,16,128]{4,3,2,1,0:T(8,128)(2,1)S(1)}, bf16[8,2,4,16,128]{4,3,2,1,0:T(8,128)(2,1)S(1)}, u32[]{:S(2)}, u32[]{:S(2)}) collective-permute-start(bf16[8,2,4,16,128]{4,3,2,1,0:T(8,128)(2,1)S(1)} %slice.72), channel_id=1, source_target_pairs={{0,4},{4,0},{8,12},{12,8},{16,20},{20,16},{24,28},{28,24},{1,5},{5... | collective-permute-start | bytes 786440 | tf_op jit(solution)/shard_map/ppermute | solution.py:818
  144.1 1.3 convert_add_fusion.1
  145.4 1.5 collective-permute-start.5
  146.9 0.1 fusion.23
  147.1 2.9 %collective-permute-done.7 = bf16[8,2,4,16,128]{4,3,2,1,0:T(8,128)(2,1)S(1)} collective-permute-done((bf16[8,2,4,16,128]{4,3,2,1,0:T(8,128)(2,1)S(1)}, bf16[8,2,4,16,128]{4,3,2,1,0:T(8,128)(2,1)S(1)}, u32[]{:S(2)}, u32[]{:S(2)}) %collective-permute-start.7) | collective-permute-done | bytes 262176 | tf_op jit(solution)/shard_map/ppermute | solution.py:818
  150.1 2.4 %collective-permute-done.5 = bf16[8,2,4,16,128]{4,3,2,1,0:T(8,128)(2,1)S(1)} collective-permute-done((bf16[8,2,4,16,128]{4,3,2,1,0:T(8,128)(2,1)S(1)}, bf16[8,2,4,16,128]{4,3,2,1,0:T(8,128)(2,1)S(1)}, u32[]{:S(2)}, u32[]{:S(2)}) %collective-permute-start.5) | collective-permute-done | bytes 262176 | tf_op jit(solution)/shard_map/ppermute | solution.py:818
  152.6 0.9 pad_maximum_fusion
  153.5 4.6 %all-to-all-start.3 = ((bf16[8,2,4,32,128]{4,3,2,1,0:T(8,128)(2,1)}), bf16[8,2,4,32,128]{4,3,2,1,0:T(8,128)(2,1)S(1)}, u32[]{:S(2)}, u32[]{:S(2)}) async-start(bf16[8,2,4,32,128]{4,3,2,1,0:T(8,128)(2,1)} %pad_maximum_fusion), calls=%async_computation.3 | async-start | bytes 1048576 | tf_op jit(solution)/shard_map/all_to_all | solution.py:831
  158.0 0.6 dynamic_slice.18.counts
  158.6 0.6 pad_maximum_fusion.2.alpha
  159.2 0.3 fusion.6
  159.6 0.7 pad_maximum_fusion.1.refs_2_
  160.3 0.7 reduce_sum.25.refs_1_
  160.9 12.5 %all-to-all-done.3 = bf16[8,2,4,32,128]{4,3,2,1,0:T(8,128)(2,1)S(1)} async-done(((bf16[8,2,4,32,128]{4,3,2,1,0:T(8,128)(2,1)}), bf16[8,2,4,32,128]{4,3,2,1,0:T(8,128)(2,1)S(1)}, u32[]{:S(2)}, u32[]{:S(2)}) %all-to-all-start.3) | async-done | bytes 524320 | tf_op jit(solution)/shard_map/all_to_all | solution.py:831
  173.4 0.8 reduce_sum.24.refs_0_
  174.2 4.0 %detect.1 = f32[1,256]{1,0:T(1,128)} custom-call(f32[2,4,12]{2,1,0:T(4,128)} %pad_maximum_fusion.2.alpha, s32[1]{0:T(128)} %dynamic_slice.18.counts, bf16[4,2,4,32,128]{4,3,2,1,0:T(8,128)(2,1)} %reduce_sum.24.refs_0_, bf16[4,32,128]{2,1,0:T(8,128)(2,1)} %reduce_sum.25.refs_1_, f32[4,2,32,128]{3,2,1,0:T(8,128)} %pad_maximum_fusion.1.refs_2_, ...), custom_call_target="tpu_custom_call" | custom-call | tf_op jit(solution)/shard_map/detect/pallas_call | solution.py:638
  178.3 0.7 slice_reduce_fusion
  178.9 0.1 reshape_squeeze.3
  179.0 0.6 copy.31
  (63 shorter events, 1.3 us)
Async XLA Ops:
  0.0 18.0 %copy-start.8 = (s32[32,4]{0,1:T(4,128)S(1)}, s32[32,4]{0,1:T(4,128)}, u32[]{:S(2)}) copy-start(s32[32,4]{0,1:T(4,128)} %param.23) | copy-start | bytes 1540
  0.0 18.2 %copy-start.7 = (s32[4,2]{0,1:T(2,128)S(1)}, s32[4,2]{0,1:T(2,128)}, u32[]{:S(2)}) copy-start(s32[4,2]{0,1:T(2,128)} %param.21) | copy-start | bytes 100
  10.7 28.9 %all-to-all-start.1 = ((bf16[8,2,208,128]{3,2,1,0:T(8,128)(2,1)}), bf16[8,2,208,128]{3,2,1,0:T(8,128)(2,1)S(1)}, u32[]{:S(2)}, u32[]{:S(2)}) async-start(bf16[8,2,208,128]{3,2,1,0:T(8,128)(2,1)} %forward_x.3), calls=%async_computation.1 | async-start | bytes 1703936 | tf_op jit(solution)/shard_map/all_to_all | solution.py:747
  21.1 28.9 %copy-start.9 = (s32[128]{0:T(128)S(1)}, s32[128]{0:T(128)}, u32[]{:S(2)}) copy-start(s32[128]{0:T(128)} %constant.269.clone) | copy-start | bytes 1540
  39.6 11.0 %copy-start.1 = (bf16[8,2,208,128]{3,2,1,0:T(8,128)(2,1)}, bf16[8,2,208,128]{3,2,1,0:T(8,128)(2,1)S(1)}, u32[]{:S(2)}) copy-start(bf16[8,2,208,128]{3,2,1,0:T(8,128)(2,1)S(1)} %all-to-all-done.1.lines) | copy-start | bytes 2555908
  39.6 25.3 %all-to-all-start = ((bf16[8,2,208,128]{3,2,1,0:T(8,128)(2,1)}), bf16[8,2,208,128]{3,2,1,0:T(8,128)(2,1)S(1)}, u32[]{:S(2)}, u32[]{:S(2)}) async-start(bf16[8,2,208,128]{3,2,1,0:T(8,128)(2,1)} %forward_x.2), calls=%async_computation | async-start | bytes 1703936 | tf_op jit(solution)/shard_map/all_to_all | solution.py:747
  46.9 20.5 %collective-permute-start = (bf16[8,2,208,128]{3,2,1,0:T(8,128)(2,1)S(1)}, bf16[8,2,208,128]{3,2,1,0:T(8,128)(2,1)S(1)}, u32[]{:S(2)}, u32[]{:S(2)}) collective-permute-start(bf16[8,2,208,128]{3,2,1,0:T(8,128)(2,1)S(1)} %all-to-all-done.1.lines), channel_id=1, source_target_pairs={{0,2},{1,3},{2,0},{3,1},{4,6},{5,7},{6,4},{7,5},{8,10},{9,11},{10,... | collective-permute-start | bytes 2555912 | tf_op jit(solution)/shard_map/ppermute | solution.py:753
  64.9 3.5 %copy-start = (bf16[8,2,208,128]{3,2,1,0:T(8,128)(2,1)}, bf16[8,2,208,128]{3,2,1,0:T(8,128)(2,1)S(1)}, u32[]{:S(2)}) copy-start(bf16[8,2,208,128]{3,2,1,0:T(8,128)(2,1)S(1)} %all-to-all-done.value) | copy-start | bytes 2555908
  67.4 1.0 copy-start.2
  68.4 19.9 %collective-permute-start.2 = (bf16[8,2,208,128]{3,2,1,0:T(8,128)(2,1)}, bf16[8,2,208,128]{3,2,1,0:T(8,128)(2,1)S(1)}, u32[]{:S(2)}, u32[]{:S(2)}) collective-permute-start(bf16[8,2,208,128]{3,2,1,0:T(8,128)(2,1)} %order.2.lines), channel_id=1, source_target_pairs={{0,2},{1,3},{2,0},{3,1},{4,6},{5,7},{6,4},{7,5},{8,10},{9,11},{10,... | collective-permute-start | bytes 2555912 | tf_op jit(solution)/shard_map/ppermute | solution.py:753
  76.1 24.7 %collective-permute-start.1 = (bf16[32,208,128]{2,1,0:T(8,128)(2,1)}, bf16[32,208,128]{2,1,0:T(8,128)(2,1)S(1)}, u32[]{:S(2)}, u32[]{:S(2)}) collective-permute-start(bf16[32,208,128]{2,1,0:T(8,128)(2,1)} %forward_y.2.refs_0_.rest_0_), channel_id=1, source_target_pairs={{0,1},{1,0},{2,3},{3,2},{4,5},{5,4},{6,7},{7,6},{8,9},{9,8},{10,11... | collective-permute-start | bytes 5111816 | tf_op jit(solution)/shard_map/ppermute | solution.py:753
  88.3 0.9 copy-start.6
  95.3 14.7 %collective-permute-start.3 = (bf16[32,208,128]{2,1,0:T(8,128)(2,1)}, bf16[32,208,128]{2,1,0:T(8,128)(2,1)}, u32[]{:S(2)}, u32[]{:S(2)}) collective-permute-start(bf16[32,208,128]{2,1,0:T(8,128)(2,1)} %forward_y.3.refs_0_), channel_id=1, source_target_pairs={{0,1},{1,0},{2,3},{3,2},{4,5},{5,4},{6,7},{7,6},{8,9},{9,8},{10,11... | collective-permute-start | bytes 5111816 | tf_op jit(solution)/shard_map/ppermute | solution.py:753
  95.3 22.8 %all-to-all-start.2 = ((bf16[8,4,32,128]{3,2,1,0:T(8,128)(2,1)}), bf16[8,4,32,128]{3,2,1,0:T(8,128)(2,1)S(1)}, u32[]{:S(2)}, u32[]{:S(2)}) async-start(bf16[8,4,32,128]{3,2,1,0:T(8,128)(2,1)} %order.3), calls=%async_computation.2 | async-start | bytes 524288 | tf_op jit(solution)/shard_map/all_to_all | solution.py:747
  100.8 1.2 copy-start.5
  118.1 0.7 copy-start.3
  126.8 14.3 %collective-permute-start.6 = (bf16[16,2,4,16,128]{4,3,2,1,0:T(8,128)(2,1)}, bf16[16,2,4,16,128]{4,3,2,1,0:T(8,128)(2,1)S(1)}, u32[]{:S(2)}, u32[]{:S(2)}) collective-permute-start(bf16[16,2,4,16,128]{4,3,2,1,0:T(8,128)(2,1)} %get-tuple-element.12), channel_id=1, source_target_pairs={{0,8},{4,12},{8,0},{12,4},{16,24},{20,28},{24,16},{28,20},{1,9},{5... | collective-permute-start | bytes 1572872 | tf_op jit(solution)/shard_map/ppermute | solution.py:818
  128.8 15.3 %collective-permute-start.4 = (bf16[16,2,4,16,128]{4,3,2,1,0:T(8,128)(2,1)}, bf16[16,2,4,16,128]{4,3,2,1,0:T(8,128)(2,1)S(1)}, u32[]{:S(2)}, u32[]{:S(2)}) collective-permute-start(bf16[16,2,4,16,128]{4,3,2,1,0:T(8,128)(2,1)} %get-tuple-element.9.refs_3_), channel_id=1, source_target_pairs={{0,4},{4,0},{8,12},{12,8},{16,20},{20,16},{24,28},{28,24},{1,5},{5... | collective-permute-start | bytes 1572872 | tf_op jit(solution)/shard_map/ppermute | solution.py:818
  138.9 8.0 %copy-start.10 = (f32[4]{0:T(128)S(1)}, f32[4]{0:T(128)}, u32[]{:S(2)}) copy-start(f32[4]{0:T(128)} %param.22) | copy-start | bytes 52
  142.3 7.7 %collective-permute-start.7 = (bf16[8,2,4,16,128]{4,3,2,1,0:T(8,128)(2,1)S(1)}, bf16[8,2,4,16,128]{4,3,2,1,0:T(8,128)(2,1)S(1)}, u32[]{:S(2)}, u32[]{:S(2)}) collective-permute-start(bf16[8,2,4,16,128]{4,3,2,1,0:T(8,128)(2,1)S(1)} %slice.72), channel_id=1, source_target_pairs={{0,4},{4,0},{8,12},{12,8},{16,20},{20,16},{24,28},{28,24},{1,5},{5... | collective-permute-start | bytes 786440 | tf_op jit(solution)/shard_map/ppermute | solution.py:818
  144.1 13.9 %copy-start.11 = (s32[32]{0:T(128)S(1)}, s32[32]{0:T(128)}, u32[]{:S(2)}) copy-start(s32[32]{0:T(128)} %param.24) | copy-start | bytes 388
  144.1 16.2 %copy-start.4 = (bf16[8,4,32,128]{3,2,1,0:T(8,128)(2,1)S(1)}, bf16[8,4,32,128]{3,2,1,0:T(8,128)(2,1)}, u32[]{:S(2)}) copy-start(bf16[8,4,32,128]{3,2,1,0:T(8,128)(2,1)} %copy-done.3) | copy-start | bytes 786436
  145.4 7.1 %collective-permute-start.5 = (bf16[8,2,4,16,128]{4,3,2,1,0:T(8,128)(2,1)S(1)}, bf16[8,2,4,16,128]{4,3,2,1,0:T(8,128)(2,1)S(1)}, u32[]{:S(2)}, u32[]{:S(2)}) collective-permute-start(bf16[8,2,4,16,128]{4,3,2,1,0:T(8,128)(2,1)S(1)} %slice.73), channel_id=1, source_target_pairs={{0,8},{4,12},{8,0},{12,4},{16,24},{20,28},{24,16},{28,20},{1,9},{5... | collective-permute-start | bytes 786440 | tf_op jit(solution)/shard_map/ppermute | solution.py:818
  153.5 19.9 %all-to-all-start.3 = ((bf16[8,2,4,32,128]{4,3,2,1,0:T(8,128)(2,1)}), bf16[8,2,4,32,128]{4,3,2,1,0:T(8,128)(2,1)S(1)}, u32[]{:S(2)}, u32[]{:S(2)}) async-start(bf16[8,2,4,32,128]{4,3,2,1,0:T(8,128)(2,1)} %pad_maximum_fusion), calls=%async_computation.3 | async-start | bytes 1048576 | tf_op jit(solution)/shard_map/all_to_all | solution.py:831

commit v12 on v11

--- a/solution.py
+++ b/solution.py
@@ -156,25 +156,26 @@
     return jnp.dot(a, b, preferred_element_type=F32)
 
 
-def forward_x_kernel(sel, pot, section, last, perm, out, cos_ref, sin_ref, twisted):
-    fields = out.shape[0]
-    lanes = out.shape[3]
+def forward_x_kernel(sel, pot, section, last, perm, out, *scratch):
+    fields, steps, _, lanes = out.shape
+    waves, twisted = scratch[: 2 * steps], scratch[2 * steps :]
     half = section.shape[1] // 2
-
-    def chunk(t, carry):
-        block = pot[:, 0, :, pl.ds(pl.multiple_of(t * LANES, LANES), LANES)]
+    chunks = N // LANES
+
+    def fill(h, t):
+        cos_ref, sin_ref = waves[2 * h], waves[2 * h + 1]
+        block = pot[:, h, :, pl.ds(pl.multiple_of(t * LANES, LANES), LANES)]
         values = block.reshape(lanes, LANES).T.astype(F32)
         sine, cosine = sine_cosine(values)
         cos_ref[pl.ds(2 * t, 2)] = cosine.astype(BF).reshape(2, A, lanes)
         sin_ref[pl.ds(2 * t, 2)] = sine.astype(BF).reshape(2, A, lanes)
-        return carry
-
-    lax.fori_loop(0, N // LANES, chunk, 0, unroll=4)
-    table = section[0]
-    for m in range(HIGH):
-        span = slice(m * SUB, (m + 1) * SUB)
-        part_cos = cos_ref[:, span, :].reshape(A * SUB, lanes)
-        part_sin = sin_ref[:, span, :].reshape(A * SUB, lanes)
+
+    def multiply(h, m):
+        cos_ref, sin_ref = waves[2 * h], waves[2 * h + 1]
+        start = pl.multiple_of(m * SUB, SUB)
+        part_cos = cos_ref[:, pl.ds(start, SUB), :].reshape(A * SUB, lanes)
+        part_sin = sin_ref[:, pl.ds(start, SUB), :].reshape(A * SUB, lanes)
+        table = section[0]
         if lanes % LANES == 0:
             both = dot(table, jnp.concatenate([part_cos, part_sin], axis=1))
             of_cos, of_sin = both[:, :lanes], both[:, lanes:]
@@ -182,38 +183,51 @@
             of_cos, of_sin = dot(table, part_cos), dot(table, part_sin)
         real = of_cos[:half] - of_sin[half:]
         imag = of_cos[half:] + of_sin[:half]
-        twisted[:, m * SUB : (m + 1) * SUB, :] = real.astype(BF).reshape(2 * fields, SUB, lanes)
-        twisted[:, A + m * SUB : A + (m + 1) * SUB, :] = imag.astype(BF).reshape(
-            2 * fields, SUB, lanes
-        )
-    for d in range(fields):
-        lines = twisted[2 * d : 2 * d + 2].reshape(4 * A, lanes)
-        out[d, 0] = dot(dot(last[0, d], lines).astype(BF), perm[...]).astype(BF)
+        shape = (2 * fields, SUB, lanes)
+        twisted[h][:, pl.ds(start, SUB), :] = real.astype(BF).reshape(shape)
+        twisted[h][:, pl.ds(A + start, SUB), :] = imag.astype(BF).reshape(shape)
+
+    def first(t, carry):
+        fill(0, t)
+        return carry
+
+    lax.fori_loop(0, chunks, first, 0, unroll=4)
+    for h in range(steps):
+
+        def both(m, carry, h=h):
+            multiply(h, m)
+            if h + 1 < steps:
+                for c in range(chunks // HIGH):
+                    fill(h + 1, m * (chunks // HIGH) + c)
+            return carry
+
+        lax.fori_loop(0, HIGH, both, 0)
+        for d in range(fields):
+            lines = twisted[h][2 * d : 2 * d + 2].reshape(4 * A, lanes)
+            out[d, h] = dot(dot(last[0, d], lines).astype(BF), perm[...]).astype(BF)
 
 
 def forward_x(sel, pot, section, last, fields, part):
     groups = pot.shape[0] // A
     lanes = groups * SUB
     steps = HIGH // PARTS
+    shape = (fields, steps, ROWS, lanes)
     return pl.pallas_call(
         forward_x_kernel,
         grid_spec=pltpu.PrefetchScalarGridSpec(
             num_scalar_prefetch=1,
-            grid=(steps,),
+            grid=(1,),
             in_specs=[
-                pl.BlockSpec((groups, 1, SUB, N), lambda i, s: (0, part * steps + i, 0, 0)),
+                pl.BlockSpec((groups, steps, SUB, N), lambda i, s: (0, part, 0, 0)),
                 pl.BlockSpec((1,) + section.shape[1:], lambda i, s: (s[0], 0, 0)),
                 pl.BlockSpec((1,) + last.shape[1:], lambda i, s: (s[0], 0, 0, 0)),
                 pl.BlockSpec((lanes, lanes), lambda i, s: (0, 0)),
             ],
-            out_specs=pl.BlockSpec((fields, 1, ROWS, lanes), lambda i, s: (0, i, 0, 0)),
-            scratch_shapes=[
-                pltpu.VMEM((A, A, lanes), BF),
-                pltpu.VMEM((A, A, lanes), BF),
-                pltpu.VMEM((2 * fields, 2 * A, lanes), BF),
-            ],
+            out_specs=pl.BlockSpec(shape, lambda i, s: (0, 0, 0, 0)),
+            scratch_shapes=[pltpu.VMEM((A, A, lanes), BF)] * (2 * steps)
+            + [pltpu.VMEM((2 * fields, 2 * A, lanes), BF)] * steps,
         ),
-        out_shape=jax.ShapeDtypeStruct((fields, steps, ROWS, lanes), BF),
+        out_shape=jax.ShapeDtypeStruct(shape, BF),
         compiler_params=pltpu.CompilerParams(vmem_limit_bytes=VMEM),
         cost_estimate=SMALL,
         name="forward_x",
@@ -799,7 +813,7 @@
             earlier = [forward_y_first(received[f][0], section_y) for f in range(far)]
     waves = []
     for f in range(far):
-        spec = forward_y(received[f][1], section_y, earlier[f], last_y, [])
+        spec = forward_y(received[f][1], section_y, earlier[f], last_y, [crops] if f else [])
         ready = [spec] + [swap(spec, x) for x in range(1, near)]
         if f == 0:
             crops = order(crops.reshape(field_count, own_slots, HALF, LANES), [spec])

time: 181 us -> 176 us (0.972)
  starting transfers between devices: 30.7 us -> 26.2 us
    ppermute x4, waiting for transfers between devices: 11.4 us -> 2.52 us  [swap(): return lax.ppermute(value, 'slab', [(i, i ^ x) for i in range(hold_count)])]
    all_to_all x3, waiting for transfers between devices: 11.4 us -> 15.7 us  [trade(): return lax.all_to_all(value, axis, split_axis=0, concat_axis=0, tiled=True)]
    ppermute x4, starting transfers between devices: 6.81 us -> 3.13 us  [hop(): return lax.ppermute(value, 'beam', pairs).astype(F32)]
    ppermute x4, waiting for transfers between devices: 7.48 us -> 10.7 us  [hop(): return lax.ppermute(value, 'beam', pairs).astype(F32)]
  transfers between devices with their start and end apart: 12 -> 12, of which waited for: 8 -> 8; matrix products, arithmetic and copies ran while one was open for 8% -> 8% of each run, Pallas kernels for 34% -> 30%
where the time goes in v12:
time: 176 us; the launch traced here: 175 us
  Pallas kernels  84.8 us (48%)
  waiting for transfers between devices  41.2 us (23%)
  starting transfers between devices  26.2 us (15%)
  other arithmetic  11.1 us (6%)
  local copies, waits for them, and re-layouts  9.97 us (6%)
    pallas_call x2, Pallas kernels, forward_x(): pl.pallas_call(forward_x_kernel, grid_spec=pltpu.PrefetchScalarGridSpec(n...  22.8 us
    all_to_all x3, starting transfers between devices, trade(): return lax.all_to_all(value, axis, split_axis=0, concat_axis=0, tiled=True)  16.6 us
    pallas_call x2, Pallas kernels, inverse(): pl.pallas_call(functools.partial(inverse_kernel, steps, which, near), gri...  16.1 us
    pallas_call x2, Pallas kernels, collect(): pl.pallas_call(functools.partial(collect_kernel, len(sheets)), grid_spec=...  15.8 us
    all_to_all x3, waiting for transfers between devices, trade(): return lax.all_to_all(value, axis, split_axis=0, concat_axis=0, tiled=True)  15.7 us
    all_to_all x1, waiting for transfers between devices, shards(): lax.all_to_all(tiles, ('beam', 'slab'), split_axis=0, concat_axis=0, axis...  12.4 us
    pallas_call x2, Pallas kernels, forward_y(): pl.pallas_call(forward_y_kernel, grid=(1 + steps,), in_specs=[pl.BlockSpe...  12.2 us
    ppermute x4, waiting for transfers between devices, hop(): return lax.ppermute(value, 'beam', pairs).astype(F32)  10.7 us
  transfers between devices with their start and end apart: 12, of which 8 were waited for; matrix products, arithmetic and copies ran while one was open for 8% of the time, Pallas kernels for 30%

profile of v12, /device:TPU:0, one launch (start us, length us, event | category | flops | bytes accessed | tf_op | source)
XLA Modules:
  0.0 174.9 jit_solution(17331789217200386362)
XLA Ops:
  0.0 11.4 %forward_x.3 = bf16[8,2,208,128]{3,2,1,0:T(8,128)(2,1)} custom-call(s32[1]{0:T(128)} %bitcast.3.sel, bf16[8,4,16,4096]{3,2,1,0:T(8,128)(2,1)} %bitcast.40, bf16[4,512,1024]{2,1,0:T(8,128)(2,1)} %constant.270.clone.section, bf16[4,8,208,256]{3,2,1,0:T(8,128)(2,1)} %constant.271.clone.last, bf16[128,128]{1,0:T(8,128)(2,1)} %constant.272.clone.perm), custom_call_target="tpu_custom_call" | custom-call | flops 1048576 | tf_op jit(solution)/shard_map/forward_x/pallas_call | solution.py:215
  11.4 7.3 %all-to-all-start.1 = ((bf16[8,2,208,128]{3,2,1,0:T(8,128)(2,1)}), bf16[8,2,208,128]{3,2,1,0:T(8,128)(2,1)S(1)}, u32[]{:S(2)}, u32[]{:S(2)}) async-start(bf16[8,2,208,128]{3,2,1,0:T(8,128)(2,1)} %forward_x.3), calls=%async_computation.1 | async-start | bytes 1703936 | tf_op jit(solution)/shard_map/all_to_all | solution.py:761
  18.8 0.1 reshape_reshape.3
  19.0 0.6 fusion.24
  20.4 0.1 copy.28
  20.6 0.6 gather_fusion
  21.2 0.6 gather_fusion.1
  21.7 0.1 stack.54
  21.9 11.4 %forward_x.2 = bf16[8,2,208,128]{3,2,1,0:T(8,128)(2,1)} custom-call(s32[1]{0:T(128)} %bitcast.3.sel, bf16[8,4,16,4096]{3,2,1,0:T(8,128)(2,1)} %bitcast.41, bf16[4,512,1024]{2,1,0:T(8,128)(2,1)} %constant.270.clone.section, bf16[4,8,208,256]{3,2,1,0:T(8,128)(2,1)} %constant.271.clone.last, bf16[128,128]{1,0:T(8,128)(2,1)} %constant.272.clone.perm), custom_call_target="tpu_custom_call" | custom-call | flops 1048576 | tf_op jit(solution)/shard_map/forward_x/pallas_call | solution.py:215
  33.4 6.9 %all-to-all-done.1.lines = bf16[8,2,208,128]{3,2,1,0:T(8,128)(2,1)S(1)} async-done(((bf16[8,2,208,128]{3,2,1,0:T(8,128)(2,1)}), bf16[8,2,208,128]{3,2,1,0:T(8,128)(2,1)S(1)}, u32[]{:S(2)}, u32[]{:S(2)}) %all-to-all-start.1) | async-done | bytes 852000 | tf_op jit(solution)/shard_map/all_to_all | solution.py:761
  40.4 3.5 %all-to-all-start = ((bf16[8,2,208,128]{3,2,1,0:T(8,128)(2,1)}), bf16[8,2,208,128]{3,2,1,0:T(8,128)(2,1)S(1)}, u32[]{:S(2)}, u32[]{:S(2)}) async-start(bf16[8,2,208,128]{3,2,1,0:T(8,128)(2,1)} %forward_x.2), calls=%async_computation | async-start | bytes 1703936 | tf_op jit(solution)/shard_map/all_to_all | solution.py:761
  43.9 0.1 stack.55
  44.7 0.7 reshape.1008.rest_3_.sel
  45.4 0.1 copy.27
  45.6 1.4 fusion.15
  47.0 0.6 broadcast_add_fusion
  47.6 1.5 collective-permute-start
  49.1 0.5 compare_convert_fusion
  49.6 0.5 and_select_fusion.5
  50.1 0.5 and_select_fusion.6
  50.6 0.7 multiply_convert_fusion.rest_1_.refs_3_
  51.3 3.3 %forward_y_first.2.after.earlier = bf16[64,2,32,128]{3,2,1,0:T(8,128)(2,1)} custom-call(bf16[8,2,208,128]{3,2,1,0:T(8,128)(2,1)} %copy-done.3, bf16[512,256]{1,0:T(8,128)(2,1)} %constant.273.clone.section), custom_call_target="tpu_custom_call" | custom-call | flops 1048576 | tf_op jit(solution)/shard_map/forward_y_first/pallas_call | solution.py:284
  54.6 7.1 %crop.1.rest_0_ = bf16[32,32,128]{2,1,0:T(8,128)(2,1)} custom-call(s32[32]{0:T(128)} %get-tuple-element.38.rows, s32[32]{0:T(128)} %get-tuple-element.37.cols, s32[32]{0:T(128)} %get-tuple-element.18.odd, s32[32]{0:T(128)} %get-tuple-element.15.mine, bf16[512,4096]{1,0:T(8,128)(2,1)} %pot.1, bf16[64,2,32,128]{3,2,1,0:T(8,128)(2,1)} %forward_y_first.2.after.earlier), custom_call_target="tpu_custom_call" | custom-call | flops 1048576 | tf_op jit(solution)/shard_map/crop/pallas_call | solution.py:586
  61.7 3.9 %all-to-all-done.value = bf16[8,2,208,128]{3,2,1,0:T(8,128)(2,1)S(1)} async-done(((bf16[8,2,208,128]{3,2,1,0:T(8,128)(2,1)}), bf16[8,2,208,128]{3,2,1,0:T(8,128)(2,1)S(1)}, u32[]{:S(2)}, u32[]{:S(2)}) %all-to-all-start) | async-done | bytes 852000 | tf_op jit(solution)/shard_map/all_to_all | solution.py:761
  65.6 2.5 %collective-permute-done.rest_4_.lines = bf16[8,2,208,128]{3,2,1,0:T(8,128)(2,1)S(1)} collective-permute-done((bf16[8,2,208,128]{3,2,1,0:T(8,128)(2,1)S(1)}, bf16[8,2,208,128]{3,2,1,0:T(8,128)(2,1)S(1)}, u32[]{:S(2)}, u32[]{:S(2)}) %collective-permute-start) | collective-permute-done | bytes 852000 | tf_op jit(solution)/shard_map/ppermute | solution.py:767
  68.1 1.0 broadcast_in_dim.2.rest_2_.refs_2_
  69.1 1.5 collective-permute-start.2
  70.6 6.1 %forward_y.2.refs_0_.rest_0_ = bf16[32,208,128]{2,1,0:T(8,128)(2,1)} custom-call(bf16[8,2,208,128]{3,2,1,0:T(8,128)(2,1)} %order.2.lines, bf16[512,256]{1,0:T(8,128)(2,1)} %constant.273.clone.section, bf16[64,2,32,128]{3,2,1,0:T(8,128)(2,1)} %forward_y_first.2.after.earlier, bf16[32,208,256]{2,1,0:T(8,128)(2,1)} %constant.274.clone.last), custom_call_target="tpu_custom_call" | custom-call | flops 1048576 | tf_op jit(solution)/shard_map/forward_y/pallas_call | solution.py:330
  76.7 5.7 %all-to-all-start.2 = ((bf16[8,4,32,128]{3,2,1,0:T(8,128)(2,1)}), bf16[8,4,32,128]{3,2,1,0:T(8,128)(2,1)S(1)}, u32[]{:S(2)}, u32[]{:S(2)}) async-start(bf16[8,4,32,128]{3,2,1,0:T(8,128)(2,1)} %order.3), calls=%async_computation.2 | async-start | bytes 524288 | tf_op jit(solution)/shard_map/all_to_all | solution.py:761
  82.5 3.4 %forward_y_first.3.earlier = bf16[64,2,32,128]{3,2,1,0:T(8,128)(2,1)} custom-call(bf16[8,2,208,128]{3,2,1,0:T(8,128)(2,1)} %copy-done.4, bf16[512,256]{1,0:T(8,128)(2,1)} %constant.273.clone.section), custom_call_target="tpu_custom_call" | custom-call | flops 1048576 | tf_op jit(solution)/shard_map/forward_y_first/pallas_call | solution.py:284
  85.8 4.9 %all-to-all-done.2.rest_0_.refs_3_ = bf16[8,4,32,128]{3,2,1,0:T(8,128)(2,1)S(1)} async-done(((bf16[8,4,32,128]{3,2,1,0:T(8,128)(2,1)}), bf16[8,4,32,128]{3,2,1,0:T(8,128)(2,1)S(1)}, u32[]{:S(2)}, u32[]{:S(2)}) %all-to-all-start.2) | async-done | bytes 262176 | tf_op jit(solution)/shard_map/all_to_all | solution.py:761
  90.7 0.7 copy-done.1
  91.4 0.9 copy-done.6
  92.3 6.1 %forward_y.3.refs_0_ = bf16[32,208,128]{2,1,0:T(8,128)(2,1)} custom-call(bf16[8,2,208,128]{3,2,1,0:T(8,128)(2,1)} %copy-done.6, bf16[512,256]{1,0:T(8,128)(2,1)} %constant.273.clone.section, bf16[64,2,32,128]{3,2,1,0:T(8,128)(2,1)} %forward_y_first.3.earlier, bf16[32,208,256]{2,1,0:T(8,128)(2,1)} %constant.274.clone.last, bf16[8,4,32,128]{3,2,1,0:T(8,128)(2,1)} %copy-done.1), custom_call_target="tpu_custom_call" | custom-call | flops 1048576 | tf_op jit(solution)/shard_map/forward_y/pallas_call | solution.py:330
  98.4 1.2 copy-done.5
  99.6 8.0 %inverse.2.refs_7_.refs_0_ = bf16[32,256,256]{2,1,0:T(8,128)(2,1)} custom-call(s32[12]{0:T(128)} %reshape.1008.rest_3_.sel, bf16[32,208,128]{2,1,0:T(8,128)(2,1)} %forward_y.2.refs_0_.rest_0_, bf16[32,208,128]{2,1,0:T(8,128)(2,1)} %copy-done.5, f32[208,128]{1,0:T(8,128)} %constant.275.clone.refs_2_, f32[4,1,128]{2,1,0:T(1,128)} %multiply_convert_fusion.rest_1_.refs_3_, ...), custom_call_target="tpu_custom_call" | custom-call | flops 1048576 | tf_op jit(solution)/shard_map/inverse/pallas_call | solution.py:438
  107.6 8.1 %inverse.3.refs_1_ = bf16[32,256,256]{2,1,0:T(8,128)(2,1)} custom-call(s32[12]{0:T(128)} %reshape.1008.rest_3_.sel, bf16[32,208,128]{2,1,0:T(8,128)(2,1)} %forward_y.3.refs_0_, bf16[32,208,128]{2,1,0:T(8,128)(2,1)} %collective-permute-done.3.refs_1_, f32[208,128]{1,0:T(8,128)} %constant.275.clone.refs_2_, f32[4,1,128]{2,1,0:T(1,128)} %multiply_convert_fusion.rest_1_.refs_3_, ...), custom_call_target="tpu_custom_call" | custom-call | flops 1048576 | tf_op jit(solution)/shard_map/inverse/pallas_call | solution.py:438
  115.7 7.9 %collect.2 = (bf16[16,2,4,16,128]{4,3,2,1,0:T(8,128)(2,1)}, bf16[16,2,4,16,128]{4,3,2,1,0:T(8,128)(2,1)}) custom-call(s32[4]{0:T(128)} %get-tuple-element.14.k1_pairs, bf16[32,256,256]{2,1,0:T(8,128)(2,1)} %inverse.2.refs_7_.refs_0_, bf16[32,256,256]{2,1,0:T(8,128)(2,1)} %inverse.3.refs_1_, s32[2,2,2,64,128]{4,3,2,1,0:T(8,128)} %broadcast_in_dim.2.rest_2_.refs_2_, ...), custom_call_target="tpu_custom_call" | custom-call | flops 1048576 | tf_op jit(solution)/shard_map/collect/pallas_call | solution.py:529
  123.7 0.2 dynamic-slice_reduce_fusion
  123.9 1.5 collective-permute-start.4
  125.5 0.1 add.415
  125.6 0.1 add.417
  126.0 7.9 %collect.3 = (bf16[16,2,4,16,128]{4,3,2,1,0:T(8,128)(2,1)}, bf16[16,2,4,16,128]{4,3,2,1,0:T(8,128)(2,1)}) custom-call(s32[4]{0:T(128)} %get-tuple-element.14.k1_pairs, bf16[32,256,256]{2,1,0:T(8,128)(2,1)} %inverse.2.refs_7_.refs_0_, bf16[32,256,256]{2,1,0:T(8,128)(2,1)} %inverse.3.refs_1_, s32[2,2,2,64,128]{4,3,2,1,0:T(8,128)} %broadcast_in_dim.2.rest_2_.refs_2_, ...), custom_call_target="tpu_custom_call" | custom-call | flops 1048576 | tf_op jit(solution)/shard_map/collect/pallas_call | solution.py:529
  133.9 4.4 %collective-permute-done.6 = bf16[16,2,4,16,128]{4,3,2,1,0:T(8,128)(2,1)S(1)} collective-permute-done((bf16[16,2,4,16,128]{4,3,2,1,0:T(8,128)(2,1)}, bf16[16,2,4,16,128]{4,3,2,1,0:T(8,128)(2,1)S(1)}, u32[]{:S(2)}, u32[]{:S(2)}) %collective-permute-start.6) | collective-permute-done | bytes 524320 | tf_op jit(solution)/shard_map/ppermute | solution.py:832
  138.2 1.2 convert_add_fusion
  139.5 0.1 collective-permute-start.7
  139.6 1.3 convert_add_fusion.1
  140.9 1.5 collective-permute-start.5
  142.4 0.1 fusion.23
  142.5 5.0 %collective-permute-done.7 = bf16[8,2,4,16,128]{4,3,2,1,0:T(8,128)(2,1)S(1)} collective-permute-done((bf16[8,2,4,16,128]{4,3,2,1,0:T(8,128)(2,1)S(1)}, bf16[8,2,4,16,128]{4,3,2,1,0:T(8,128)(2,1)S(1)}, u32[]{:S(2)}, u32[]{:S(2)}) %collective-permute-start.7) | collective-permute-done | bytes 262176 | tf_op jit(solution)/shard_map/ppermute | solution.py:832
  147.6 1.4 collective-permute-done.5
  149.0 0.9 pad_maximum_fusion
  149.9 3.5 %all-to-all-start.3 = ((bf16[8,2,4,32,128]{4,3,2,1,0:T(8,128)(2,1)}), bf16[8,2,4,32,128]{4,3,2,1,0:T(8,128)(2,1)S(1)}, u32[]{:S(2)}, u32[]{:S(2)}) async-start(bf16[8,2,4,32,128]{4,3,2,1,0:T(8,128)(2,1)} %pad_maximum_fusion), calls=%async_computation.3 | async-start | bytes 1048576 | tf_op jit(solution)/shard_map/all_to_all | solution.py:845
  153.4 0.6 dynamic_slice.18.counts
  154.0 0.6 pad_maximum_fusion.2.alpha
  154.6 0.3 fusion.6
  155.0 0.7 pad_maximum_fusion.1.refs_2_
  155.6 0.7 reduce_sum.25.refs_1_
  156.3 12.4 %all-to-all-done.3 = bf16[8,2,4,32,128]{4,3,2,1,0:T(8,128)(2,1)S(1)} async-done(((bf16[8,2,4,32,128]{4,3,2,1,0:T(8,128)(2,1)}), bf16[8,2,4,32,128]{4,3,2,1,0:T(8,128)(2,1)S(1)}, u32[]{:S(2)}, u32[]{:S(2)}) %all-to-all-start.3) | async-done | bytes 524320 | tf_op jit(solution)/shard_map/all_to_all | solution.py:845
  168.7 0.8 reduce_sum.24.refs_0_
  169.5 4.0 %detect.1 = f32[1,256]{1,0:T(1,128)} custom-call(f32[2,4,12]{2,1,0:T(4,128)} %pad_maximum_fusion.2.alpha, s32[1]{0:T(128)} %dynamic_slice.18.counts, bf16[4,2,4,32,128]{4,3,2,1,0:T(8,128)(2,1)} %reduce_sum.24.refs_0_, bf16[4,32,128]{2,1,0:T(8,128)(2,1)} %reduce_sum.25.refs_1_, f32[4,2,32,128]{3,2,1,0:T(8,128)} %pad_maximum_fusion.1.refs_2_, ...), custom_call_target="tpu_custom_call" | custom-call | tf_op jit(solution)/shard_map/detect/pallas_call | solution.py:652
  173.5 0.7 slice_reduce_fusion
  174.2 0.1 reshape_squeeze.3
  174.3 0.6 copy.31
  (63 shorter events, 1.2 us)
Async XLA Ops:
  0.0 18.7 %copy-start.8 = (s32[32,4]{0,1:T(4,128)S(1)}, s32[32,4]{0,1:T(4,128)}, u32[]{:S(2)}) copy-start(s32[32,4]{0,1:T(4,128)} %param.23) | copy-start | bytes 1540
  0.0 18.9 %copy-start.7 = (s32[4,2]{0,1:T(2,128)S(1)}, s32[4,2]{0,1:T(2,128)}, u32[]{:S(2)}) copy-start(s32[4,2]{0,1:T(2,128)} %param.21) | copy-start | bytes 100
  11.4 28.9 %all-to-all-start.1 = ((bf16[8,2,208,128]{3,2,1,0:T(8,128)(2,1)}), bf16[8,2,208,128]{3,2,1,0:T(8,128)(2,1)S(1)}, u32[]{:S(2)}, u32[]{:S(2)}) async-start(bf16[8,2,208,128]{3,2,1,0:T(8,128)(2,1)} %forward_x.3), calls=%async_computation.1 | async-start | bytes 1703936 | tf_op jit(solution)/shard_map/all_to_all | solution.py:761
  21.8 28.8 %copy-start.9 = (s32[128]{0:T(128)S(1)}, s32[128]{0:T(128)}, u32[]{:S(2)}) copy-start(s32[128]{0:T(128)} %constant.269.clone) | copy-start | bytes 1540
  40.4 10.9 %copy-start.3 = (bf16[8,2,208,128]{3,2,1,0:T(8,128)(2,1)}, bf16[8,2,208,128]{3,2,1,0:T(8,128)(2,1)S(1)}, u32[]{:S(2)}) copy-start(bf16[8,2,208,128]{3,2,1,0:T(8,128)(2,1)S(1)} %all-to-all-done.1.lines) | copy-start | bytes 2555908
  40.4 25.3 %all-to-all-start = ((bf16[8,2,208,128]{3,2,1,0:T(8,128)(2,1)}), bf16[8,2,208,128]{3,2,1,0:T(8,128)(2,1)S(1)}, u32[]{:S(2)}, u32[]{:S(2)}) async-start(bf16[8,2,208,128]{3,2,1,0:T(8,128)(2,1)} %forward_x.2), calls=%async_computation | async-start | bytes 1703936 | tf_op jit(solution)/shard_map/all_to_all | solution.py:761
  47.6 20.5 %collective-permute-start = (bf16[8,2,208,128]{3,2,1,0:T(8,128)(2,1)S(1)}, bf16[8,2,208,128]{3,2,1,0:T(8,128)(2,1)S(1)}, u32[]{:S(2)}, u32[]{:S(2)}) collective-permute-start(bf16[8,2,208,128]{3,2,1,0:T(8,128)(2,1)S(1)} %all-to-all-done.1.lines), channel_id=1, source_target_pairs={{0,2},{1,3},{2,0},{3,1},{4,6},{5,7},{6,4},{7,5},{8,10},{9,11},{10,... | collective-permute-start | bytes 2555912 | tf_op jit(solution)/shard_map/ppermute | solution.py:767
  65.6 3.5 %copy-start = (bf16[8,2,208,128]{3,2,1,0:T(8,128)(2,1)}, bf16[8,2,208,128]{3,2,1,0:T(8,128)(2,1)S(1)}, u32[]{:S(2)}) copy-start(bf16[8,2,208,128]{3,2,1,0:T(8,128)(2,1)S(1)} %all-to-all-done.value) | copy-start | bytes 2555908
  68.1 1.0 copy-start.4
  69.1 21.6 %collective-permute-start.2 = (bf16[8,2,208,128]{3,2,1,0:T(8,128)(2,1)}, bf16[8,2,208,128]{3,2,1,0:T(8,128)(2,1)S(1)}, u32[]{:S(2)}, u32[]{:S(2)}) collective-permute-start(bf16[8,2,208,128]{3,2,1,0:T(8,128)(2,1)} %order.2.lines), channel_id=1, source_target_pairs={{0,2},{1,3},{2,0},{3,1},{4,6},{5,7},{6,4},{7,5},{8,10},{9,11},{10,... | collective-permute-start | bytes 2555912 | tf_op jit(solution)/shard_map/ppermute | solution.py:767
  76.7 13.9 %all-to-all-start.2 = ((bf16[8,4,32,128]{3,2,1,0:T(8,128)(2,1)}), bf16[8,4,32,128]{3,2,1,0:T(8,128)(2,1)S(1)}, u32[]{:S(2)}, u32[]{:S(2)}) async-start(bf16[8,4,32,128]{3,2,1,0:T(8,128)(2,1)} %order.3), calls=%async_computation.2 | async-start | bytes 524288 | tf_op jit(solution)/shard_map/all_to_all | solution.py:761
  82.4 15.9 %collective-permute-start.1 = (bf16[32,208,128]{2,1,0:T(8,128)(2,1)}, bf16[32,208,128]{2,1,0:T(8,128)(2,1)S(1)}, u32[]{:S(2)}, u32[]{:S(2)}) collective-permute-start(bf16[32,208,128]{2,1,0:T(8,128)(2,1)} %forward_y.2.refs_0_.rest_0_), channel_id=1, source_target_pairs={{0,1},{1,0},{2,3},{3,2},{4,5},{5,4},{6,7},{7,6},{8,9},{9,8},{10,11... | collective-permute-start | bytes 5111816 | tf_op jit(solution)/shard_map/ppermute | solution.py:767
  90.7 0.7 copy-start.1
  91.4 0.9 copy-start.6
  98.4 9.2 %collective-permute-start.3 = (bf16[32,208,128]{2,1,0:T(8,128)(2,1)}, bf16[32,208,128]{2,1,0:T(8,128)(2,1)}, u32[]{:S(2)}, u32[]{:S(2)}) collective-permute-start(bf16[32,208,128]{2,1,0:T(8,128)(2,1)} %forward_y.3.refs_0_), channel_id=1, source_target_pairs={{0,1},{1,0},{2,3},{3,2},{4,5},{5,4},{6,7},{7,6},{8,9},{9,8},{10,11... | collective-permute-start | bytes 5111816 | tf_op jit(solution)/shard_map/ppermute | solution.py:767
  98.4 1.2 copy-start.5
  123.7 14.6 %collective-permute-start.6 = (bf16[16,2,4,16,128]{4,3,2,1,0:T(8,128)(2,1)}, bf16[16,2,4,16,128]{4,3,2,1,0:T(8,128)(2,1)S(1)}, u32[]{:S(2)}, u32[]{:S(2)}) collective-permute-start(bf16[16,2,4,16,128]{4,3,2,1,0:T(8,128)(2,1)} %get-tuple-element.12), channel_id=1, source_target_pairs={{0,8},{4,12},{8,0},{12,4},{16,24},{20,28},{24,16},{28,20},{1,9},{5... | collective-permute-start | bytes 1572872 | tf_op jit(solution)/shard_map/ppermute | solution.py:832
  123.9 15.7 %collective-permute-start.4 = (bf16[16,2,4,16,128]{4,3,2,1,0:T(8,128)(2,1)}, bf16[16,2,4,16,128]{4,3,2,1,0:T(8,128)(2,1)S(1)}, u32[]{:S(2)}, u32[]{:S(2)}) collective-permute-start(bf16[16,2,4,16,128]{4,3,2,1,0:T(8,128)(2,1)} %get-tuple-element.9.refs_3_), channel_id=1, source_target_pairs={{0,4},{4,0},{8,12},{12,8},{16,20},{20,16},{24,28},{28,24},{1,5},{5... | collective-permute-start | bytes 1572872 | tf_op jit(solution)/shard_map/ppermute | solution.py:832
  133.9 8.6 %copy-start.10 = (f32[4]{0:T(128)S(1)}, f32[4]{0:T(128)}, u32[]{:S(2)}) copy-start(f32[4]{0:T(128)} %param.22) | copy-start | bytes 52
  139.5 8.0 %collective-permute-start.7 = (bf16[8,2,4,16,128]{4,3,2,1,0:T(8,128)(2,1)S(1)}, bf16[8,2,4,16,128]{4,3,2,1,0:T(8,128)(2,1)S(1)}, u32[]{:S(2)}, u32[]{:S(2)}) collective-permute-start(bf16[8,2,4,16,128]{4,3,2,1,0:T(8,128)(2,1)S(1)} %slice.72), channel_id=1, source_target_pairs={{0,4},{4,0},{8,12},{12,8},{16,20},{20,16},{24,28},{28,24},{1,5},{5... | collective-permute-start | bytes 786440 | tf_op jit(solution)/shard_map/ppermute | solution.py:832
  139.6 13.8 %copy-start.11 = (s32[32]{0:T(128)S(1)}, s32[32]{0:T(128)}, u32[]{:S(2)}) copy-start(s32[32]{0:T(128)} %param.24) | copy-start | bytes 388
  139.6 16.0 %copy-start.2 = (bf16[8,4,32,128]{3,2,1,0:T(8,128)(2,1)S(1)}, bf16[8,4,32,128]{3,2,1,0:T(8,128)(2,1)}, u32[]{:S(2)}) copy-start(bf16[8,4,32,128]{3,2,1,0:T(8,128)(2,1)} %copy-done.1) | copy-start | bytes 786436
  140.9 8.0 %collective-permute-start.5 = (bf16[8,2,4,16,128]{4,3,2,1,0:T(8,128)(2,1)S(1)}, bf16[8,2,4,16,128]{4,3,2,1,0:T(8,128)(2,1)S(1)}, u32[]{:S(2)}, u32[]{:S(2)}) collective-permute-start(bf16[8,2,4,16,128]{4,3,2,1,0:T(8,128)(2,1)S(1)} %slice.73), channel_id=1, source_target_pairs={{0,8},{4,12},{8,0},{12,4},{16,24},{20,28},{24,16},{28,20},{1,9},{5... | collective-permute-start | bytes 786440 | tf_op jit(solution)/shard_map/ppermute | solution.py:832
  149.9 18.8 %all-to-all-start.3 = ((bf16[8,2,4,32,128]{4,3,2,1,0:T(8,128)(2,1)}), bf16[8,2,4,32,128]{4,3,2,1,0:T(8,128)(2,1)S(1)}, u32[]{:S(2)}, u32[]{:S(2)}) async-start(bf16[8,2,4,32,128]{4,3,2,1,0:T(8,128)(2,1)} %pad_maximum_fusion), calls=%async_computation.3 | async-start | bytes 1048576 | tf_op jit(solution)/shard_map/all_to_all | solution.py:845

commit v13 on v11

--- a/solution.py
+++ b/solution.py
@@ -169,7 +169,7 @@
         sin_ref[pl.ds(2 * t, 2)] = sine.astype(BF).reshape(2, A, lanes)
         return carry
 
-    lax.fori_loop(0, N // LANES, chunk, 0, unroll=4)
+    lax.fori_loop(0, N // LANES, chunk, 0, unroll=8)
     table = section[0]
     for m in range(HIGH):
         span = slice(m * SUB, (m + 1) * SUB)
@@ -756,6 +756,7 @@
     tile_y, tile_x = ids // across, ids % across
     mine = (tile_y // band_tiles == field_pos).astype(jnp.int32)
     rows = jnp.clip(tile_y - field_pos * band_tiles, 0, band_tiles - 1)
+    columns, odd = tile_x // 2, tile_x % 2
 
     beam_row = lax.dynamic_index_in_dim(beam_index, hold_pos, 0, keepdims=False)
     pair_ids = share ^ jnp.arange(sheets, dtype=jnp.int32)
@@ -783,7 +784,10 @@
     received = [[] for _ in range(far)]
     earlier = []
     for part in range(PARTS):
-        lines = trade(forward_x(sel, pot_first, section_x, last_x, field_count, part), "beam")
+        lines = forward_x(sel, pot_first, section_x, last_x, field_count, part)
+        if part:
+            lines = order(lines, [places, scalars, square_x, rows, columns, odd, mine])
+        lines = trade(lines, "beam")
         if lines.shape[3] != LANES:
             ratio = LANES // lines.shape[3]
             lines = lines.reshape(
@@ -791,19 +795,18 @@
             )
             lines = lines.transpose(0, 2, 3, 4, 1, 5).reshape(-1, HIGH // PARTS, ROWS, LANES)
         if part:
-            crops = crop(rows, tile_x // 2, tile_x % 2, mine, pot_second, earlier[0])
-            lines = order(lines, [crops, square_x, places, scalars] + [r[0] for r in received[1:]])
+            crops = crop(rows, columns, odd, mine, pot_second, earlier[0])
+            lines = order(lines, [crops] + [r[0] for r in received[1:]])
         for f in range(far):
             received[f].append(swap(lines, f * near) if f else lines)
         if part == 0:
             earlier = [forward_y_first(received[f][0], section_y) for f in range(far)]
+    crops = order(crops.reshape(field_count, own_slots, HALF, LANES), received[0][1:])
+    crops = trade(crops, "beam")
     waves = []
     for f in range(far):
-        spec = forward_y(received[f][1], section_y, earlier[f], last_y, [])
+        spec = forward_y(received[f][1], section_y, earlier[f], last_y, [crops] if f else [])
         ready = [spec] + [swap(spec, x) for x in range(1, near)]
-        if f == 0:
-            crops = order(crops.reshape(field_count, own_slots, HALF, LANES), [spec])
-            crops = trade(crops, "beam")
         waves.append(
             inverse(
                 f * near, scalars, ready, freq_y, square_x, inverse_y, inverse_x, waves[-1:]

time: 181 us -> 173 us (0.956)
  waiting for transfers between devices: 42.8 us -> 38.1 us
  starting transfers between devices: 30.7 us -> 27.3 us
    ppermute x4, waiting for transfers between devices: 11.4 us -> 4.48 us  [swap(): return lax.ppermute(value, 'slab', [(i, i ^ x) for i in range(hold_count)])]
    ppermute x4, waiting for transfers between devices: 7.48 us -> 10.7 us  [hop(): return lax.ppermute(value, 'beam', pairs).astype(F32)]
  transfers between devices with their start and end apart: 12 -> 12, of which waited for: 8 -> 7; matrix products, arithmetic and copies ran while one was open for 8% -> 9% of each run, Pallas kernels for 34% -> 30%
where the time goes in v13:
time: 173 us; the launch traced here: 172 us
  Pallas kernels  82.4 us (48%)
  waiting for transfers between devices  38.1 us (22%)
  starting transfers between devices  27.3 us (16%)
  other arithmetic  11.2 us (6%)
  local copies, waits for them, and re-layouts  10.9 us (6%)
    pallas_call x2, Pallas kernels, forward_x(): pl.pallas_call(forward_x_kernel, grid_spec=pltpu.PrefetchScalarGridSpec(n...  20.4 us
    pallas_call x2, Pallas kernels, inverse(): pl.pallas_call(functools.partial(inverse_kernel, steps, which, near), gri...  16.1 us
    pallas_call x2, Pallas kernels, collect(): pl.pallas_call(functools.partial(collect_kernel, len(sheets)), grid_spec=...  15.8 us
    all_to_all x3, starting transfers between devices, trade(): return lax.all_to_all(value, axis, split_axis=0, concat_axis=0, tiled=True)  15.6 us
    all_to_all x1, waiting for transfers between devices, shards(): lax.all_to_all(tiles, ('beam', 'slab'), split_axis=0, concat_axis=0, axis...  12.5 us
    pallas_call x2, Pallas kernels, forward_y(): pl.pallas_call(forward_y_kernel, grid=(1 + steps,), in_specs=[pl.BlockSpe...  12.2 us
    ppermute x4, waiting for transfers between devices, hop(): return lax.ppermute(value, 'beam', pairs).astype(F32)  10.7 us
    all_to_all x3, waiting for transfers between devices, trade(): return lax.all_to_all(value, axis, split_axis=0, concat_axis=0, tiled=True)  10.5 us
  transfers between devices with their start and end apart: 12, of which 7 were waited for; matrix products, arithmetic and copies ran while one was open for 9% of the time, Pallas kernels for 30%

profile of v13, /device:TPU:0, one launch (start us, length us, event | category | flops | bytes accessed | tf_op | source)
XLA Modules:
  0.0 171.7 jit_solution(8594626060796871152)
XLA Ops:
  0.0 10.2 %forward_x.3 = bf16[8,2,208,128]{3,2,1,0:T(8,128)(2,1)} custom-call(s32[1]{0:T(128)} %bitcast.3.sel, bf16[8,4,16,4096]{3,2,1,0:T(8,128)(2,1)} %bitcast.40, bf16[4,512,1024]{2,1,0:T(8,128)(2,1)} %constant.270.clone.section, bf16[4,8,208,256]{3,2,1,0:T(8,128)(2,1)} %constant.271.clone.last, bf16[128,128]{1,0:T(8,128)(2,1)} %constant.272.clone.perm), custom_call_target="tpu_custom_call" | custom-call | flops 1048576 | tf_op jit(solution)/shard_map/forward_x/pallas_call | solution.py:198
  10.2 7.3 %all-to-all-start.1 = ((bf16[8,2,208,128]{3,2,1,0:T(8,128)(2,1)}), bf16[8,2,208,128]{3,2,1,0:T(8,128)(2,1)S(1)}, u32[]{:S(2)}, u32[]{:S(2)}) async-start(bf16[8,2,208,128]{3,2,1,0:T(8,128)(2,1)} %forward_x.3), calls=%async_computation.1 | async-start | bytes 1703936 | tf_op jit(solution)/shard_map/all_to_all | solution.py:747
  17.6 0.6 fusion.24
  19.0 0.1 reshape_reshape.3
  19.1 0.1 copy.28
  19.3 0.6 gather_fusion
  19.9 0.6 gather_fusion.1
  20.5 0.1 stack.55
  20.6 0.1 stack.54
  21.5 0.7 reshape.1008.rest_1_.sel
  22.2 1.3 fusion.15
  23.7 0.1 copy.31
  23.9 10.2 %forward_x.2.value = bf16[8,2,208,128]{3,2,1,0:T(8,128)(2,1)} custom-call(s32[1]{0:T(128)} %bitcast.3.sel, bf16[8,4,16,4096]{3,2,1,0:T(8,128)(2,1)} %bitcast.41, bf16[4,512,1024]{2,1,0:T(8,128)(2,1)} %constant.270.clone.section, bf16[4,8,208,256]{3,2,1,0:T(8,128)(2,1)} %constant.271.clone.last, bf16[128,128]{1,0:T(8,128)(2,1)} %constant.272.clone.perm), custom_call_target="tpu_custom_call" | custom-call | flops 1048576 | tf_op jit(solution)/shard_map/forward_x/pallas_call | solution.py:198
  34.1 0.6 broadcast_add_fusion
  34.7 0.6 compare_convert_fusion
  35.3 0.5 and_select_fusion.5
  35.8 0.6 and_select_fusion.6
  36.4 0.7 multiply_convert_fusion.rest_2_.refs_3_
  37.1 0.9 broadcast_in_dim.2.rest_0_.refs_2_
  37.9 1.2 all-to-all-done.1.lines
  39.2 4.7 %all-to-all-start = ((bf16[8,2,208,128]{3,2,1,0:T(8,128)(2,1)}), bf16[8,2,208,128]{3,2,1,0:T(8,128)(2,1)S(1)}, u32[]{:S(2)}, u32[]{:S(2)}) async-start(bf16[8,2,208,128]{3,2,1,0:T(8,128)(2,1)} %order.3), calls=%async_computation | async-start | bytes 1703936 | tf_op jit(solution)/shard_map/all_to_all | solution.py:747
  43.9 1.5 collective-permute-start
  45.4 3.3 %forward_y_first.2.after.earlier = bf16[64,2,32,128]{3,2,1,0:T(8,128)(2,1)} custom-call(bf16[8,2,208,128]{3,2,1,0:T(8,128)(2,1)} %copy-done.3, bf16[512,256]{1,0:T(8,128)(2,1)} %constant.273.clone.section), custom_call_target="tpu_custom_call" | custom-call | flops 1048576 | tf_op jit(solution)/shard_map/forward_y_first/pallas_call | solution.py:270
  48.7 7.1 %crop.1.rest_0_ = bf16[32,32,128]{2,1,0:T(8,128)(2,1)} custom-call(s32[32]{0:T(128)} %get-tuple-element.38.rest_3_.rows, s32[32]{0:T(128)} %get-tuple-element.37.rest_4_.cols, s32[32]{0:T(128)} %get-tuple-element.16.rest_5_.odd, s32[32]{0:T(128)} %get-tuple-element.13.rest_6_.mine, bf16[512,4096]{1,0:T(8,128)(2,1)} %pot.1, ...), custom_call_target="tpu_custom_call" | custom-call | flops 1048576 | tf_op jit(solution)/shard_map/crop/pallas_call | solution.py:572
  55.8 9.2 %all-to-all-done.value = bf16[8,2,208,128]{3,2,1,0:T(8,128)(2,1)S(1)} async-done(((bf16[8,2,208,128]{3,2,1,0:T(8,128)(2,1)}), bf16[8,2,208,128]{3,2,1,0:T(8,128)(2,1)S(1)}, u32[]{:S(2)}, u32[]{:S(2)}) %all-to-all-start) | async-done | bytes 852000 | tf_op jit(solution)/shard_map/all_to_all | solution.py:747
  65.1 0.9 copy-done
  66.0 0.9 copy-done.4
  66.9 1.5 collective-permute-start.2
  68.4 3.6 %all-to-all-start.2 = ((bf16[8,4,32,128]{3,2,1,0:T(8,128)(2,1)}), bf16[8,4,32,128]{3,2,1,0:T(8,128)(2,1)S(1)}, u32[]{:S(2)}, u32[]{:S(2)}) async-start(bf16[8,4,32,128]{3,2,1,0:T(8,128)(2,1)} %order.5), calls=%async_computation.2 | async-start | bytes 524288 | tf_op jit(solution)/shard_map/all_to_all | solution.py:747
  72.0 6.1 %forward_y.2.refs_0_ = bf16[32,208,128]{2,1,0:T(8,128)(2,1)} custom-call(bf16[8,2,208,128]{3,2,1,0:T(8,128)(2,1)} %order.4.lines.rest_0_, bf16[512,256]{1,0:T(8,128)(2,1)} %constant.273.clone.section, bf16[64,2,32,128]{3,2,1,0:T(8,128)(2,1)} %forward_y_first.2.after.earlier, bf16[32,208,256]{2,1,0:T(8,128)(2,1)} %constant.274.clone.last), custom_call_target="tpu_custom_call" | custom-call | flops 1048576 | tf_op jit(solution)/shard_map/forward_y/pallas_call | solution.py:316
  78.1 3.4 %forward_y_first.3.earlier = bf16[64,2,32,128]{3,2,1,0:T(8,128)(2,1)} custom-call(bf16[8,2,208,128]{3,2,1,0:T(8,128)(2,1)} %copy-done.4, bf16[512,256]{1,0:T(8,128)(2,1)} %constant.273.clone.section), custom_call_target="tpu_custom_call" | custom-call | flops 1048576 | tf_op jit(solution)/shard_map/forward_y_first/pallas_call | solution.py:270
  81.5 4.5 %collective-permute-done.2.lines = bf16[8,2,208,128]{3,2,1,0:T(8,128)(2,1)S(1)} collective-permute-done((bf16[8,2,208,128]{3,2,1,0:T(8,128)(2,1)}, bf16[8,2,208,128]{3,2,1,0:T(8,128)(2,1)S(1)}, u32[]{:S(2)}, u32[]{:S(2)}) %collective-permute-start.2) | collective-permute-done | bytes 852000 | tf_op jit(solution)/shard_map/ppermute | solution.py:753
  86.0 0.9 copy-done.6
  86.9 6.1 %forward_y.3.refs_0_ = bf16[32,208,128]{2,1,0:T(8,128)(2,1)} custom-call(bf16[8,2,208,128]{3,2,1,0:T(8,128)(2,1)} %copy-done.6, bf16[512,256]{1,0:T(8,128)(2,1)} %constant.273.clone.section, bf16[64,2,32,128]{3,2,1,0:T(8,128)(2,1)} %forward_y_first.3.earlier, bf16[32,208,256]{2,1,0:T(8,128)(2,1)} %constant.274.clone.last, bf16[8,4,32,128]{3,2,1,0:T(8,128)(2,1)} %copy-done.1), custom_call_target="tpu_custom_call" | custom-call | flops 1048576 | tf_op jit(solution)/shard_map/forward_y/pallas_call | solution.py:316
  93.0 1.2 copy-done.5
  94.2 8.0 %inverse.2.refs_7_.refs_0_ = bf16[32,256,256]{2,1,0:T(8,128)(2,1)} custom-call(s32[12]{0:T(128)} %reshape.1008.rest_1_.sel, bf16[32,208,128]{2,1,0:T(8,128)(2,1)} %forward_y.2.refs_0_, bf16[32,208,128]{2,1,0:T(8,128)(2,1)} %copy-done.5, f32[208,128]{1,0:T(8,128)} %constant.275.clone.refs_2_, f32[4,1,128]{2,1,0:T(1,128)} %multiply_convert_fusion.rest_2_.refs_3_, ...), custom_call_target="tpu_custom_call" | custom-call | flops 1048576 | tf_op jit(solution)/shard_map/inverse/pallas_call | solution.py:424
  102.2 8.1 %inverse.3.refs_1_ = bf16[32,256,256]{2,1,0:T(8,128)(2,1)} custom-call(s32[12]{0:T(128)} %reshape.1008.rest_1_.sel, bf16[32,208,128]{2,1,0:T(8,128)(2,1)} %forward_y.3.refs_0_, bf16[32,208,128]{2,1,0:T(8,128)(2,1)} %collective-permute-done.3.refs_1_, f32[208,128]{1,0:T(8,128)} %constant.275.clone.refs_2_, f32[4,1,128]{2,1,0:T(1,128)} %multiply_convert_fusion.rest_2_.refs_3_, ...), custom_call_target="tpu_custom_call" | custom-call | flops 1048576 | tf_op jit(solution)/shard_map/inverse/pallas_call | solution.py:424
  110.3 7.9 %collect.2 = (bf16[16,2,4,16,128]{4,3,2,1,0:T(8,128)(2,1)}, bf16[16,2,4,16,128]{4,3,2,1,0:T(8,128)(2,1)}) custom-call(s32[4]{0:T(128)} %get-tuple-element.19.k1_pairs, bf16[32,256,256]{2,1,0:T(8,128)(2,1)} %inverse.2.refs_7_.refs_0_, bf16[32,256,256]{2,1,0:T(8,128)(2,1)} %inverse.3.refs_1_, s32[2,2,2,64,128]{4,3,2,1,0:T(8,128)} %broadcast_in_dim.2.rest_0_.refs_2_, ...), custom_call_target="tpu_custom_call" | custom-call | flops 1048576 | tf_op jit(solution)/shard_map/collect/pallas_call | solution.py:515
  118.2 0.2 dynamic-slice_reduce_fusion
  118.5 2.3 %collective-permute-start.4 = (bf16[16,2,4,16,128]{4,3,2,1,0:T(8,128)(2,1)}, bf16[16,2,4,16,128]{4,3,2,1,0:T(8,128)(2,1)S(1)}, u32[]{:S(2)}, u32[]{:S(2)}) collective-permute-start(bf16[16,2,4,16,128]{4,3,2,1,0:T(8,128)(2,1)} %get-tuple-element.9.refs_3_), channel_id=1, source_target_pairs={{0,4},{4,0},{8,12},{12,8},{16,20},{20,16},{24,28},{28,24},{1,5},{5... | collective-permute-start | bytes 1572872 | tf_op jit(solution)/shard_map/ppermute | solution.py:821
  120.9 0.1 add.415
  121.2 0.1 add.406
  121.3 7.9 %collect.3 = (bf16[16,2,4,16,128]{4,3,2,1,0:T(8,128)(2,1)}, bf16[16,2,4,16,128]{4,3,2,1,0:T(8,128)(2,1)}) custom-call(s32[4]{0:T(128)} %get-tuple-element.19.k1_pairs, bf16[32,256,256]{2,1,0:T(8,128)(2,1)} %inverse.2.refs_7_.refs_0_, bf16[32,256,256]{2,1,0:T(8,128)(2,1)} %inverse.3.refs_1_, s32[2,2,2,64,128]{4,3,2,1,0:T(8,128)} %broadcast_in_dim.2.rest_0_.refs_2_, ...), custom_call_target="tpu_custom_call" | custom-call | flops 1048576 | tf_op jit(solution)/shard_map/collect/pallas_call | solution.py:515
  129.2 3.5 %collective-permute-done.6 = bf16[16,2,4,16,128]{4,3,2,1,0:T(8,128)(2,1)S(1)} collective-permute-done((bf16[16,2,4,16,128]{4,3,2,1,0:T(8,128)(2,1)}, bf16[16,2,4,16,128]{4,3,2,1,0:T(8,128)(2,1)S(1)}, u32[]{:S(2)}, u32[]{:S(2)}) %collective-permute-start.6) | collective-permute-done | bytes 524320 | tf_op jit(solution)/shard_map/ppermute | solution.py:821
  132.8 1.2 convert_add_fusion
  134.1 2.3 %collective-permute-start.7 = (bf16[8,2,4,16,128]{4,3,2,1,0:T(8,128)(2,1)S(1)}, bf16[8,2,4,16,128]{4,3,2,1,0:T(8,128)(2,1)S(1)}, u32[]{:S(2)}, u32[]{:S(2)}) collective-permute-start(bf16[8,2,4,16,128]{4,3,2,1,0:T(8,128)(2,1)S(1)} %slice.72), channel_id=1, source_target_pairs={{0,4},{4,0},{8,12},{12,8},{16,20},{20,16},{24,28},{28,24},{1,5},{5... | collective-permute-start | bytes 786440 | tf_op jit(solution)/shard_map/ppermute | solution.py:821
  136.4 1.3 convert_add_fusion.1
  137.7 0.3 collective-permute-start.5
  138.1 0.1 fusion.23
  138.2 4.4 %collective-permute-done.7 = bf16[8,2,4,16,128]{4,3,2,1,0:T(8,128)(2,1)S(1)} collective-permute-done((bf16[8,2,4,16,128]{4,3,2,1,0:T(8,128)(2,1)S(1)}, bf16[8,2,4,16,128]{4,3,2,1,0:T(8,128)(2,1)S(1)}, u32[]{:S(2)}, u32[]{:S(2)}) %collective-permute-start.7) | collective-permute-done | bytes 262176 | tf_op jit(solution)/shard_map/ppermute | solution.py:821
  142.6 2.8 %collective-permute-done.5 = bf16[8,2,4,16,128]{4,3,2,1,0:T(8,128)(2,1)S(1)} collective-permute-done((bf16[8,2,4,16,128]{4,3,2,1,0:T(8,128)(2,1)S(1)}, bf16[8,2,4,16,128]{4,3,2,1,0:T(8,128)(2,1)S(1)}, u32[]{:S(2)}, u32[]{:S(2)}) %collective-permute-start.5) | collective-permute-done | bytes 262176 | tf_op jit(solution)/shard_map/ppermute | solution.py:821
  145.5 0.9 pad_maximum_fusion
  146.4 3.7 %all-to-all-start.3 = ((bf16[8,2,4,32,128]{4,3,2,1,0:T(8,128)(2,1)}), bf16[8,2,4,32,128]{4,3,2,1,0:T(8,128)(2,1)S(1)}, u32[]{:S(2)}, u32[]{:S(2)}) async-start(bf16[8,2,4,32,128]{4,3,2,1,0:T(8,128)(2,1)} %pad_maximum_fusion), calls=%async_computation.3 | async-start | bytes 1048576 | tf_op jit(solution)/shard_map/all_to_all | solution.py:834
  150.1 0.6 dynamic_slice.18.counts
  150.7 0.6 pad_maximum_fusion.2.alpha
  151.3 0.3 fusion.6
  151.6 0.7 pad_maximum_fusion.1.refs_2_
  152.3 0.7 reduce_sum.25.refs_1_
  153.0 12.5 %all-to-all-done.3 = bf16[8,2,4,32,128]{4,3,2,1,0:T(8,128)(2,1)S(1)} async-done(((bf16[8,2,4,32,128]{4,3,2,1,0:T(8,128)(2,1)}), bf16[8,2,4,32,128]{4,3,2,1,0:T(8,128)(2,1)S(1)}, u32[]{:S(2)}, u32[]{:S(2)}) %all-to-all-start.3) | async-done | bytes 524320 | tf_op jit(solution)/shard_map/all_to_all | solution.py:834
  165.4 0.8 reduce_sum.24.refs_0_
  166.3 4.0 %detect.1 = f32[1,256]{1,0:T(1,128)} custom-call(f32[2,4,12]{2,1,0:T(4,128)} %pad_maximum_fusion.2.alpha, s32[1]{0:T(128)} %dynamic_slice.18.counts, bf16[4,2,4,32,128]{4,3,2,1,0:T(8,128)(2,1)} %reduce_sum.24.refs_0_, bf16[4,32,128]{2,1,0:T(8,128)(2,1)} %reduce_sum.25.refs_1_, f32[4,2,32,128]{3,2,1,0:T(8,128)} %pad_maximum_fusion.1.refs_2_, ...), custom_call_target="tpu_custom_call" | custom-call | tf_op jit(solution)/shard_map/detect/pallas_call | solution.py:638
  170.3 0.7 slice_reduce_fusion
  171.0 0.1 reshape_squeeze.3
  171.1 0.6 copy.32
  (64 shorter events, 1.2 us)
Async XLA Ops:
  0.0 17.6 %copy-start.7 = (s32[4,2]{0,1:T(2,128)S(1)}, s32[4,2]{0,1:T(2,128)}, u32[]{:S(2)}) copy-start(s32[4,2]{0,1:T(2,128)} %param.21) | copy-start | bytes 100
  0.0 19.0 %copy-start.8 = (s32[32,4]{0,1:T(4,128)S(1)}, s32[32,4]{0,1:T(4,128)}, u32[]{:S(2)}) copy-start(s32[32,4]{0,1:T(4,128)} %param.23) | copy-start | bytes 1540
  10.2 28.9 %all-to-all-start.1 = ((bf16[8,2,208,128]{3,2,1,0:T(8,128)(2,1)}), bf16[8,2,208,128]{3,2,1,0:T(8,128)(2,1)S(1)}, u32[]{:S(2)}, u32[]{:S(2)}) async-start(bf16[8,2,208,128]{3,2,1,0:T(8,128)(2,1)} %forward_x.3), calls=%async_computation.1 | async-start | bytes 1703936 | tf_op jit(solution)/shard_map/all_to_all | solution.py:747
  23.9 12.5 %copy-start.9 = (s32[128]{0:T(128)S(1)}, s32[128]{0:T(128)}, u32[]{:S(2)}) copy-start(s32[128]{0:T(128)} %constant.269.clone) | copy-start | bytes 1540
  39.2 6.2 %copy-start.3 = (bf16[8,2,208,128]{3,2,1,0:T(8,128)(2,1)}, bf16[8,2,208,128]{3,2,1,0:T(8,128)(2,1)S(1)}, u32[]{:S(2)}) copy-start(bf16[8,2,208,128]{3,2,1,0:T(8,128)(2,1)S(1)} %all-to-all-done.1.lines) | copy-start | bytes 2555908
  39.2 25.9 %all-to-all-start = ((bf16[8,2,208,128]{3,2,1,0:T(8,128)(2,1)}), bf16[8,2,208,128]{3,2,1,0:T(8,128)(2,1)S(1)}, u32[]{:S(2)}, u32[]{:S(2)}) async-start(bf16[8,2,208,128]{3,2,1,0:T(8,128)(2,1)} %order.3), calls=%async_computation | async-start | bytes 1703936 | tf_op jit(solution)/shard_map/all_to_all | solution.py:747
  43.9 21.2 %collective-permute-start = (bf16[8,2,208,128]{3,2,1,0:T(8,128)(2,1)S(1)}, bf16[8,2,208,128]{3,2,1,0:T(8,128)(2,1)S(1)}, u32[]{:S(2)}, u32[]{:S(2)}) collective-permute-start(bf16[8,2,208,128]{3,2,1,0:T(8,128)(2,1)S(1)} %all-to-all-done.1.lines), channel_id=1, source_target_pairs={{0,2},{1,3},{2,0},{3,1},{4,6},{5,7},{6,4},{7,5},{8,10},{9,11},{10,... | collective-permute-start | bytes 2555912 | tf_op jit(solution)/shard_map/ppermute | solution.py:753
  65.1 0.9 copy-start
  66.0 0.9 copy-start.4
  66.9 19.1 %collective-permute-start.2 = (bf16[8,2,208,128]{3,2,1,0:T(8,128)(2,1)}, bf16[8,2,208,128]{3,2,1,0:T(8,128)(2,1)S(1)}, u32[]{:S(2)}, u32[]{:S(2)}) collective-permute-start(bf16[8,2,208,128]{3,2,1,0:T(8,128)(2,1)} %order.4.lines.rest_0_), channel_id=1, source_target_pairs={{0,2},{1,3},{2,0},{3,1},{4,6},{5,7},{6,4},{7,5},{8,10},{9,11},{10,... | collective-permute-start | bytes 2555912 | tf_op jit(solution)/shard_map/ppermute | solution.py:753
  68.4 13.1 %all-to-all-start.2 = ((bf16[8,4,32,128]{3,2,1,0:T(8,128)(2,1)}), bf16[8,4,32,128]{3,2,1,0:T(8,128)(2,1)S(1)}, u32[]{:S(2)}, u32[]{:S(2)}) async-start(bf16[8,4,32,128]{3,2,1,0:T(8,128)(2,1)} %order.5), calls=%async_computation.2 | async-start | bytes 524288 | tf_op jit(solution)/shard_map/all_to_all | solution.py:747
  78.1 14.8 %collective-permute-start.1 = (bf16[32,208,128]{2,1,0:T(8,128)(2,1)}, bf16[32,208,128]{2,1,0:T(8,128)(2,1)S(1)}, u32[]{:S(2)}, u32[]{:S(2)}) collective-permute-start(bf16[32,208,128]{2,1,0:T(8,128)(2,1)} %forward_y.2.refs_0_), channel_id=1, source_target_pairs={{0,1},{1,0},{2,3},{3,2},{4,5},{5,4},{6,7},{7,6},{8,9},{9,8},{10,11... | collective-permute-start | bytes 5111816 | tf_op jit(solution)/shard_map/ppermute | solution.py:753
  81.5 4.5 %copy-start.1 = (bf16[8,4,32,128]{3,2,1,0:T(8,128)(2,1)}, bf16[8,4,32,128]{3,2,1,0:T(8,128)(2,1)S(1)}, u32[]{:S(2)}) copy-start(bf16[8,4,32,128]{3,2,1,0:T(8,128)(2,1)S(1)} %all-to-all-done.2.rest_0_.refs_3_) | copy-start | bytes 786436
  86.0 0.9 copy-start.6
  93.0 9.2 %collective-permute-start.3 = (bf16[32,208,128]{2,1,0:T(8,128)(2,1)}, bf16[32,208,128]{2,1,0:T(8,128)(2,1)}, u32[]{:S(2)}, u32[]{:S(2)}) collective-permute-start(bf16[32,208,128]{2,1,0:T(8,128)(2,1)} %forward_y.3.refs_0_), channel_id=1, source_target_pairs={{0,1},{1,0},{2,3},{3,2},{4,5},{5,4},{6,7},{7,6},{8,9},{9,8},{10,11... | collective-permute-start | bytes 5111816 | tf_op jit(solution)/shard_map/ppermute | solution.py:753
  93.0 1.2 copy-start.5
  118.2 14.5 %collective-permute-start.6 = (bf16[16,2,4,16,128]{4,3,2,1,0:T(8,128)(2,1)}, bf16[16,2,4,16,128]{4,3,2,1,0:T(8,128)(2,1)S(1)}, u32[]{:S(2)}, u32[]{:S(2)}) collective-permute-start(bf16[16,2,4,16,128]{4,3,2,1,0:T(8,128)(2,1)} %get-tuple-element.12), channel_id=1, source_target_pairs={{0,8},{4,12},{8,0},{12,4},{16,24},{20,28},{24,16},{28,20},{1,9},{5... | collective-permute-start | bytes 1572872 | tf_op jit(solution)/shard_map/ppermute | solution.py:821
  118.5 17.9 %collective-permute-start.4 = (bf16[16,2,4,16,128]{4,3,2,1,0:T(8,128)(2,1)}, bf16[16,2,4,16,128]{4,3,2,1,0:T(8,128)(2,1)S(1)}, u32[]{:S(2)}, u32[]{:S(2)}) collective-permute-start(bf16[16,2,4,16,128]{4,3,2,1,0:T(8,128)(2,1)} %get-tuple-element.9.refs_3_), channel_id=1, source_target_pairs={{0,4},{4,0},{8,12},{12,8},{16,20},{20,16},{24,28},{28,24},{1,5},{5... | collective-permute-start | bytes 1572872 | tf_op jit(solution)/shard_map/ppermute | solution.py:821
  129.2 8.8 %copy-start.10 = (f32[4]{0:T(128)S(1)}, f32[4]{0:T(128)}, u32[]{:S(2)}) copy-start(f32[4]{0:T(128)} %param.22) | copy-start | bytes 52
  134.1 8.5 %collective-permute-start.7 = (bf16[8,2,4,16,128]{4,3,2,1,0:T(8,128)(2,1)S(1)}, bf16[8,2,4,16,128]{4,3,2,1,0:T(8,128)(2,1)S(1)}, u32[]{:S(2)}, u32[]{:S(2)}) collective-permute-start(bf16[8,2,4,16,128]{4,3,2,1,0:T(8,128)(2,1)S(1)} %slice.72), channel_id=1, source_target_pairs={{0,4},{4,0},{8,12},{12,8},{16,20},{20,16},{24,28},{28,24},{1,5},{5... | collective-permute-start | bytes 786440 | tf_op jit(solution)/shard_map/ppermute | solution.py:821
  136.4 13.7 %copy-start.11 = (s32[32]{0:T(128)S(1)}, s32[32]{0:T(128)}, u32[]{:S(2)}) copy-start(s32[32]{0:T(128)} %param.24) | copy-start | bytes 388
  136.4 15.9 %copy-start.2 = (bf16[8,4,32,128]{3,2,1,0:T(8,128)(2,1)S(1)}, bf16[8,4,32,128]{3,2,1,0:T(8,128)(2,1)}, u32[]{:S(2)}) copy-start(bf16[8,4,32,128]{3,2,1,0:T(8,128)(2,1)} %copy-done.1) | copy-start | bytes 786436
  137.7 7.7 %collective-permute-start.5 = (bf16[8,2,4,16,128]{4,3,2,1,0:T(8,128)(2,1)S(1)}, bf16[8,2,4,16,128]{4,3,2,1,0:T(8,128)(2,1)S(1)}, u32[]{:S(2)}, u32[]{:S(2)}) collective-permute-start(bf16[8,2,4,16,128]{4,3,2,1,0:T(8,128)(2,1)S(1)} %slice.73), channel_id=1, source_target_pairs={{0,8},{4,12},{8,0},{12,4},{16,24},{20,28},{24,16},{28,20},{1,9},{5... | collective-permute-start | bytes 786440 | tf_op jit(solution)/shard_map/ppermute | solution.py:821
  146.4 19.0 %all-to-all-start.3 = ((bf16[8,2,4,32,128]{4,3,2,1,0:T(8,128)(2,1)}), bf16[8,2,4,32,128]{4,3,2,1,0:T(8,128)(2,1)S(1)}, u32[]{:S(2)}, u32[]{:S(2)}) async-start(bf16[8,2,4,32,128]{4,3,2,1,0:T(8,128)(2,1)} %pad_maximum_fusion), calls=%async_computation.3 | async-start | bytes 1048576 | tf_op jit(solution)/shard_map/all_to_all | solution.py:834

commit v14 on v13

--- a/solution.py
+++ b/solution.py
@@ -627,19 +627,24 @@
         block, slot = divmod(i // G, slots // counts.shape[0])
         active = slot < counts[block]
         held[i * NDET : (i + 1) * NDET, :] = jnp.where(active, sums, 0.0)
-    out[...] = jnp.sum(held[...].T, axis=0, keepdims=True)
+    sums = jnp.sum(held[...].T, axis=0, keepdims=True)
+    each = slots // counts.shape[0]
+    for i in range(total):
+        block, slot = divmod(i // G, each)
+        out[block, slot, i % G : i % G + 1, :] = sums[:, i * NDET : (i + 1) * NDET]
 
 
 def detect(alpha, counts, fields, pot, plane, across, down, bins):
     slots = fields[0].shape[2]
     rows = -(-slots * G * NDET // LANES) * LANES
+    blocks = counts.shape[0]
     smem = pl.BlockSpec(memory_space=pltpu.SMEM)
     vmem = pl.BlockSpec(memory_space=pltpu.VMEM)
     return pl.pallas_call(
         functools.partial(detect_kernel, len(fields)),
         in_specs=[smem, smem] + [vmem] * (5 + len(fields)),
         out_specs=vmem,
-        out_shape=jax.ShapeDtypeStruct((1, rows), F32),
+        out_shape=jax.ShapeDtypeStruct((blocks, slots // blocks, G, NDET), F32),
         scratch_shapes=[
             pltpu.VMEM((2 * slots * G, HALF, LANES), BF),
             pltpu.VMEM((rows, LANES), F32),
@@ -817,16 +822,18 @@
     partial = other + collect(waves, k1_pairs, places, owners, 1, other[:1])
 
     def hop(value, bit):
-        pairs = [(i, i ^ (1 << bit)) for i in range(field_count)]
-        return lax.ppermute(value, "beam", pairs).astype(F32)
-
-    totals = []
+        return lax.ppermute(value, "beam", [(i, i ^ (1 << bit)) for i in range(field_count)])
+
+    def total(arrays, span):
+        return functools.reduce(jnp.add, [array[span].astype(F32) for array in arrays])
+
+    moving, staying = slice(0, owners // 2), slice(owners // 2, owners)
     arrived = [hop(partial[part], part) for part in range(PARTS)]
-    for part in range(PARTS):
-        own = partial[PARTS + part].astype(F32) + arrived[part]
-        rest = own[: owners // 2].astype(BF)
-        totals.append(own[owners // 2 :] + hop(rest, 1 - part))
-    tiles = jnp.concatenate(totals, axis=3).astype(BF)
+    halves = [[partial[PARTS + part], arrived[part]] for part in range(PARTS)]
+    passed = [hop(total(halves[part], moving).astype(BF), 1 - part) for part in range(PARTS)]
+    tiles = jnp.concatenate(
+        [total(halves[part], staying) + passed[part].astype(F32) for part in range(PARTS)], axis=3
+    ).astype(BF)
     groups = [
         [b * hold_count + h for b in range(g, field_count, 4) for h in range(hold_count)]
         for g in range(4)
@@ -850,8 +857,7 @@
     first_block = (field_pos * hold_count + hold_pos) * blocks_dev
     counts = lax.dynamic_slice_in_dim(tile_count, first_block, blocks_dev, 0)
     bins = detect_tables(beam_total)
-    sums = detect(alpha, counts, fields, crops, plane_waves(beam_index), *bins)
-    return sums[0, : own_slots * G * NDET].reshape(blocks_dev, slot_count, G, NDET)
+    return detect(alpha, counts, fields, crops, plane_waves(beam_index), *bins)
 
 
 def solution(mesh):

time: 173 us -> 173 us (level)
    add x2 -> x0, other arithmetic: 2.47 us -> none  [shards(): own = partial[PARTS + part].astype(F32) + arrived[part]]
    convert_element_type x0 -> x2, other arithmetic: none -> 2.05 us  [shards(): total(halves[part], moving).astype(BF)]
    another operation x2, other arithmetic: 0.14 us -> 2.12 us
where the time goes in v14:
time: 173 us; the launch traced here: 172 us
  Pallas kernels  82.5 us (48%)
  waiting for transfers between devices  37.3 us (22%)
  starting transfers between devices  27.1 us (16%)
  other arithmetic  12.7 us (7%)
  local copies, waits for them, and re-layouts  10.7 us (6%)
    pallas_call x2, Pallas kernels, forward_x(): pl.pallas_call(forward_x_kernel, grid_spec=pltpu.PrefetchScalarGridSpec(n...  20.4 us
    pallas_call x2, Pallas kernels, inverse(): pl.pallas_call(functools.partial(inverse_kernel, steps, which, near), gri...  16.1 us
    pallas_call x2, Pallas kernels, collect(): pl.pallas_call(functools.partial(collect_kernel, len(sheets)), grid_spec=...  16 us
    all_to_all x3, starting transfers between devices, trade(): return lax.all_to_all(value, axis, split_axis=0, concat_axis=0, tiled=True)  15.4 us
    all_to_all x1, waiting for transfers between devices, shards(): lax.all_to_all(tiles, ('beam', 'slab'), split_axis=0, concat_axis=0, axis...  12.5 us
    pallas_call x2, Pallas kernels, forward_y(): pl.pallas_call(forward_y_kernel, grid=(1 + steps,), in_specs=[pl.BlockSpe...  12.2 us
    all_to_all x3, waiting for transfers between devices, trade(): return lax.all_to_all(value, axis, split_axis=0, concat_axis=0, tiled=True)  10.7 us
    ppermute x4, waiting for transfers between devices, hop(): lax.ppermute(value, 'beam', [(i, i ^ 1 << bit) for i in range(field_count)])  9.56 us
  transfers between devices with their start and end apart: 12, of which 7 were waited for; matrix products, arithmetic and copies ran while one was open for 9% of the time, Pallas kernels for 30%

profile of v14, /device:TPU:0, one launch (start us, length us, event | category | flops | bytes accessed | tf_op | source)
XLA Modules:
  0.0 171.8 jit_solution(16808258516582177396)
XLA Ops:
  0.0 10.2 %forward_x.3 = bf16[8,2,208,128]{3,2,1,0:T(8,128)(2,1)} custom-call(s32[1]{0:T(128)} %bitcast.3.sel, bf16[8,4,16,4096]{3,2,1,0:T(8,128)(2,1)} %bitcast.40, bf16[4,512,1024]{2,1,0:T(8,128)(2,1)} %constant.270.clone.section, bf16[4,8,208,256]{3,2,1,0:T(8,128)(2,1)} %constant.271.clone.last, bf16[128,128]{1,0:T(8,128)(2,1)} %constant.272.clone.perm), custom_call_target="tpu_custom_call" | custom-call | flops 1048576 | tf_op jit(solution)/shard_map/forward_x/pallas_call | solution.py:198
  10.2 7.3 %all-to-all-start.1 = ((bf16[8,2,208,128]{3,2,1,0:T(8,128)(2,1)}), bf16[8,2,208,128]{3,2,1,0:T(8,128)(2,1)S(1)}, u32[]{:S(2)}, u32[]{:S(2)}) async-start(bf16[8,2,208,128]{3,2,1,0:T(8,128)(2,1)} %forward_x.3), calls=%async_computation.1 | async-start | bytes 1703936 | tf_op jit(solution)/shard_map/all_to_all | solution.py:752
  17.6 0.6 fusion.22
  18.9 0.1 reshape_reshape.3
  19.0 0.1 copy.28
  19.2 0.6 gather_fusion
  19.8 0.6 gather_fusion.1
  20.4 0.1 stack.55
  20.5 0.1 stack.54
  21.4 0.7 reshape.1008.rest_1_.sel
  22.1 1.3 fusion.13
  23.5 0.1 copy.31
  23.7 10.2 %forward_x.2.value = bf16[8,2,208,128]{3,2,1,0:T(8,128)(2,1)} custom-call(s32[1]{0:T(128)} %bitcast.3.sel, bf16[8,4,16,4096]{3,2,1,0:T(8,128)(2,1)} %bitcast.41, bf16[4,512,1024]{2,1,0:T(8,128)(2,1)} %constant.270.clone.section, bf16[4,8,208,256]{3,2,1,0:T(8,128)(2,1)} %constant.271.clone.last, bf16[128,128]{1,0:T(8,128)(2,1)} %constant.272.clone.perm), custom_call_target="tpu_custom_call" | custom-call | flops 1048576 | tf_op jit(solution)/shard_map/forward_x/pallas_call | solution.py:198
  33.9 0.6 broadcast_add_fusion
  34.5 0.6 compare_convert_fusion
  35.0 0.6 and_select_fusion.5
  35.6 0.6 and_select_fusion.6
  36.2 0.7 multiply_convert_fusion.rest_2_.refs_3_
  36.8 0.8 broadcast_in_dim.2.rest_0_.refs_2_
  37.7 1.4 all-to-all-done.1.lines
  39.1 4.5 %all-to-all-start = ((bf16[8,2,208,128]{3,2,1,0:T(8,128)(2,1)}), bf16[8,2,208,128]{3,2,1,0:T(8,128)(2,1)S(1)}, u32[]{:S(2)}, u32[]{:S(2)}) async-start(bf16[8,2,208,128]{3,2,1,0:T(8,128)(2,1)} %order.3), calls=%async_computation | async-start | bytes 1703936 | tf_op jit(solution)/shard_map/all_to_all | solution.py:752
  43.7 1.5 collective-permute-start
  45.1 3.3 %forward_y_first.2.after.earlier = bf16[64,2,32,128]{3,2,1,0:T(8,128)(2,1)} custom-call(bf16[8,2,208,128]{3,2,1,0:T(8,128)(2,1)} %copy-done.3, bf16[512,256]{1,0:T(8,128)(2,1)} %constant.273.clone.section), custom_call_target="tpu_custom_call" | custom-call | flops 1048576 | tf_op jit(solution)/shard_map/forward_y_first/pallas_call | solution.py:270
  48.5 7.1 %crop.1.rest_0_ = bf16[32,32,128]{2,1,0:T(8,128)(2,1)} custom-call(s32[32]{0:T(128)} %get-tuple-element.38.rest_3_.rows, s32[32]{0:T(128)} %get-tuple-element.37.rest_4_.cols, s32[32]{0:T(128)} %get-tuple-element.16.rest_5_.odd, s32[32]{0:T(128)} %get-tuple-element.13.rest_6_.mine, bf16[512,4096]{1,0:T(8,128)(2,1)} %pot.1, ...), custom_call_target="tpu_custom_call" | custom-call | flops 1048576 | tf_op jit(solution)/shard_map/crop/pallas_call | solution.py:572
  55.6 9.2 %all-to-all-done.value = bf16[8,2,208,128]{3,2,1,0:T(8,128)(2,1)S(1)} async-done(((bf16[8,2,208,128]{3,2,1,0:T(8,128)(2,1)}), bf16[8,2,208,128]{3,2,1,0:T(8,128)(2,1)S(1)}, u32[]{:S(2)}, u32[]{:S(2)}) %all-to-all-start) | async-done | bytes 852000 | tf_op jit(solution)/shard_map/all_to_all | solution.py:752
  64.8 0.9 copy-done
  65.7 0.9 copy-done.4
  66.6 1.5 collective-permute-start.2
  68.1 3.6 %all-to-all-start.2 = ((bf16[8,4,32,128]{3,2,1,0:T(8,128)(2,1)}), bf16[8,4,32,128]{3,2,1,0:T(8,128)(2,1)S(1)}, u32[]{:S(2)}, u32[]{:S(2)}) async-start(bf16[8,4,32,128]{3,2,1,0:T(8,128)(2,1)} %order.5), calls=%async_computation.2 | async-start | bytes 524288 | tf_op jit(solution)/shard_map/all_to_all | solution.py:752
  71.7 6.1 %forward_y.2.refs_0_ = bf16[32,208,128]{2,1,0:T(8,128)(2,1)} custom-call(bf16[8,2,208,128]{3,2,1,0:T(8,128)(2,1)} %order.4.lines.rest_0_, bf16[512,256]{1,0:T(8,128)(2,1)} %constant.273.clone.section, bf16[64,2,32,128]{3,2,1,0:T(8,128)(2,1)} %forward_y_first.2.after.earlier, bf16[32,208,256]{2,1,0:T(8,128)(2,1)} %constant.274.clone.last), custom_call_target="tpu_custom_call" | custom-call | flops 1048576 | tf_op jit(solution)/shard_map/forward_y/pallas_call | solution.py:316
  77.8 3.3 %forward_y_first.3.earlier = bf16[64,2,32,128]{3,2,1,0:T(8,128)(2,1)} custom-call(bf16[8,2,208,128]{3,2,1,0:T(8,128)(2,1)} %copy-done.4, bf16[512,256]{1,0:T(8,128)(2,1)} %constant.273.clone.section), custom_call_target="tpu_custom_call" | custom-call | flops 1048576 | tf_op jit(solution)/shard_map/forward_y_first/pallas_call | solution.py:270
  81.2 4.5 %collective-permute-done.2.lines = bf16[8,2,208,128]{3,2,1,0:T(8,128)(2,1)S(1)} collective-permute-done((bf16[8,2,208,128]{3,2,1,0:T(8,128)(2,1)}, bf16[8,2,208,128]{3,2,1,0:T(8,128)(2,1)S(1)}, u32[]{:S(2)}, u32[]{:S(2)}) %collective-permute-start.2) | collective-permute-done | bytes 852000 | tf_op jit(solution)/shard_map/ppermute | solution.py:758
  85.7 0.9 copy-done.6
  86.6 6.1 %forward_y.3.refs_0_ = bf16[32,208,128]{2,1,0:T(8,128)(2,1)} custom-call(bf16[8,2,208,128]{3,2,1,0:T(8,128)(2,1)} %copy-done.6, bf16[512,256]{1,0:T(8,128)(2,1)} %constant.273.clone.section, bf16[64,2,32,128]{3,2,1,0:T(8,128)(2,1)} %forward_y_first.3.earlier, bf16[32,208,256]{2,1,0:T(8,128)(2,1)} %constant.274.clone.last, bf16[8,4,32,128]{3,2,1,0:T(8,128)(2,1)} %copy-done.1), custom_call_target="tpu_custom_call" | custom-call | flops 1048576 | tf_op jit(solution)/shard_map/forward_y/pallas_call | solution.py:316
  92.7 1.2 copy-done.5
  93.9 8.0 %inverse.2.refs_7_.refs_0_ = bf16[32,256,256]{2,1,0:T(8,128)(2,1)} custom-call(s32[12]{0:T(128)} %reshape.1008.rest_1_.sel, bf16[32,208,128]{2,1,0:T(8,128)(2,1)} %forward_y.2.refs_0_, bf16[32,208,128]{2,1,0:T(8,128)(2,1)} %copy-done.5, f32[208,128]{1,0:T(8,128)} %constant.275.clone.refs_2_, f32[4,1,128]{2,1,0:T(1,128)} %multiply_convert_fusion.rest_2_.refs_3_, ...), custom_call_target="tpu_custom_call" | custom-call | flops 1048576 | tf_op jit(solution)/shard_map/inverse/pallas_call | solution.py:424
  101.9 8.1 %inverse.3.refs_1_ = bf16[32,256,256]{2,1,0:T(8,128)(2,1)} custom-call(s32[12]{0:T(128)} %reshape.1008.rest_1_.sel, bf16[32,208,128]{2,1,0:T(8,128)(2,1)} %forward_y.3.refs_0_, bf16[32,208,128]{2,1,0:T(8,128)(2,1)} %collective-permute-done.3.refs_1_, f32[208,128]{1,0:T(8,128)} %constant.275.clone.refs_2_, f32[4,1,128]{2,1,0:T(1,128)} %multiply_convert_fusion.rest_2_.refs_3_, ...), custom_call_target="tpu_custom_call" | custom-call | flops 1048576 | tf_op jit(solution)/shard_map/inverse/pallas_call | solution.py:424
  110.0 7.9 %collect.2 = (bf16[16,2,4,16,128]{4,3,2,1,0:T(8,128)(2,1)}, bf16[16,2,4,16,128]{4,3,2,1,0:T(8,128)(2,1)}) custom-call(s32[4]{0:T(128)} %get-tuple-element.19.k1_pairs, bf16[32,256,256]{2,1,0:T(8,128)(2,1)} %inverse.2.refs_7_.refs_0_, bf16[32,256,256]{2,1,0:T(8,128)(2,1)} %inverse.3.refs_1_, s32[2,2,2,64,128]{4,3,2,1,0:T(8,128)} %broadcast_in_dim.2.rest_0_.refs_2_, ...), custom_call_target="tpu_custom_call" | custom-call | flops 1048576 | tf_op jit(solution)/shard_map/collect/pallas_call | solution.py:515
  118.0 0.2 dynamic-slice_reduce_fusion
  118.2 2.3 %collective-permute-start.4 = (bf16[16,2,4,16,128]{4,3,2,1,0:T(8,128)(2,1)}, bf16[16,2,4,16,128]{4,3,2,1,0:T(8,128)(2,1)S(1)}, u32[]{:S(2)}, u32[]{:S(2)}) collective-permute-start(bf16[16,2,4,16,128]{4,3,2,1,0:T(8,128)(2,1)} %get-tuple-element.9.refs_3_), channel_id=1, source_target_pairs={{0,4},{4,0},{8,12},{12,8},{16,20},{20,16},{24,28},{28,24},{1,5},{5... | collective-permute-start | bytes 1572872 | tf_op jit(solution)/shard_map/ppermute | solution.py:825
  120.6 0.1 add.421
  120.7 0.1 add.423
  121.1 8.0 %collect.3 = (bf16[16,2,4,16,128]{4,3,2,1,0:T(8,128)(2,1)}, bf16[16,2,4,16,128]{4,3,2,1,0:T(8,128)(2,1)}) custom-call(s32[4]{0:T(128)} %get-tuple-element.19.k1_pairs, bf16[32,256,256]{2,1,0:T(8,128)(2,1)} %inverse.2.refs_7_.refs_0_, bf16[32,256,256]{2,1,0:T(8,128)(2,1)} %inverse.3.refs_1_, s32[2,2,2,64,128]{4,3,2,1,0:T(8,128)} %broadcast_in_dim.2.rest_0_.refs_2_, ...), custom_call_target="tpu_custom_call" | custom-call | flops 1048576 | tf_op jit(solution)/shard_map/collect/pallas_call | solution.py:515
  129.1 3.4 %collective-permute-done.6 = bf16[16,2,4,16,128]{4,3,2,1,0:T(8,128)(2,1)S(1)} collective-permute-done((bf16[16,2,4,16,128]{4,3,2,1,0:T(8,128)(2,1)}, bf16[16,2,4,16,128]{4,3,2,1,0:T(8,128)(2,1)S(1)}, u32[]{:S(2)}, u32[]{:S(2)}) %collective-permute-start.6) | collective-permute-done | bytes 524320 | tf_op jit(solution)/shard_map/ppermute | solution.py:825
  132.5 1.0 add_convert_fusion.1
  133.5 2.3 %collective-permute-start.7 = (bf16[8,2,4,16,128]{4,3,2,1,0:T(8,128)(2,1)S(1)}, bf16[8,2,4,16,128]{4,3,2,1,0:T(8,128)(2,1)S(1)}, u32[]{:S(2)}, u32[]{:S(2)}) collective-permute-start(bf16[8,2,4,16,128]{4,3,2,1,0:T(8,128)(2,1)S(1)} %add_convert_fusion.1), channel_id=1, source_target_pairs={{0,4},{4,0},{8,12},{12,8},{16,20},{20,16},{24,28},{28,24},{1,5},{5... | collective-permute-start | bytes 786440 | tf_op jit(solution)/shard_map/ppermute | solution.py:825
  135.9 1.0 add_convert_fusion.3
  136.9 0.3 collective-permute-start.5
  137.3 0.1 fusion.21
  137.4 4.7 %collective-permute-done.7 = bf16[8,2,4,16,128]{4,3,2,1,0:T(8,128)(2,1)S(1)} collective-permute-done((bf16[8,2,4,16,128]{4,3,2,1,0:T(8,128)(2,1)S(1)}, bf16[8,2,4,16,128]{4,3,2,1,0:T(8,128)(2,1)S(1)}, u32[]{:S(2)}, u32[]{:S(2)}) %collective-permute-start.7) | collective-permute-done | bytes 262176 | tf_op jit(solution)/shard_map/ppermute | solution.py:825
  142.1 1.1 add_convert_fusion
  143.2 1.5 collective-permute-done.5
  144.6 1.1 add_convert_fusion.2
  145.7 0.8 pad_maximum_fusion
  146.5 3.7 %all-to-all-start.3 = ((bf16[8,2,4,32,128]{4,3,2,1,0:T(8,128)(2,1)}), bf16[8,2,4,32,128]{4,3,2,1,0:T(8,128)(2,1)S(1)}, u32[]{:S(2)}, u32[]{:S(2)}) async-start(bf16[8,2,4,32,128]{4,3,2,1,0:T(8,128)(2,1)} %pad_maximum_fusion), calls=%async_computation.3 | async-start | bytes 1048576 | tf_op jit(solution)/shard_map/all_to_all | solution.py:841
  150.2 0.6 dynamic_slice.18.counts
  150.8 0.6 pad_maximum_fusion.2.alpha
  151.4 0.3 fusion.4
  151.8 0.7 pad_maximum_fusion.1.refs_2_
  152.4 0.6 reduce_sum.25.refs_1_
  153.1 12.5 %all-to-all-done.3 = bf16[8,2,4,32,128]{4,3,2,1,0:T(8,128)(2,1)S(1)} async-done(((bf16[8,2,4,32,128]{4,3,2,1,0:T(8,128)(2,1)}), bf16[8,2,4,32,128]{4,3,2,1,0:T(8,128)(2,1)S(1)}, u32[]{:S(2)}, u32[]{:S(2)}) %all-to-all-start.3) | async-done | bytes 524320 | tf_op jit(solution)/shard_map/all_to_all | solution.py:841
  165.6 0.8 reduce_sum.24.refs_0_
  166.4 4.1 %detect.1 = f32[1,4,3,16]{3,2,1,0:T(4,128)} custom-call(f32[2,4,12]{2,1,0:T(4,128)} %pad_maximum_fusion.2.alpha, s32[1]{0:T(128)} %dynamic_slice.18.counts, bf16[4,2,4,32,128]{4,3,2,1,0:T(8,128)(2,1)} %reduce_sum.24.refs_0_, bf16[4,32,128]{2,1,0:T(8,128)(2,1)} %reduce_sum.25.refs_1_, f32[4,2,32,128]{3,2,1,0:T(8,128)} %pad_maximum_fusion.1.refs_2_, ...), custom_call_target="tpu_custom_call" | custom-call | tf_op jit(solution)/shard_map/detect/pallas_call | solution.py:643
  170.5 1.3 copy.32
  (60 shorter events, 1.0 us)
Async XLA Ops:
  0.0 17.5 %copy-start.7 = (s32[4,2]{0,1:T(2,128)S(1)}, s32[4,2]{0,1:T(2,128)}, u32[]{:S(2)}) copy-start(s32[4,2]{0,1:T(2,128)} %param.21) | copy-start | bytes 100
  0.0 18.9 %copy-start.8 = (s32[32,4]{0,1:T(4,128)S(1)}, s32[32,4]{0,1:T(4,128)}, u32[]{:S(2)}) copy-start(s32[32,4]{0,1:T(4,128)} %param.23) | copy-start | bytes 1540
  10.2 28.9 %all-to-all-start.1 = ((bf16[8,2,208,128]{3,2,1,0:T(8,128)(2,1)}), bf16[8,2,208,128]{3,2,1,0:T(8,128)(2,1)S(1)}, u32[]{:S(2)}, u32[]{:S(2)}) async-start(bf16[8,2,208,128]{3,2,1,0:T(8,128)(2,1)} %forward_x.3), calls=%async_computation.1 | async-start | bytes 1703936 | tf_op jit(solution)/shard_map/all_to_all | solution.py:752
  23.7 12.5 %copy-start.9 = (s32[128]{0:T(128)S(1)}, s32[128]{0:T(128)}, u32[]{:S(2)}) copy-start(s32[128]{0:T(128)} %constant.269.clone) | copy-start | bytes 1540
  39.1 6.0 %copy-start.3 = (bf16[8,2,208,128]{3,2,1,0:T(8,128)(2,1)}, bf16[8,2,208,128]{3,2,1,0:T(8,128)(2,1)S(1)}, u32[]{:S(2)}) copy-start(bf16[8,2,208,128]{3,2,1,0:T(8,128)(2,1)S(1)} %all-to-all-done.1.lines) | copy-start | bytes 2555908
  39.1 25.7 %all-to-all-start = ((bf16[8,2,208,128]{3,2,1,0:T(8,128)(2,1)}), bf16[8,2,208,128]{3,2,1,0:T(8,128)(2,1)S(1)}, u32[]{:S(2)}, u32[]{:S(2)}) async-start(bf16[8,2,208,128]{3,2,1,0:T(8,128)(2,1)} %order.3), calls=%async_computation | async-start | bytes 1703936 | tf_op jit(solution)/shard_map/all_to_all | solution.py:752
  43.7 21.2 %collective-permute-start = (bf16[8,2,208,128]{3,2,1,0:T(8,128)(2,1)S(1)}, bf16[8,2,208,128]{3,2,1,0:T(8,128)(2,1)S(1)}, u32[]{:S(2)}, u32[]{:S(2)}) collective-permute-start(bf16[8,2,208,128]{3,2,1,0:T(8,128)(2,1)S(1)} %all-to-all-done.1.lines), channel_id=1, source_target_pairs={{0,2},{1,3},{2,0},{3,1},{4,6},{5,7},{6,4},{7,5},{8,10},{9,11},{10,... | collective-permute-start | bytes 2555912 | tf_op jit(solution)/shard_map/ppermute | solution.py:758
  64.8 0.9 copy-start
  65.7 0.9 copy-start.4
  66.6 19.1 %collective-permute-start.2 = (bf16[8,2,208,128]{3,2,1,0:T(8,128)(2,1)}, bf16[8,2,208,128]{3,2,1,0:T(8,128)(2,1)S(1)}, u32[]{:S(2)}, u32[]{:S(2)}) collective-permute-start(bf16[8,2,208,128]{3,2,1,0:T(8,128)(2,1)} %order.4.lines.rest_0_), channel_id=1, source_target_pairs={{0,2},{1,3},{2,0},{3,1},{4,6},{5,7},{6,4},{7,5},{8,10},{9,11},{10,... | collective-permute-start | bytes 2555912 | tf_op jit(solution)/shard_map/ppermute | solution.py:758
  68.1 13.1 %all-to-all-start.2 = ((bf16[8,4,32,128]{3,2,1,0:T(8,128)(2,1)}), bf16[8,4,32,128]{3,2,1,0:T(8,128)(2,1)S(1)}, u32[]{:S(2)}, u32[]{:S(2)}) async-start(bf16[8,4,32,128]{3,2,1,0:T(8,128)(2,1)} %order.5), calls=%async_computation.2 | async-start | bytes 524288 | tf_op jit(solution)/shard_map/all_to_all | solution.py:752
  77.8 14.9 %collective-permute-start.1 = (bf16[32,208,128]{2,1,0:T(8,128)(2,1)}, bf16[32,208,128]{2,1,0:T(8,128)(2,1)S(1)}, u32[]{:S(2)}, u32[]{:S(2)}) collective-permute-start(bf16[32,208,128]{2,1,0:T(8,128)(2,1)} %forward_y.2.refs_0_), channel_id=1, source_target_pairs={{0,1},{1,0},{2,3},{3,2},{4,5},{5,4},{6,7},{7,6},{8,9},{9,8},{10,11... | collective-permute-start | bytes 5111816 | tf_op jit(solution)/shard_map/ppermute | solution.py:758
  81.2 4.5 %copy-start.1 = (bf16[8,4,32,128]{3,2,1,0:T(8,128)(2,1)}, bf16[8,4,32,128]{3,2,1,0:T(8,128)(2,1)S(1)}, u32[]{:S(2)}) copy-start(bf16[8,4,32,128]{3,2,1,0:T(8,128)(2,1)S(1)} %all-to-all-done.2.rest_0_.refs_3_) | copy-start | bytes 786436
  85.7 0.9 copy-start.6
  92.7 9.2 %collective-permute-start.3 = (bf16[32,208,128]{2,1,0:T(8,128)(2,1)}, bf16[32,208,128]{2,1,0:T(8,128)(2,1)}, u32[]{:S(2)}, u32[]{:S(2)}) collective-permute-start(bf16[32,208,128]{2,1,0:T(8,128)(2,1)} %forward_y.3.refs_0_), channel_id=1, source_target_pairs={{0,1},{1,0},{2,3},{3,2},{4,5},{5,4},{6,7},{7,6},{8,9},{9,8},{10,11... | collective-permute-start | bytes 5111816 | tf_op jit(solution)/shard_map/ppermute | solution.py:758
  92.7 1.2 copy-start.5
  118.0 14.5 %collective-permute-start.6 = (bf16[16,2,4,16,128]{4,3,2,1,0:T(8,128)(2,1)}, bf16[16,2,4,16,128]{4,3,2,1,0:T(8,128)(2,1)S(1)}, u32[]{:S(2)}, u32[]{:S(2)}) collective-permute-start(bf16[16,2,4,16,128]{4,3,2,1,0:T(8,128)(2,1)} %get-tuple-element.12), channel_id=1, source_target_pairs={{0,8},{4,12},{8,0},{12,4},{16,24},{20,28},{24,16},{28,20},{1,9},{5... | collective-permute-start | bytes 1572872 | tf_op jit(solution)/shard_map/ppermute | solution.py:825
  118.2 17.7 %collective-permute-start.4 = (bf16[16,2,4,16,128]{4,3,2,1,0:T(8,128)(2,1)}, bf16[16,2,4,16,128]{4,3,2,1,0:T(8,128)(2,1)S(1)}, u32[]{:S(2)}, u32[]{:S(2)}) collective-permute-start(bf16[16,2,4,16,128]{4,3,2,1,0:T(8,128)(2,1)} %get-tuple-element.9.refs_3_), channel_id=1, source_target_pairs={{0,4},{4,0},{8,12},{12,8},{16,20},{20,16},{24,28},{28,24},{1,5},{5... | collective-permute-start | bytes 1572872 | tf_op jit(solution)/shard_map/ppermute | solution.py:825
  121.1 16.2 %copy-start.10 = (f32[4]{0:T(128)S(1)}, f32[4]{0:T(128)}, u32[]{:S(2)}) copy-start(f32[4]{0:T(128)} %param.22) | copy-start | bytes 52
  129.1 21.1 %copy-start.11 = (s32[32]{0:T(128)S(1)}, s32[32]{0:T(128)}, u32[]{:S(2)}) copy-start(s32[32]{0:T(128)} %param.24) | copy-start | bytes 388
  129.1 23.3 %copy-start.2 = (bf16[8,4,32,128]{3,2,1,0:T(8,128)(2,1)S(1)}, bf16[8,4,32,128]{3,2,1,0:T(8,128)(2,1)}, u32[]{:S(2)}) copy-start(bf16[8,4,32,128]{3,2,1,0:T(8,128)(2,1)} %copy-done.1) | copy-start | bytes 786436
  133.5 8.5 %collective-permute-start.7 = (bf16[8,2,4,16,128]{4,3,2,1,0:T(8,128)(2,1)S(1)}, bf16[8,2,4,16,128]{4,3,2,1,0:T(8,128)(2,1)S(1)}, u32[]{:S(2)}, u32[]{:S(2)}) collective-permute-start(bf16[8,2,4,16,128]{4,3,2,1,0:T(8,128)(2,1)S(1)} %add_convert_fusion.1), channel_id=1, source_target_pairs={{0,4},{4,0},{8,12},{12,8},{16,20},{20,16},{24,28},{28,24},{1,5},{5... | collective-permute-start | bytes 786440 | tf_op jit(solution)/shard_map/ppermute | solution.py:825
  136.9 7.7 %collective-permute-start.5 = (bf16[8,2,4,16,128]{4,3,2,1,0:T(8,128)(2,1)S(1)}, bf16[8,2,4,16,128]{4,3,2,1,0:T(8,128)(2,1)S(1)}, u32[]{:S(2)}, u32[]{:S(2)}) collective-permute-start(bf16[8,2,4,16,128]{4,3,2,1,0:T(8,128)(2,1)S(1)} %add_convert_fusion.3), channel_id=1, source_target_pairs={{0,8},{4,12},{8,0},{12,4},{16,24},{20,28},{24,16},{28,20},{1,9},{5... | collective-permute-start | bytes 786440 | tf_op jit(solution)/shard_map/ppermute | solution.py:825
  146.5 19.0 %all-to-all-start.3 = ((bf16[8,2,4,32,128]{4,3,2,1,0:T(8,128)(2,1)}), bf16[8,2,4,32,128]{4,3,2,1,0:T(8,128)(2,1)S(1)}, u32[]{:S(2)}, u32[]{:S(2)}) async-start(bf16[8,2,4,32,128]{4,3,2,1,0:T(8,128)(2,1)} %pad_maximum_fusion), calls=%async_computation.3 | async-start | bytes 1048576 | tf_op jit(solution)/shard_map/all_to_all | solution.py:841

commit v15 on v14

--- a/solution.py
+++ b/solution.py
@@ -169,7 +169,7 @@
         sin_ref[pl.ds(2 * t, 2)] = sine.astype(BF).reshape(2, A, lanes)
         return carry
 
-    lax.fori_loop(0, N // LANES, chunk, 0, unroll=8)
+    lax.fori_loop(0, N // LANES, chunk, 0, unroll=16)
     table = section[0]
     for m in range(HIGH):
         span = slice(m * SUB, (m + 1) * SUB)
@@ -381,7 +381,7 @@
                         ]
             return carry
 
-        lax.fori_loop(0, count, pair, 0, unroll=8)
+        lax.fori_loop(0, count, pair, 0, unroll=16)
 
     @pl.when(step >= steps)
     def _():
@@ -403,7 +403,7 @@
                         ]
             return carry
 
-        lax.fori_loop(0, each, line, 0, unroll=8)
+        lax.fori_loop(0, each, line, 0, unroll=16)
 
 
 def inverse(which, sel, specs, freq_y, square_x, table_y, table_x, after):

time: 173 us -> 171 us (0.988)
  Pallas kernels: 82.5 us -> 80.5 us
where the time goes in v15:
time: 171 us; the launch traced here: 170 us
  Pallas kernels  80.5 us (47%)
  waiting for transfers between devices  37.5 us (22%)
  starting transfers between devices  26.9 us (16%)
  other arithmetic  12.7 us (7%)
  local copies, waits for them, and re-layouts  10.7 us (6%)
    pallas_call x2, Pallas kernels, forward_x(): pl.pallas_call(forward_x_kernel, grid_spec=pltpu.PrefetchScalarGridSpec(n...  19.9 us
    pallas_call x2, Pallas kernels, collect(): pl.pallas_call(functools.partial(collect_kernel, len(sheets)), grid_spec=...  16 us
    all_to_all x3, starting transfers between devices, trade(): return lax.all_to_all(value, axis, split_axis=0, concat_axis=0, tiled=True)  15.2 us
    pallas_call x2, Pallas kernels, inverse(): pl.pallas_call(functools.partial(inverse_kernel, steps, which, near), gri...  14.6 us
    all_to_all x1, waiting for transfers between devices, shards(): lax.all_to_all(tiles, ('beam', 'slab'), split_axis=0, concat_axis=0, axis...  12.5 us
    pallas_call x2, Pallas kernels, forward_y(): pl.pallas_call(forward_y_kernel, grid=(1 + steps,), in_specs=[pl.BlockSpe...  12.2 us
    all_to_all x3, waiting for transfers between devices, trade(): return lax.all_to_all(value, axis, split_axis=0, concat_axis=0, tiled=True)  10.9 us
    ppermute x4, waiting for transfers between devices, hop(): lax.ppermute(value, 'beam', [(i, i ^ 1 << bit) for i in range(field_count)])  9.53 us
  transfers between devices with their start and end apart: 12, of which 7 were waited for; matrix products, arithmetic and copies ran while one was open for 9% of the time, Pallas kernels for 30%

profile of v15, /device:TPU:0, one launch (start us, length us, event | category | flops | bytes accessed | tf_op | source)
XLA Modules:
  0.0 169.8 jit_solution(8771995697921910096)
XLA Ops:
  0.0 10.0 %forward_x.3 = bf16[8,2,208,128]{3,2,1,0:T(8,128)(2,1)} custom-call(s32[1]{0:T(128)} %bitcast.3.sel, bf16[8,4,16,4096]{3,2,1,0:T(8,128)(2,1)} %bitcast.40, bf16[4,512,1024]{2,1,0:T(8,128)(2,1)} %constant.270.clone.section, bf16[4,8,208,256]{3,2,1,0:T(8,128)(2,1)} %constant.271.clone.last, bf16[128,128]{1,0:T(8,128)(2,1)} %constant.272.clone.perm), custom_call_target="tpu_custom_call" | custom-call | flops 1048576 | tf_op jit(solution)/shard_map/forward_x/pallas_call | solution.py:198
  10.0 7.3 %all-to-all-start.1 = ((bf16[8,2,208,128]{3,2,1,0:T(8,128)(2,1)}), bf16[8,2,208,128]{3,2,1,0:T(8,128)(2,1)S(1)}, u32[]{:S(2)}, u32[]{:S(2)}) async-start(bf16[8,2,208,128]{3,2,1,0:T(8,128)(2,1)} %forward_x.3), calls=%async_computation.1 | async-start | bytes 1703936 | tf_op jit(solution)/shard_map/all_to_all | solution.py:752
  17.4 0.6 fusion.22
  18.7 0.1 reshape_reshape.3
  18.8 0.1 copy.28
  19.0 0.6 gather_fusion
  19.6 0.6 gather_fusion.1
  20.2 0.1 stack.55
  20.3 0.1 stack.54
  21.2 0.7 reshape.1008.rest_1_.sel
  21.8 1.3 fusion.13
  23.2 0.1 copy.31
  23.4 10.0 %forward_x.2.value = bf16[8,2,208,128]{3,2,1,0:T(8,128)(2,1)} custom-call(s32[1]{0:T(128)} %bitcast.3.sel, bf16[8,4,16,4096]{3,2,1,0:T(8,128)(2,1)} %bitcast.41, bf16[4,512,1024]{2,1,0:T(8,128)(2,1)} %constant.270.clone.section, bf16[4,8,208,256]{3,2,1,0:T(8,128)(2,1)} %constant.271.clone.last, bf16[128,128]{1,0:T(8,128)(2,1)} %constant.272.clone.perm), custom_call_target="tpu_custom_call" | custom-call | flops 1048576 | tf_op jit(solution)/shard_map/forward_x/pallas_call | solution.py:198
  33.4 0.6 broadcast_add_fusion
  34.0 0.6 compare_convert_fusion
  34.6 0.6 and_select_fusion.5
  35.2 0.6 and_select_fusion.6
  35.7 0.7 multiply_convert_fusion.rest_2_.refs_3_
  36.4 0.8 broadcast_in_dim.2.rest_0_.refs_2_
  37.2 1.7 all-to-all-done.1.lines
  38.9 4.3 %all-to-all-start = ((bf16[8,2,208,128]{3,2,1,0:T(8,128)(2,1)}), bf16[8,2,208,128]{3,2,1,0:T(8,128)(2,1)S(1)}, u32[]{:S(2)}, u32[]{:S(2)}) async-start(bf16[8,2,208,128]{3,2,1,0:T(8,128)(2,1)} %order.3), calls=%async_computation | async-start | bytes 1703936 | tf_op jit(solution)/shard_map/all_to_all | solution.py:752
  43.2 1.5 collective-permute-start
  44.7 3.3 %forward_y_first.2.after.earlier = bf16[64,2,32,128]{3,2,1,0:T(8,128)(2,1)} custom-call(bf16[8,2,208,128]{3,2,1,0:T(8,128)(2,1)} %copy-done.3, bf16[512,256]{1,0:T(8,128)(2,1)} %constant.273.clone.section), custom_call_target="tpu_custom_call" | custom-call | flops 1048576 | tf_op jit(solution)/shard_map/forward_y_first/pallas_call | solution.py:270
  48.0 7.1 %crop.1.rest_0_ = bf16[32,32,128]{2,1,0:T(8,128)(2,1)} custom-call(s32[32]{0:T(128)} %get-tuple-element.38.rest_3_.rows, s32[32]{0:T(128)} %get-tuple-element.37.rest_4_.cols, s32[32]{0:T(128)} %get-tuple-element.16.rest_5_.odd, s32[32]{0:T(128)} %get-tuple-element.13.rest_6_.mine, bf16[512,4096]{1,0:T(8,128)(2,1)} %pot.1, ...), custom_call_target="tpu_custom_call" | custom-call | flops 1048576 | tf_op jit(solution)/shard_map/crop/pallas_call | solution.py:572
  55.1 9.2 %all-to-all-done.value = bf16[8,2,208,128]{3,2,1,0:T(8,128)(2,1)S(1)} async-done(((bf16[8,2,208,128]{3,2,1,0:T(8,128)(2,1)}), bf16[8,2,208,128]{3,2,1,0:T(8,128)(2,1)S(1)}, u32[]{:S(2)}, u32[]{:S(2)}) %all-to-all-start) | async-done | bytes 852000 | tf_op jit(solution)/shard_map/all_to_all | solution.py:752
  64.4 0.9 copy-done
  65.3 0.9 copy-done.4
  66.2 1.5 collective-permute-start.2
  67.7 3.6 %all-to-all-start.2 = ((bf16[8,4,32,128]{3,2,1,0:T(8,128)(2,1)}), bf16[8,4,32,128]{3,2,1,0:T(8,128)(2,1)S(1)}, u32[]{:S(2)}, u32[]{:S(2)}) async-start(bf16[8,4,32,128]{3,2,1,0:T(8,128)(2,1)} %order.5), calls=%async_computation.2 | async-start | bytes 524288 | tf_op jit(solution)/shard_map/all_to_all | solution.py:752
  71.3 6.1 %forward_y.2.refs_0_ = bf16[32,208,128]{2,1,0:T(8,128)(2,1)} custom-call(bf16[8,2,208,128]{3,2,1,0:T(8,128)(2,1)} %order.4.lines.rest_0_, bf16[512,256]{1,0:T(8,128)(2,1)} %constant.273.clone.section, bf16[64,2,32,128]{3,2,1,0:T(8,128)(2,1)} %forward_y_first.2.after.earlier, bf16[32,208,256]{2,1,0:T(8,128)(2,1)} %constant.274.clone.last), custom_call_target="tpu_custom_call" | custom-call | flops 1048576 | tf_op jit(solution)/shard_map/forward_y/pallas_call | solution.py:316
  77.4 3.3 %forward_y_first.3.earlier = bf16[64,2,32,128]{3,2,1,0:T(8,128)(2,1)} custom-call(bf16[8,2,208,128]{3,2,1,0:T(8,128)(2,1)} %copy-done.4, bf16[512,256]{1,0:T(8,128)(2,1)} %constant.273.clone.section), custom_call_target="tpu_custom_call" | custom-call | flops 1048576 | tf_op jit(solution)/shard_map/forward_y_first/pallas_call | solution.py:270
  80.7 4.5 %collective-permute-done.2.lines = bf16[8,2,208,128]{3,2,1,0:T(8,128)(2,1)S(1)} collective-permute-done((bf16[8,2,208,128]{3,2,1,0:T(8,128)(2,1)}, bf16[8,2,208,128]{3,2,1,0:T(8,128)(2,1)S(1)}, u32[]{:S(2)}, u32[]{:S(2)}) %collective-permute-start.2) | collective-permute-done | bytes 852000 | tf_op jit(solution)/shard_map/ppermute | solution.py:758
  85.2 0.9 copy-done.6
  86.2 6.1 %forward_y.3.refs_0_ = bf16[32,208,128]{2,1,0:T(8,128)(2,1)} custom-call(bf16[8,2,208,128]{3,2,1,0:T(8,128)(2,1)} %copy-done.6, bf16[512,256]{1,0:T(8,128)(2,1)} %constant.273.clone.section, bf16[64,2,32,128]{3,2,1,0:T(8,128)(2,1)} %forward_y_first.3.earlier, bf16[32,208,256]{2,1,0:T(8,128)(2,1)} %constant.274.clone.last, bf16[8,4,32,128]{3,2,1,0:T(8,128)(2,1)} %copy-done.1), custom_call_target="tpu_custom_call" | custom-call | flops 1048576 | tf_op jit(solution)/shard_map/forward_y/pallas_call | solution.py:316
  92.3 1.2 copy-done.5
  93.4 7.3 %inverse.2.refs_7_.refs_0_ = bf16[32,256,256]{2,1,0:T(8,128)(2,1)} custom-call(s32[12]{0:T(128)} %reshape.1008.rest_1_.sel, bf16[32,208,128]{2,1,0:T(8,128)(2,1)} %forward_y.2.refs_0_, bf16[32,208,128]{2,1,0:T(8,128)(2,1)} %copy-done.5, f32[208,128]{1,0:T(8,128)} %constant.275.clone.refs_2_, f32[4,1,128]{2,1,0:T(1,128)} %multiply_convert_fusion.rest_2_.refs_3_, ...), custom_call_target="tpu_custom_call" | custom-call | flops 1048576 | tf_op jit(solution)/shard_map/inverse/pallas_call | solution.py:424
  100.7 7.3 %inverse.3.refs_1_ = bf16[32,256,256]{2,1,0:T(8,128)(2,1)} custom-call(s32[12]{0:T(128)} %reshape.1008.rest_1_.sel, bf16[32,208,128]{2,1,0:T(8,128)(2,1)} %forward_y.3.refs_0_, bf16[32,208,128]{2,1,0:T(8,128)(2,1)} %collective-permute-done.3.refs_1_, f32[208,128]{1,0:T(8,128)} %constant.275.clone.refs_2_, f32[4,1,128]{2,1,0:T(1,128)} %multiply_convert_fusion.rest_2_.refs_3_, ...), custom_call_target="tpu_custom_call" | custom-call | flops 1048576 | tf_op jit(solution)/shard_map/inverse/pallas_call | solution.py:424
  108.0 7.9 %collect.2 = (bf16[16,2,4,16,128]{4,3,2,1,0:T(8,128)(2,1)}, bf16[16,2,4,16,128]{4,3,2,1,0:T(8,128)(2,1)}) custom-call(s32[4]{0:T(128)} %get-tuple-element.19.k1_pairs, bf16[32,256,256]{2,1,0:T(8,128)(2,1)} %inverse.2.refs_7_.refs_0_, bf16[32,256,256]{2,1,0:T(8,128)(2,1)} %inverse.3.refs_1_, s32[2,2,2,64,128]{4,3,2,1,0:T(8,128)} %broadcast_in_dim.2.rest_0_.refs_2_, ...), custom_call_target="tpu_custom_call" | custom-call | flops 1048576 | tf_op jit(solution)/shard_map/collect/pallas_call | solution.py:515
  116.0 0.2 dynamic-slice_reduce_fusion
  116.2 2.3 %collective-permute-start.4 = (bf16[16,2,4,16,128]{4,3,2,1,0:T(8,128)(2,1)}, bf16[16,2,4,16,128]{4,3,2,1,0:T(8,128)(2,1)S(1)}, u32[]{:S(2)}, u32[]{:S(2)}) collective-permute-start(bf16[16,2,4,16,128]{4,3,2,1,0:T(8,128)(2,1)} %get-tuple-element.9.refs_3_), channel_id=1, source_target_pairs={{0,4},{4,0},{8,12},{12,8},{16,20},{20,16},{24,28},{28,24},{1,5},{5... | collective-permute-start | bytes 1572872 | tf_op jit(solution)/shard_map/ppermute | solution.py:825
  118.7 0.1 add.421
  118.7 0.1 add.423
  119.1 8.1 %collect.3 = (bf16[16,2,4,16,128]{4,3,2,1,0:T(8,128)(2,1)}, bf16[16,2,4,16,128]{4,3,2,1,0:T(8,128)(2,1)}) custom-call(s32[4]{0:T(128)} %get-tuple-element.19.k1_pairs, bf16[32,256,256]{2,1,0:T(8,128)(2,1)} %inverse.2.refs_7_.refs_0_, bf16[32,256,256]{2,1,0:T(8,128)(2,1)} %inverse.3.refs_1_, s32[2,2,2,64,128]{4,3,2,1,0:T(8,128)} %broadcast_in_dim.2.rest_0_.refs_2_, ...), custom_call_target="tpu_custom_call" | custom-call | flops 1048576 | tf_op jit(solution)/shard_map/collect/pallas_call | solution.py:515
  127.2 3.4 %collective-permute-done.6 = bf16[16,2,4,16,128]{4,3,2,1,0:T(8,128)(2,1)S(1)} collective-permute-done((bf16[16,2,4,16,128]{4,3,2,1,0:T(8,128)(2,1)}, bf16[16,2,4,16,128]{4,3,2,1,0:T(8,128)(2,1)S(1)}, u32[]{:S(2)}, u32[]{:S(2)}) %collective-permute-start.6) | collective-permute-done | bytes 524320 | tf_op jit(solution)/shard_map/ppermute | solution.py:825
  130.5 1.0 add_convert_fusion.1
  131.5 2.4 %collective-permute-start.7 = (bf16[8,2,4,16,128]{4,3,2,1,0:T(8,128)(2,1)S(1)}, bf16[8,2,4,16,128]{4,3,2,1,0:T(8,128)(2,1)S(1)}, u32[]{:S(2)}, u32[]{:S(2)}) collective-permute-start(bf16[8,2,4,16,128]{4,3,2,1,0:T(8,128)(2,1)S(1)} %add_convert_fusion.1), channel_id=1, source_target_pairs={{0,4},{4,0},{8,12},{12,8},{16,20},{20,16},{24,28},{28,24},{1,5},{5... | collective-permute-start | bytes 786440 | tf_op jit(solution)/shard_map/ppermute | solution.py:825
  133.9 1.0 add_convert_fusion.3
  134.9 0.3 collective-permute-start.5
  135.3 0.1 fusion.21
  135.4 4.7 %collective-permute-done.7 = bf16[8,2,4,16,128]{4,3,2,1,0:T(8,128)(2,1)S(1)} collective-permute-done((bf16[8,2,4,16,128]{4,3,2,1,0:T(8,128)(2,1)S(1)}, bf16[8,2,4,16,128]{4,3,2,1,0:T(8,128)(2,1)S(1)}, u32[]{:S(2)}, u32[]{:S(2)}) %collective-permute-start.7) | collective-permute-done | bytes 262176 | tf_op jit(solution)/shard_map/ppermute | solution.py:825
  140.1 1.1 add_convert_fusion
  141.2 1.5 collective-permute-done.5
  142.7 1.1 add_convert_fusion.2
  143.7 0.8 pad_maximum_fusion
  144.6 3.7 %all-to-all-start.3 = ((bf16[8,2,4,32,128]{4,3,2,1,0:T(8,128)(2,1)}), bf16[8,2,4,32,128]{4,3,2,1,0:T(8,128)(2,1)S(1)}, u32[]{:S(2)}, u32[]{:S(2)}) async-start(bf16[8,2,4,32,128]{4,3,2,1,0:T(8,128)(2,1)} %pad_maximum_fusion), calls=%async_computation.3 | async-start | bytes 1048576 | tf_op jit(solution)/shard_map/all_to_all | solution.py:841
  148.2 0.6 dynamic_slice.18.counts
  148.8 0.6 pad_maximum_fusion.2.alpha
  149.4 0.3 fusion.4
  149.8 0.7 pad_maximum_fusion.1.refs_2_
  150.4 0.6 reduce_sum.25.refs_1_
  151.1 12.5 %all-to-all-done.3 = bf16[8,2,4,32,128]{4,3,2,1,0:T(8,128)(2,1)S(1)} async-done(((bf16[8,2,4,32,128]{4,3,2,1,0:T(8,128)(2,1)}), bf16[8,2,4,32,128]{4,3,2,1,0:T(8,128)(2,1)S(1)}, u32[]{:S(2)}, u32[]{:S(2)}) %all-to-all-start.3) | async-done | bytes 524320 | tf_op jit(solution)/shard_map/all_to_all | solution.py:841
  163.6 0.8 reduce_sum.24.refs_0_
  164.4 4.1 %detect.1 = f32[1,4,3,16]{3,2,1,0:T(4,128)} custom-call(f32[2,4,12]{2,1,0:T(4,128)} %pad_maximum_fusion.2.alpha, s32[1]{0:T(128)} %dynamic_slice.18.counts, bf16[4,2,4,32,128]{4,3,2,1,0:T(8,128)(2,1)} %reduce_sum.24.refs_0_, bf16[4,32,128]{2,1,0:T(8,128)(2,1)} %reduce_sum.25.refs_1_, f32[4,2,32,128]{3,2,1,0:T(8,128)} %pad_maximum_fusion.1.refs_2_, ...), custom_call_target="tpu_custom_call" | custom-call | tf_op jit(solution)/shard_map/detect/pallas_call | solution.py:643
  168.5 1.3 copy.32
  (60 shorter events, 1.0 us)
Async XLA Ops:
  0.0 17.3 %copy-start.7 = (s32[4,2]{0,1:T(2,128)S(1)}, s32[4,2]{0,1:T(2,128)}, u32[]{:S(2)}) copy-start(s32[4,2]{0,1:T(2,128)} %param.21) | copy-start | bytes 100
  0.0 18.7 %copy-start.8 = (s32[32,4]{0,1:T(4,128)S(1)}, s32[32,4]{0,1:T(4,128)}, u32[]{:S(2)}) copy-start(s32[32,4]{0,1:T(4,128)} %param.23) | copy-start | bytes 1540
  10.0 28.9 %all-to-all-start.1 = ((bf16[8,2,208,128]{3,2,1,0:T(8,128)(2,1)}), bf16[8,2,208,128]{3,2,1,0:T(8,128)(2,1)S(1)}, u32[]{:S(2)}, u32[]{:S(2)}) async-start(bf16[8,2,208,128]{3,2,1,0:T(8,128)(2,1)} %forward_x.3), calls=%async_computation.1 | async-start | bytes 1703936 | tf_op jit(solution)/shard_map/all_to_all | solution.py:752
  23.4 12.3 %copy-start.9 = (s32[128]{0:T(128)S(1)}, s32[128]{0:T(128)}, u32[]{:S(2)}) copy-start(s32[128]{0:T(128)} %constant.269.clone) | copy-start | bytes 1540
  38.9 5.8 %copy-start.3 = (bf16[8,2,208,128]{3,2,1,0:T(8,128)(2,1)}, bf16[8,2,208,128]{3,2,1,0:T(8,128)(2,1)S(1)}, u32[]{:S(2)}) copy-start(bf16[8,2,208,128]{3,2,1,0:T(8,128)(2,1)S(1)} %all-to-all-done.1.lines) | copy-start | bytes 2555908
  38.9 25.5 %all-to-all-start = ((bf16[8,2,208,128]{3,2,1,0:T(8,128)(2,1)}), bf16[8,2,208,128]{3,2,1,0:T(8,128)(2,1)S(1)}, u32[]{:S(2)}, u32[]{:S(2)}) async-start(bf16[8,2,208,128]{3,2,1,0:T(8,128)(2,1)} %order.3), calls=%async_computation | async-start | bytes 1703936 | tf_op jit(solution)/shard_map/all_to_all | solution.py:752
  43.2 21.2 %collective-permute-start = (bf16[8,2,208,128]{3,2,1,0:T(8,128)(2,1)S(1)}, bf16[8,2,208,128]{3,2,1,0:T(8,128)(2,1)S(1)}, u32[]{:S(2)}, u32[]{:S(2)}) collective-permute-start(bf16[8,2,208,128]{3,2,1,0:T(8,128)(2,1)S(1)} %all-to-all-done.1.lines), channel_id=1, source_target_pairs={{0,2},{1,3},{2,0},{3,1},{4,6},{5,7},{6,4},{7,5},{8,10},{9,11},{10,... | collective-permute-start | bytes 2555912 | tf_op jit(solution)/shard_map/ppermute | solution.py:758
  64.4 0.9 copy-start
  65.3 0.9 copy-start.4
  66.2 19.1 %collective-permute-start.2 = (bf16[8,2,208,128]{3,2,1,0:T(8,128)(2,1)}, bf16[8,2,208,128]{3,2,1,0:T(8,128)(2,1)S(1)}, u32[]{:S(2)}, u32[]{:S(2)}) collective-permute-start(bf16[8,2,208,128]{3,2,1,0:T(8,128)(2,1)} %order.4.lines.rest_0_), channel_id=1, source_target_pairs={{0,2},{1,3},{2,0},{3,1},{4,6},{5,7},{6,4},{7,5},{8,10},{9,11},{10,... | collective-permute-start | bytes 2555912 | tf_op jit(solution)/shard_map/ppermute | solution.py:758
  67.7 13.0 %all-to-all-start.2 = ((bf16[8,4,32,128]{3,2,1,0:T(8,128)(2,1)}), bf16[8,4,32,128]{3,2,1,0:T(8,128)(2,1)S(1)}, u32[]{:S(2)}, u32[]{:S(2)}) async-start(bf16[8,4,32,128]{3,2,1,0:T(8,128)(2,1)} %order.5), calls=%async_computation.2 | async-start | bytes 524288 | tf_op jit(solution)/shard_map/all_to_all | solution.py:752
  77.4 14.9 %collective-permute-start.1 = (bf16[32,208,128]{2,1,0:T(8,128)(2,1)}, bf16[32,208,128]{2,1,0:T(8,128)(2,1)S(1)}, u32[]{:S(2)}, u32[]{:S(2)}) collective-permute-start(bf16[32,208,128]{2,1,0:T(8,128)(2,1)} %forward_y.2.refs_0_), channel_id=1, source_target_pairs={{0,1},{1,0},{2,3},{3,2},{4,5},{5,4},{6,7},{7,6},{8,9},{9,8},{10,11... | collective-permute-start | bytes 5111816 | tf_op jit(solution)/shard_map/ppermute | solution.py:758
  80.7 4.5 %copy-start.1 = (bf16[8,4,32,128]{3,2,1,0:T(8,128)(2,1)}, bf16[8,4,32,128]{3,2,1,0:T(8,128)(2,1)S(1)}, u32[]{:S(2)}) copy-start(bf16[8,4,32,128]{3,2,1,0:T(8,128)(2,1)S(1)} %all-to-all-done.2.rest_0_.refs_3_) | copy-start | bytes 786436
  85.2 0.9 copy-start.6
  92.2 8.5 %collective-permute-start.3 = (bf16[32,208,128]{2,1,0:T(8,128)(2,1)}, bf16[32,208,128]{2,1,0:T(8,128)(2,1)}, u32[]{:S(2)}, u32[]{:S(2)}) collective-permute-start(bf16[32,208,128]{2,1,0:T(8,128)(2,1)} %forward_y.3.refs_0_), channel_id=1, source_target_pairs={{0,1},{1,0},{2,3},{3,2},{4,5},{5,4},{6,7},{7,6},{8,9},{9,8},{10,11... | collective-permute-start | bytes 5111816 | tf_op jit(solution)/shard_map/ppermute | solution.py:758
  92.2 1.2 copy-start.5
  116.0 14.5 %collective-permute-start.6 = (bf16[16,2,4,16,128]{4,3,2,1,0:T(8,128)(2,1)}, bf16[16,2,4,16,128]{4,3,2,1,0:T(8,128)(2,1)S(1)}, u32[]{:S(2)}, u32[]{:S(2)}) collective-permute-start(bf16[16,2,4,16,128]{4,3,2,1,0:T(8,128)(2,1)} %get-tuple-element.12), channel_id=1, source_target_pairs={{0,8},{4,12},{8,0},{12,4},{16,24},{20,28},{24,16},{28,20},{1,9},{5... | collective-permute-start | bytes 1572872 | tf_op jit(solution)/shard_map/ppermute | solution.py:825
  116.2 17.7 %collective-permute-start.4 = (bf16[16,2,4,16,128]{4,3,2,1,0:T(8,128)(2,1)}, bf16[16,2,4,16,128]{4,3,2,1,0:T(8,128)(2,1)S(1)}, u32[]{:S(2)}, u32[]{:S(2)}) collective-permute-start(bf16[16,2,4,16,128]{4,3,2,1,0:T(8,128)(2,1)} %get-tuple-element.9.refs_3_), channel_id=1, source_target_pairs={{0,4},{4,0},{8,12},{12,8},{16,20},{20,16},{24,28},{28,24},{1,5},{5... | collective-permute-start | bytes 1572872 | tf_op jit(solution)/shard_map/ppermute | solution.py:825
  119.1 16.2 %copy-start.10 = (f32[4]{0:T(128)S(1)}, f32[4]{0:T(128)}, u32[]{:S(2)}) copy-start(f32[4]{0:T(128)} %param.22) | copy-start | bytes 52
  127.2 21.1 %copy-start.11 = (s32[32]{0:T(128)S(1)}, s32[32]{0:T(128)}, u32[]{:S(2)}) copy-start(s32[32]{0:T(128)} %param.24) | copy-start | bytes 388
  127.2 23.3 %copy-start.2 = (bf16[8,4,32,128]{3,2,1,0:T(8,128)(2,1)S(1)}, bf16[8,4,32,128]{3,2,1,0:T(8,128)(2,1)}, u32[]{:S(2)}) copy-start(bf16[8,4,32,128]{3,2,1,0:T(8,128)(2,1)} %copy-done.1) | copy-start | bytes 786436
  131.5 8.5 %collective-permute-start.7 = (bf16[8,2,4,16,128]{4,3,2,1,0:T(8,128)(2,1)S(1)}, bf16[8,2,4,16,128]{4,3,2,1,0:T(8,128)(2,1)S(1)}, u32[]{:S(2)}, u32[]{:S(2)}) collective-permute-start(bf16[8,2,4,16,128]{4,3,2,1,0:T(8,128)(2,1)S(1)} %add_convert_fusion.1), channel_id=1, source_target_pairs={{0,4},{4,0},{8,12},{12,8},{16,20},{20,16},{24,28},{28,24},{1,5},{5... | collective-permute-start | bytes 786440 | tf_op jit(solution)/shard_map/ppermute | solution.py:825
  134.9 7.7 %collective-permute-start.5 = (bf16[8,2,4,16,128]{4,3,2,1,0:T(8,128)(2,1)S(1)}, bf16[8,2,4,16,128]{4,3,2,1,0:T(8,128)(2,1)S(1)}, u32[]{:S(2)}, u32[]{:S(2)}) collective-permute-start(bf16[8,2,4,16,128]{4,3,2,1,0:T(8,128)(2,1)S(1)} %add_convert_fusion.3), channel_id=1, source_target_pairs={{0,8},{4,12},{8,0},{12,4},{16,24},{20,28},{24,16},{28,20},{1,9},{5... | collective-permute-start | bytes 786440 | tf_op jit(solution)/shard_map/ppermute | solution.py:825
  144.6 19.0 %all-to-all-start.3 = ((bf16[8,2,4,32,128]{4,3,2,1,0:T(8,128)(2,1)}), bf16[8,2,4,32,128]{4,3,2,1,0:T(8,128)(2,1)S(1)}, u32[]{:S(2)}, u32[]{:S(2)}) async-start(bf16[8,2,4,32,128]{4,3,2,1,0:T(8,128)(2,1)} %pad_maximum_fusion), calls=%async_computation.3 | async-start | bytes 1048576 | tf_op jit(solution)/shard_map/all_to_all | solution.py:841

commit v16 on v15

--- a/solution.py
+++ b/solution.py
@@ -429,7 +429,7 @@
             in_specs=[pl.BlockSpec((count, ROWS, LANES), lambda i, s: (early(i, s), 0, 0))] * near
             + [
                 pl.BlockSpec((ROWS, LANES), lambda i, s: (0, 0)),
-                pl.BlockSpec((near, 1, LANES), lambda i, s: (which // near, 0, 0)),
+                pl.BlockSpec((near, 1, LANES), lambda i, s: (0, 0, 0)),
                 pl.BlockSpec((count, 2, 2 * A, PART), lambda i, s: (early(i, s), 0, 0, 0)),
             ]
             + [table_spec(x) for x in range(near)]
@@ -510,14 +510,17 @@
     steps = 2
     shape = (devices, 2, tiles // devices, lines, LANES)
     depth = sum(sheet.shape[1] for sheet in sheets)
-    sheet_spec = pl.BlockSpec((lines // steps,) + sheets[0].shape[1:], lambda i, s: (i, 0, 0))
+    sheet_specs = [
+        pl.BlockSpec((lines // steps,) + sheet.shape[1:], lambda i, s: (i, 0, 0))
+        for sheet in sheets
+    ]
     block = pl.BlockSpec(shape, lambda i, s: (0, 0, 0, 0, 0))
     return pl.pallas_call(
         functools.partial(collect_kernel, len(sheets)),
         grid_spec=pltpu.PrefetchScalarGridSpec(
             num_scalar_prefetch=1,
             grid=(PARTS * steps,),
-            in_specs=[sheet_spec] * len(sheets)
+            in_specs=sheet_specs
             + [
                 pl.BlockSpec(
                     (1, 1) + places.shape[2:], lambda i, s: (which, i // steps, 0, 0, 0)
@@ -809,14 +812,24 @@
     crops = order(crops.reshape(field_count, own_slots, HALF, LANES), received[0][1:])
     crops = trade(crops, "beam")
     waves = []
+    ready = []
+
+    def invert(stop, after):
+        start = stop - len(ready)
+        limits = square_x[start:stop]
+        waves.append(
+            inverse(start, scalars, ready[:], freq_y, limits, inverse_y, inverse_x, after)
+        )
+        ready.clear()
+
     for f in range(far):
-        spec = forward_y(received[f][1], section_y, earlier[f], last_y, [crops] if f else [])
-        ready = [spec] + [swap(spec, x) for x in range(1, near)]
-        waves.append(
-            inverse(
-                f * near, scalars, ready, freq_y, square_x, inverse_y, inverse_x, waves[-1:]
-            )
-        )
+        spec = forward_y(received[f][1], section_y, earlier[f], last_y, [crops] + waves if f else [])
+        for x in range(near):
+            ready.append(swap(spec, x) if x else spec)
+            if x == 0:
+                invert(f * near + 1, waves[1:])
+    if ready:
+        invert(sheets, waves[-1:])
     owners = field_count // 2 * hold_count
     other = collect(waves, k1_pairs, places, owners, 0, [crops])
     partial = other + collect(waves, k1_pairs, places, owners, 1, other[:1])

time: 171 us -> 170 us (level)
  waiting for transfers between devices: 37.5 us -> 30.5 us
  Pallas kernels: 80.5 us -> 83.9 us
  starting transfers between devices: 26.9 us -> 28.8 us
    ppermute x4, waiting for transfers between devices: 4.52 us -> 0.01 us  [swap(): return lax.ppermute(value, 'slab', [(i, i ^ x) for i in range(hold_count)])]
    pallas_call x2 -> x3, Pallas kernels: 14.6 us -> 18 us  [inverse(): pl.pallas_call(functools.partial(inverse_kernel, steps, which, near), gri...]
    ppermute x4, waiting for transfers between devices: 9.53 us -> 6.48 us  [hop(): lax.ppermute(value, 'beam', [(i, i ^ 1 << bit) for i in range(field_count)])]
    ppermute x4, starting transfers between devices: 5.06 us -> 6.78 us  [hop(): lax.ppermute(value, 'beam', [(i, i ^ 1 << bit) for i in range(field_count)])]
    unnamed x25 -> x27, local copies, waits for them, and re-layouts: 3.94 us -> 4.66 us
  transfers between devices with their start and end apart: 12 -> 12, of which waited for: 7 -> 6; matrix products, arithmetic and copies ran while one was open for 9% -> 10% of each run, Pallas kernels for 30% -> 33%
where the time goes in v16:
time: 170 us
  Pallas kernels  83.9 us (49%)
  waiting for transfers between devices  30.5 us (18%)
  starting transfers between devices  28.8 us (17%)
  other arithmetic  12.5 us (7%)
  local copies, waits for them, and re-layouts  12.4 us (7%)
    pallas_call x2, Pallas kernels, forward_x(): pl.pallas_call(forward_x_kernel, grid_spec=pltpu.PrefetchScalarGridSpec(n...  20 us
    pallas_call x3, Pallas kernels, inverse(): pl.pallas_call(functools.partial(inverse_kernel, steps, which, near), gri...  18 us
    pallas_call x2, Pallas kernels, collect(): pl.pallas_call(functools.partial(collect_kernel, len(sheets)), grid_spec=...  15.9 us
    all_to_all x3, starting transfers between devices, trade(): return lax.all_to_all(value, axis, split_axis=0, concat_axis=0, tiled=True)  14.9 us
    all_to_all x1, waiting for transfers between devices, shards(): lax.all_to_all(tiles, ('beam', 'slab'), split_axis=0, concat_axis=0, axis...  12.5 us
    pallas_call x2, Pallas kernels, forward_y(): pl.pallas_call(forward_y_kernel, grid=(1 + steps,), in_specs=[pl.BlockSpe...  12.2 us
    all_to_all x3, waiting for transfers between devices, trade(): return lax.all_to_all(value, axis, split_axis=0, concat_axis=0, tiled=True)  11.5 us
    pallas_call x1, Pallas kernels, crop(): pl.pallas_call(crop_kernel, in_specs=[pl.BlockSpec(memory_space=pltpu.SME...  7.08 us
  transfers between devices with their start and end apart: 12, of which 6 were waited for; matrix products, arithmetic and copies ran while one was open for 10% of the time, Pallas kernels for 33%

profile of v16, /device:TPU:0, one launch (start us, length us, event | category | flops | bytes accessed | tf_op | source)
XLA Modules:
  0.0 169.5 jit_solution(18181109212950316400)
XLA Ops:
  0.0 10.0 %forward_x.3 = bf16[8,2,208,128]{3,2,1,0:T(8,128)(2,1)} custom-call(s32[1]{0:T(128)} %bitcast.3.sel, bf16[8,4,16,4096]{3,2,1,0:T(8,128)(2,1)} %bitcast.40, bf16[4,512,1024]{2,1,0:T(8,128)(2,1)} %constant.270.clone.section, bf16[4,8,208,256]{3,2,1,0:T(8,128)(2,1)} %constant.271.clone.last, bf16[128,128]{1,0:T(8,128)(2,1)} %constant.272.clone.perm), custom_call_target="tpu_custom_call" | custom-call | flops 1048576 | tf_op jit(solution)/shard_map/forward_x/pallas_call | solution.py:198
  10.0 7.3 %all-to-all-start.1 = ((bf16[8,2,208,128]{3,2,1,0:T(8,128)(2,1)}), bf16[8,2,208,128]{3,2,1,0:T(8,128)(2,1)S(1)}, u32[]{:S(2)}, u32[]{:S(2)}) async-start(bf16[8,2,208,128]{3,2,1,0:T(8,128)(2,1)} %forward_x.3), calls=%async_computation.1 | async-start | bytes 1703936 | tf_op jit(solution)/shard_map/all_to_all | solution.py:755
  17.4 0.5 fusion.23
  18.7 0.1 copy.28
  19.0 0.6 gather_fusion
  19.6 0.6 gather_fusion.1
  21.1 0.6 reshape.1008.rest_1_.sel
  21.7 1.2 fusion.13
  23.0 0.1 copy.31
  23.3 10.0 %forward_x.2.value = bf16[8,2,208,128]{3,2,1,0:T(8,128)(2,1)} custom-call(s32[1]{0:T(128)} %bitcast.3.sel, bf16[8,4,16,4096]{3,2,1,0:T(8,128)(2,1)} %bitcast.41, bf16[4,512,1024]{2,1,0:T(8,128)(2,1)} %constant.270.clone.section, bf16[4,8,208,256]{3,2,1,0:T(8,128)(2,1)} %constant.271.clone.last, bf16[128,128]{1,0:T(8,128)(2,1)} %constant.272.clone.perm), custom_call_target="tpu_custom_call" | custom-call | flops 1048576 | tf_op jit(solution)/shard_map/forward_x/pallas_call | solution.py:198
  33.2 0.5 broadcast_add_fusion
  33.8 0.6 compare_convert_fusion
  34.3 0.5 and_select_fusion.5
  34.9 0.6 and_select_fusion.6
  35.4 0.7 multiply_convert_fusion.rest_2_
  36.1 0.8 broadcast_in_dim.2.rest_0_.refs_3_
  36.9 2.0 %all-to-all-done.1.lines = bf16[8,2,208,128]{3,2,1,0:T(8,128)(2,1)S(1)} async-done(((bf16[8,2,208,128]{3,2,1,0:T(8,128)(2,1)}), bf16[8,2,208,128]{3,2,1,0:T(8,128)(2,1)S(1)}, u32[]{:S(2)}, u32[]{:S(2)}) %all-to-all-start.1) | async-done | bytes 852000 | tf_op jit(solution)/shard_map/all_to_all | solution.py:755
  38.9 4.0 %all-to-all-start = ((bf16[8,2,208,128]{3,2,1,0:T(8,128)(2,1)}), bf16[8,2,208,128]{3,2,1,0:T(8,128)(2,1)S(1)}, u32[]{:S(2)}, u32[]{:S(2)}) async-start(bf16[8,2,208,128]{3,2,1,0:T(8,128)(2,1)} %order.3), calls=%async_computation | async-start | bytes 1703936 | tf_op jit(solution)/shard_map/all_to_all | solution.py:755
  42.9 1.5 collective-permute-start
  44.4 3.3 %forward_y_first.2.after.earlier = bf16[64,2,32,128]{3,2,1,0:T(8,128)(2,1)} custom-call(bf16[8,2,208,128]{3,2,1,0:T(8,128)(2,1)} %copy-done.3, bf16[512,256]{1,0:T(8,128)(2,1)} %constant.273.clone.section), custom_call_target="tpu_custom_call" | custom-call | flops 1048576 | tf_op jit(solution)/shard_map/forward_y_first/pallas_call | solution.py:270
  47.7 7.1 %crop.1.rest_0_ = bf16[32,32,128]{2,1,0:T(8,128)(2,1)} custom-call(s32[32]{0:T(128)} %get-tuple-element.40.rest_3_.rows, s32[32]{0:T(128)} %get-tuple-element.39.rest_4_.cols, s32[32]{0:T(128)} %get-tuple-element.16.rest_5_.odd, s32[32]{0:T(128)} %get-tuple-element.13.rest_6_.mine, bf16[512,4096]{1,0:T(8,128)(2,1)} %pot.1, ...), custom_call_target="tpu_custom_call" | custom-call | flops 1048576 | tf_op jit(solution)/shard_map/crop/pallas_call | solution.py:575
  54.8 9.5 %all-to-all-done.value = bf16[8,2,208,128]{3,2,1,0:T(8,128)(2,1)S(1)} async-done(((bf16[8,2,208,128]{3,2,1,0:T(8,128)(2,1)}), bf16[8,2,208,128]{3,2,1,0:T(8,128)(2,1)S(1)}, u32[]{:S(2)}, u32[]{:S(2)}) %all-to-all-start) | async-done | bytes 852000 | tf_op jit(solution)/shard_map/all_to_all | solution.py:755
  64.3 0.9 copy-done
  65.2 0.9 copy-done.4
  66.1 1.5 collective-permute-start.2
  67.6 3.6 %all-to-all-start.2 = ((bf16[8,4,32,128]{3,2,1,0:T(8,128)(2,1)}), bf16[8,4,32,128]{3,2,1,0:T(8,128)(2,1)S(1)}, u32[]{:S(2)}, u32[]{:S(2)}) async-start(bf16[8,4,32,128]{3,2,1,0:T(8,128)(2,1)} %order.5), calls=%async_computation.2 | async-start | bytes 524288 | tf_op jit(solution)/shard_map/all_to_all | solution.py:755
  71.3 0.5 fusion.22
  71.8 6.1 %forward_y.2.refs_0_ = bf16[32,208,128]{2,1,0:T(8,128)(2,1)} custom-call(bf16[8,2,208,128]{3,2,1,0:T(8,128)(2,1)} %order.4.lines.rest_0_, bf16[512,256]{1,0:T(8,128)(2,1)} %constant.273.clone.section, bf16[64,2,32,128]{3,2,1,0:T(8,128)(2,1)} %forward_y_first.2.after.earlier, bf16[32,208,256]{2,1,0:T(8,128)(2,1)} %constant.274.clone.last), custom_call_target="tpu_custom_call" | custom-call | flops 1048576 | tf_op jit(solution)/shard_map/forward_y/pallas_call | solution.py:316
  77.9 5.3 %inverse.3.rest_1_.refs_0_ = bf16[32,128,256]{2,1,0:T(8,128)(2,1)} custom-call(s32[12]{0:T(128)} %reshape.1008.rest_1_.sel, bf16[32,208,128]{2,1,0:T(8,128)(2,1)} %forward_y.2.refs_0_, f32[208,128]{1,0:T(8,128)} %constant.275.clone.refs_1_.refs_2_, f32[1,1,128]{2,1,0:T(1,128)} %get-tuple-element.25.refs_2_, ...), custom_call_target="tpu_custom_call" | custom-call | flops 1048576 | tf_op jit(solution)/shard_map/inverse/pallas_call | solution.py:424
  83.2 3.3 %forward_y_first.3.earlier = bf16[64,2,32,128]{3,2,1,0:T(8,128)(2,1)} custom-call(bf16[8,2,208,128]{3,2,1,0:T(8,128)(2,1)} %copy-done.4, bf16[512,256]{1,0:T(8,128)(2,1)} %constant.273.clone.section), custom_call_target="tpu_custom_call" | custom-call | flops 1048576 | tf_op jit(solution)/shard_map/forward_y_first/pallas_call | solution.py:270
  86.6 0.7 copy-done.1
  87.3 0.9 copy-done.6
  88.2 6.1 %forward_y.3.refs_1_ = bf16[32,208,128]{2,1,0:T(8,128)(2,1)} custom-call(bf16[8,2,208,128]{3,2,1,0:T(8,128)(2,1)} %copy-done.6, bf16[512,256]{1,0:T(8,128)(2,1)} %constant.273.clone.section, bf16[64,2,32,128]{3,2,1,0:T(8,128)(2,1)} %forward_y_first.3.earlier, bf16[32,208,256]{2,1,0:T(8,128)(2,1)} %constant.274.clone.last, bf16[8,4,32,128]{3,2,1,0:T(8,128)(2,1)} %copy-done.1, ...), custom_call_target="tpu_custom_call" | custom-call | flops 1048576 | tf_op jit(solution)/shard_map/forward_y/pallas_call | solution.py:316
  94.3 0.5 collective-permute-start.3
  94.8 0.6 slice.71.refs_3_
  95.4 1.2 copy-done.5
  96.6 7.3 %inverse.4.refs_5_.refs_1_ = bf16[32,256,256]{2,1,0:T(8,128)(2,1)} custom-call(s32[12]{0:T(128)} %reshape.1008.rest_1_.sel, bf16[32,208,128]{2,1,0:T(8,128)(2,1)} %copy-done.5, bf16[32,208,128]{2,1,0:T(8,128)(2,1)} %forward_y.3.refs_1_, f32[208,128]{1,0:T(8,128)} %constant.275.clone.refs_1_.refs_2_, f32[2,1,128]{2,1,0:T(1,128)} %slice.71.refs_3_, ...), custom_call_target="tpu_custom_call" | custom-call | flops 1048576 | tf_op jit(solution)/shard_map/inverse/pallas_call | solution.py:424
  103.9 5.4 %inverse.5.refs_2_ = bf16[32,128,256]{2,1,0:T(8,128)(2,1)} custom-call(s32[12]{0:T(128)} %reshape.1008.rest_1_.sel, bf16[32,208,128]{2,1,0:T(8,128)(2,1)} %collective-permute-done.3.refs_0_, f32[208,128]{1,0:T(8,128)} %constant.275.clone.refs_1_.refs_2_, f32[1,1,128]{2,1,0:T(1,128)} %get-tuple-element.24.refs_2_, ...), custom_call_target="tpu_custom_call" | custom-call | flops 1048576 | tf_op jit(solution)/shard_map/inverse/pallas_call | solution.py:424
  109.3 7.9 %collect.2 = (bf16[16,2,4,16,128]{4,3,2,1,0:T(8,128)(2,1)}, bf16[16,2,4,16,128]{4,3,2,1,0:T(8,128)(2,1)}) custom-call(s32[4]{0:T(128)} %get-tuple-element.19.k1_pairs, bf16[32,128,256]{2,1,0:T(8,128)(2,1)} %inverse.3.rest_1_.refs_0_, bf16[32,256,256]{2,1,0:T(8,128)(2,1)} %inverse.4.refs_5_.refs_1_, bf16[32,128,256]{2,1,0:T(8,128)(2,1)} %inverse.5.refs_2_, ...), custom_call_target="tpu_custom_call" | custom-call | flops 1048576 | tf_op jit(solution)/shard_map/collect/pallas_call | solution.py:518
  117.2 1.9 %collective-permute-start.6 = (bf16[16,2,4,16,128]{4,3,2,1,0:T(8,128)(2,1)}, bf16[16,2,4,16,128]{4,3,2,1,0:T(8,128)(2,1)S(1)}, u32[]{:S(2)}, u32[]{:S(2)}) collective-permute-start(bf16[16,2,4,16,128]{4,3,2,1,0:T(8,128)(2,1)} %get-tuple-element.12), channel_id=1, source_target_pairs={{0,8},{4,12},{8,0},{12,4},{16,24},{20,28},{24,16},{28,20},{1,9},{5... | collective-permute-start | bytes 1572872 | tf_op jit(solution)/shard_map/ppermute | solution.py:838
  119.1 0.2 dynamic-slice_reduce_fusion
  119.3 1.5 collective-permute-start.4
  121.4 8.0 %collect.3 = (bf16[16,2,4,16,128]{4,3,2,1,0:T(8,128)(2,1)}, bf16[16,2,4,16,128]{4,3,2,1,0:T(8,128)(2,1)}) custom-call(s32[4]{0:T(128)} %get-tuple-element.19.k1_pairs, bf16[32,128,256]{2,1,0:T(8,128)(2,1)} %inverse.3.rest_1_.refs_0_, bf16[32,256,256]{2,1,0:T(8,128)(2,1)} %inverse.4.refs_5_.refs_1_, bf16[32,128,256]{2,1,0:T(8,128)(2,1)} %inverse.5.refs_2_, ...), custom_call_target="tpu_custom_call" | custom-call | flops 1048576 | tf_op jit(solution)/shard_map/collect/pallas_call | solution.py:518
  129.4 2.0 %collective-permute-done.6 = bf16[16,2,4,16,128]{4,3,2,1,0:T(8,128)(2,1)S(1)} collective-permute-done((bf16[16,2,4,16,128]{4,3,2,1,0:T(8,128)(2,1)}, bf16[16,2,4,16,128]{4,3,2,1,0:T(8,128)(2,1)S(1)}, u32[]{:S(2)}, u32[]{:S(2)}) %collective-permute-start.6) | collective-permute-done | bytes 524320 | tf_op jit(solution)/shard_map/ppermute | solution.py:838
  131.4 1.0 add_convert_fusion.1
  132.4 1.8 %collective-permute-start.7 = (bf16[8,2,4,16,128]{4,3,2,1,0:T(8,128)(2,1)S(1)}, bf16[8,2,4,16,128]{4,3,2,1,0:T(8,128)(2,1)S(1)}, u32[]{:S(2)}, u32[]{:S(2)}) collective-permute-start(bf16[8,2,4,16,128]{4,3,2,1,0:T(8,128)(2,1)S(1)} %add_convert_fusion.1), channel_id=1, source_target_pairs={{0,4},{4,0},{8,12},{12,8},{16,20},{20,16},{24,28},{28,24},{1,5},{5... | collective-permute-start | bytes 786440 | tf_op jit(solution)/shard_map/ppermute | solution.py:838
  134.2 1.0 add_convert_fusion.3
  135.3 1.5 collective-permute-start.5
  136.8 0.1 fusion.21
  136.9 3.1 %collective-permute-done.7 = bf16[8,2,4,16,128]{4,3,2,1,0:T(8,128)(2,1)S(1)} collective-permute-done((bf16[8,2,4,16,128]{4,3,2,1,0:T(8,128)(2,1)S(1)}, bf16[8,2,4,16,128]{4,3,2,1,0:T(8,128)(2,1)S(1)}, u32[]{:S(2)}, u32[]{:S(2)}) %collective-permute-start.7) | collective-permute-done | bytes 262176 | tf_op jit(solution)/shard_map/ppermute | solution.py:838
  140.0 1.1 add_convert_fusion
  141.1 1.3 collective-permute-done.5
  142.4 1.1 add_convert_fusion.2
  143.5 0.8 pad_maximum_fusion
  144.3 3.6 %all-to-all-start.3 = ((bf16[8,2,4,32,128]{4,3,2,1,0:T(8,128)(2,1)}), bf16[8,2,4,32,128]{4,3,2,1,0:T(8,128)(2,1)S(1)}, u32[]{:S(2)}, u32[]{:S(2)}) async-start(bf16[8,2,4,32,128]{4,3,2,1,0:T(8,128)(2,1)} %pad_maximum_fusion), calls=%async_computation.3 | async-start | bytes 1048576 | tf_op jit(solution)/shard_map/all_to_all | solution.py:854
  148.0 0.6 dynamic_slice.18.counts
  148.6 0.6 pad_maximum_fusion.2.alpha
  149.2 0.3 fusion.4
  149.5 0.7 pad_maximum_fusion.1.refs_2_
  150.2 0.6 reduce_sum.25.refs_1_
  150.8 12.5 %all-to-all-done.3 = bf16[8,2,4,32,128]{4,3,2,1,0:T(8,128)(2,1)S(1)} async-done(((bf16[8,2,4,32,128]{4,3,2,1,0:T(8,128)(2,1)}), bf16[8,2,4,32,128]{4,3,2,1,0:T(8,128)(2,1)S(1)}, u32[]{:S(2)}, u32[]{:S(2)}) %all-to-all-start.3) | async-done | bytes 524320 | tf_op jit(solution)/shard_map/all_to_all | solution.py:854
  163.3 0.8 reduce_sum.24.refs_0_
  164.1 4.1 %detect.1 = f32[1,4,3,16]{3,2,1,0:T(4,128)} custom-call(f32[2,4,12]{2,1,0:T(4,128)} %pad_maximum_fusion.2.alpha, s32[1]{0:T(128)} %dynamic_slice.18.counts, bf16[4,2,4,32,128]{4,3,2,1,0:T(8,128)(2,1)} %reduce_sum.24.refs_0_, bf16[4,32,128]{2,1,0:T(8,128)(2,1)} %reduce_sum.25.refs_1_, f32[4,2,32,128]{3,2,1,0:T(8,128)} %pad_maximum_fusion.1.refs_2_, ...), custom_call_target="tpu_custom_call" | custom-call | tf_op jit(solution)/shard_map/detect/pallas_call | solution.py:646
  168.2 1.3 copy.32
  (65 shorter events, 1.4 us)
Async XLA Ops:
  0.0 17.3 %copy-start.8 = (s32[4,2]{0,1:T(2,128)S(1)}, s32[4,2]{0,1:T(2,128)}, u32[]{:S(2)}) copy-start(s32[4,2]{0,1:T(2,128)} %param.21) | copy-start | bytes 100
  0.0 18.6 %copy-start.9 = (s32[32,4]{0,1:T(4,128)S(1)}, s32[32,4]{0,1:T(4,128)}, u32[]{:S(2)}) copy-start(s32[32,4]{0,1:T(4,128)} %param.23) | copy-start | bytes 1540
  10.0 28.9 %all-to-all-start.1 = ((bf16[8,2,208,128]{3,2,1,0:T(8,128)(2,1)}), bf16[8,2,208,128]{3,2,1,0:T(8,128)(2,1)S(1)}, u32[]{:S(2)}, u32[]{:S(2)}) async-start(bf16[8,2,208,128]{3,2,1,0:T(8,128)(2,1)} %forward_x.3), calls=%async_computation.1 | async-start | bytes 1703936 | tf_op jit(solution)/shard_map/all_to_all | solution.py:755
  23.3 12.2 %copy-start.10 = (s32[128]{0:T(128)S(1)}, s32[128]{0:T(128)}, u32[]{:S(2)}) copy-start(s32[128]{0:T(128)} %constant.269.clone) | copy-start | bytes 1540
  38.9 5.5 %copy-start.3 = (bf16[8,2,208,128]{3,2,1,0:T(8,128)(2,1)}, bf16[8,2,208,128]{3,2,1,0:T(8,128)(2,1)S(1)}, u32[]{:S(2)}) copy-start(bf16[8,2,208,128]{3,2,1,0:T(8,128)(2,1)S(1)} %all-to-all-done.1.lines) | copy-start | bytes 2555908
  38.9 25.4 %all-to-all-start = ((bf16[8,2,208,128]{3,2,1,0:T(8,128)(2,1)}), bf16[8,2,208,128]{3,2,1,0:T(8,128)(2,1)S(1)}, u32[]{:S(2)}, u32[]{:S(2)}) async-start(bf16[8,2,208,128]{3,2,1,0:T(8,128)(2,1)} %order.3), calls=%async_computation | async-start | bytes 1703936 | tf_op jit(solution)/shard_map/all_to_all | solution.py:755
  42.9 21.4 %collective-permute-start = (bf16[8,2,208,128]{3,2,1,0:T(8,128)(2,1)S(1)}, bf16[8,2,208,128]{3,2,1,0:T(8,128)(2,1)S(1)}, u32[]{:S(2)}, u32[]{:S(2)}) collective-permute-start(bf16[8,2,208,128]{3,2,1,0:T(8,128)(2,1)S(1)} %all-to-all-done.1.lines), channel_id=1, source_target_pairs={{0,2},{1,3},{2,0},{3,1},{4,6},{5,7},{6,4},{7,5},{8,10},{9,11},{10,... | collective-permute-start | bytes 2555912 | tf_op jit(solution)/shard_map/ppermute | solution.py:761
  54.8 16.4 %copy-start.7 = (f32[4,1,128]{2,1,0:T(1,128)S(1)}, f32[4,1,128]{2,1,0:T(1,128)}, u32[]{:S(2)}) copy-start(f32[4,1,128]{2,1,0:T(1,128)} %multiply_convert_fusion.rest_2_) | copy-start | bytes 6148
  64.3 0.9 copy-start
  65.2 0.9 copy-start.4
  66.1 20.4 %collective-permute-start.2 = (bf16[8,2,208,128]{3,2,1,0:T(8,128)(2,1)}, bf16[8,2,208,128]{3,2,1,0:T(8,128)(2,1)S(1)}, u32[]{:S(2)}, u32[]{:S(2)}) collective-permute-start(bf16[8,2,208,128]{3,2,1,0:T(8,128)(2,1)} %order.4.lines.rest_0_), channel_id=1, source_target_pairs={{0,2},{1,3},{2,0},{3,1},{4,6},{5,7},{6,4},{7,5},{8,10},{9,11},{10,... | collective-permute-start | bytes 2555912 | tf_op jit(solution)/shard_map/ppermute | solution.py:761
  67.6 18.9 %all-to-all-start.2 = ((bf16[8,4,32,128]{3,2,1,0:T(8,128)(2,1)}), bf16[8,4,32,128]{3,2,1,0:T(8,128)(2,1)S(1)}, u32[]{:S(2)}, u32[]{:S(2)}) async-start(bf16[8,4,32,128]{3,2,1,0:T(8,128)(2,1)} %order.5), calls=%async_computation.2 | async-start | bytes 524288 | tf_op jit(solution)/shard_map/all_to_all | solution.py:755
  77.9 17.5 %collective-permute-start.1 = (bf16[32,208,128]{2,1,0:T(8,128)(2,1)}, bf16[32,208,128]{2,1,0:T(8,128)(2,1)S(1)}, u32[]{:S(2)}, u32[]{:S(2)}) collective-permute-start(bf16[32,208,128]{2,1,0:T(8,128)(2,1)} %forward_y.2.refs_0_), channel_id=1, source_target_pairs={{0,1},{1,0},{2,3},{3,2},{4,5},{5,4},{6,7},{7,6},{8,9},{9,8},{10,11... | collective-permute-start | bytes 5111816 | tf_op jit(solution)/shard_map/ppermute | solution.py:761
  86.6 0.7 copy-start.1
  87.3 0.9 copy-start.6
  94.3 9.5 %collective-permute-start.3 = (bf16[32,208,128]{2,1,0:T(8,128)(2,1)}, bf16[32,208,128]{2,1,0:T(8,128)(2,1)}, u32[]{:S(2)}, u32[]{:S(2)}) collective-permute-start(bf16[32,208,128]{2,1,0:T(8,128)(2,1)} %forward_y.3.refs_1_), channel_id=1, source_target_pairs={{0,1},{1,0},{2,3},{3,2},{4,5},{5,4},{6,7},{7,6},{8,9},{9,8},{10,11... | collective-permute-start | bytes 5111816 | tf_op jit(solution)/shard_map/ppermute | solution.py:761
  95.4 1.2 copy-start.5
  117.2 14.2 %collective-permute-start.6 = (bf16[16,2,4,16,128]{4,3,2,1,0:T(8,128)(2,1)}, bf16[16,2,4,16,128]{4,3,2,1,0:T(8,128)(2,1)S(1)}, u32[]{:S(2)}, u32[]{:S(2)}) collective-permute-start(bf16[16,2,4,16,128]{4,3,2,1,0:T(8,128)(2,1)} %get-tuple-element.12), channel_id=1, source_target_pairs={{0,8},{4,12},{8,0},{12,4},{16,24},{20,28},{24,16},{28,20},{1,9},{5... | collective-permute-start | bytes 1572872 | tf_op jit(solution)/shard_map/ppermute | solution.py:838
  119.3 14.9 %collective-permute-start.4 = (bf16[16,2,4,16,128]{4,3,2,1,0:T(8,128)(2,1)}, bf16[16,2,4,16,128]{4,3,2,1,0:T(8,128)(2,1)S(1)}, u32[]{:S(2)}, u32[]{:S(2)}) collective-permute-start(bf16[16,2,4,16,128]{4,3,2,1,0:T(8,128)(2,1)} %get-tuple-element.9.refs_4_), channel_id=1, source_target_pairs={{0,4},{4,0},{8,12},{12,8},{16,20},{20,16},{24,28},{28,24},{1,5},{5... | collective-permute-start | bytes 1572872 | tf_op jit(solution)/shard_map/ppermute | solution.py:838
  121.4 15.4 %copy-start.11 = (f32[4]{0:T(128)S(1)}, f32[4]{0:T(128)}, u32[]{:S(2)}) copy-start(f32[4]{0:T(128)} %param.22) | copy-start | bytes 52
  129.4 18.6 %copy-start.12 = (s32[32]{0:T(128)S(1)}, s32[32]{0:T(128)}, u32[]{:S(2)}) copy-start(s32[32]{0:T(128)} %param.24) | copy-start | bytes 388
  129.4 20.8 %copy-start.2 = (bf16[8,4,32,128]{3,2,1,0:T(8,128)(2,1)S(1)}, bf16[8,4,32,128]{3,2,1,0:T(8,128)(2,1)}, u32[]{:S(2)}) copy-start(bf16[8,4,32,128]{3,2,1,0:T(8,128)(2,1)} %copy-done.1) | copy-start | bytes 786436
  132.4 7.6 %collective-permute-start.7 = (bf16[8,2,4,16,128]{4,3,2,1,0:T(8,128)(2,1)S(1)}, bf16[8,2,4,16,128]{4,3,2,1,0:T(8,128)(2,1)S(1)}, u32[]{:S(2)}, u32[]{:S(2)}) collective-permute-start(bf16[8,2,4,16,128]{4,3,2,1,0:T(8,128)(2,1)S(1)} %add_convert_fusion.1), channel_id=1, source_target_pairs={{0,4},{4,0},{8,12},{12,8},{16,20},{20,16},{24,28},{28,24},{1,5},{5... | collective-permute-start | bytes 786440 | tf_op jit(solution)/shard_map/ppermute | solution.py:838
  135.3 7.2 %collective-permute-start.5 = (bf16[8,2,4,16,128]{4,3,2,1,0:T(8,128)(2,1)S(1)}, bf16[8,2,4,16,128]{4,3,2,1,0:T(8,128)(2,1)S(1)}, u32[]{:S(2)}, u32[]{:S(2)}) collective-permute-start(bf16[8,2,4,16,128]{4,3,2,1,0:T(8,128)(2,1)S(1)} %add_convert_fusion.3), channel_id=1, source_target_pairs={{0,8},{4,12},{8,0},{12,4},{16,24},{20,28},{24,16},{28,20},{1,9},{5... | collective-permute-start | bytes 786440 | tf_op jit(solution)/shard_map/ppermute | solution.py:838
  144.3 19.0 %all-to-all-start.3 = ((bf16[8,2,4,32,128]{4,3,2,1,0:T(8,128)(2,1)}), bf16[8,2,4,32,128]{4,3,2,1,0:T(8,128)(2,1)S(1)}, u32[]{:S(2)}, u32[]{:S(2)}) async-start(bf16[8,2,4,32,128]{4,3,2,1,0:T(8,128)(2,1)} %pad_maximum_fusion), calls=%async_computation.3 | async-start | bytes 1048576 | tf_op jit(solution)/shard_map/all_to_all | solution.py:854

commit v17 on v16

--- a/solution.py
+++ b/solution.py
@@ -367,7 +367,7 @@
             row_square = row_freq * row_freq
             values = []
             for x in range(near):
-                inside = row_square + square_x[x] <= limit
+                inside = row_square + square_x[which + x] <= limit
                 values.append(jnp.where(inside, specs[x][q].astype(F32), 0.0))
             for e in range(2):
                 half = [v[e * PART : (e + 1) * PART].astype(BF) for v in values]
@@ -429,7 +429,7 @@
             in_specs=[pl.BlockSpec((count, ROWS, LANES), lambda i, s: (early(i, s), 0, 0))] * near
             + [
                 pl.BlockSpec((ROWS, LANES), lambda i, s: (0, 0)),
-                pl.BlockSpec((near, 1, LANES), lambda i, s: (0, 0, 0)),
+                pl.BlockSpec(square_x.shape, lambda i, s: (0, 0, 0)),
                 pl.BlockSpec((count, 2, 2 * A, PART), lambda i, s: (early(i, s), 0, 0, 0)),
             ]
             + [table_spec(x) for x in range(near)]
@@ -501,7 +501,7 @@
 
         @pl.when((step == steps - 1) & (part_id == p))
         def _(device=device):
-            lax.fori_loop(0, devices, device, 0, unroll=4)
+            lax.fori_loop(0, devices, device, 0, unroll=16)
 
 
 def collect(sheets, k1_pairs, places, devices, which, after):
@@ -816,9 +816,8 @@
 
     def invert(stop, after):
         start = stop - len(ready)
-        limits = square_x[start:stop]
         waves.append(
-            inverse(start, scalars, ready[:], freq_y, limits, inverse_y, inverse_x, after)
+            inverse(start, scalars, ready[:], freq_y, square_x, inverse_y, inverse_x, after)
         )
         ready.clear()
 

time: 170 us -> 169 us (level)
    unnamed x27 -> x25, local copies, waits for them, and re-layouts: 4.66 us -> 4.67 us
  transfers between devices with their start and end apart: 12 -> 12, of which waited for: 6 -> 6; matrix products, arithmetic and copies ran while one was open for 10% -> 9% of each run, Pallas kernels for 33% -> 34%
where the time goes in v17:
time: 169 us; the launch traced here: 168 us
  Pallas kernels  84 us (50%)
  waiting for transfers between devices  29.7 us (18%)
  starting transfers between devices  29.2 us (17%)
  other arithmetic  12.7 us (8%)
  local copies, waits for them, and re-layouts  11.4 us (7%)
    pallas_call x2, Pallas kernels, forward_x(): pl.pallas_call(forward_x_kernel, grid_spec=pltpu.PrefetchScalarGridSpec(n...  19.9 us
    pallas_call x3, Pallas kernels, inverse(): pl.pallas_call(functools.partial(inverse_kernel, steps, which, near), gri...  18.1 us
    pallas_call x2, Pallas kernels, collect(): pl.pallas_call(functools.partial(collect_kernel, len(sheets)), grid_spec=...  15.8 us
    all_to_all x3, starting transfers between devices, trade(): return lax.all_to_all(value, axis, split_axis=0, concat_axis=0, tiled=True)  15.2 us
    all_to_all x1, waiting for transfers between devices, shards(): lax.all_to_all(tiles, ('beam', 'slab'), split_axis=0, concat_axis=0, axis...  12.5 us
    pallas_call x2, Pallas kernels, forward_y(): pl.pallas_call(forward_y_kernel, grid=(1 + steps,), in_specs=[pl.BlockSpe...  12.3 us
    all_to_all x3, waiting for transfers between devices, trade(): return lax.all_to_all(value, axis, split_axis=0, concat_axis=0, tiled=True)  10.9 us
    pallas_call x1, Pallas kernels, crop(): pl.pallas_call(crop_kernel, in_specs=[pl.BlockSpec(memory_space=pltpu.SME...  7.08 us
  transfers between devices with their start and end apart: 12, of which 6 were waited for; matrix products, arithmetic and copies ran while one was open for 9% of the time, Pallas kernels for 34%

profile of v17, /device:TPU:0, one launch (start us, length us, event | category | flops | bytes accessed | tf_op | source)
XLA Modules:
  0.0 168.5 jit_solution(13807818039950843463)
XLA Ops:
  0.0 10.0 %forward_x.3 = bf16[8,2,208,128]{3,2,1,0:T(8,128)(2,1)} custom-call(s32[1]{0:T(128)} %bitcast.3.sel, bf16[8,4,16,4096]{3,2,1,0:T(8,128)(2,1)} %bitcast.40, bf16[4,512,1024]{2,1,0:T(8,128)(2,1)} %constant.270.clone.section, bf16[4,8,208,256]{3,2,1,0:T(8,128)(2,1)} %constant.271.clone.last, bf16[128,128]{1,0:T(8,128)(2,1)} %constant.272.clone.perm), custom_call_target="tpu_custom_call" | custom-call | flops 1048576 | tf_op jit(solution)/shard_map/forward_x/pallas_call | solution.py:198
  10.0 7.3 %all-to-all-start.1 = ((bf16[8,2,208,128]{3,2,1,0:T(8,128)(2,1)}), bf16[8,2,208,128]{3,2,1,0:T(8,128)(2,1)S(1)}, u32[]{:S(2)}, u32[]{:S(2)}) async-start(bf16[8,2,208,128]{3,2,1,0:T(8,128)(2,1)} %forward_x.3), calls=%async_computation.1 | async-start | bytes 1703936 | tf_op jit(solution)/shard_map/all_to_all | solution.py:755
  17.4 0.6 fusion.22
  18.8 0.1 copy.28
  19.0 0.6 gather_fusion
  19.6 0.6 gather_fusion.1
  20.2 0.1 stack.55
  20.3 0.1 stack.54
  21.2 0.7 reshape.1008.rest_1_.sel
  21.8 1.3 fusion.13
  23.2 0.1 copy.31
  23.4 10.0 %forward_x.2.value = bf16[8,2,208,128]{3,2,1,0:T(8,128)(2,1)} custom-call(s32[1]{0:T(128)} %bitcast.3.sel, bf16[8,4,16,4096]{3,2,1,0:T(8,128)(2,1)} %bitcast.41, bf16[4,512,1024]{2,1,0:T(8,128)(2,1)} %constant.270.clone.section, bf16[4,8,208,256]{3,2,1,0:T(8,128)(2,1)} %constant.271.clone.last, bf16[128,128]{1,0:T(8,128)(2,1)} %constant.272.clone.perm), custom_call_target="tpu_custom_call" | custom-call | flops 1048576 | tf_op jit(solution)/shard_map/forward_x/pallas_call | solution.py:198
  33.4 0.6 broadcast_add_fusion
  34.0 0.6 compare_convert_fusion
  34.6 0.6 and_select_fusion.5
  35.2 0.6 and_select_fusion.6
  35.7 0.7 multiply_convert_fusion.rest_2_.refs_2_.refs_3_
  36.4 0.8 broadcast_in_dim.2.rest_0_.refs_3_
  37.2 1.7 all-to-all-done.1.lines
  38.9 4.3 %all-to-all-start = ((bf16[8,2,208,128]{3,2,1,0:T(8,128)(2,1)}), bf16[8,2,208,128]{3,2,1,0:T(8,128)(2,1)S(1)}, u32[]{:S(2)}, u32[]{:S(2)}) async-start(bf16[8,2,208,128]{3,2,1,0:T(8,128)(2,1)} %order.3), calls=%async_computation | async-start | bytes 1703936 | tf_op jit(solution)/shard_map/all_to_all | solution.py:755
  43.2 1.5 collective-permute-start
  44.7 3.3 %forward_y_first.2.after.earlier = bf16[64,2,32,128]{3,2,1,0:T(8,128)(2,1)} custom-call(bf16[8,2,208,128]{3,2,1,0:T(8,128)(2,1)} %copy-done.3, bf16[512,256]{1,0:T(8,128)(2,1)} %constant.273.clone.section), custom_call_target="tpu_custom_call" | custom-call | flops 1048576 | tf_op jit(solution)/shard_map/forward_y_first/pallas_call | solution.py:270
  48.0 7.1 %crop.1.rest_0_ = bf16[32,32,128]{2,1,0:T(8,128)(2,1)} custom-call(s32[32]{0:T(128)} %get-tuple-element.38.rest_3_.rows, s32[32]{0:T(128)} %get-tuple-element.37.rest_4_.cols, s32[32]{0:T(128)} %get-tuple-element.16.rest_5_.odd, s32[32]{0:T(128)} %get-tuple-element.13.rest_6_.mine, bf16[512,4096]{1,0:T(8,128)(2,1)} %pot.1, ...), custom_call_target="tpu_custom_call" | custom-call | flops 1048576 | tf_op jit(solution)/shard_map/crop/pallas_call | solution.py:575
  55.1 9.3 %all-to-all-done.value = bf16[8,2,208,128]{3,2,1,0:T(8,128)(2,1)S(1)} async-done(((bf16[8,2,208,128]{3,2,1,0:T(8,128)(2,1)}), bf16[8,2,208,128]{3,2,1,0:T(8,128)(2,1)S(1)}, u32[]{:S(2)}, u32[]{:S(2)}) %all-to-all-start) | async-done | bytes 852000 | tf_op jit(solution)/shard_map/all_to_all | solution.py:755
  64.4 0.9 copy-done
  65.3 0.9 copy-done.4
  66.2 1.5 collective-permute-start.2
  67.7 3.6 %all-to-all-start.2 = ((bf16[8,4,32,128]{3,2,1,0:T(8,128)(2,1)}), bf16[8,4,32,128]{3,2,1,0:T(8,128)(2,1)S(1)}, u32[]{:S(2)}, u32[]{:S(2)}) async-start(bf16[8,4,32,128]{3,2,1,0:T(8,128)(2,1)} %order.5), calls=%async_computation.2 | async-start | bytes 524288 | tf_op jit(solution)/shard_map/all_to_all | solution.py:755
  71.3 6.1 %forward_y.2.refs_0_ = bf16[32,208,128]{2,1,0:T(8,128)(2,1)} custom-call(bf16[8,2,208,128]{3,2,1,0:T(8,128)(2,1)} %order.4.lines.rest_0_, bf16[512,256]{1,0:T(8,128)(2,1)} %constant.273.clone.section, bf16[64,2,32,128]{3,2,1,0:T(8,128)(2,1)} %forward_y_first.2.after.earlier, bf16[32,208,256]{2,1,0:T(8,128)(2,1)} %constant.274.clone.last), custom_call_target="tpu_custom_call" | custom-call | flops 1048576 | tf_op jit(solution)/shard_map/forward_y/pallas_call | solution.py:316
  77.4 5.4 %inverse.3.rest_1_.refs_0_ = bf16[32,128,256]{2,1,0:T(8,128)(2,1)} custom-call(s32[12]{0:T(128)} %reshape.1008.rest_1_.sel, bf16[32,208,128]{2,1,0:T(8,128)(2,1)} %forward_y.2.refs_0_, f32[208,128]{1,0:T(8,128)} %constant.275.clone.refs_1_.refs_2_, f32[4,1,128]{2,1,0:T(1,128)} %multiply_convert_fusion.rest_2_.refs_2_.refs_3_, ...), custom_call_target="tpu_custom_call" | custom-call | flops 1048576 | tf_op jit(solution)/shard_map/inverse/pallas_call | solution.py:424
  82.8 3.3 %forward_y_first.3.earlier = bf16[64,2,32,128]{3,2,1,0:T(8,128)(2,1)} custom-call(bf16[8,2,208,128]{3,2,1,0:T(8,128)(2,1)} %copy-done.4, bf16[512,256]{1,0:T(8,128)(2,1)} %constant.273.clone.section), custom_call_target="tpu_custom_call" | custom-call | flops 1048576 | tf_op jit(solution)/shard_map/forward_y_first/pallas_call | solution.py:270
  86.2 0.7 copy-done.1
  86.9 0.9 copy-done.6
  87.8 6.1 %forward_y.3.refs_1_ = bf16[32,208,128]{2,1,0:T(8,128)(2,1)} custom-call(bf16[8,2,208,128]{3,2,1,0:T(8,128)(2,1)} %copy-done.6, bf16[512,256]{1,0:T(8,128)(2,1)} %constant.273.clone.section, bf16[64,2,32,128]{3,2,1,0:T(8,128)(2,1)} %forward_y_first.3.earlier, bf16[32,208,256]{2,1,0:T(8,128)(2,1)} %constant.274.clone.last, bf16[8,4,32,128]{3,2,1,0:T(8,128)(2,1)} %copy-done.1, ...), custom_call_target="tpu_custom_call" | custom-call | flops 1048576 | tf_op jit(solution)/shard_map/forward_y/pallas_call | solution.py:316
  93.9 0.5 collective-permute-start.3
  94.4 1.2 copy-done.5
  95.6 7.3 %inverse.4.refs_5_.refs_1_ = bf16[32,256,256]{2,1,0:T(8,128)(2,1)} custom-call(s32[12]{0:T(128)} %reshape.1008.rest_1_.sel, bf16[32,208,128]{2,1,0:T(8,128)(2,1)} %copy-done.5, bf16[32,208,128]{2,1,0:T(8,128)(2,1)} %forward_y.3.refs_1_, f32[208,128]{1,0:T(8,128)} %constant.275.clone.refs_1_.refs_2_, ...), custom_call_target="tpu_custom_call" | custom-call | flops 1048576 | tf_op jit(solution)/shard_map/inverse/pallas_call | solution.py:424
  102.9 5.5 %inverse.5.refs_2_ = bf16[32,128,256]{2,1,0:T(8,128)(2,1)} custom-call(s32[12]{0:T(128)} %reshape.1008.rest_1_.sel, bf16[32,208,128]{2,1,0:T(8,128)(2,1)} %collective-permute-done.3.refs_0_, f32[208,128]{1,0:T(8,128)} %constant.275.clone.refs_1_.refs_2_, f32[4,1,128]{2,1,0:T(1,128)} %multiply_convert_fusion.rest_2_.refs_2_.refs_3_, ...), custom_call_target="tpu_custom_call" | custom-call | flops 1048576 | tf_op jit(solution)/shard_map/inverse/pallas_call | solution.py:424
  108.4 7.9 %collect.2 = (bf16[16,2,4,16,128]{4,3,2,1,0:T(8,128)(2,1)}, bf16[16,2,4,16,128]{4,3,2,1,0:T(8,128)(2,1)}) custom-call(s32[4]{0:T(128)} %get-tuple-element.19.k1_pairs, bf16[32,128,256]{2,1,0:T(8,128)(2,1)} %inverse.3.rest_1_.refs_0_, bf16[32,256,256]{2,1,0:T(8,128)(2,1)} %inverse.4.refs_5_.refs_1_, bf16[32,128,256]{2,1,0:T(8,128)(2,1)} %inverse.5.refs_2_, ...), custom_call_target="tpu_custom_call" | custom-call | flops 1048576 | tf_op jit(solution)/shard_map/collect/pallas_call | solution.py:518
  116.2 1.9 %collective-permute-start.6 = (bf16[16,2,4,16,128]{4,3,2,1,0:T(8,128)(2,1)}, bf16[16,2,4,16,128]{4,3,2,1,0:T(8,128)(2,1)S(1)}, u32[]{:S(2)}, u32[]{:S(2)}) collective-permute-start(bf16[16,2,4,16,128]{4,3,2,1,0:T(8,128)(2,1)} %get-tuple-element.12), channel_id=1, source_target_pairs={{0,8},{4,12},{8,0},{12,4},{16,24},{20,28},{24,16},{28,20},{1,9},{5... | collective-permute-start | bytes 1572872 | tf_op jit(solution)/shard_map/ppermute | solution.py:837
  118.1 0.2 dynamic-slice_reduce_fusion
  118.3 1.5 collective-permute-start.4
  120.4 8.0 %collect.3 = (bf16[16,2,4,16,128]{4,3,2,1,0:T(8,128)(2,1)}, bf16[16,2,4,16,128]{4,3,2,1,0:T(8,128)(2,1)}) custom-call(s32[4]{0:T(128)} %get-tuple-element.19.k1_pairs, bf16[32,128,256]{2,1,0:T(8,128)(2,1)} %inverse.3.rest_1_.refs_0_, bf16[32,256,256]{2,1,0:T(8,128)(2,1)} %inverse.4.refs_5_.refs_1_, bf16[32,128,256]{2,1,0:T(8,128)(2,1)} %inverse.5.refs_2_, ...), custom_call_target="tpu_custom_call" | custom-call | flops 1048576 | tf_op jit(solution)/shard_map/collect/pallas_call | solution.py:518
  128.3 2.0 %collective-permute-done.6 = bf16[16,2,4,16,128]{4,3,2,1,0:T(8,128)(2,1)S(1)} collective-permute-done((bf16[16,2,4,16,128]{4,3,2,1,0:T(8,128)(2,1)}, bf16[16,2,4,16,128]{4,3,2,1,0:T(8,128)(2,1)S(1)}, u32[]{:S(2)}, u32[]{:S(2)}) %collective-permute-start.6) | collective-permute-done | bytes 524320 | tf_op jit(solution)/shard_map/ppermute | solution.py:837
  130.4 1.0 add_convert_fusion.1
  131.4 1.8 %collective-permute-start.7 = (bf16[8,2,4,16,128]{4,3,2,1,0:T(8,128)(2,1)S(1)}, bf16[8,2,4,16,128]{4,3,2,1,0:T(8,128)(2,1)S(1)}, u32[]{:S(2)}, u32[]{:S(2)}) collective-permute-start(bf16[8,2,4,16,128]{4,3,2,1,0:T(8,128)(2,1)S(1)} %add_convert_fusion.1), channel_id=1, source_target_pairs={{0,4},{4,0},{8,12},{12,8},{16,20},{20,16},{24,28},{28,24},{1,5},{5... | collective-permute-start | bytes 786440 | tf_op jit(solution)/shard_map/ppermute | solution.py:837
  133.2 1.0 add_convert_fusion.3
  134.2 1.6 collective-permute-start.5
  135.8 0.1 fusion.21
  136.0 2.9 %collective-permute-done.7 = bf16[8,2,4,16,128]{4,3,2,1,0:T(8,128)(2,1)S(1)} collective-permute-done((bf16[8,2,4,16,128]{4,3,2,1,0:T(8,128)(2,1)S(1)}, bf16[8,2,4,16,128]{4,3,2,1,0:T(8,128)(2,1)S(1)}, u32[]{:S(2)}, u32[]{:S(2)}) %collective-permute-start.7) | collective-permute-done | bytes 262176 | tf_op jit(solution)/shard_map/ppermute | solution.py:837
  138.9 1.1 add_convert_fusion
  140.0 1.3 collective-permute-done.5
  141.3 1.1 add_convert_fusion.2
  142.4 0.8 pad_maximum_fusion
  143.2 3.7 %all-to-all-start.3 = ((bf16[8,2,4,32,128]{4,3,2,1,0:T(8,128)(2,1)}), bf16[8,2,4,32,128]{4,3,2,1,0:T(8,128)(2,1)S(1)}, u32[]{:S(2)}, u32[]{:S(2)}) async-start(bf16[8,2,4,32,128]{4,3,2,1,0:T(8,128)(2,1)} %pad_maximum_fusion), calls=%async_computation.3 | async-start | bytes 1048576 | tf_op jit(solution)/shard_map/all_to_all | solution.py:853
  147.0 0.6 dynamic_slice.18.counts
  147.5 0.6 pad_maximum_fusion.2.alpha
  148.2 0.3 fusion.4
  148.5 0.7 pad_maximum_fusion.1.refs_2_
  149.2 0.6 reduce_sum.25.refs_1_
  149.8 12.5 %all-to-all-done.3 = bf16[8,2,4,32,128]{4,3,2,1,0:T(8,128)(2,1)S(1)} async-done(((bf16[8,2,4,32,128]{4,3,2,1,0:T(8,128)(2,1)}), bf16[8,2,4,32,128]{4,3,2,1,0:T(8,128)(2,1)S(1)}, u32[]{:S(2)}, u32[]{:S(2)}) %all-to-all-start.3) | async-done | bytes 524320 | tf_op jit(solution)/shard_map/all_to_all | solution.py:853
  162.3 0.8 reduce_sum.24.refs_0_
  163.1 4.1 %detect.1 = f32[1,4,3,16]{3,2,1,0:T(4,128)} custom-call(f32[2,4,12]{2,1,0:T(4,128)} %pad_maximum_fusion.2.alpha, s32[1]{0:T(128)} %dynamic_slice.18.counts, bf16[4,2,4,32,128]{4,3,2,1,0:T(8,128)(2,1)} %reduce_sum.24.refs_0_, bf16[4,32,128]{2,1,0:T(8,128)(2,1)} %reduce_sum.25.refs_1_, f32[4,2,32,128]{3,2,1,0:T(8,128)} %pad_maximum_fusion.1.refs_2_, ...), custom_call_target="tpu_custom_call" | custom-call | tf_op jit(solution)/shard_map/detect/pallas_call | solution.py:646
  167.2 1.3 copy.32
  (61 shorter events, 1.3 us)
Async XLA Ops:
  0.0 17.3 %copy-start.7 = (s32[4,2]{0,1:T(2,128)S(1)}, s32[4,2]{0,1:T(2,128)}, u32[]{:S(2)}) copy-start(s32[4,2]{0,1:T(2,128)} %param.21) | copy-start | bytes 100
  0.0 18.7 %copy-start.8 = (s32[32,4]{0,1:T(4,128)S(1)}, s32[32,4]{0,1:T(4,128)}, u32[]{:S(2)}) copy-start(s32[32,4]{0,1:T(4,128)} %param.23) | copy-start | bytes 1540
  10.0 28.9 %all-to-all-start.1 = ((bf16[8,2,208,128]{3,2,1,0:T(8,128)(2,1)}), bf16[8,2,208,128]{3,2,1,0:T(8,128)(2,1)S(1)}, u32[]{:S(2)}, u32[]{:S(2)}) async-start(bf16[8,2,208,128]{3,2,1,0:T(8,128)(2,1)} %forward_x.3), calls=%async_computation.1 | async-start | bytes 1703936 | tf_op jit(solution)/shard_map/all_to_all | solution.py:755
  23.4 12.3 %copy-start.9 = (s32[128]{0:T(128)S(1)}, s32[128]{0:T(128)}, u32[]{:S(2)}) copy-start(s32[128]{0:T(128)} %constant.269.clone) | copy-start | bytes 1540
  38.9 5.8 %copy-start.3 = (bf16[8,2,208,128]{3,2,1,0:T(8,128)(2,1)}, bf16[8,2,208,128]{3,2,1,0:T(8,128)(2,1)S(1)}, u32[]{:S(2)}) copy-start(bf16[8,2,208,128]{3,2,1,0:T(8,128)(2,1)S(1)} %all-to-all-done.1.lines) | copy-start | bytes 2555908
  38.9 25.5 %all-to-all-start = ((bf16[8,2,208,128]{3,2,1,0:T(8,128)(2,1)}), bf16[8,2,208,128]{3,2,1,0:T(8,128)(2,1)S(1)}, u32[]{:S(2)}, u32[]{:S(2)}) async-start(bf16[8,2,208,128]{3,2,1,0:T(8,128)(2,1)} %order.3), calls=%async_computation | async-start | bytes 1703936 | tf_op jit(solution)/shard_map/all_to_all | solution.py:755
  43.2 21.2 %collective-permute-start = (bf16[8,2,208,128]{3,2,1,0:T(8,128)(2,1)S(1)}, bf16[8,2,208,128]{3,2,1,0:T(8,128)(2,1)S(1)}, u32[]{:S(2)}, u32[]{:S(2)}) collective-permute-start(bf16[8,2,208,128]{3,2,1,0:T(8,128)(2,1)S(1)} %all-to-all-done.1.lines), channel_id=1, source_target_pairs={{0,2},{1,3},{2,0},{3,1},{4,6},{5,7},{6,4},{7,5},{8,10},{9,11},{10,... | collective-permute-start | bytes 2555912 | tf_op jit(solution)/shard_map/ppermute | solution.py:761
  64.4 0.9 copy-start
  65.3 0.9 copy-start.4
  66.2 20.0 %collective-permute-start.2 = (bf16[8,2,208,128]{3,2,1,0:T(8,128)(2,1)}, bf16[8,2,208,128]{3,2,1,0:T(8,128)(2,1)S(1)}, u32[]{:S(2)}, u32[]{:S(2)}) collective-permute-start(bf16[8,2,208,128]{3,2,1,0:T(8,128)(2,1)} %order.4.lines.rest_0_), channel_id=1, source_target_pairs={{0,2},{1,3},{2,0},{3,1},{4,6},{5,7},{6,4},{7,5},{8,10},{9,11},{10,... | collective-permute-start | bytes 2555912 | tf_op jit(solution)/shard_map/ppermute | solution.py:761
  67.7 18.5 %all-to-all-start.2 = ((bf16[8,4,32,128]{3,2,1,0:T(8,128)(2,1)}), bf16[8,4,32,128]{3,2,1,0:T(8,128)(2,1)S(1)}, u32[]{:S(2)}, u32[]{:S(2)}) async-start(bf16[8,4,32,128]{3,2,1,0:T(8,128)(2,1)} %order.5), calls=%async_computation.2 | async-start | bytes 524288 | tf_op jit(solution)/shard_map/all_to_all | solution.py:755
  77.4 17.0 %collective-permute-start.1 = (bf16[32,208,128]{2,1,0:T(8,128)(2,1)}, bf16[32,208,128]{2,1,0:T(8,128)(2,1)S(1)}, u32[]{:S(2)}, u32[]{:S(2)}) collective-permute-start(bf16[32,208,128]{2,1,0:T(8,128)(2,1)} %forward_y.2.refs_0_), channel_id=1, source_target_pairs={{0,1},{1,0},{2,3},{3,2},{4,5},{5,4},{6,7},{7,6},{8,9},{9,8},{10,11... | collective-permute-start | bytes 5111816 | tf_op jit(solution)/shard_map/ppermute | solution.py:761
  86.2 0.7 copy-start.1
  86.9 0.9 copy-start.6
  93.9 9.0 %collective-permute-start.3 = (bf16[32,208,128]{2,1,0:T(8,128)(2,1)}, bf16[32,208,128]{2,1,0:T(8,128)(2,1)}, u32[]{:S(2)}, u32[]{:S(2)}) collective-permute-start(bf16[32,208,128]{2,1,0:T(8,128)(2,1)} %forward_y.3.refs_1_), channel_id=1, source_target_pairs={{0,1},{1,0},{2,3},{3,2},{4,5},{5,4},{6,7},{7,6},{8,9},{9,8},{10,11... | collective-permute-start | bytes 5111816 | tf_op jit(solution)/shard_map/ppermute | solution.py:761
  94.4 1.2 copy-start.5
  116.2 14.1 %collective-permute-start.6 = (bf16[16,2,4,16,128]{4,3,2,1,0:T(8,128)(2,1)}, bf16[16,2,4,16,128]{4,3,2,1,0:T(8,128)(2,1)S(1)}, u32[]{:S(2)}, u32[]{:S(2)}) collective-permute-start(bf16[16,2,4,16,128]{4,3,2,1,0:T(8,128)(2,1)} %get-tuple-element.12), channel_id=1, source_target_pairs={{0,8},{4,12},{8,0},{12,4},{16,24},{20,28},{24,16},{28,20},{1,9},{5... | collective-permute-start | bytes 1572872 | tf_op jit(solution)/shard_map/ppermute | solution.py:837
  118.3 14.9 %collective-permute-start.4 = (bf16[16,2,4,16,128]{4,3,2,1,0:T(8,128)(2,1)}, bf16[16,2,4,16,128]{4,3,2,1,0:T(8,128)(2,1)S(1)}, u32[]{:S(2)}, u32[]{:S(2)}) collective-permute-start(bf16[16,2,4,16,128]{4,3,2,1,0:T(8,128)(2,1)} %get-tuple-element.9.refs_4_), channel_id=1, source_target_pairs={{0,4},{4,0},{8,12},{12,8},{16,20},{20,16},{24,28},{28,24},{1,5},{5... | collective-permute-start | bytes 1572872 | tf_op jit(solution)/shard_map/ppermute | solution.py:837
  120.3 15.5 %copy-start.10 = (f32[4]{0:T(128)S(1)}, f32[4]{0:T(128)}, u32[]{:S(2)}) copy-start(f32[4]{0:T(128)} %param.22) | copy-start | bytes 52
  128.3 18.6 %copy-start.11 = (s32[32]{0:T(128)S(1)}, s32[32]{0:T(128)}, u32[]{:S(2)}) copy-start(s32[32]{0:T(128)} %param.24) | copy-start | bytes 388
  128.3 20.8 %copy-start.2 = (bf16[8,4,32,128]{3,2,1,0:T(8,128)(2,1)S(1)}, bf16[8,4,32,128]{3,2,1,0:T(8,128)(2,1)}, u32[]{:S(2)}) copy-start(bf16[8,4,32,128]{3,2,1,0:T(8,128)(2,1)} %copy-done.1) | copy-start | bytes 786436
  131.4 7.5 %collective-permute-start.7 = (bf16[8,2,4,16,128]{4,3,2,1,0:T(8,128)(2,1)S(1)}, bf16[8,2,4,16,128]{4,3,2,1,0:T(8,128)(2,1)S(1)}, u32[]{:S(2)}, u32[]{:S(2)}) collective-permute-start(bf16[8,2,4,16,128]{4,3,2,1,0:T(8,128)(2,1)S(1)} %add_convert_fusion.1), channel_id=1, source_target_pairs={{0,4},{4,0},{8,12},{12,8},{16,20},{20,16},{24,28},{28,24},{1,5},{5... | collective-permute-start | bytes 786440 | tf_op jit(solution)/shard_map/ppermute | solution.py:837
  134.2 7.1 %collective-permute-start.5 = (bf16[8,2,4,16,128]{4,3,2,1,0:T(8,128)(2,1)S(1)}, bf16[8,2,4,16,128]{4,3,2,1,0:T(8,128)(2,1)S(1)}, u32[]{:S(2)}, u32[]{:S(2)}) collective-permute-start(bf16[8,2,4,16,128]{4,3,2,1,0:T(8,128)(2,1)S(1)} %add_convert_fusion.3), channel_id=1, source_target_pairs={{0,8},{4,12},{8,0},{12,4},{16,24},{20,28},{24,16},{28,20},{1,9},{5... | collective-permute-start | bytes 786440 | tf_op jit(solution)/shard_map/ppermute | solution.py:837
  143.2 19.1 %all-to-all-start.3 = ((bf16[8,2,4,32,128]{4,3,2,1,0:T(8,128)(2,1)}), bf16[8,2,4,32,128]{4,3,2,1,0:T(8,128)(2,1)S(1)}, u32[]{:S(2)}, u32[]{:S(2)}) async-start(bf16[8,2,4,32,128]{4,3,2,1,0:T(8,128)(2,1)} %pad_maximum_fusion), calls=%async_computation.3 | async-start | bytes 1048576 | tf_op jit(solution)/shard_map/all_to_all | solution.py:853
